TPU v7x, 32 devices: a whole 2x2x4 slice. The times are simulated.
32 devices in a mesh: grp: 2 (over x), lon: 16 (over z, y, core), lat: 1.
Axes of the slice: x: 2, y: 2, z: 4, core: 2. Of those that a mesh axis runs over, the one named last changes fastest.
Arguments:
- tokens: bfloat16 [4, 8, 128, 1536], P('grp', 'lat', 'lon'), parts along dimension 0, may hold values from -6 to 6
- land: int32 [16, 128], P(('grp', 'lat'), 'lon'), parts along dimension 0, may hold values 0 or 1
- surface: float32 [2, 1536], replicated, may hold values from -4 to 4
- gain: float32 [1536], replicated, may hold values from 0.25 to 1.75
- weights: bfloat16 [1536, 3072], P('lon'), may hold values from -0.15625 to 0.15625
- shifts: int32 [2, 2], replicated, may hold values from 1 to 7, as said below
- index_table: int32 [64, 64], replicated, may hold values from 0 to 224
- bias_table: float32 [2, 225, 12], P('lat'), as said below
- cotangent: bfloat16 [4, 8, 128, 1536], P('grp', 'lat', 'lon'), parts along dimension 0, may hold values from -6 to 6
Outputs:
- output: bfloat16 [4, 8, 128, 1536], P('grp', 'lat', 'lon'), parts along dimension 0
- grad_tokens: bfloat16 [4, 8, 128, 1536], P('grp', 'lat', 'lon'), parts along dimension 0
- grad_weights: float32 [3072, 3072], P(('grp', 'lon')), parts along dimension 0
There are 2 independent parts, one for each index of `grp`. A program takes and returns all parts, laid end to end along the dimension named above; an argument that names none is the same for every part. Nothing has to cross between parts.
Inputs may be any that keep to these rules, and one draw needn't show every extreme that they name: `shifts`: row l holds level l's offsets along latitude and longitude; taken together the entries include 1 and 7. `bias_table`: every entry is finite.
All inputs are finite; a program needn't handle non-finite values. No bound on the sum of `land` on one device may be relied on, other than what follows from the above.
Results may differ from a plain program's by a relative error of at most 0.023.
Values may be sent and summed in bfloat16 or wider, within the bound.
No kernel may reach another device: no remote copies, remote signals or barrier semaphores. Data moves between devices by JAX's collectives and lax.ppermute only.
A program may use at most 128 MiB of HBM per device.

v0:
```python
import functools
import math

import jax
import jax.numpy as jnp
from jax import lax
from jax.experimental import pallas as pl
from jax.experimental.pallas import tpu as pltpu
from jax.sharding import Mesh
from jax.sharding import PartitionSpec as P

epsilon = 1e-05
LON = ("far", "near", "side", "core")


def along_lon(shard, by):
    count = math.prod(lax.axis_size(axis) for axis in LON)
    return lax.ppermute(shard, LON, [(i, (i + by) % count) for i in range(count)])


def along_lat(shard, by):
    count = lax.axis_size("lat")
    return lax.ppermute(shard, "lat", [(i, (i + by) % count) for i in range(count)])


def swap(shard, axis):
    return lax.ppermute(shard, axis, [(0, 1), (1, 0)])


def pick(rows, cols, levels, side, over_rows):
    tile = levels * side * side
    shape = (tile, 2 * tile)
    target = lax.broadcasted_iota(jnp.int32, shape, 0)
    source = lax.broadcasted_iota(jnp.int32, shape, 1)
    level = target // (side * side)
    row = target // side % side
    col = target % side
    from_row = jnp.full_like(row, rows[levels - 1])
    from_col = jnp.full_like(col, cols[levels - 1])
    for l in range(levels - 1):
        from_row = jnp.where(level == l, rows[l], from_row)
        from_col = jnp.where(level == l, cols[l], from_col)
    from_row = row + from_row
    from_col = col + from_col
    which = (from_row if over_rows else from_col) // side
    wanted = which * tile + level * side * side + from_row % side * side + from_col % side
    return (source == wanted).astype(jnp.bfloat16)


def picked(onehot, first, second):
    both = jnp.concatenate([first, second], axis=0)
    return jnp.dot(onehot, both, preferred_element_type=jnp.float32).astype(jnp.bfloat16)


def roll_back(field, shifts, levels, side):
    zeros = jnp.zeros_like(shifts[:, 0])
    rows = side - shifts[:, 0]
    more = lax.axis_size("lat") > 1
    field = picked(
        pick(zeros if more else rows, side - shifts[:, 1], levels, side, False),
        along_lon(field, 1),
        field,
    )
    if more:
        field = picked(pick(rows, zeros, levels, side, True), along_lat(field, 1), field)
    return field


def turned_rolls(info_ref, gain_ref, *refs):
    fields, (kept_ref, sent_ref, both_ref, turned_ref, sems) = refs[:4], refs[4:]
    tile = fields[0].shape[0]
    rows = kept_ref.shape[1] // 8
    levels, side = 2, 8
    area = tile // levels
    copies = [
        pltpu.make_async_copy(field, both_ref.at[i // 2, pl.ds(i % 2 * tile, tile), :], sems.at[i])
        for i, field in enumerate(fields)
    ]
    for copy in copies:
        copy.start()
    target = lax.broadcasted_iota(jnp.int32, (tile, 2 * tile), 0)
    source = lax.broadcasted_iota(jnp.int32, (tile, 2 * tile), 1)
    upper = target < area
    row = ((target >> 3) & 7) + jnp.where(upper, info_ref[0], info_ref[2])
    col = (target & 7) + jnp.where(upper, info_ref[1], info_ref[3])
    wanted = jnp.where(col >= side, tile, 0) + jnp.where(upper, 0, area) + (row & 7) * side + (col & 7)
    onehot = jnp.where(source == wanted, 1.0, 0.0).astype(jnp.bfloat16)
    for k in (1, 0):
        copies[2 * k].wait()
        copies[2 * k + 1].wait()
        rolled = jnp.dot(onehot, both_ref[k], preferred_element_type=jnp.float32)
        if k == 0:
            center = rolled - jnp.mean(rolled, axis=-1, keepdims=True)
            spread = lax.rsqrt(jnp.mean(center * center, axis=-1, keepdims=True) + epsilon)
            rolled = center * spread * gain_ref[...]
        turned_ref[...] = rolled.T.astype(jnp.bfloat16)
        for i in range(8):
            at = pl.ds(i * rows, rows)
            kept_ref[k, at, :] = turned_ref[pl.ds(pl.multiple_of(info_ref[4 + i] * rows, 16), rows), :]
            sent_ref[k, at, :] = turned_ref[pl.ds(pl.multiple_of(info_ref[12 + i] * rows, 16), rows), :]


def down(a, b):
    return lax.dot_general(a, b, (((0,), (0,)), ((), ())), preferred_element_type=jnp.float32)


def across(a, b):
    return lax.dot_general(a, b, (((1,), (1,)), ((), ())), preferred_element_type=jnp.float32)


def products_kernel(place_ref, *refs):
    tiles, pieces = refs[:4], refs[4:12]
    kept_ref, sent_ref, full_ref, tile_ref, w_ref, sems, out_sem = refs[12:]
    tile = tiles[0].shape[2]
    part = w_ref.shape[1] // 4
    copies = []
    for i, piece in enumerate(pieces):
        rows = pl.ds(pl.multiple_of(place_ref[i] * piece.shape[0], 16), piece.shape[0])
        copies.append(pltpu.make_async_copy(piece, w_ref.at[rows, :], sems.at[i]))
    for j, source in enumerate(tiles):
        copies.append(pltpu.make_async_copy(source, tile_ref.at[j], sems.at[8 + j]))
    for copy in copies:
        copy.start()
    for copy in copies:
        copy.wait()
    out_copy = pltpu.make_async_copy(w_ref, full_ref, out_sem)
    out_copy.start()
    for j in (1, 3, 0, 2):
        rows = pl.ds(j // 2 * tile, tile)
        for n in range(4):
            cols = pl.ds(n * part, part)
            product = down(tile_ref[j, n // 3], w_ref[:, cols])
            if j % 2:
                sent_ref[rows, cols] = product.astype(jnp.bfloat16)
            else:
                kept_ref[rows, cols] = product
    out_copy.wait()


def attention_kernel(area, head, kept_ref, came_ref, bias_ref, grad_ref, qkv_ref, scores_ref, toward_ref, probs_ref, back_ref):
    part = grad_ref.shape[1] // 4
    levels, pairs = bias_ref.shape[:2]
    scale = 1.0 / math.sqrt(head)
    lane = lax.broadcasted_iota(jnp.int32, (area, 2 * head), 1)
    left = lane < head

    def stacked(pair):
        zero = jnp.zeros_like(pair)
        return jnp.concatenate([jnp.where(left, pair, zero), jnp.where(left, zero, pair)], axis=0)

    def unstacked(product):
        return jnp.where(left, product[:area], product[area:]).astype(jnp.bfloat16)

    windows = grad_ref.shape[0] // area
    groups = [(w * pairs + p, w, p) for w in range(windows) for p in range(pairs)]

    def view(w, p, n):
        return pl.ds(w * area, area), pl.ds(n * part + p * 2 * head, 2 * head)

    qkv_ref[...] = (kept_ref[...] + came_ref[...].astype(jnp.float32)).astype(jnp.bfloat16)
    for g, w, p in groups:
        scores_ref[g] = across(stacked(qkv_ref[view(w, p, 0)]), qkv_ref[view(w, p, 1)])
        toward_ref[g] = across(stacked(qkv_ref[view(w, p, 3)]), qkv_ref[view(w, p, 2)])
    for g, w, p in groups:
        scores = scores_ref[g] * scale + bias_ref[w % levels, p]
        expo = jnp.exp(scores - jnp.max(scores, axis=-1, keepdims=True))
        probs = expo / jnp.sum(expo, axis=-1, keepdims=True)
        grad_probs = toward_ref[g]
        inner = jnp.sum(probs * grad_probs, axis=-1, keepdims=True)
        probs_ref[g] = probs.astype(jnp.bfloat16)
        back_ref[g] = (probs * (grad_probs - inner) * scale).astype(jnp.bfloat16)
    for g, w, p in groups:
        probs_b, grad_scores = probs_ref[g], back_ref[g]
        grad_ref[view(w, p, 3)] = unstacked(
            jnp.dot(probs_b, qkv_ref[view(w, p, 2)], preferred_element_type=jnp.float32)
        )
        grad_ref[view(w, p, 0)] = unstacked(
            jnp.dot(grad_scores, qkv_ref[view(w, p, 1)], preferred_element_type=jnp.float32)
        )
        grad_ref[view(w, p, 2)] = down(probs_b, stacked(qkv_ref[view(w, p, 3)])).astype(jnp.bfloat16)
        grad_ref[view(w, p, 1)] = down(grad_scores, stacked(qkv_ref[view(w, p, 0)])).astype(jnp.bfloat16)


def weights_kernel(near_ref, *refs):
    tiles, (own_ref, other_ref), out_refs = refs[:4], refs[4:6], refs[6:14]
    tile_ref, sum_ref, sems = refs[14:]
    tile = tiles[0].shape[2]
    part = own_ref.shape[1] // 4
    rows = out_refs[0].shape[0]
    copies = [pltpu.make_async_copy(source, tile_ref.at[j], sems.at[j]) for j, source in enumerate(tiles)]
    for copy in copies:
        copy.start()
    for copy in copies:
        copy.wait()
    for n in range(4):
        cols = pl.ds(n * part, part)
        total = None
        for t in range(2):
            tokens = pl.ds(t * tile, tile)
            left = jnp.concatenate([tile_ref[2 * t, n // 3], tile_ref[2 * t + 1, n // 3]], axis=1)
            right = jnp.concatenate([own_ref[tokens, cols], other_ref[tokens, cols]], axis=0)
            product = jnp.dot(left, right, preferred_element_type=jnp.float32)
            total = product if total is None else total + product
        sum_ref[:, cols] = total.astype(jnp.bfloat16)
    near = near_ref[0]
    for i, out_ref in enumerate(out_refs):
        wanted = 1 - near if i % 2 == 0 else near
        out_ref[...] = sum_ref[pl.ds(pl.multiple_of((i // 2 * 2 + wanted) * rows, 16), rows), :]


def outer_kernel(place_ref, grad_ref, mine_ref, theirs_ref, own_ref, other_ref, w_ref, sems):
    tile = own_ref.shape[0]
    width = w_ref.shape[0]
    rows = width // 16
    part = w_ref.shape[1] // 4
    step = width // 4
    copies = []
    for i in range(16):
        source = (mine_ref if i < 8 else theirs_ref).at[pl.ds(i % 8 * rows, rows), :]
        into = w_ref.at[pl.ds(pl.multiple_of(place_ref[i] * rows, 16), rows), :]
        copies.append(pltpu.make_async_copy(source, into, sems.at[i]))
    for copy in copies:
        copy.start()
    for copy in copies:
        copy.wait()
    for n in range(4):
        at = pl.ds(n * step, step)
        for k, w_cols in enumerate((pl.ds(3 * part, part), pl.ds(0, 3 * part))):
            product = across(grad_ref[:, w_cols], w_ref[at, w_cols])
            cols = pl.ds(k * width + n * step, step)
            own_ref[:, cols] = product[:tile]
            other_ref[:, cols] = product[tile:].astype(jnp.bfloat16)


def after(value, earlier):
    return lax.optimization_barrier((value, earlier))[0]


def kernel_call(body, outs, in_specs, out_specs, scratch, flops, moved, name):
    return pl.pallas_call(
        body,
        out_shape=outs,
        in_specs=in_specs,
        out_specs=out_specs,
        scratch_shapes=scratch,
        compiler_params=pltpu.CompilerParams(vmem_limit_bytes=58 * 1024 * 1024),
        cost_estimate=pl.CostEstimate(flops=flops, bytes_accessed=moved, transcendentals=0),
        name=name,
    )


def on_device(tokens, land, surface, gain, weights, shifts, index_table, bias_table, cotangent):
    levels, side, _, width = tokens.shape
    area = side * side
    tile = levels * area
    heads = bias_table.shape[2]
    entries = bias_table.shape[1]
    own_rows = weights.shape[0]
    part = weights.shape[1] // 8
    head = weights.shape[1] // 4 // heads
    own_heads = heads // 2
    far, near, beside, core = (lax.axis_index(axis) for axis in LON)
    grp = lax.axis_index("grp")
    first = near == 0
    f32 = jnp.float32

    def place(f, n, s, c):
        return ((far ^ f) * 4 + (near ^ n) * 2 + (beside ^ s)) * 2 + (core ^ c)

    low = jnp.concatenate([weights[:, 2 * k * part : (2 * k + 1) * part] for k in range(4)], axis=1)
    high = jnp.concatenate([weights[:, (2 * k + 1) * part : (2 * k + 2) * part] for k in range(4)], axis=1)
    mine = jnp.where(first, low, high)
    came = swap(jnp.where(first, high, low), "near")
    flat_cot = cotangent.reshape(tile, width)
    surface_term = jnp.where(land[None, :, :, None] == 1, surface[1], surface[0])
    stream = (tokens.astype(f32) + surface_term).astype(jnp.bfloat16).reshape(tile, width)
    values = stream.astype(f32)
    center = values - jnp.mean(values, axis=-1, keepdims=True)
    spread = lax.rsqrt(jnp.mean(center * center, axis=-1, keepdims=True) + epsilon)

    held = near ^ grp
    mine_side = swap(mine, "side")
    came_side = swap(came, "side")
    across_far = swap(jnp.where(grp == 0, mine, came), "far")
    order = [(f, s, n) for f in (1, 0) for s in (1, 0) for n in (0, 1)]
    natural = [place(f, near ^ n, s, c) for c in (0, 1) for f, s, n in order]

    vmem = pl.BlockSpec(memory_space=pltpu.VMEM)
    smem = pl.BlockSpec(memory_space=pltpu.SMEM)
    anywhere = pl.BlockSpec(memory_space=pl.ANY)
    dma = pltpu.SemaphoreType.DMA

    rows, below, below_cot = shifts[:, 0], stream, flat_cot
    if lax.axis_size("lat") > 1:
        zeros = jnp.zeros_like(rows)
        onehot_rows = pick(rows, zeros, levels, side, True)
        below = picked(onehot_rows, stream, along_lat(stream, -1))
        below_cot = picked(onehot_rows, flat_cot, along_lat(flat_cot, -1))
        rows = zeros
    info = jnp.concatenate(
        [jnp.stack([rows, shifts[:, 1]], axis=1).reshape(-1), jnp.stack(natural)]
    ).astype(jnp.int32)
    half = width // 2
    turned = jax.ShapeDtypeStruct((2, half, tile), jnp.bfloat16)
    own_turned, sent_turned = kernel_call(
        turned_rolls,
        (turned, turned),
        [smem, vmem] + [anywhere] * 4,
        (vmem, vmem),
        [
            pltpu.VMEM((2, 2 * tile, width), jnp.bfloat16),
            pltpu.VMEM((width, tile), jnp.bfloat16),
            dma((4,)),
        ],
        2 * 2 * 2 * tile * tile * width,
        3_000_000,
        "turned_rolls",
    )(after(info, (mine_side, came_side)), gain.reshape(1, -1), below, along_lon(below, -1), below_cot, along_lon(below_cot, -1))
    far_side = swap(across_far, "side")
    pieces = [
        (mine, 0, 0, near),
        (came, 0, 0, 1 - near),
        (mine_side, 0, 1, near),
        (came_side, 0, 1, 1 - near),
        (across_far, 1, 0, held),
        (swap(across_far, "grp"), 1, 0, 1 - held),
        (far_side, 1, 1, held),
        (swap(far_side, "grp"), 1, 1, 1 - held),
    ]
    places = jnp.stack([(1 - f) * 4 + (1 - s) * 2 + n for _, f, s, n in pieces]).astype(jnp.int32)
    own_near, sent_near = swap(own_turned, "near"), swap(sent_turned, "near")
    tiles = [own_turned, swap(sent_turned, "core"), own_near, swap(sent_near, "core")]

    onehot = (index_table[:, :, None] == jnp.arange(entries, dtype=jnp.int32)).astype(f32)
    own_table = lax.dynamic_slice_in_dim(bias_table, near * own_heads, own_heads, 2)
    bias = jnp.einsum("qkr,lrh->lhqk", onehot, own_table, precision=lax.Precision.HIGHEST)
    row_number = lax.axis_index("lat") * side + jnp.arange(side, dtype=jnp.int32)
    group = row_number[None, :] >= (side * lax.axis_size("lat") - shifts[:, 0])[:, None]
    group = jnp.repeat(group, side, axis=1)
    allowed = group[:, :, None] == group[:, None, :]
    bias = jnp.where(allowed[:, None], bias, -1e30).reshape(levels, own_heads // 2, 2 * area, area)

    bf16 = jnp.bfloat16
    kept, sent, w_mine = kernel_call(
        products_kernel,
        (
            jax.ShapeDtypeStruct((2 * tile, 4 * part), f32),
            jax.ShapeDtypeStruct((2 * tile, 4 * part), bf16),
            jax.ShapeDtypeStruct((half, 4 * part), bf16),
        ),
        [smem] + [anywhere] * 12,
        (vmem, vmem, anywhere),
        [
            pltpu.VMEM((4, 2, half, tile), bf16),
            pltpu.VMEM((half, 4 * part), bf16),
            dma((12,)),
            dma,
        ],
        1_200_000_000,
        9_000_000,
        "products",
    )(after(places, bias), *tiles, *[piece for piece, *_ in pieces])
    crossed = swap(sent, "core")
    grad = kernel_call(
        functools.partial(attention_kernel, area, head),
        jax.ShapeDtypeStruct((2 * tile, 4 * part), bf16),
        [vmem] * 3,
        vmem,
        [pltpu.VMEM((2 * tile, 4 * part), bf16)]
        + [pltpu.VMEM((2 * tile // area * own_heads // 2, 2 * area, area), kind) for kind in (f32, f32, bf16, bf16)],
        1_000_000_000,
        4_000_000,
        "attention",
    )(kept, crossed, bias)
    w_theirs = swap(after(w_mine, crossed), "core")
    grad_theirs = swap(grad, "core")
    blocks = kernel_call(
        weights_kernel,
        [jax.ShapeDtypeStruct((own_rows, 4 * part), bf16)] * 8,
        [smem] + [anywhere] * 4 + [vmem] * 2,
        [vmem] * 8,
        [
            pltpu.VMEM((4, 2, half, tile), bf16),
            pltpu.VMEM((half, 4 * part), bf16),
            dma((4,)),
        ],
        1_200_000_000,
        6_000_000,
        "weight_gradient",
    )(near.astype(jnp.int32).reshape(1), *tiles, grad, grad_theirs)

    def block(f, s, n):
        return blocks[((1 - f) * 2 + 1 - s) * 2 + 1 - n]

    attended_own, attended_other = kernel_call(
        outer_kernel,
        (
            jax.ShapeDtypeStruct((tile, 2 * width), f32),
            jax.ShapeDtypeStruct((tile, 2 * width), bf16),
        ),
        [smem, vmem, anywhere, anywhere],
        (vmem, vmem),
        [pltpu.VMEM((width, 4 * part), bf16), dma((16,))],
        1_200_000_000,
        8_000_000,
        "projections",
    )(after(jnp.stack(natural).astype(jnp.int32), blocks[0]), grad, w_mine, w_theirs)
    side_far_1 = after(swap(block(1, 1, 1), "side"), attended_other)
    arrived_back = swap(attended_other, "near")
    side_far_0 = swap(after(block(1, 1, 0), side_far_1), "side")
    far_1 = swap((block(1, 0, 1).astype(f32) + side_far_1.astype(f32)).astype(bf16), "far")
    far_0 = swap(after((block(1, 0, 0).astype(f32) + side_far_0.astype(f32)).astype(bf16), (far_1, arrived_back)), "far")
    side_1 = swap(after(block(0, 1, 1), side_far_0), "side")
    side_0 = swap(after(block(0, 1, 0), side_1), "side")
    total_1 = (block(0, 0, 1).astype(f32) + side_1.astype(f32) + far_1.astype(f32)).astype(bf16)
    theirs = swap(total_1, "near").astype(f32)

    back = (attended_own + arrived_back.astype(f32)).astype(jnp.bfloat16)
    back = roll_back(back, shifts, levels, side)
    output = (values + back[:, :width].astype(f32)).astype(jnp.bfloat16)
    scaled = center * spread
    upstream = back[:, width:].astype(f32) * gain
    grad_stream = spread * (
        upstream
        - jnp.mean(upstream, axis=-1, keepdims=True)
        - scaled * jnp.mean(upstream * scaled, axis=-1, keepdims=True)
    )
    grad_tokens = (flat_cot.astype(f32) + grad_stream).astype(jnp.bfloat16)

    far_0 = after(far_0, (output, grad_tokens))
    total_0 = block(0, 0, 0).astype(f32) + side_0.astype(f32) + far_0.astype(f32)
    token_count = tile * lax.axis_size("lat") * math.prod(lax.axis_size(axis) for axis in LON)
    columns = []
    for k in range(4):
        cols = slice(k * part, (k + 1) * part)
        columns += [
            jnp.where(first, total_0[:, cols], theirs[:, cols]),
            jnp.where(first, theirs[:, cols], total_0[:, cols]),
        ]
    summed = jnp.concatenate(columns, axis=1)
    if lax.axis_size("lat") > 1:
        summed = lax.psum(summed.astype(jnp.bfloat16), "lat").astype(f32)
    grad_weights = summed * (1.0 / math.sqrt(token_count))
    return (output.reshape(tokens.shape), grad_tokens.reshape(tokens.shape), grad_weights)


def solution(mesh):
    sizes = dict(mesh.shape)
    devices = mesh.devices.reshape(sizes["grp"], sizes["lon"] // 8, 2, 2, 2, sizes["lat"])
    finer = Mesh(devices, ("grp",) + LON + ("lat",))
    return jax.shard_map(
        on_device,
        mesh=finer,
        in_specs=(
            P("grp", "lat", LON, None),
            P(("grp", "lat"), LON),
            P(),
            P(),
            P(LON, None),
            P(),
            P(),
            P("lat", None, None),
            P("grp", "lat", LON, None),
        ),
        out_specs=(
            P("grp", "lat", LON, None),
            P("grp", "lat", LON, None),
            P(("grp",) + LON, None),
        ),
        check_vma=False,
    )
```

profile of v0, /device:TPU:6, one launch (start us, length us, event | category | flops | bytes accessed | tf_op | source)
XLA Modules:
  0.0 155.3 jit_solution(2207488012879889682)
XLA Ops:
  2.0 1.6 %collective-permute-start.1 = (bf16[96,1536]{1,0:T(8,128)(2,1)S(1)}, bf16[96,1536]{1,0:T(8,128)(2,1)S(1)}, u32[]{:S(2)}, u32[]{:S(2)}) collective-permute-start(bf16[96,1536]{1,0:T(8,128)(2,1)S(1)} %broadcast_select_fusion.1), channel_id=1, source_target_pairs={{0,4},{4,0},{1,5},{5,1},{2,6},{6,2},{3,7},{7,3},{8,12},{12,8},{9,1... | collective-permute-start | bytes 884744 | tf_op jit(solution)/shard_map/ppermute | solution.py:27
  4.7 6.1 %collective-permute-done.1.refs_5_ = bf16[96,1536]{1,0:T(8,128)(2,1)S(1)} collective-permute-done((bf16[96,1536]{1,0:T(8,128)(2,1)S(1)}, bf16[96,1536]{1,0:T(8,128)(2,1)S(1)}, u32[]{:S(2)}, u32[]{:S(2)}) %collective-permute-start.1) | collective-permute-done | bytes 294944 | tf_op jit(solution)/shard_map/ppermute | solution.py:27
  11.6 1.5 collective-permute-start.2
  13.1 2.6 %collective-permute-start.9 = (bf16[96,1536]{1,0:T(8,128)(2,1)S(1)}, bf16[96,1536]{1,0:T(8,128)(2,1)}, u32[]{:S(2)}, u32[]{:S(2)}) collective-permute-start(bf16[96,1536]{1,0:T(8,128)(2,1)S(1)} %get-tuple-element.59), channel_id=1, source_target_pairs={{0,8},{8,0},{1,9},{9,1},{2,10},{10,2},{3,11},{11,3},{4,12},{12,4},... | collective-permute-start | bytes 884744 | tf_op jit(solution)/shard_map/ppermute | solution.py:27
  17.0 8.6 %collective-permute-done.refs_6_ = bf16[96,1536]{1,0:T(8,128)(2,1)S(1)} collective-permute-done((bf16[96,1536]{1,0:T(8,128)(2,1)S(1)}, bf16[96,1536]{1,0:T(8,128)(2,1)S(1)}, u32[]{:S(2)}, u32[]{:S(2)}) %collective-permute-start) | collective-permute-done | bytes 294944 | tf_op jit(solution)/shard_map/ppermute | solution.py:27
  25.6 6.2 %collective-permute-done.2.refs_7_ = bf16[96,1536]{1,0:T(8,128)(2,1)S(1)} collective-permute-done((bf16[96,1536]{1,0:T(8,128)(2,1)S(1)}, bf16[96,1536]{1,0:T(8,128)(2,1)S(1)}, u32[]{:S(2)}, u32[]{:S(2)}) %collective-permute-start.2) | collective-permute-done | bytes 294944 | tf_op jit(solution)/shard_map/ppermute | solution.py:27
  33.4 4.0 %turned_rolls.1 = (bf16[2,768,128]{2,1,0:T(8,128)(2,1)}, bf16[2,768,128]{2,1,0:T(8,128)(2,1)}) custom-call(s32[20]{0:T(128)} %concatenate.15.info_ref, f32[1,1536]{1,0:T(1,128)} %reshape.97.gain_ref, bf16[128,1536]{1,0:T(8,128)(2,1)} %bitcast.49, bf16[128,1536]{1,0:T(8,128)(2,1)} %copy-done.7, bf16[128,1536]{1,0:T(8,128)(2,1)} %bitcast.50, ...), custom_call_target="tpu_custom_call" | custom-call | flops 201326592 | bytes 3000000 | tf_op jit(solution)/shard_map/turned_rolls/pallas_call | solution.py:305
  38.0 2.1 %collective-permute-start.6 = (bf16[2,768,128]{2,1,0:T(8,128)(2,1)}, bf16[2,768,128]{2,1,0:T(8,128)(2,1)S(1)}, u32[]{:S(2)}, u32[]{:S(2)}) collective-permute-start(bf16[2,768,128]{2,1,0:T(8,128)(2,1)} %get-tuple-element.29.refs_0_), channel_id=1, source_target_pairs={{0,4},{4,0},{1,5},{5,1},{2,6},{6,2},{3,7},{7,3},{8,12},{12,8},{9,1... | collective-permute-start | bytes 1179656 | tf_op jit(solution)/shard_map/ppermute | solution.py:27
  40.1 9.6 %collective-permute-done.7 = bf16[2,768,128]{2,1,0:T(8,128)(2,1)S(1)} collective-permute-done((bf16[2,768,128]{2,1,0:T(8,128)(2,1)}, bf16[2,768,128]{2,1,0:T(8,128)(2,1)S(1)}, u32[]{:S(2)}, u32[]{:S(2)}) %collective-permute-start.7) | collective-permute-done | bytes 393248 | tf_op jit(solution)/shard_map/ppermute | solution.py:27
  50.3 1.7 %collective-permute-start.12 = (bf16[96,1536]{1,0:T(8,128)(2,1)S(1)}, bf16[96,1536]{1,0:T(8,128)(2,1)S(1)}, u32[]{:S(2)}, u32[]{:S(2)}) collective-permute-start(bf16[96,1536]{1,0:T(8,128)(2,1)S(1)} %collective-permute-done.11.refs_10_), channel_id=1, source_target_pairs={{0,16},{16,0},{1,17},{17,1},{2,18},{18,2},{3,19},{19,3},{4,20},{20... | collective-permute-start | bytes 884744 | tf_op jit(solution)/shard_map/ppermute | solution.py:27
  51.9 2.6 %fusion.7 = f32[2,6,64,64]{3,1,2,0:T(8,128)S(1)} fusion(s32[64,64]{1,0:T(8,128)S(1)} %copy-done.31, pred[2,64,64]{2,1,0:T(8,128)(4,1)S(1)} %broadcast_compare_fusion, f32[2,225,6]{1,0,2:T(2,128)S(1)} %constant_dynamic-slice_fusion), kind=kOutput, calls=%fused_computation.9 | convolution fusion | flops 133681152 | bytes 231984 | tf_op jit(solution)/shard_map/qkr,lrh->lhqk/dot_general | solution.py:336
  56.0 3.9 %collective-permute-done.10.refs_9_ = bf16[96,1536]{1,0:T(8,128)(2,1)S(1)} collective-permute-done((bf16[96,1536]{1,0:T(8,128)(2,1)}, bf16[96,1536]{1,0:T(8,128)(2,1)S(1)}, u32[]{:S(2)}, u32[]{:S(2)}) %collective-permute-start.10) | collective-permute-done | bytes 294944 | tf_op jit(solution)/shard_map/ppermute | solution.py:27
  59.9 5.9 %collective-permute-done.12.refs_11_ = bf16[96,1536]{1,0:T(8,128)(2,1)S(1)} collective-permute-done((bf16[96,1536]{1,0:T(8,128)(2,1)S(1)}, bf16[96,1536]{1,0:T(8,128)(2,1)S(1)}, u32[]{:S(2)}, u32[]{:S(2)}) %collective-permute-start.12) | collective-permute-done | bytes 294944 | tf_op jit(solution)/shard_map/ppermute | solution.py:27
  67.4 6.1 %products.1 = (f32[256,1536]{1,0:T(8,128)}, bf16[256,1536]{1,0:T(8,128)(2,1)}, bf16[768,1536]{1,0:T(8,128)(2,1)}) custom-call(s32[8]{0:T(128)} %stack.120.place_ref, bf16[2,768,128]{2,1,0:T(8,128)(2,1)} %get-tuple-element.29.refs_0_, bf16[2,768,128]{2,1,0:T(8,128)(2,1)} %copy-done.20, bf16[2,768,128]{2,1,0:T(8,128)(2,1)} %copy-done.21, ...), custom_call_target="tpu_custom_call" | custom-call | flops 1200000000 | bytes 9000000 | tf_op jit(solution)/shard_map/products/pallas_call | solution.py:344
  73.5 2.5 %collective-permute-done.13.came_ref = bf16[256,1536]{1,0:T(8,128)(2,1)S(1)} collective-permute-done((bf16[256,1536]{1,0:T(8,128)(2,1)}, bf16[256,1536]{1,0:T(8,128)(2,1)S(1)}, u32[]{:S(2)}, u32[]{:S(2)}) %collective-permute-start.13) | collective-permute-done | bytes 786464 | tf_op jit(solution)/shard_map/ppermute | solution.py:27
  76.9 4.2 %attention.1.refs_4_.grad_ref = bf16[256,1536]{1,0:T(8,128)(2,1)} custom-call(f32[256,1536]{1,0:T(8,128)} %get-tuple-element.32.kept_ref, bf16[256,1536]{1,0:T(8,128)(2,1)} %copy-done.19, f32[2,3,128,64]{3,2,1,0:T(8,128)} %bitcast.52), custom_call_target="tpu_custom_call" | custom-call | flops 1000000000 | bytes 4000000 | tf_op jit(solution)/shard_map/attention/pallas_call | solution.py:364
  82.4 1.3 collective-permute-done.14.refs_5_
  83.8 6.0 %weight_gradient.1 = (bf16[96,1536]{1,0:T(8,128)(2,1)}, bf16[96,1536]{1,0:T(8,128)(2,1)}, bf16[96,1536]{1,0:T(8,128)(2,1)}, bf16[96,1536]{1,0:T(8,128)(2,1)}, bf...) custom-call(s32[1]{0:T(128)} %bitcast.21.near_ref, ...), custom_call_target="tpu_custom_call" | custom-call | flops 1200000000 | bytes 6000000 | tf_op jit(solution)/shard_map/weight_gradient/pallas_call | solution.py:377
  89.9 1.4 copy-done.3
  91.3 7.0 %projections.1 = (f32[128,3072]{1,0:T(8,128)}, bf16[128,3072]{1,0:T(8,128)(2,1)}) custom-call(s32[16]{0:T(128)} %stack.111.place_ref, bf16[256,1536]{1,0:T(8,128)(2,1)} %attention.1.refs_4_.grad_ref, bf16[768,1536]{1,0:T(8,128)(2,1)} %get-tuple-element.37.mine_ref, bf16[768,1536]{1,0:T(8,128)(2,1)} %copy-done.3), custom_call_target="tpu_custom_call" | custom-call | flops 1200000000 | bytes 8000000 | tf_op jit(solution)/shard_map/projections/pallas_call | solution.py:395
  99.1 2.0 %collective-permute-start.19 = (bf16[96,1536]{1,0:T(8,128)(2,1)S(1)}, bf16[96,1536]{1,0:T(8,128)(2,1)S(1)}, u32[]{:S(2)}, u32[]{:S(2)}) collective-permute-start(bf16[96,1536]{1,0:T(8,128)(2,1)S(1)} %copy-done.30), channel_id=1, source_target_pairs={{0,2},{2,0},{1,3},{3,1},{4,6},{6,4},{5,7},{7,5},{8,10},{10,8},{9,1... | collective-permute-start | bytes 884744 | tf_op jit(solution)/shard_map/ppermute | solution.py:27
  101.2 4.2 %collective-permute-start.22 = (bf16[96,1536]{1,0:T(8,128)(2,1)S(1)}, bf16[96,1536]{1,0:T(8,128)(2,1)S(1)}, u32[]{:S(2)}, u32[]{:S(2)}) collective-permute-start(bf16[96,1536]{1,0:T(8,128)(2,1)S(1)} %add_convert_fusion.3), channel_id=1, source_target_pairs={{0,8},{8,0},{1,9},{9,1},{2,10},{10,2},{3,11},{11,3},{4,12},{12,4},... | collective-permute-start | bytes 884744 | tf_op jit(solution)/shard_map/ppermute | solution.py:27
  105.3 2.8 %collective-permute-done.19 = bf16[96,1536]{1,0:T(8,128)(2,1)S(1)} collective-permute-done((bf16[96,1536]{1,0:T(8,128)(2,1)S(1)}, bf16[96,1536]{1,0:T(8,128)(2,1)S(1)}, u32[]{:S(2)}, u32[]{:S(2)}) %collective-permute-start.19) | collective-permute-done | bytes 294944 | tf_op jit(solution)/shard_map/ppermute | solution.py:27
  108.1 1.7 %collective-permute-start.20 = (bf16[96,1536]{1,0:T(8,128)(2,1)S(1)}, bf16[96,1536]{1,0:T(8,128)(2,1)S(1)}, u32[]{:S(2)}, u32[]{:S(2)}) collective-permute-start(bf16[96,1536]{1,0:T(8,128)(2,1)S(1)} %copy-done.27), channel_id=1, source_target_pairs={{0,2},{2,0},{1,3},{3,1},{4,6},{6,4},{5,7},{7,5},{8,10},{10,8},{9,1... | collective-permute-start | bytes 884744 | tf_op jit(solution)/shard_map/ppermute | solution.py:27
  109.9 14.6 %collective-permute-done.16 = bf16[128,3072]{1,0:T(8,128)(2,1)S(1)} collective-permute-done((bf16[128,3072]{1,0:T(8,128)(2,1)}, bf16[128,3072]{1,0:T(8,128)(2,1)S(1)}, u32[]{:S(2)}, u32[]{:S(2)}) %collective-permute-start.16) | collective-permute-done | bytes 786464 | tf_op jit(solution)/shard_map/ppermute | solution.py:27
  124.5 1.6 %add_convert_fusion = bf16[128,3072]{1,0:T(8,128)(2,1)S(1)} fusion(f32[128,3072]{1,0:T(8,128)} %get-tuple-element.38, bf16[128,3072]{1,0:T(8,128)(2,1)S(1)} %collective-permute-done.16), kind=kLoop, calls=%fused_computation.8 | loop fusion | flops 1179648 | bytes 3145728 | tf_op jit(solution)/shard_map/convert_element_type | solution.py:418
  127.4 1.8 %collective-permute-start.21 = (bf16[96,1536]{1,0:T(8,128)(2,1)S(1)}, bf16[96,1536]{1,0:T(8,128)(2,1)S(1)}, u32[]{:S(2)}, u32[]{:S(2)}) collective-permute-start(bf16[96,1536]{1,0:T(8,128)(2,1)S(1)} %copy-done.25), channel_id=1, source_target_pairs={{0,2},{2,0},{1,3},{3,1},{4,6},{6,4},{5,7},{7,5},{8,10},{10,8},{9,1... | collective-permute-start | bytes 884744 | tf_op jit(solution)/shard_map/ppermute | solution.py:27
  129.2 3.3 %collective-permute-start.23 = (bf16[96,1536]{1,0:T(8,128)(2,1)S(1)}, bf16[96,1536]{1,0:T(8,128)(2,1)S(1)}, u32[]{:S(2)}, u32[]{:S(2)}) collective-permute-start(bf16[96,1536]{1,0:T(8,128)(2,1)S(1)} %add_convert_fusion.4), channel_id=1, source_target_pairs={{0,8},{8,0},{1,9},{9,1},{2,10},{10,2},{3,11},{11,3},{4,12},{12,4},... | collective-permute-start | bytes 884744 | tf_op jit(solution)/shard_map/ppermute | solution.py:27
  132.4 10.4 %collective-permute-done.24 = bf16[96,1536]{1,0:T(8,128)(2,1)S(1)} collective-permute-done((bf16[96,1536]{1,0:T(8,128)(2,1)S(1)}, bf16[96,1536]{1,0:T(8,128)(2,1)S(1)}, u32[]{:S(2)}, u32[]{:S(2)}) %collective-permute-start.24) | collective-permute-done | bytes 294944 | tf_op jit(solution)/shard_map/ppermute | solution.py:27
  142.9 3.2 %convolution_convert_fusion = bf16[128,3072]{1,0:T(8,128)(2,1)S(1)} fusion(bf16[128,3072]{1,0:T(8,128)(2,1)S(1)} %add_convert_fusion, bf16[128,3072]{1,0:T(8,128)(2,1)S(1)} %collective-permute-done.17, s32[]{:T(128)} %bitcast.4, s32[]{:T(128)} %bitcast.3, s32[128]{0:T(128)S(1)} %get-tuple-element.83, s32[128]{0:T(128)S(1)} %get-tuple-element.85, ...), kind=kOutput, calls=%fused_computation.3 | convolution fusion | flops 206700544 | bytes 2362768 | tf_op jit(solution)/shard_map/dot_general | solution.py:52
  146.5 1.4 fusion.18
  147.8 6.0 %collective-permute-done.23 = bf16[96,1536]{1,0:T(8,128)(2,1)S(1)} collective-permute-done((bf16[96,1536]{1,0:T(8,128)(2,1)S(1)}, bf16[96,1536]{1,0:T(8,128)(2,1)S(1)}, u32[]{:S(2)}, u32[]{:S(2)}) %collective-permute-start.23) | collective-permute-done | bytes 294944 | tf_op jit(solution)/shard_map/ppermute | solution.py:27
  (138 shorter events, 16.1 us)
Async XLA Ops:
  0.6 51.3 %copy-start = (f32[2,225,12]{1,0,2:T(2,128)S(1)}, f32[2,225,12]{1,0,2:T(2,128)}, u32[]{:S(2)}) copy-start(f32[2,225,12]{1,0,2:T(2,128)} %param.16) | copy-start | bytes 64804
  2.0 8.8 %collective-permute-start.1 = (bf16[96,1536]{1,0:T(8,128)(2,1)S(1)}, bf16[96,1536]{1,0:T(8,128)(2,1)S(1)}, u32[]{:S(2)}, u32[]{:S(2)}) collective-permute-start(bf16[96,1536]{1,0:T(8,128)(2,1)S(1)} %broadcast_select_fusion.1), channel_id=1, source_target_pairs={{0,4},{4,0},{1,5},{5,1},{2,6},{6,2},{3,7},{7,3},{8,12},{12,8},{9,1... | collective-permute-start | bytes 884744 | tf_op jit(solution)/shard_map/ppermute | solution.py:27
  3.9 11.9 %copy-start.15 = (f32[1536]{0:T(1024)S(1)}, f32[1536]{0:T(1024)}, u32[]{:S(2)}) copy-start(f32[1536]{0:T(1024)} %param.12) | copy-start | bytes 18436
  4.0 27.8 %copy-start.1 = (bf16[2,8,8,1536]{3,2,1,0:T(8,128)(2,1)}, bf16[2,8,8,1536]{3,2,1,0:T(8,128)(2,1)S(1)}, u32[]{:S(2)}) copy-start(bf16[2,8,8,1536]{3,2,1,0:T(8,128)(2,1)S(1)} %get-tuple-element.58) | copy-start | bytes 1179652
  4.1 27.8 %collective-permute-start.3 = (bf16[128,1536]{1,0:T(8,128)(2,1)S(1)}, bf16[128,1536]{1,0:T(8,128)(2,1)S(1)}, u32[]{:S(2)}, u32[]{:S(2)}) collective-permute-start(bf16[128,1536]{1,0:T(8,128)(2,1)S(1)} %bitcast.48), channel_id=1, source_target_pairs={{0,15},{1,0},{2,1},{3,2},{4,3},{5,4},{6,5},{7,6},{8,7},{9,8},{10,9... | collective-permute-start | bytes 1179656 | tf_op jit(solution)/shard_map/ppermute | solution.py:18
  4.1 27.8 %collective-permute-start.4 = (bf16[128,1536]{1,0:T(8,128)(2,1)S(1)}, bf16[128,1536]{1,0:T(8,128)(2,1)S(1)}, u32[]{:S(2)}, u32[]{:S(2)}) collective-permute-start(bf16[128,1536]{1,0:T(8,128)(2,1)S(1)} %bitcast.51), channel_id=1, source_target_pairs={{0,15},{1,0},{2,1},{3,2},{4,3},{5,4},{6,5},{7,6},{8,7},{9,8},{10,9... | collective-permute-start | bytes 1179656 | tf_op jit(solution)/shard_map/ppermute | solution.py:18
  10.9 26.6 %copy-start.9 = (bf16[96,1536]{1,0:T(8,128)(2,1)}, bf16[96,1536]{1,0:T(8,128)(2,1)S(1)}, u32[]{:S(2)}) copy-start(bf16[96,1536]{1,0:T(8,128)(2,1)S(1)} %collective-permute-done.1.refs_5_) | copy-start | bytes 884740
  11.0 54.9 %copy-start.10 = (bf16[96,1536]{1,0:T(8,128)(2,1)}, bf16[96,1536]{1,0:T(8,128)(2,1)S(1)}, u32[]{:S(2)}) copy-start(bf16[96,1536]{1,0:T(8,128)(2,1)S(1)} %get-tuple-element.60.refs_4_) | copy-start | bytes 884740
  11.0 40.9 %copy-start.31 = (s32[64,64]{1,0:T(8,128)S(1)}, s32[64,64]{1,0:T(8,128)}, u32[]{:S(2)}) copy-start(s32[64,64]{1,0:T(8,128)} %param.15) | copy-start | bytes 49156
  11.0 14.6 %collective-permute-start = (bf16[96,1536]{1,0:T(8,128)(2,1)S(1)}, bf16[96,1536]{1,0:T(8,128)(2,1)S(1)}, u32[]{:S(2)}, u32[]{:S(2)}) collective-permute-start(bf16[96,1536]{1,0:T(8,128)(2,1)S(1)} %get-tuple-element.60.refs_4_), channel_id=1, source_target_pairs={{0,2},{2,0},{1,3},{3,1},{4,6},{6,4},{5,7},{7,5},{8,10},{10,8},{9,1... | collective-permute-start | bytes 884744 | tf_op jit(solution)/shard_map/ppermute | solution.py:27
  11.6 20.3 %collective-permute-start.2 = (bf16[96,1536]{1,0:T(8,128)(2,1)S(1)}, bf16[96,1536]{1,0:T(8,128)(2,1)S(1)}, u32[]{:S(2)}, u32[]{:S(2)}) collective-permute-start(bf16[96,1536]{1,0:T(8,128)(2,1)S(1)} %collective-permute-done.1.refs_5_), channel_id=1, source_target_pairs={{0,2},{2,0},{1,3},{3,1},{4,6},{6,4},{5,7},{7,5},{8,10},{10,8},{9,1... | collective-permute-start | bytes 884744 | tf_op jit(solution)/shard_map/ppermute | solution.py:27
  13.1 24.6 %collective-permute-start.9 = (bf16[96,1536]{1,0:T(8,128)(2,1)S(1)}, bf16[96,1536]{1,0:T(8,128)(2,1)}, u32[]{:S(2)}, u32[]{:S(2)}) collective-permute-start(bf16[96,1536]{1,0:T(8,128)(2,1)S(1)} %get-tuple-element.59), channel_id=1, source_target_pairs={{0,8},{8,0},{1,9},{9,1},{2,10},{10,2},{3,11},{11,3},{4,12},{12,4},... | collective-permute-start | bytes 884744 | tf_op jit(solution)/shard_map/ppermute | solution.py:27
  37.5 12.3 %collective-permute-start.7 = (bf16[2,768,128]{2,1,0:T(8,128)(2,1)}, bf16[2,768,128]{2,1,0:T(8,128)(2,1)S(1)}, u32[]{:S(2)}, u32[]{:S(2)}) collective-permute-start(bf16[2,768,128]{2,1,0:T(8,128)(2,1)} %get-tuple-element.30), channel_id=1, source_target_pairs={{0,4},{4,0},{1,5},{5,1},{2,6},{6,2},{3,7},{7,3},{8,12},{12,8},{9,1... | collective-permute-start | bytes 1179656 | tf_op jit(solution)/shard_map/ppermute | solution.py:27
  37.7 12.6 %collective-permute-start.11 = (bf16[96,1536]{1,0:T(8,128)(2,1)}, bf16[96,1536]{1,0:T(8,128)(2,1)S(1)}, u32[]{:S(2)}, u32[]{:S(2)}) collective-permute-start(bf16[96,1536]{1,0:T(8,128)(2,1)} %collective-permute-done.9.refs_8_), channel_id=1, source_target_pairs={{0,2},{2,0},{1,3},{3,1},{4,6},{6,4},{5,7},{7,5},{8,10},{10,8},{9,1... | collective-permute-start | bytes 884744 | tf_op jit(solution)/shard_map/ppermute | solution.py:27
  38.0 21.9 %collective-permute-start.5 = (bf16[2,768,128]{2,1,0:T(8,128)(2,1)}, bf16[2,768,128]{2,1,0:T(8,128)(2,1)S(1)}, u32[]{:S(2)}, u32[]{:S(2)}) collective-permute-start(bf16[2,768,128]{2,1,0:T(8,128)(2,1)} %get-tuple-element.30), channel_id=1, source_target_pairs={{0,1},{1,0},{2,3},{3,2},{4,5},{5,4},{6,7},{7,6},{8,9},{9,8},{10,11... | collective-permute-start | bytes 1179656 | tf_op jit(solution)/shard_map/ppermute | solution.py:27
  38.0 21.9 %collective-permute-start.6 = (bf16[2,768,128]{2,1,0:T(8,128)(2,1)}, bf16[2,768,128]{2,1,0:T(8,128)(2,1)S(1)}, u32[]{:S(2)}, u32[]{:S(2)}) collective-permute-start(bf16[2,768,128]{2,1,0:T(8,128)(2,1)} %get-tuple-element.29.refs_0_), channel_id=1, source_target_pairs={{0,4},{4,0},{1,5},{5,1},{2,6},{6,2},{3,7},{7,3},{8,12},{12,8},{9,1... | collective-permute-start | bytes 1179656 | tf_op jit(solution)/shard_map/ppermute | solution.py:27
  49.7 16.1 %collective-permute-start.8 = (bf16[2,768,128]{2,1,0:T(8,128)(2,1)S(1)}, bf16[2,768,128]{2,1,0:T(8,128)(2,1)S(1)}, u32[]{:S(2)}, u32[]{:S(2)}) collective-permute-start(bf16[2,768,128]{2,1,0:T(8,128)(2,1)S(1)} %collective-permute-done.7), channel_id=1, source_target_pairs={{0,1},{1,0},{2,3},{3,2},{4,5},{5,4},{6,7},{7,6},{8,9},{9,8},{10,11... | collective-permute-start | bytes 1179656 | tf_op jit(solution)/shard_map/ppermute | solution.py:27
  49.8 10.1 %collective-permute-start.10 = (bf16[96,1536]{1,0:T(8,128)(2,1)}, bf16[96,1536]{1,0:T(8,128)(2,1)S(1)}, u32[]{:S(2)}, u32[]{:S(2)}) collective-permute-start(bf16[96,1536]{1,0:T(8,128)(2,1)} %collective-permute-done.9.refs_8_), channel_id=1, source_target_pairs={{0,16},{16,0},{1,17},{17,1},{2,18},{18,2},{3,19},{19,3},{4,20},{20... | collective-permute-start | bytes 884744 | tf_op jit(solution)/shard_map/ppermute | solution.py:27
  50.3 15.6 %collective-permute-start.12 = (bf16[96,1536]{1,0:T(8,128)(2,1)S(1)}, bf16[96,1536]{1,0:T(8,128)(2,1)S(1)}, u32[]{:S(2)}, u32[]{:S(2)}) collective-permute-start(bf16[96,1536]{1,0:T(8,128)(2,1)S(1)} %collective-permute-done.11.refs_10_), channel_id=1, source_target_pairs={{0,16},{16,0},{1,17},{17,1},{2,18},{18,2},{3,19},{19,3},{4,20},{20... | collective-permute-start | bytes 884744 | tf_op jit(solution)/shard_map/ppermute | solution.py:27
  73.5 2.6 %collective-permute-start.13 = (bf16[256,1536]{1,0:T(8,128)(2,1)}, bf16[256,1536]{1,0:T(8,128)(2,1)S(1)}, u32[]{:S(2)}, u32[]{:S(2)}) collective-permute-start(bf16[256,1536]{1,0:T(8,128)(2,1)} %get-tuple-element.33), channel_id=1, source_target_pairs={{0,1},{1,0},{2,3},{3,2},{4,5},{5,4},{6,7},{7,6},{8,9},{9,8},{10,11... | collective-permute-start | bytes 2359304 | tf_op jit(solution)/shard_map/ppermute | solution.py:27
  76.0 13.8 %collective-permute-start.15 = (bf16[768,1536]{1,0:T(8,128)(2,1)}, bf16[768,1536]{1,0:T(8,128)(2,1)S(1)}, u32[]{:S(2)}, u32[]{:S(2)}) collective-permute-start(bf16[768,1536]{1,0:T(8,128)(2,1)} %get-tuple-element.37.mine_ref), channel_id=1, source_target_pairs={{0,1},{1,0},{2,3},{3,2},{4,5},{5,4},{6,7},{7,6},{8,9},{9,8},{10,11... | collective-permute-start | bytes 7077896 | tf_op jit(solution)/shard_map/ppermute | solution.py:27
  81.2 2.6 %collective-permute-start.14 = (bf16[256,1536]{1,0:T(8,128)(2,1)}, bf16[256,1536]{1,0:T(8,128)(2,1)}, u32[]{:S(2)}, u32[]{:S(2)}) collective-permute-start(bf16[256,1536]{1,0:T(8,128)(2,1)} %attention.1.refs_4_.grad_ref), channel_id=1, source_target_pairs={{0,1},{1,0},{2,3},{3,2},{4,5},{5,4},{6,7},{7,6},{8,9},{9,8},{10,11... | collective-permute-start | bytes 2359304 | tf_op jit(solution)/shard_map/ppermute | solution.py:27
  89.8 18.4 %copy-start.27 = (bf16[96,1536]{1,0:T(8,128)(2,1)S(1)}, bf16[96,1536]{1,0:T(8,128)(2,1)}, u32[]{:S(2)}) copy-start(bf16[96,1536]{1,0:T(8,128)(2,1)} %get-tuple-element.46) | copy-start | bytes 884740
  89.8 9.3 %collective-permute-start.18 = (bf16[96,1536]{1,0:T(8,128)(2,1)}, bf16[96,1536]{1,0:T(8,128)(2,1)S(1)}, u32[]{:S(2)}, u32[]{:S(2)}) collective-permute-start(bf16[96,1536]{1,0:T(8,128)(2,1)} %get-tuple-element.34), channel_id=1, source_target_pairs={{0,2},{2,0},{1,3},{3,1},{4,6},{6,4},{5,7},{7,5},{8,10},{10,8},{9,1... | collective-permute-start | bytes 884744 | tf_op jit(solution)/shard_map/ppermute | solution.py:27
  98.3 26.2 %collective-permute-start.16 = (bf16[128,3072]{1,0:T(8,128)(2,1)}, bf16[128,3072]{1,0:T(8,128)(2,1)S(1)}, u32[]{:S(2)}, u32[]{:S(2)}) collective-permute-start(bf16[128,3072]{1,0:T(8,128)(2,1)} %get-tuple-element.39), channel_id=1, source_target_pairs={{0,4},{4,0},{1,5},{5,1},{2,6},{6,2},{3,7},{7,3},{8,12},{12,8},{9,1... | collective-permute-start | bytes 2359304 | tf_op jit(solution)/shard_map/ppermute | solution.py:27
  99.1 9.0 %collective-permute-start.19 = (bf16[96,1536]{1,0:T(8,128)(2,1)S(1)}, bf16[96,1536]{1,0:T(8,128)(2,1)S(1)}, u32[]{:S(2)}, u32[]{:S(2)}) collective-permute-start(bf16[96,1536]{1,0:T(8,128)(2,1)S(1)} %copy-done.30), channel_id=1, source_target_pairs={{0,2},{2,0},{1,3},{3,1},{4,6},{6,4},{5,7},{7,5},{8,10},{10,8},{9,1... | collective-permute-start | bytes 884744 | tf_op jit(solution)/shard_map/ppermute | solution.py:27
  101.2 25.1 %collective-permute-start.22 = (bf16[96,1536]{1,0:T(8,128)(2,1)S(1)}, bf16[96,1536]{1,0:T(8,128)(2,1)S(1)}, u32[]{:S(2)}, u32[]{:S(2)}) collective-permute-start(bf16[96,1536]{1,0:T(8,128)(2,1)S(1)} %add_convert_fusion.3), channel_id=1, source_target_pairs={{0,8},{8,0},{1,9},{9,1},{2,10},{10,2},{3,11},{11,3},{4,12},{12,4},... | collective-permute-start | bytes 884744 | tf_op jit(solution)/shard_map/ppermute | solution.py:27
  108.1 18.1 %collective-permute-start.20 = (bf16[96,1536]{1,0:T(8,128)(2,1)S(1)}, bf16[96,1536]{1,0:T(8,128)(2,1)S(1)}, u32[]{:S(2)}, u32[]{:S(2)}) collective-permute-start(bf16[96,1536]{1,0:T(8,128)(2,1)S(1)} %copy-done.27), channel_id=1, source_target_pairs={{0,2},{2,0},{1,3},{3,1},{4,6},{6,4},{5,7},{7,5},{8,10},{10,8},{9,1... | collective-permute-start | bytes 884744 | tf_op jit(solution)/shard_map/ppermute | solution.py:27
  126.1 16.7 %collective-permute-start.17 = (bf16[128,3072]{1,0:T(8,128)(2,1)S(1)}, bf16[128,3072]{1,0:T(8,128)(2,1)S(1)}, u32[]{:S(2)}, u32[]{:S(2)}) collective-permute-start(bf16[128,3072]{1,0:T(8,128)(2,1)S(1)} %add_convert_fusion), channel_id=1, source_target_pairs={{0,1},{1,2},{2,3},{3,4},{4,5},{5,6},{6,7},{7,8},{8,9},{9,10},{10,1... | collective-permute-start | bytes 2359304 | tf_op jit(solution)/shard_map/ppermute | solution.py:18
  126.4 16.5 %collective-permute-start.24 = (bf16[96,1536]{1,0:T(8,128)(2,1)S(1)}, bf16[96,1536]{1,0:T(8,128)(2,1)S(1)}, u32[]{:S(2)}, u32[]{:S(2)}) collective-permute-start(bf16[96,1536]{1,0:T(8,128)(2,1)S(1)} %add_convert_fusion.2), channel_id=1, source_target_pairs={{0,4},{4,0},{1,5},{5,1},{2,6},{6,2},{3,7},{7,3},{8,12},{12,8},{9,1... | collective-permute-start | bytes 884744 | tf_op jit(solution)/shard_map/ppermute | solution.py:27
  127.4 26.4 %collective-permute-start.21 = (bf16[96,1536]{1,0:T(8,128)(2,1)S(1)}, bf16[96,1536]{1,0:T(8,128)(2,1)S(1)}, u32[]{:S(2)}, u32[]{:S(2)}) collective-permute-start(bf16[96,1536]{1,0:T(8,128)(2,1)S(1)} %copy-done.25), channel_id=1, source_target_pairs={{0,2},{2,0},{1,3},{3,1},{4,6},{6,4},{5,7},{7,5},{8,10},{10,8},{9,1... | collective-permute-start | bytes 884744 | tf_op jit(solution)/shard_map/ppermute | solution.py:27
  129.2 24.6 %collective-permute-start.23 = (bf16[96,1536]{1,0:T(8,128)(2,1)S(1)}, bf16[96,1536]{1,0:T(8,128)(2,1)S(1)}, u32[]{:S(2)}, u32[]{:S(2)}) collective-permute-start(bf16[96,1536]{1,0:T(8,128)(2,1)S(1)} %add_convert_fusion.4), channel_id=1, source_target_pairs={{0,8},{8,0},{1,9},{9,1},{2,10},{10,2},{3,11},{11,3},{4,12},{12,4},... | collective-permute-start | bytes 884744 | tf_op jit(solution)/shard_map/ppermute | solution.py:27
  (25 other events, 110.0 us)
where the time goes:
time: 158 us; the launch traced here: 155 us
  waiting for transfers between devices  78.2 us (49%)
  Pallas kernels  27.3 us (17%)
  starting transfers between devices  25.7 us (16%)
  local copies, waits for them, and re-layouts  11 us (7%)
  other arithmetic  6.07 us (4%)
  matrix products  5.87 us (4%)
    ppermute x22, waiting for transfers between devices, swap(): return lax.ppermute(shard, axis, [(0, 1), (1, 0)])  78.2 us
    ppermute x22, starting transfers between devices, swap(): return lax.ppermute(shard, axis, [(0, 1), (1, 0)])  25 us
    pallas_call x1, Pallas kernels, on_device(): kernel_call(outer_kernel, (jax.ShapeDtypeStruct((tile, 2 * width), f32),...  6.98 us
    pallas_call x1, Pallas kernels, on_device(): kernel_call(products_kernel, (jax.ShapeDtypeStruct((2 * tile, 4 * part),...  6.09 us
    pallas_call x1, Pallas kernels, on_device(): kernel_call(weights_kernel, [jax.ShapeDtypeStruct((own_rows, 4 * part), b...  5.96 us
    unnamed x64, local copies, waits for them, and re-layouts  5.3 us
    pallas_call x1, Pallas kernels, on_device(): kernel_call(functools.partial(attention_kernel, area, head), jax.ShapeDty...  4.24 us
    pallas_call x1, Pallas kernels, on_device(): kernel_call(turned_rolls, (turned, turned), [smem, vmem] + [anywhere] * 4...  4.02 us
  transfers between devices with their start and end apart: 25, of which 13 were waited for; matrix products, arithmetic and copies ran while one was open for 10% of the time, Pallas kernels for 14%

commit v1 on v0

--- a/solution.py
+++ b/solution.py
@@ -236,14 +236,14 @@
     return lax.optimization_barrier((value, earlier))[0]
 
 
-def kernel_call(body, outs, in_specs, out_specs, scratch, flops, moved, name):
+def kernel_call(body, outs, in_specs, out_specs, scratch, flops, moved, name, room=58):
     return pl.pallas_call(
         body,
         out_shape=outs,
         in_specs=in_specs,
         out_specs=out_specs,
         scratch_shapes=scratch,
-        compiler_params=pltpu.CompilerParams(vmem_limit_bytes=58 * 1024 * 1024),
+        compiler_params=pltpu.CompilerParams(vmem_limit_bytes=room * 1024 * 1024),
         cost_estimate=pl.CostEstimate(flops=flops, bytes_accessed=moved, transcendentals=0),
         name=name,
     )
@@ -279,8 +279,6 @@
     spread = lax.rsqrt(jnp.mean(center * center, axis=-1, keepdims=True) + epsilon)
 
     held = near ^ grp
-    mine_side = swap(mine, "side")
-    came_side = swap(came, "side")
     across_far = swap(jnp.where(grp == 0, mine, came), "far")
     order = [(f, s, n) for f in (1, 0) for s in (1, 0) for n in (0, 1)]
     natural = [place(f, near ^ n, s, c) for c in (0, 1) for f, s, n in order]
@@ -315,8 +313,10 @@
         2 * 2 * 2 * tile * tile * width,
         3_000_000,
         "turned_rolls",
-    )(after(info, (mine_side, came_side)), gain.reshape(1, -1), below, along_lon(below, -1), below_cot, along_lon(below_cot, -1))
+    )(info, gain.reshape(1, -1), below, along_lon(below, -1), below_cot, along_lon(below_cot, -1))
+    mine_side = swap(after(mine, own_turned), "side")
     far_side = swap(across_far, "side")
+    came_side = swap(after(came, far_side), "side")
     pieces = [
         (mine, 0, 0, near),
         (came, 0, 0, 1 - near),
@@ -371,9 +371,24 @@
         1_000_000_000,
         4_000_000,
         "attention",
+        24,
     )(kept, crossed, bias)
     w_theirs = swap(after(w_mine, crossed), "core")
     grad_theirs = swap(grad, "core")
+    attended_own, attended_other = kernel_call(
+        outer_kernel,
+        (
+            jax.ShapeDtypeStruct((tile, 2 * width), f32),
+            jax.ShapeDtypeStruct((tile, 2 * width), bf16),
+        ),
+        [smem, vmem, anywhere, anywhere],
+        (vmem, vmem),
+        [pltpu.VMEM((width, 4 * part), bf16), dma((16,))],
+        1_200_000_000,
+        8_000_000,
+        "projections",
+        24,
+    )(jnp.stack(natural).astype(jnp.int32), grad, w_mine, w_theirs)
     blocks = kernel_call(
         weights_kernel,
         [jax.ShapeDtypeStruct((own_rows, 4 * part), bf16)] * 8,
@@ -387,29 +402,17 @@
         1_200_000_000,
         6_000_000,
         "weight_gradient",
-    )(near.astype(jnp.int32).reshape(1), *tiles, grad, grad_theirs)
+        24,
+    )(after(near.astype(jnp.int32).reshape(1), attended_other), *tiles, grad, grad_theirs)
 
     def block(f, s, n):
         return blocks[((1 - f) * 2 + 1 - s) * 2 + 1 - n]
 
-    attended_own, attended_other = kernel_call(
-        outer_kernel,
-        (
-            jax.ShapeDtypeStruct((tile, 2 * width), f32),
-            jax.ShapeDtypeStruct((tile, 2 * width), bf16),
-        ),
-        [smem, vmem, anywhere, anywhere],
-        (vmem, vmem),
-        [pltpu.VMEM((width, 4 * part), bf16), dma((16,))],
-        1_200_000_000,
-        8_000_000,
-        "projections",
-    )(after(jnp.stack(natural).astype(jnp.int32), blocks[0]), grad, w_mine, w_theirs)
-    side_far_1 = after(swap(block(1, 1, 1), "side"), attended_other)
+    side_far_1 = swap(block(1, 1, 1), "side")
     arrived_back = swap(attended_other, "near")
     side_far_0 = swap(after(block(1, 1, 0), side_far_1), "side")
-    far_1 = swap((block(1, 0, 1).astype(f32) + side_far_1.astype(f32)).astype(bf16), "far")
-    far_0 = swap(after((block(1, 0, 0).astype(f32) + side_far_0.astype(f32)).astype(bf16), (far_1, arrived_back)), "far")
+    far_1 = swap(after((block(1, 0, 1).astype(f32) + side_far_1.astype(f32)).astype(bf16), arrived_back), "far")
+    far_0 = swap(after((block(1, 0, 0).astype(f32) + side_far_0.astype(f32)).astype(bf16), far_1), "far")
     side_1 = swap(after(block(0, 1, 1), side_far_0), "side")
     side_0 = swap(after(block(0, 1, 0), side_1), "side")
     total_1 = (block(0, 0, 1).astype(f32) + side_1.astype(f32) + far_1.astype(f32)).astype(bf16)

time: 158 us -> 145 us (0.918)
  waiting for transfers between devices: 78.2 us -> 70.3 us
  Pallas kernels: 27.3 us -> 20.6 us
  starting transfers between devices: 25.7 us -> 30 us
    ppermute x22, waiting for transfers between devices: 78.2 us -> 70.3 us  [swap(): return lax.ppermute(shard, axis, [(0, 1), (1, 0)])]
    ppermute x22, starting transfers between devices: 25 us -> 29.3 us  [swap(): return lax.ppermute(shard, axis, [(0, 1), (1, 0)])]
    pallas_call x1, Pallas kernels: 4.24 us -> 1.6 us  [on_device(): kernel_call(functools.partial(attention_kernel, area, head), jax.ShapeDty...]
    pallas_call x1, Pallas kernels: 5.96 us -> 3.87 us  [on_device(): kernel_call(weights_kernel, [jax.ShapeDtypeStruct((own_rows, 4 * part), b...]
    pallas_call x1, Pallas kernels: 6.98 us -> 5 us  [on_device(): kernel_call(outer_kernel, (jax.ShapeDtypeStruct((tile, 2 * width), f32),...]
  transfers between devices with their start and end apart: 25 -> 25, of which waited for: 13 -> 10; matrix products, arithmetic and copies ran while one was open for 10% -> 9% of each run, Pallas kernels for 14% -> 10%
where the time goes in v1:
time: 145 us; the launch traced here: 144 us
  waiting for transfers between devices  70.3 us (48%)
  starting transfers between devices  30 us (21%)
  Pallas kernels  20.6 us (14%)
  local copies, waits for them, and re-layouts  11.1 us (8%)
  matrix products  5.73 us (4%)
  other arithmetic  4.65 us (3%)
    ppermute x22, waiting for transfers between devices, swap(): return lax.ppermute(shard, axis, [(0, 1), (1, 0)])  70.3 us
    ppermute x22, starting transfers between devices, swap(): return lax.ppermute(shard, axis, [(0, 1), (1, 0)])  29.3 us
    pallas_call x1, Pallas kernels, on_device(): kernel_call(products_kernel, (jax.ShapeDtypeStruct((2 * tile, 4 * part),...  6.11 us
    unnamed x64, local copies, waits for them, and re-layouts  6.01 us
    pallas_call x1, Pallas kernels, on_device(): kernel_call(outer_kernel, (jax.ShapeDtypeStruct((tile, 2 * width), f32),...  5 us
    pallas_call x1, Pallas kernels, on_device(): kernel_call(turned_rolls, (turned, turned), [smem, vmem] + [anywhere] * 4...  4.04 us
    pallas_call x1, Pallas kernels, on_device(): kernel_call(weights_kernel, [jax.ShapeDtypeStruct((own_rows, 4 * part), b...  3.87 us
    dot_general x1, matrix products, picked(): jnp.dot(onehot, both, preferred_element_type=jnp.float32)  3.1 us
  transfers between devices with their start and end apart: 25, of which 10 were waited for; matrix products, arithmetic and copies ran while one was open for 9% of the time, Pallas kernels for 10%

profile of v1, /device:TPU:6, one launch (start us, length us, event | category | flops | bytes accessed | tf_op | source)
XLA Modules:
  0.0 143.5 jit_solution(14164170616019425552)
XLA Ops:
  0.7 1.3 fusion.81
  2.0 1.6 %collective-permute-start.6 = (bf16[96,1536]{1,0:T(8,128)(2,1)S(1)}, bf16[96,1536]{1,0:T(8,128)(2,1)S(1)}, u32[]{:S(2)}, u32[]{:S(2)}) collective-permute-start(bf16[96,1536]{1,0:T(8,128)(2,1)S(1)} %broadcast_select_fusion.1), channel_id=1, source_target_pairs={{0,4},{4,0},{1,5},{5,1},{2,6},{6,2},{3,7},{7,3},{8,12},{12,8},{9,1... | collective-permute-start | bytes 884744 | tf_op jit(solution)/shard_map/ppermute | solution.py:27
  4.7 6.1 %collective-permute-done.6.refs_5_ = bf16[96,1536]{1,0:T(8,128)(2,1)S(1)} collective-permute-done((bf16[96,1536]{1,0:T(8,128)(2,1)S(1)}, bf16[96,1536]{1,0:T(8,128)(2,1)S(1)}, u32[]{:S(2)}, u32[]{:S(2)}) %collective-permute-start.6) | collective-permute-done | bytes 294944 | tf_op jit(solution)/shard_map/ppermute | solution.py:27
  11.0 2.7 %collective-permute-start.8 = (bf16[96,1536]{1,0:T(8,128)(2,1)S(1)}, bf16[96,1536]{1,0:T(8,128)(2,1)S(1)}, u32[]{:S(2)}, u32[]{:S(2)}) collective-permute-start(bf16[96,1536]{1,0:T(8,128)(2,1)S(1)} %get-tuple-element.61), channel_id=1, source_target_pairs={{0,8},{8,0},{1,9},{9,1},{2,10},{10,2},{3,11},{11,3},{4,12},{12,4},... | collective-permute-start | bytes 884744 | tf_op jit(solution)/shard_map/ppermute | solution.py:27
  16.5 4.0 %turned_rolls.1 = (bf16[2,768,128]{2,1,0:T(8,128)(2,1)}, bf16[2,768,128]{2,1,0:T(8,128)(2,1)}) custom-call(s32[20]{0:T(128)} %concatenate.15.info_ref, f32[1,1536]{1,0:T(1,128)} %reshape.97.gain_ref, bf16[128,1536]{1,0:T(8,128)(2,1)} %bitcast.50, bf16[128,1536]{1,0:T(8,128)(2,1)} %copy-done.19, bf16[128,1536]{1,0:T(8,128)(2,1)} %bitcast.51, ...), custom_call_target="tpu_custom_call" | custom-call | flops 201326592 | bytes 3000000 | tf_op jit(solution)/shard_map/turned_rolls/pallas_call | solution.py:303
  20.6 1.6 %collective-permute-start.4 = (bf16[2,768,128]{2,1,0:T(8,128)(2,1)}, bf16[2,768,128]{2,1,0:T(8,128)(2,1)S(1)}, u32[]{:S(2)}, u32[]{:S(2)}) collective-permute-start(bf16[2,768,128]{2,1,0:T(8,128)(2,1)} %get-tuple-element.31), channel_id=1, source_target_pairs={{0,4},{4,0},{1,5},{5,1},{2,6},{6,2},{3,7},{7,3},{8,12},{12,8},{9,1... | collective-permute-start | bytes 1179656 | tf_op jit(solution)/shard_map/ppermute | solution.py:27
  22.3 5.7 %collective-permute-start.2 = (bf16[2,768,128]{2,1,0:T(8,128)(2,1)}, bf16[2,768,128]{2,1,0:T(8,128)(2,1)S(1)}, u32[]{:S(2)}, u32[]{:S(2)}) collective-permute-start(bf16[2,768,128]{2,1,0:T(8,128)(2,1)} %get-tuple-element.31), channel_id=1, source_target_pairs={{0,1},{1,0},{2,3},{3,2},{4,5},{5,4},{6,7},{7,6},{8,9},{9,8},{10,11... | collective-permute-start | bytes 1179656 | tf_op jit(solution)/shard_map/ppermute | solution.py:27
  28.0 2.0 %collective-permute-start.9 = (bf16[96,1536]{1,0:T(8,128)(2,1)S(1)}, bf16[96,1536]{1,0:T(8,128)(2,1)S(1)}, u32[]{:S(2)}, u32[]{:S(2)}) collective-permute-start(bf16[96,1536]{1,0:T(8,128)(2,1)S(1)} %collective-permute-done.8.refs_8_), channel_id=1, source_target_pairs={{0,2},{2,0},{1,3},{3,1},{4,6},{6,4},{5,7},{7,5},{8,10},{10,8},{9,1... | collective-permute-start | bytes 884744 | tf_op jit(solution)/shard_map/ppermute | solution.py:27
  30.3 3.0 %collective-permute-start.3 = (bf16[2,768,128]{2,1,0:T(8,128)(2,1)}, bf16[2,768,128]{2,1,0:T(8,128)(2,1)S(1)}, u32[]{:S(2)}, u32[]{:S(2)}) collective-permute-start(bf16[2,768,128]{2,1,0:T(8,128)(2,1)} %get-tuple-element.30.refs_0_), channel_id=1, source_target_pairs={{0,4},{4,0},{1,5},{5,1},{2,6},{6,2},{3,7},{7,3},{8,12},{12,8},{9,1... | collective-permute-start | bytes 1179656 | tf_op jit(solution)/shard_map/ppermute | solution.py:27
  33.3 1.4 collective-permute-start.5
  34.8 8.5 %collective-permute-done.9.refs_10_ = bf16[96,1536]{1,0:T(8,128)(2,1)S(1)} collective-permute-done((bf16[96,1536]{1,0:T(8,128)(2,1)S(1)}, bf16[96,1536]{1,0:T(8,128)(2,1)S(1)}, u32[]{:S(2)}, u32[]{:S(2)}) %collective-permute-start.9) | collective-permute-done | bytes 294944 | tf_op jit(solution)/shard_map/ppermute | solution.py:27
  44.1 1.6 %collective-permute-start.12 = (bf16[96,1536]{1,0:T(8,128)(2,1)S(1)}, bf16[96,1536]{1,0:T(8,128)(2,1)}, u32[]{:S(2)}, u32[]{:S(2)}) collective-permute-start(bf16[96,1536]{1,0:T(8,128)(2,1)S(1)} %collective-permute-done.9.refs_10_), channel_id=1, source_target_pairs={{0,16},{16,0},{1,17},{17,1},{2,18},{18,2},{3,19},{19,3},{4,20},{20... | collective-permute-start | bytes 884744 | tf_op jit(solution)/shard_map/ppermute | solution.py:27
  45.7 2.6 %fusion.7 = f32[2,6,64,64]{3,1,2,0:T(8,128)S(1)} fusion(s32[64,64]{1,0:T(8,128)S(1)} %copy-done.31, pred[2,64,64]{2,1,0:T(8,128)(4,1)S(1)} %broadcast_compare_fusion, f32[2,225,6]{1,0,2:T(2,128)S(1)} %constant_dynamic-slice_fusion), kind=kOutput, calls=%fused_computation.9 | convolution fusion | flops 133681152 | bytes 231984 | tf_op jit(solution)/shard_map/qkr,lrh->lhqk/dot_general | solution.py:336
  49.8 3.5 %collective-permute-done.11.refs_9_ = bf16[96,1536]{1,0:T(8,128)(2,1)S(1)} collective-permute-done((bf16[96,1536]{1,0:T(8,128)(2,1)S(1)}, bf16[96,1536]{1,0:T(8,128)(2,1)S(1)}, u32[]{:S(2)}, u32[]{:S(2)}) %collective-permute-start.11) | collective-permute-done | bytes 294944 | tf_op jit(solution)/shard_map/ppermute | solution.py:27
  53.3 4.6 %collective-permute-done.12.refs_11_ = bf16[96,1536]{1,0:T(8,128)(2,1)} collective-permute-done((bf16[96,1536]{1,0:T(8,128)(2,1)S(1)}, bf16[96,1536]{1,0:T(8,128)(2,1)}, u32[]{:S(2)}, u32[]{:S(2)}) %collective-permute-start.12) | collective-permute-done | bytes 294944 | tf_op jit(solution)/shard_map/ppermute | solution.py:27
  57.9 6.1 %products.1 = (f32[256,1536]{1,0:T(8,128)}, bf16[256,1536]{1,0:T(8,128)(2,1)}, bf16[768,1536]{1,0:T(8,128)(2,1)}) custom-call(s32[8]{0:T(128)} %stack.120.place_ref, bf16[2,768,128]{2,1,0:T(8,128)(2,1)} %get-tuple-element.30.refs_0_, bf16[2,768,128]{2,1,0:T(8,128)(2,1)} %copy-done.6, bf16[2,768,128]{2,1,0:T(8,128)(2,1)} %copy-done.8, ...), custom_call_target="tpu_custom_call" | custom-call | flops 1200000000 | bytes 9000000 | tf_op jit(solution)/shard_map/products/pallas_call | solution.py:344
  64.1 2.5 %collective-permute-done.13.came_ref = bf16[256,1536]{1,0:T(8,128)(2,1)S(1)} collective-permute-done((bf16[256,1536]{1,0:T(8,128)(2,1)}, bf16[256,1536]{1,0:T(8,128)(2,1)S(1)}, u32[]{:S(2)}, u32[]{:S(2)}) %collective-permute-start.13) | collective-permute-done | bytes 786464 | tf_op jit(solution)/shard_map/ppermute | solution.py:27
  69.9 1.4 copy-done.12
  71.3 1.6 %attention.1.grad_ref.refs_4_ = bf16[256,1536]{1,0:T(8,128)(2,1)S(1)} custom-call(f32[256,1536]{1,0:T(8,128)S(1)} %copy-done.12, bf16[256,1536]{1,0:T(8,128)(2,1)S(1)} %copy-done.4, f32[2,3,128,64]{3,2,1,0:T(8,128)S(1)} %bitcast.48), custom_call_target="tpu_custom_call" | custom-call | flops 1000000000 | bytes 4000000 | tf_op jit(solution)/shard_map/attention/pallas_call | solution.py:364
  73.8 5.0 %projections.1 = (f32[128,3072]{1,0:T(8,128)S(1)}, bf16[128,3072]{1,0:T(8,128)(2,1)S(1)}) custom-call(s32[16]{0:T(128)S(1)} %stack.111.place_ref, bf16[256,1536]{1,0:T(8,128)(2,1)S(1)} %attention.1.grad_ref.refs_4_, bf16[768,1536]{1,0:T(8,128)(2,1)S(1)} %copy-done.1, bf16[768,1536]{1,0:T(8,128)(2,1)} %collective-permute-done.14.theirs_ref), custom_call_target="tpu_custom_call" | custom-call | flops 1200000000 | bytes 8000000 | tf_op jit(solution)/shard_map/projections/pallas_call | solution.py:378
  79.6 3.9 %weight_gradient.1 = (bf16[96,1536]{1,0:T(8,128)(2,1)S(1)}, bf16[96,1536]{1,0:T(8,128)(2,1)S(1)}, bf16[96,1536]{1,0:T(8,128)(2,1)S(1)}, bf16[96,1536]{1,0:T(8,12...) custom-call(s32[1]{0:T(128)} %bitcast.36.near_ref, ...), custom_call_target="tpu_custom_call" | custom-call | flops 1200000000 | bytes 6000000 | tf_op jit(solution)/shard_map/weight_gradient/pallas_call | solution.py:392
  83.5 1.8 %collective-permute-start.18 = (bf16[96,1536]{1,0:T(8,128)(2,1)S(1)}, bf16[96,1536]{1,0:T(8,128)(2,1)S(1)}, u32[]{:S(2)}, u32[]{:S(2)}) collective-permute-start(bf16[96,1536]{1,0:T(8,128)(2,1)S(1)} %get-tuple-element.45), channel_id=1, source_target_pairs={{0,2},{2,0},{1,3},{3,1},{4,6},{6,4},{5,7},{7,5},{8,10},{10,8},{9,1... | collective-permute-start | bytes 884744 | tf_op jit(solution)/shard_map/ppermute | solution.py:27
  85.9 6.4 %collective-permute-done.18 = bf16[96,1536]{1,0:T(8,128)(2,1)S(1)} collective-permute-done((bf16[96,1536]{1,0:T(8,128)(2,1)S(1)}, bf16[96,1536]{1,0:T(8,128)(2,1)S(1)}, u32[]{:S(2)}, u32[]{:S(2)}) %collective-permute-start.18) | collective-permute-done | bytes 294944 | tf_op jit(solution)/shard_map/ppermute | solution.py:27
  92.3 1.7 %collective-permute-start.19 = (bf16[96,1536]{1,0:T(8,128)(2,1)S(1)}, bf16[96,1536]{1,0:T(8,128)(2,1)S(1)}, u32[]{:S(2)}, u32[]{:S(2)}) collective-permute-start(bf16[96,1536]{1,0:T(8,128)(2,1)S(1)} %get-tuple-element.46), channel_id=1, source_target_pairs={{0,2},{2,0},{1,3},{3,1},{4,6},{6,4},{5,7},{7,5},{8,10},{10,8},{9,1... | collective-permute-start | bytes 884744 | tf_op jit(solution)/shard_map/ppermute | solution.py:27
  94.1 6.1 %collective-permute-done.19 = bf16[96,1536]{1,0:T(8,128)(2,1)S(1)} collective-permute-done((bf16[96,1536]{1,0:T(8,128)(2,1)S(1)}, bf16[96,1536]{1,0:T(8,128)(2,1)S(1)}, u32[]{:S(2)}, u32[]{:S(2)}) %collective-permute-start.19) | collective-permute-done | bytes 294944 | tf_op jit(solution)/shard_map/ppermute | solution.py:27
  100.2 1.7 %collective-permute-start.20 = (bf16[96,1536]{1,0:T(8,128)(2,1)S(1)}, bf16[96,1536]{1,0:T(8,128)(2,1)S(1)}, u32[]{:S(2)}, u32[]{:S(2)}) collective-permute-start(bf16[96,1536]{1,0:T(8,128)(2,1)S(1)} %get-tuple-element.47), channel_id=1, source_target_pairs={{0,2},{2,0},{1,3},{3,1},{4,6},{6,4},{5,7},{7,5},{8,10},{10,8},{9,1... | collective-permute-start | bytes 884744 | tf_op jit(solution)/shard_map/ppermute | solution.py:27
  101.9 1.9 %collective-permute-start.22 = (bf16[96,1536]{1,0:T(8,128)(2,1)S(1)}, bf16[96,1536]{1,0:T(8,128)(2,1)S(1)}, u32[]{:S(2)}, u32[]{:S(2)}) collective-permute-start(bf16[96,1536]{1,0:T(8,128)(2,1)S(1)} %add_convert_fusion.3), channel_id=1, source_target_pairs={{0,8},{8,0},{1,9},{9,1},{2,10},{10,2},{3,11},{11,3},{4,12},{12,4},... | collective-permute-start | bytes 884744 | tf_op jit(solution)/shard_map/ppermute | solution.py:27
  104.1 3.0 %collective-permute-done.20 = bf16[96,1536]{1,0:T(8,128)(2,1)S(1)} collective-permute-done((bf16[96,1536]{1,0:T(8,128)(2,1)S(1)}, bf16[96,1536]{1,0:T(8,128)(2,1)S(1)}, u32[]{:S(2)}, u32[]{:S(2)}) %collective-permute-start.20) | collective-permute-done | bytes 294944 | tf_op jit(solution)/shard_map/ppermute | solution.py:27
  107.2 17.1 %collective-permute-done.22 = bf16[96,1536]{1,0:T(8,128)(2,1)S(1)} collective-permute-done((bf16[96,1536]{1,0:T(8,128)(2,1)S(1)}, bf16[96,1536]{1,0:T(8,128)(2,1)S(1)}, u32[]{:S(2)}, u32[]{:S(2)}) %collective-permute-start.22) | collective-permute-done | bytes 294944 | tf_op jit(solution)/shard_map/ppermute | solution.py:27
  124.7 12.4 %collective-permute-done.24 = bf16[96,1536]{1,0:T(8,128)(2,1)S(1)} collective-permute-done((bf16[96,1536]{1,0:T(8,128)(2,1)S(1)}, bf16[96,1536]{1,0:T(8,128)(2,1)S(1)}, u32[]{:S(2)}, u32[]{:S(2)}) %collective-permute-start.24) | collective-permute-done | bytes 294944 | tf_op jit(solution)/shard_map/ppermute | solution.py:27
  137.2 3.1 %convolution_convert_fusion = bf16[128,3072]{1,0:T(8,128)(2,1)S(1)} fusion(bf16[128,3072]{1,0:T(8,128)(2,1)S(1)} %add_convert_fusion, bf16[128,3072]{1,0:T(8,128)(2,1)S(1)} %collective-permute-done.16, s32[]{:T(128)} %bitcast.4, s32[]{:T(128)} %bitcast.3, s32[128]{0:T(128)S(1)} %get-tuple-element.85, s32[128]{0:T(128)S(1)} %get-tuple-element.87, ...), kind=kOutput, calls=%fused_computation.3 | convolution fusion | flops 206700544 | bytes 2362768 | tf_op jit(solution)/shard_map/dot_general | solution.py:52
  140.7 1.4 fusion.18
  (138 shorter events, 14.8 us)
Async XLA Ops:
  0.6 45.1 %copy-start = (f32[2,225,12]{1,0,2:T(2,128)S(1)}, f32[2,225,12]{1,0,2:T(2,128)}, u32[]{:S(2)}) copy-start(f32[2,225,12]{1,0,2:T(2,128)} %param.16) | copy-start | bytes 64804
  2.0 8.8 %collective-permute-start.6 = (bf16[96,1536]{1,0:T(8,128)(2,1)S(1)}, bf16[96,1536]{1,0:T(8,128)(2,1)S(1)}, u32[]{:S(2)}, u32[]{:S(2)}) collective-permute-start(bf16[96,1536]{1,0:T(8,128)(2,1)S(1)} %broadcast_select_fusion.1), channel_id=1, source_target_pairs={{0,4},{4,0},{1,5},{5,1},{2,6},{6,2},{3,7},{7,3},{8,12},{12,8},{9,1... | collective-permute-start | bytes 884744 | tf_op jit(solution)/shard_map/ppermute | solution.py:27
  3.9 9.9 %copy-start.23 = (f32[1536]{0:T(1024)S(1)}, f32[1536]{0:T(1024)}, u32[]{:S(2)}) copy-start(f32[1536]{0:T(1024)} %param.12) | copy-start | bytes 18436
  4.1 11.0 %copy-start.13 = (bf16[2,8,8,1536]{3,2,1,0:T(8,128)(2,1)}, bf16[2,8,8,1536]{3,2,1,0:T(8,128)(2,1)S(1)}, u32[]{:S(2)}) copy-start(bf16[2,8,8,1536]{3,2,1,0:T(8,128)(2,1)S(1)} %get-tuple-element.60) | copy-start | bytes 1179652
  4.1 10.9 %collective-permute-start = (bf16[128,1536]{1,0:T(8,128)(2,1)S(1)}, bf16[128,1536]{1,0:T(8,128)(2,1)S(1)}, u32[]{:S(2)}, u32[]{:S(2)}) collective-permute-start(bf16[128,1536]{1,0:T(8,128)(2,1)S(1)} %bitcast.49), channel_id=1, source_target_pairs={{0,15},{1,0},{2,1},{3,2},{4,3},{5,4},{6,5},{7,6},{8,7},{9,8},{10,9... | collective-permute-start | bytes 1179656 | tf_op jit(solution)/shard_map/ppermute | solution.py:18
  4.1 10.9 %collective-permute-start.1 = (bf16[128,1536]{1,0:T(8,128)(2,1)S(1)}, bf16[128,1536]{1,0:T(8,128)(2,1)S(1)}, u32[]{:S(2)}, u32[]{:S(2)}) collective-permute-start(bf16[128,1536]{1,0:T(8,128)(2,1)S(1)} %bitcast.52), channel_id=1, source_target_pairs={{0,15},{1,0},{2,1},{3,2},{4,3},{5,4},{6,5},{7,6},{8,7},{9,8},{10,9... | collective-permute-start | bytes 1179656 | tf_op jit(solution)/shard_map/ppermute | solution.py:18
  10.9 32.8 %copy-start.21 = (bf16[96,1536]{1,0:T(8,128)(2,1)}, bf16[96,1536]{1,0:T(8,128)(2,1)S(1)}, u32[]{:S(2)}) copy-start(bf16[96,1536]{1,0:T(8,128)(2,1)S(1)} %collective-permute-done.6.refs_5_) | copy-start | bytes 884740
  11.0 46.9 %copy-start.22 = (bf16[96,1536]{1,0:T(8,128)(2,1)}, bf16[96,1536]{1,0:T(8,128)(2,1)S(1)}, u32[]{:S(2)}) copy-start(bf16[96,1536]{1,0:T(8,128)(2,1)S(1)} %get-tuple-element.32.refs_4_) | copy-start | bytes 884740
  11.0 34.7 %copy-start.31 = (s32[64,64]{1,0:T(8,128)S(1)}, s32[64,64]{1,0:T(8,128)}, u32[]{:S(2)}) copy-start(s32[64,64]{1,0:T(8,128)} %param.15) | copy-start | bytes 49156
  11.0 17.0 %collective-permute-start.8 = (bf16[96,1536]{1,0:T(8,128)(2,1)S(1)}, bf16[96,1536]{1,0:T(8,128)(2,1)S(1)}, u32[]{:S(2)}, u32[]{:S(2)}) collective-permute-start(bf16[96,1536]{1,0:T(8,128)(2,1)S(1)} %get-tuple-element.61), channel_id=1, source_target_pairs={{0,8},{8,0},{1,9},{9,1},{2,10},{10,2},{3,11},{11,3},{4,12},{12,4},... | collective-permute-start | bytes 884744 | tf_op jit(solution)/shard_map/ppermute | solution.py:27
  20.6 12.7 %collective-permute-start.4 = (bf16[2,768,128]{2,1,0:T(8,128)(2,1)}, bf16[2,768,128]{2,1,0:T(8,128)(2,1)S(1)}, u32[]{:S(2)}, u32[]{:S(2)}) collective-permute-start(bf16[2,768,128]{2,1,0:T(8,128)(2,1)} %get-tuple-element.31), channel_id=1, source_target_pairs={{0,4},{4,0},{1,5},{5,1},{2,6},{6,2},{3,7},{7,3},{8,12},{12,8},{9,1... | collective-permute-start | bytes 1179656 | tf_op jit(solution)/shard_map/ppermute | solution.py:27
  22.3 21.7 %collective-permute-start.2 = (bf16[2,768,128]{2,1,0:T(8,128)(2,1)}, bf16[2,768,128]{2,1,0:T(8,128)(2,1)S(1)}, u32[]{:S(2)}, u32[]{:S(2)}) collective-permute-start(bf16[2,768,128]{2,1,0:T(8,128)(2,1)} %get-tuple-element.31), channel_id=1, source_target_pairs={{0,1},{1,0},{2,3},{3,2},{4,5},{5,4},{6,7},{7,6},{8,9},{9,8},{10,11... | collective-permute-start | bytes 1179656 | tf_op jit(solution)/shard_map/ppermute | solution.py:27
  28.0 15.7 %collective-permute-start.7 = (bf16[96,1536]{1,0:T(8,128)(2,1)S(1)}, bf16[96,1536]{1,0:T(8,128)(2,1)S(1)}, u32[]{:S(2)}, u32[]{:S(2)}) collective-permute-start(bf16[96,1536]{1,0:T(8,128)(2,1)S(1)} %get-tuple-element.32.refs_4_), channel_id=1, source_target_pairs={{0,2},{2,0},{1,3},{3,1},{4,6},{6,4},{5,7},{7,5},{8,10},{10,8},{9,1... | collective-permute-start | bytes 884744 | tf_op jit(solution)/shard_map/ppermute | solution.py:27
  28.0 21.2 %copy-start.27 = (bf16[96,1536]{1,0:T(8,128)(2,1)}, bf16[96,1536]{1,0:T(8,128)(2,1)S(1)}, u32[]{:S(2)}) copy-start(bf16[96,1536]{1,0:T(8,128)(2,1)S(1)} %collective-permute-done.8.refs_8_) | copy-start | bytes 884740
  28.0 15.3 %collective-permute-start.9 = (bf16[96,1536]{1,0:T(8,128)(2,1)S(1)}, bf16[96,1536]{1,0:T(8,128)(2,1)S(1)}, u32[]{:S(2)}, u32[]{:S(2)}) collective-permute-start(bf16[96,1536]{1,0:T(8,128)(2,1)S(1)} %collective-permute-done.8.refs_8_), channel_id=1, source_target_pairs={{0,2},{2,0},{1,3},{3,1},{4,6},{6,4},{5,7},{7,5},{8,10},{10,8},{9,1... | collective-permute-start | bytes 884744 | tf_op jit(solution)/shard_map/ppermute | solution.py:27
  30.3 19.5 %collective-permute-start.3 = (bf16[2,768,128]{2,1,0:T(8,128)(2,1)}, bf16[2,768,128]{2,1,0:T(8,128)(2,1)S(1)}, u32[]{:S(2)}, u32[]{:S(2)}) collective-permute-start(bf16[2,768,128]{2,1,0:T(8,128)(2,1)} %get-tuple-element.30.refs_0_), channel_id=1, source_target_pairs={{0,4},{4,0},{1,5},{5,1},{2,6},{6,2},{3,7},{7,3},{8,12},{12,8},{9,1... | collective-permute-start | bytes 1179656 | tf_op jit(solution)/shard_map/ppermute | solution.py:27
  33.3 20.0 %collective-permute-start.5 = (bf16[2,768,128]{2,1,0:T(8,128)(2,1)S(1)}, bf16[2,768,128]{2,1,0:T(8,128)(2,1)S(1)}, u32[]{:S(2)}, u32[]{:S(2)}) collective-permute-start(bf16[2,768,128]{2,1,0:T(8,128)(2,1)S(1)} %collective-permute-done.4), channel_id=1, source_target_pairs={{0,1},{1,0},{2,3},{3,2},{4,5},{5,4},{6,7},{7,6},{8,9},{9,8},{10,11... | collective-permute-start | bytes 1179656 | tf_op jit(solution)/shard_map/ppermute | solution.py:27
  43.3 9.9 %collective-permute-start.11 = (bf16[96,1536]{1,0:T(8,128)(2,1)S(1)}, bf16[96,1536]{1,0:T(8,128)(2,1)S(1)}, u32[]{:S(2)}, u32[]{:S(2)}) collective-permute-start(bf16[96,1536]{1,0:T(8,128)(2,1)S(1)} %collective-permute-done.8.refs_8_), channel_id=1, source_target_pairs={{0,16},{16,0},{1,17},{17,1},{2,18},{18,2},{3,19},{19,3},{4,20},{20... | collective-permute-start | bytes 884744 | tf_op jit(solution)/shard_map/ppermute | solution.py:27
  43.7 9.6 %collective-permute-start.10 = (bf16[96,1536]{1,0:T(8,128)(2,1)S(1)}, bf16[96,1536]{1,0:T(8,128)(2,1)}, u32[]{:S(2)}, u32[]{:S(2)}) collective-permute-start(bf16[96,1536]{1,0:T(8,128)(2,1)S(1)} %collective-permute-done.6.refs_5_), channel_id=1, source_target_pairs={{0,2},{2,0},{1,3},{3,1},{4,6},{6,4},{5,7},{7,5},{8,10},{10,8},{9,1... | collective-permute-start | bytes 884744 | tf_op jit(solution)/shard_map/ppermute | solution.py:27
  44.1 13.8 %collective-permute-start.12 = (bf16[96,1536]{1,0:T(8,128)(2,1)S(1)}, bf16[96,1536]{1,0:T(8,128)(2,1)}, u32[]{:S(2)}, u32[]{:S(2)}) collective-permute-start(bf16[96,1536]{1,0:T(8,128)(2,1)S(1)} %collective-permute-done.9.refs_10_), channel_id=1, source_target_pairs={{0,16},{16,0},{1,17},{17,1},{2,18},{18,2},{3,19},{19,3},{4,20},{20... | collective-permute-start | bytes 884744 | tf_op jit(solution)/shard_map/ppermute | solution.py:27
  64.0 2.6 %collective-permute-start.13 = (bf16[256,1536]{1,0:T(8,128)(2,1)}, bf16[256,1536]{1,0:T(8,128)(2,1)S(1)}, u32[]{:S(2)}, u32[]{:S(2)}) collective-permute-start(bf16[256,1536]{1,0:T(8,128)(2,1)} %get-tuple-element.35), channel_id=1, source_target_pairs={{0,1},{1,0},{2,3},{3,2},{4,5},{5,4},{6,7},{7,6},{8,9},{9,8},{10,11... | collective-permute-start | bytes 2359304 | tf_op jit(solution)/shard_map/ppermute | solution.py:27
  67.5 6.3 %collective-permute-start.14 = (bf16[768,1536]{1,0:T(8,128)(2,1)}, bf16[768,1536]{1,0:T(8,128)(2,1)}, u32[]{:S(2)}, u32[]{:S(2)}) collective-permute-start(bf16[768,1536]{1,0:T(8,128)(2,1)} %get-tuple-element.37.mine_ref), channel_id=1, source_target_pairs={{0,1},{1,0},{2,3},{3,2},{4,5},{5,4},{6,7},{7,6},{8,9},{9,8},{10,11... | collective-permute-start | bytes 7077896 | tf_op jit(solution)/shard_map/ppermute | solution.py:27
  72.9 6.6 %collective-permute-start.17 = (bf16[256,1536]{1,0:T(8,128)(2,1)S(1)}, bf16[256,1536]{1,0:T(8,128)(2,1)}, u32[]{:S(2)}, u32[]{:S(2)}) collective-permute-start(bf16[256,1536]{1,0:T(8,128)(2,1)S(1)} %attention.1.grad_ref.refs_4_), channel_id=1, source_target_pairs={{0,1},{1,0},{2,3},{3,2},{4,5},{5,4},{6,7},{7,6},{8,9},{9,8},{10,11... | collective-permute-start | bytes 2359304 | tf_op jit(solution)/shard_map/ppermute | solution.py:27
  78.8 23.1 %collective-permute-start.15 = (bf16[128,3072]{1,0:T(8,128)(2,1)S(1)}, bf16[128,3072]{1,0:T(8,128)(2,1)S(1)}, u32[]{:S(2)}, u32[]{:S(2)}) collective-permute-start(bf16[128,3072]{1,0:T(8,128)(2,1)S(1)} %get-tuple-element.39), channel_id=1, source_target_pairs={{0,4},{4,0},{1,5},{5,1},{2,6},{6,2},{3,7},{7,3},{8,12},{12,8},{9,1... | collective-permute-start | bytes 2359304 | tf_op jit(solution)/shard_map/ppermute | solution.py:27
  83.5 8.8 %collective-permute-start.18 = (bf16[96,1536]{1,0:T(8,128)(2,1)S(1)}, bf16[96,1536]{1,0:T(8,128)(2,1)S(1)}, u32[]{:S(2)}, u32[]{:S(2)}) collective-permute-start(bf16[96,1536]{1,0:T(8,128)(2,1)S(1)} %get-tuple-element.45), channel_id=1, source_target_pairs={{0,2},{2,0},{1,3},{3,1},{4,6},{6,4},{5,7},{7,5},{8,10},{10,8},{9,1... | collective-permute-start | bytes 884744 | tf_op jit(solution)/shard_map/ppermute | solution.py:27
  92.3 7.9 %collective-permute-start.19 = (bf16[96,1536]{1,0:T(8,128)(2,1)S(1)}, bf16[96,1536]{1,0:T(8,128)(2,1)S(1)}, u32[]{:S(2)}, u32[]{:S(2)}) collective-permute-start(bf16[96,1536]{1,0:T(8,128)(2,1)S(1)} %get-tuple-element.46), channel_id=1, source_target_pairs={{0,2},{2,0},{1,3},{3,1},{4,6},{6,4},{5,7},{7,5},{8,10},{10,8},{9,1... | collective-permute-start | bytes 884744 | tf_op jit(solution)/shard_map/ppermute | solution.py:27
  100.2 7.0 %collective-permute-start.20 = (bf16[96,1536]{1,0:T(8,128)(2,1)S(1)}, bf16[96,1536]{1,0:T(8,128)(2,1)S(1)}, u32[]{:S(2)}, u32[]{:S(2)}) collective-permute-start(bf16[96,1536]{1,0:T(8,128)(2,1)S(1)} %get-tuple-element.47), channel_id=1, source_target_pairs={{0,2},{2,0},{1,3},{3,1},{4,6},{6,4},{5,7},{7,5},{8,10},{10,8},{9,1... | collective-permute-start | bytes 884744 | tf_op jit(solution)/shard_map/ppermute | solution.py:27
  101.9 22.3 %collective-permute-start.22 = (bf16[96,1536]{1,0:T(8,128)(2,1)S(1)}, bf16[96,1536]{1,0:T(8,128)(2,1)S(1)}, u32[]{:S(2)}, u32[]{:S(2)}) collective-permute-start(bf16[96,1536]{1,0:T(8,128)(2,1)S(1)} %add_convert_fusion.3), channel_id=1, source_target_pairs={{0,8},{8,0},{1,9},{9,1},{2,10},{10,2},{3,11},{11,3},{4,12},{12,4},... | collective-permute-start | bytes 884744 | tf_op jit(solution)/shard_map/ppermute | solution.py:27
  104.1 33.1 %collective-permute-start.16 = (bf16[128,3072]{1,0:T(8,128)(2,1)S(1)}, bf16[128,3072]{1,0:T(8,128)(2,1)S(1)}, u32[]{:S(2)}, u32[]{:S(2)}) collective-permute-start(bf16[128,3072]{1,0:T(8,128)(2,1)S(1)} %add_convert_fusion), channel_id=1, source_target_pairs={{0,1},{1,2},{2,3},{3,4},{4,5},{5,6},{6,7},{7,8},{8,9},{9,10},{10,1... | collective-permute-start | bytes 2359304 | tf_op jit(solution)/shard_map/ppermute | solution.py:18
  124.4 12.7 %collective-permute-start.24 = (bf16[96,1536]{1,0:T(8,128)(2,1)S(1)}, bf16[96,1536]{1,0:T(8,128)(2,1)S(1)}, u32[]{:S(2)}, u32[]{:S(2)}) collective-permute-start(bf16[96,1536]{1,0:T(8,128)(2,1)S(1)} %add_convert_fusion.2), channel_id=1, source_target_pairs={{0,4},{4,0},{1,5},{5,1},{2,6},{6,2},{3,7},{7,3},{8,12},{12,8},{9,1... | collective-permute-start | bytes 884744 | tf_op jit(solution)/shard_map/ppermute | solution.py:27
  124.5 17.5 %collective-permute-start.21 = (bf16[96,1536]{1,0:T(8,128)(2,1)S(1)}, bf16[96,1536]{1,0:T(8,128)(2,1)S(1)}, u32[]{:S(2)}, u32[]{:S(2)}) collective-permute-start(bf16[96,1536]{1,0:T(8,128)(2,1)S(1)} %get-tuple-element.48), channel_id=1, source_target_pairs={{0,2},{2,0},{1,3},{3,1},{4,6},{6,4},{5,7},{7,5},{8,10},{10,8},{9,1... | collective-permute-start | bytes 884744 | tf_op jit(solution)/shard_map/ppermute | solution.py:27
  124.6 17.4 %collective-permute-start.23 = (bf16[96,1536]{1,0:T(8,128)(2,1)S(1)}, bf16[96,1536]{1,0:T(8,128)(2,1)S(1)}, u32[]{:S(2)}, u32[]{:S(2)}) collective-permute-start(bf16[96,1536]{1,0:T(8,128)(2,1)S(1)} %add_convert_fusion.4), channel_id=1, source_target_pairs={{0,8},{8,0},{1,9},{9,1},{2,10},{10,2},{3,11},{11,3},{4,12},{12,4},... | collective-permute-start | bytes 884744 | tf_op jit(solution)/shard_map/ppermute | solution.py:27
  (25 other events, 95.3 us)

commit v2 on v1

--- a/solution.py
+++ b/solution.py
@@ -52,13 +52,13 @@
     return jnp.dot(onehot, both, preferred_element_type=jnp.float32).astype(jnp.bfloat16)
 
 
-def roll_back(field, shifts, levels, side):
+def roll_back(field, shifts, levels, side, wait):
     zeros = jnp.zeros_like(shifts[:, 0])
     rows = side - shifts[:, 0]
     more = lax.axis_size("lat") > 1
     field = picked(
         pick(zeros if more else rows, side - shifts[:, 1], levels, side, False),
-        along_lon(field, 1),
+        after(along_lon(field, 1), wait),
         field,
     )
     if more:
@@ -279,7 +279,8 @@
     spread = lax.rsqrt(jnp.mean(center * center, axis=-1, keepdims=True) + epsilon)
 
     held = near ^ grp
-    across_far = swap(jnp.where(grp == 0, mine, came), "far")
+    half_piece = jnp.where(grp == 0, mine, came)
+    across_far = swap(half_piece, "far")
     order = [(f, s, n) for f in (1, 0) for s in (1, 0) for n in (0, 1)]
     natural = [place(f, near ^ n, s, c) for c in (0, 1) for f, s, n in order]
 
@@ -314,22 +315,22 @@
         3_000_000,
         "turned_rolls",
     )(info, gain.reshape(1, -1), below, along_lon(below, -1), below_cot, along_lon(below_cot, -1))
-    mine_side = swap(after(mine, own_turned), "side")
+    half_side = swap(after(half_piece, own_turned), "side")
     far_side = swap(across_far, "side")
-    came_side = swap(after(came, far_side), "side")
+    side_grp, far_grp = swap(half_side, "grp"), swap(across_far, "grp")
     pieces = [
         (mine, 0, 0, near),
         (came, 0, 0, 1 - near),
-        (mine_side, 0, 1, near),
-        (came_side, 0, 1, 1 - near),
+        (half_side, 0, 1, held),
+        (side_grp, 0, 1, 1 - held),
         (across_far, 1, 0, held),
-        (swap(across_far, "grp"), 1, 0, 1 - held),
+        (far_grp, 1, 0, 1 - held),
         (far_side, 1, 1, held),
         (swap(far_side, "grp"), 1, 1, 1 - held),
     ]
     places = jnp.stack([(1 - f) * 4 + (1 - s) * 2 + n for _, f, s, n in pieces]).astype(jnp.int32)
     own_near, sent_near = swap(own_turned, "near"), swap(sent_turned, "near")
-    tiles = [own_turned, swap(sent_turned, "core"), own_near, swap(sent_near, "core")]
+    tiles = [own_turned, swap(after(sent_turned, (sent_near, side_grp)), "core"), own_near, swap(after(sent_near, (far_grp, side_grp)), "core")]
 
     onehot = (index_table[:, :, None] == jnp.arange(entries, dtype=jnp.int32)).astype(f32)
     own_table = lax.dynamic_slice_in_dim(bias_table, near * own_heads, own_heads, 2)
@@ -371,7 +372,6 @@
         1_000_000_000,
         4_000_000,
         "attention",
-        24,
     )(kept, crossed, bias)
     w_theirs = swap(after(w_mine, crossed), "core")
     grad_theirs = swap(grad, "core")
@@ -410,16 +410,16 @@
 
     side_far_1 = swap(block(1, 1, 1), "side")
     arrived_back = swap(attended_other, "near")
-    side_far_0 = swap(after(block(1, 1, 0), side_far_1), "side")
-    far_1 = swap(after((block(1, 0, 1).astype(f32) + side_far_1.astype(f32)).astype(bf16), arrived_back), "far")
-    far_0 = swap(after((block(1, 0, 0).astype(f32) + side_far_0.astype(f32)).astype(bf16), far_1), "far")
+    side_far_0 = swap(after(block(1, 1, 0), (side_far_1, arrived_back)), "side")
+    far_1 = swap((block(1, 0, 1).astype(f32) + side_far_1.astype(f32)).astype(bf16), "far")
+    far_0 = swap(after((block(1, 0, 0).astype(f32) + side_far_0.astype(f32)).astype(bf16), side_far_1), "far")
     side_1 = swap(after(block(0, 1, 1), side_far_0), "side")
     side_0 = swap(after(block(0, 1, 0), side_1), "side")
     total_1 = (block(0, 0, 1).astype(f32) + side_1.astype(f32) + far_1.astype(f32)).astype(bf16)
     theirs = swap(total_1, "near").astype(f32)
 
     back = (attended_own + arrived_back.astype(f32)).astype(jnp.bfloat16)
-    back = roll_back(back, shifts, levels, side)
+    back = roll_back(back, shifts, levels, side, far_0)
     output = (values + back[:, :width].astype(f32)).astype(jnp.bfloat16)
     scaled = center * spread
     upstream = back[:, width:].astype(f32) * gain

time: 145 us -> 144 us (level)
  waiting for transfers between devices: 70.3 us -> 63.7 us
  starting transfers between devices: 30 us -> 33.8 us
  Pallas kernels: 20.6 us -> 22.2 us
    ppermute x22, waiting for transfers between devices: 70.3 us -> 63.7 us  [swap(): return lax.ppermute(shard, axis, [(0, 1), (1, 0)])]
    ppermute x22, starting transfers between devices: 29.3 us -> 33.1 us  [swap(): return lax.ppermute(shard, axis, [(0, 1), (1, 0)])]
    pallas_call x1, Pallas kernels: 1.6 us -> 4.34 us  [on_device(): kernel_call(functools.partial(attention_kernel, area, head), jax.ShapeDty...]
    unnamed x64, local copies, waits for them, and re-layouts: 6.01 us -> 4.55 us
  transfers between devices with their start and end apart: 25 -> 25, of which waited for: 10 -> 12; matrix products, arithmetic and copies ran while one was open for 9% -> 9% of each run, Pallas kernels for 10% -> 11%
where the time goes in v2:
time: 144 us; the launch traced here: 142 us
  waiting for transfers between devices  63.7 us (44%)
  starting transfers between devices  33.8 us (23%)
  Pallas kernels  22.2 us (15%)
  local copies, waits for them, and re-layouts  9.66 us (7%)
  matrix products  5.74 us (4%)
  other arithmetic  5.3 us (4%)
    ppermute x22, waiting for transfers between devices, swap(): return lax.ppermute(shard, axis, [(0, 1), (1, 0)])  63.7 us
    ppermute x22, starting transfers between devices, swap(): return lax.ppermute(shard, axis, [(0, 1), (1, 0)])  33.1 us
    pallas_call x1, Pallas kernels, on_device(): kernel_call(products_kernel, (jax.ShapeDtypeStruct((2 * tile, 4 * part),...  6.09 us
    pallas_call x1, Pallas kernels, on_device(): kernel_call(outer_kernel, (jax.ShapeDtypeStruct((tile, 2 * width), f32),...  5.01 us
    unnamed x64, local copies, waits for them, and re-layouts  4.55 us
    pallas_call x1, Pallas kernels, on_device(): kernel_call(functools.partial(attention_kernel, area, head), jax.ShapeDty...  4.34 us
    pallas_call x1, Pallas kernels, on_device(): kernel_call(turned_rolls, (turned, turned), [smem, vmem] + [anywhere] * 4...  4.01 us
    dot_general x1, matrix products, picked(): jnp.dot(onehot, both, preferred_element_type=jnp.float32)  3.09 us
  transfers between devices with their start and end apart: 25, of which 12 were waited for; matrix products, arithmetic and copies ran while one was open for 9% of the time, Pallas kernels for 11%

profile of v2, /device:TPU:6, one launch (start us, length us, event | category | flops | bytes accessed | tf_op | source)
XLA Modules:
  0.0 141.7 jit_solution(7030920166135792461)
XLA Ops:
  0.7 1.3 fusion.81
  2.1 1.6 %collective-permute-start.3 = (bf16[96,1536]{1,0:T(8,128)(2,1)S(1)}, bf16[96,1536]{1,0:T(8,128)(2,1)S(1)}, u32[]{:S(2)}, u32[]{:S(2)}) collective-permute-start(bf16[96,1536]{1,0:T(8,128)(2,1)S(1)} %broadcast_select_fusion), channel_id=1, source_target_pairs={{0,4},{4,0},{1,5},{5,1},{2,6},{6,2},{3,7},{7,3},{8,12},{12,8},{9,1... | collective-permute-start | bytes 884744 | tf_op jit(solution)/shard_map/ppermute | solution.py:27
  6.0 4.8 %collective-permute-done.3.refs_5_ = bf16[96,1536]{1,0:T(8,128)(2,1)S(1)} collective-permute-done((bf16[96,1536]{1,0:T(8,128)(2,1)S(1)}, bf16[96,1536]{1,0:T(8,128)(2,1)S(1)}, u32[]{:S(2)}, u32[]{:S(2)}) %collective-permute-start.3) | collective-permute-done | bytes 294944 | tf_op jit(solution)/shard_map/ppermute | solution.py:27
  11.7 2.6 %collective-permute-start.8 = (bf16[96,1536]{1,0:T(8,128)(2,1)S(1)}, bf16[96,1536]{1,0:T(8,128)(2,1)S(1)}, u32[]{:S(2)}, u32[]{:S(2)}) collective-permute-start(bf16[96,1536]{1,0:T(8,128)(2,1)S(1)} %get-tuple-element.33), channel_id=1, source_target_pairs={{0,8},{8,0},{1,9},{9,1},{2,10},{10,2},{3,11},{11,3},{4,12},{12,4},... | collective-permute-start | bytes 884744 | tf_op jit(solution)/shard_map/ppermute | solution.py:27
  15.8 4.0 %turned_rolls.1 = (bf16[2,768,128]{2,1,0:T(8,128)(2,1)}, bf16[2,768,128]{2,1,0:T(8,128)(2,1)}) custom-call(s32[20]{0:T(128)} %concatenate.15.info_ref, f32[1,1536]{1,0:T(1,128)} %reshape.97.gain_ref, bf16[128,1536]{1,0:T(8,128)(2,1)} %bitcast.49, bf16[128,1536]{1,0:T(8,128)(2,1)} %copy-done.17, bf16[128,1536]{1,0:T(8,128)(2,1)} %bitcast.50, ...), custom_call_target="tpu_custom_call" | custom-call | flops 201326592 | bytes 3000000 | tf_op jit(solution)/shard_map/turned_rolls/pallas_call | solution.py:304
  19.9 7.2 %collective-permute-start.4 = (bf16[96,1536]{1,0:T(8,128)(2,1)S(1)}, bf16[96,1536]{1,0:T(8,128)(2,1)S(1)}, u32[]{:S(2)}, u32[]{:S(2)}) collective-permute-start(bf16[96,1536]{1,0:T(8,128)(2,1)S(1)} %get-tuple-element.33), channel_id=1, source_target_pairs={{0,2},{2,0},{1,3},{3,1},{4,6},{6,4},{5,7},{7,5},{8,10},{10,8},{9,1... | collective-permute-start | bytes 884744 | tf_op jit(solution)/shard_map/ppermute | solution.py:27
  27.6 7.2 %collective-permute-done.4.refs_6_ = bf16[96,1536]{1,0:T(8,128)(2,1)S(1)} collective-permute-done((bf16[96,1536]{1,0:T(8,128)(2,1)S(1)}, bf16[96,1536]{1,0:T(8,128)(2,1)S(1)}, u32[]{:S(2)}, u32[]{:S(2)}) %collective-permute-start.4) | collective-permute-done | bytes 294944 | tf_op jit(solution)/shard_map/ppermute | solution.py:27
  36.1 1.1 collective-permute-done.2
  37.3 6.6 %collective-permute-done.5.refs_7_ = bf16[96,1536]{1,0:T(8,128)(2,1)S(1)} collective-permute-done((bf16[96,1536]{1,0:T(8,128)(2,1)S(1)}, bf16[96,1536]{1,0:T(8,128)(2,1)S(1)}, u32[]{:S(2)}, u32[]{:S(2)}) %collective-permute-start.5) | collective-permute-done | bytes 294944 | tf_op jit(solution)/shard_map/ppermute | solution.py:27
  44.5 1.3 collective-permute-start.12
  45.8 2.6 %fusion.7 = f32[2,6,64,64]{3,1,2,0:T(8,128)S(1)} fusion(s32[64,64]{1,0:T(8,128)S(1)} %copy-done.31, pred[2,64,64]{2,1,0:T(8,128)(4,1)S(1)} %broadcast_compare_fusion, f32[2,225,6]{1,0,2:T(2,128)S(1)} %constant_dynamic-slice_fusion), kind=kOutput, calls=%fused_computation.9 | convolution fusion | flops 133681152 | bytes 231984 | tf_op jit(solution)/shard_map/qkr,lrh->lhqk/dot_general | solution.py:337
  50.0 3.6 %collective-permute-done.12.refs_11_ = bf16[96,1536]{1,0:T(8,128)(2,1)S(1)} collective-permute-done((bf16[96,1536]{1,0:T(8,128)(2,1)S(1)}, bf16[96,1536]{1,0:T(8,128)(2,1)S(1)}, u32[]{:S(2)}, u32[]{:S(2)}) %collective-permute-start.12) | collective-permute-done | bytes 294944 | tf_op jit(solution)/shard_map/ppermute | solution.py:27
  54.6 6.1 %products.1 = (f32[256,1536]{1,0:T(8,128)}, bf16[256,1536]{1,0:T(8,128)(2,1)}, bf16[768,1536]{1,0:T(8,128)(2,1)}) custom-call(s32[8]{0:T(128)} %stack.120.place_ref, bf16[2,768,128]{2,1,0:T(8,128)(2,1)} %get-tuple-element.31.refs_0_, bf16[2,768,128]{2,1,0:T(8,128)(2,1)} %copy-done.7, bf16[2,768,128]{2,1,0:T(8,128)(2,1)} %copy-done.5, ...), custom_call_target="tpu_custom_call" | custom-call | flops 1200000000 | bytes 9000000 | tf_op jit(solution)/shard_map/products/pallas_call | solution.py:345
  60.7 2.5 %collective-permute-done.13.came_ref = bf16[256,1536]{1,0:T(8,128)(2,1)S(1)} collective-permute-done((bf16[256,1536]{1,0:T(8,128)(2,1)}, bf16[256,1536]{1,0:T(8,128)(2,1)S(1)}, u32[]{:S(2)}, u32[]{:S(2)}) %collective-permute-start.13) | collective-permute-done | bytes 786464 | tf_op jit(solution)/shard_map/ppermute | solution.py:27
  63.2 0.9 copy-done.24
  64.4 4.3 %attention.1.grad_ref.refs_4_ = bf16[256,1536]{1,0:T(8,128)(2,1)} custom-call(f32[256,1536]{1,0:T(8,128)} %get-tuple-element.36.kept_ref, bf16[256,1536]{1,0:T(8,128)(2,1)} %copy-done.24, f32[2,3,128,64]{3,2,1,0:T(8,128)} %bitcast.52), custom_call_target="tpu_custom_call" | custom-call | flops 1000000000 | bytes 4000000 | tf_op jit(solution)/shard_map/attention/pallas_call | solution.py:365
  69.6 1.1 copy-done.2
  70.7 5.0 %projections.1 = (f32[128,3072]{1,0:T(8,128)S(1)}, bf16[128,3072]{1,0:T(8,128)(2,1)S(1)}) custom-call(s32[16]{0:T(128)S(1)} %stack.111.place_ref, bf16[256,1536]{1,0:T(8,128)(2,1)S(1)} %copy-done.2, bf16[768,1536]{1,0:T(8,128)(2,1)S(1)} %copy-done.1, bf16[768,1536]{1,0:T(8,128)(2,1)} %collective-permute-done.14.theirs_ref), custom_call_target="tpu_custom_call" | custom-call | flops 1200000000 | bytes 8000000 | tf_op jit(solution)/shard_map/projections/pallas_call | solution.py:378
  75.9 2.8 %weight_gradient.1 = (bf16[96,1536]{1,0:T(8,128)(2,1)S(1)}, bf16[96,1536]{1,0:T(8,128)(2,1)S(1)}, bf16[96,1536]{1,0:T(8,128)(2,1)S(1)}, bf16[96,1536]{1,0:T(8,12...) custom-call(s32[1]{0:T(128)} %bitcast.34.near_ref, ...), custom_call_target="tpu_custom_call" | custom-call | flops 1200000000 | bytes 6000000 | tf_op jit(solution)/shard_map/weight_gradient/pallas_call | solution.py:392
  78.6 4.5 %collective-permute-start.18 = (bf16[96,1536]{1,0:T(8,128)(2,1)S(1)}, bf16[96,1536]{1,0:T(8,128)(2,1)S(1)}, u32[]{:S(2)}, u32[]{:S(2)}) collective-permute-start(bf16[96,1536]{1,0:T(8,128)(2,1)S(1)} %get-tuple-element.45), channel_id=1, source_target_pairs={{0,2},{2,0},{1,3},{3,1},{4,6},{6,4},{5,7},{7,5},{8,10},{10,8},{9,1... | collective-permute-start | bytes 884744 | tf_op jit(solution)/shard_map/ppermute | solution.py:27
  83.8 6.4 %collective-permute-done.18 = bf16[96,1536]{1,0:T(8,128)(2,1)S(1)} collective-permute-done((bf16[96,1536]{1,0:T(8,128)(2,1)S(1)}, bf16[96,1536]{1,0:T(8,128)(2,1)S(1)}, u32[]{:S(2)}, u32[]{:S(2)}) %collective-permute-start.18) | collective-permute-done | bytes 294944 | tf_op jit(solution)/shard_map/ppermute | solution.py:27
  90.3 3.4 %collective-permute-start.23 = (bf16[96,1536]{1,0:T(8,128)(2,1)S(1)}, bf16[96,1536]{1,0:T(8,128)(2,1)S(1)}, u32[]{:S(2)}, u32[]{:S(2)}) collective-permute-start(bf16[96,1536]{1,0:T(8,128)(2,1)S(1)} %add_convert_fusion.3), channel_id=1, source_target_pairs={{0,8},{8,0},{1,9},{9,1},{2,10},{10,2},{3,11},{11,3},{4,12},{12,4},... | collective-permute-start | bytes 884744 | tf_op jit(solution)/shard_map/ppermute | solution.py:27
  93.7 5.0 %collective-permute-done.15 = bf16[128,3072]{1,0:T(8,128)(2,1)S(1)} collective-permute-done((bf16[128,3072]{1,0:T(8,128)(2,1)S(1)}, bf16[128,3072]{1,0:T(8,128)(2,1)S(1)}, u32[]{:S(2)}, u32[]{:S(2)}) %collective-permute-start.15) | collective-permute-done | bytes 786464 | tf_op jit(solution)/shard_map/ppermute | solution.py:27
  98.7 5.1 %collective-permute-start.19 = (bf16[96,1536]{1,0:T(8,128)(2,1)S(1)}, bf16[96,1536]{1,0:T(8,128)(2,1)S(1)}, u32[]{:S(2)}, u32[]{:S(2)}) collective-permute-start(bf16[96,1536]{1,0:T(8,128)(2,1)S(1)} %get-tuple-element.46), channel_id=1, source_target_pairs={{0,2},{2,0},{1,3},{3,1},{4,6},{6,4},{5,7},{7,5},{8,10},{10,8},{9,1... | collective-permute-start | bytes 884744 | tf_op jit(solution)/shard_map/ppermute | solution.py:27
  104.1 14.3 %collective-permute-done.19 = bf16[96,1536]{1,0:T(8,128)(2,1)S(1)} collective-permute-done((bf16[96,1536]{1,0:T(8,128)(2,1)S(1)}, bf16[96,1536]{1,0:T(8,128)(2,1)S(1)}, u32[]{:S(2)}, u32[]{:S(2)}) %collective-permute-start.19) | collective-permute-done | bytes 294944 | tf_op jit(solution)/shard_map/ppermute | solution.py:27
  118.3 2.5 %collective-permute-start.21 = (bf16[96,1536]{1,0:T(8,128)(2,1)S(1)}, bf16[96,1536]{1,0:T(8,128)(2,1)S(1)}, u32[]{:S(2)}, u32[]{:S(2)}) collective-permute-start(bf16[96,1536]{1,0:T(8,128)(2,1)S(1)} %get-tuple-element.52), channel_id=1, source_target_pairs={{0,2},{2,0},{1,3},{3,1},{4,6},{6,4},{5,7},{7,5},{8,10},{10,8},{9,1... | collective-permute-start | bytes 884744 | tf_op jit(solution)/shard_map/ppermute | solution.py:27
  121.3 5.4 %collective-permute-done.21 = bf16[96,1536]{1,0:T(8,128)(2,1)S(1)} collective-permute-done((bf16[96,1536]{1,0:T(8,128)(2,1)S(1)}, bf16[96,1536]{1,0:T(8,128)(2,1)S(1)}, u32[]{:S(2)}, u32[]{:S(2)}) %collective-permute-start.21) | collective-permute-done | bytes 294944 | tf_op jit(solution)/shard_map/ppermute | solution.py:27
  126.9 1.8 %collective-permute-start.22 = (bf16[96,1536]{1,0:T(8,128)(2,1)S(1)}, bf16[96,1536]{1,0:T(8,128)(2,1)S(1)}, u32[]{:S(2)}, u32[]{:S(2)}) collective-permute-start(bf16[96,1536]{1,0:T(8,128)(2,1)S(1)} %get-tuple-element.53), channel_id=1, source_target_pairs={{0,2},{2,0},{1,3},{3,1},{4,6},{6,4},{5,7},{7,5},{8,10},{10,8},{9,1... | collective-permute-start | bytes 884744 | tf_op jit(solution)/shard_map/ppermute | solution.py:27
  128.7 6.2 %collective-permute-done.20 = bf16[96,1536]{1,0:T(8,128)(2,1)S(1)} collective-permute-done((bf16[96,1536]{1,0:T(8,128)(2,1)S(1)}, bf16[96,1536]{1,0:T(8,128)(2,1)S(1)}, u32[]{:S(2)}, u32[]{:S(2)}) %collective-permute-start.20) | collective-permute-done | bytes 294944 | tf_op jit(solution)/shard_map/ppermute | solution.py:27
  134.9 3.1 %convolution_convert_fusion = bf16[128,3072]{1,0:T(8,128)(2,1)S(1)} fusion(bf16[128,3072]{1,0:T(8,128)(2,1)S(1)} %add_convert_fusion, bf16[128,3072]{1,0:T(8,128)(2,1)S(1)} %collective-permute-done.16, s32[]{:T(128)} %bitcast.4, s32[]{:T(128)} %bitcast.3, s32[128]{0:T(128)S(1)} %get-tuple-element.87, s32[128]{0:T(128)S(1)} %get-tuple-element.89, ...), kind=kOutput, calls=%fused_computation.3 | convolution fusion | flops 206700544 | bytes 2362768 | tf_op jit(solution)/shard_map/dot_general | solution.py:52
  138.4 1.4 fusion.18
  140.5 1.1 broadcast_multiply_fusion
  (138 shorter events, 13.5 us)
Async XLA Ops:
  0.6 45.2 %copy-start = (f32[2,225,12]{1,0,2:T(2,128)S(1)}, f32[2,225,12]{1,0,2:T(2,128)}, u32[]{:S(2)}) copy-start(f32[2,225,12]{1,0,2:T(2,128)} %param.16) | copy-start | bytes 64804
  2.1 8.8 %collective-permute-start.3 = (bf16[96,1536]{1,0:T(8,128)(2,1)S(1)}, bf16[96,1536]{1,0:T(8,128)(2,1)S(1)}, u32[]{:S(2)}, u32[]{:S(2)}) collective-permute-start(bf16[96,1536]{1,0:T(8,128)(2,1)S(1)} %broadcast_select_fusion), channel_id=1, source_target_pairs={{0,4},{4,0},{1,5},{5,1},{2,6},{6,2},{3,7},{7,3},{8,12},{12,8},{9,1... | collective-permute-start | bytes 884744 | tf_op jit(solution)/shard_map/ppermute | solution.py:27
  4.1 10.3 %copy-start.11 = (bf16[2,8,8,1536]{3,2,1,0:T(8,128)(2,1)}, bf16[2,8,8,1536]{3,2,1,0:T(8,128)(2,1)S(1)}, u32[]{:S(2)}) copy-start(bf16[2,8,8,1536]{3,2,1,0:T(8,128)(2,1)S(1)} %get-tuple-element.62) | copy-start | bytes 1179652
  4.1 10.3 %collective-permute-start = (bf16[128,1536]{1,0:T(8,128)(2,1)S(1)}, bf16[128,1536]{1,0:T(8,128)(2,1)S(1)}, u32[]{:S(2)}, u32[]{:S(2)}) collective-permute-start(bf16[128,1536]{1,0:T(8,128)(2,1)S(1)} %bitcast.48), channel_id=1, source_target_pairs={{0,15},{1,0},{2,1},{3,2},{4,3},{5,4},{6,5},{7,6},{8,7},{9,8},{10,9... | collective-permute-start | bytes 1179656 | tf_op jit(solution)/shard_map/ppermute | solution.py:18
  4.1 10.2 %collective-permute-start.1 = (bf16[128,1536]{1,0:T(8,128)(2,1)S(1)}, bf16[128,1536]{1,0:T(8,128)(2,1)S(1)}, u32[]{:S(2)}, u32[]{:S(2)}) collective-permute-start(bf16[128,1536]{1,0:T(8,128)(2,1)S(1)} %bitcast.51), channel_id=1, source_target_pairs={{0,15},{1,0},{2,1},{3,2},{4,3},{5,4},{6,5},{7,6},{8,7},{9,8},{10,9... | collective-permute-start | bytes 1179656 | tf_op jit(solution)/shard_map/ppermute | solution.py:18
  10.9 9.0 %copy-start.19 = (bf16[96,1536]{1,0:T(8,128)(2,1)}, bf16[96,1536]{1,0:T(8,128)(2,1)S(1)}, u32[]{:S(2)}) copy-start(bf16[96,1536]{1,0:T(8,128)(2,1)S(1)} %collective-permute-done.3.refs_5_) | copy-start | bytes 884740
  11.7 34.1 %copy-start.31 = (s32[64,64]{1,0:T(8,128)S(1)}, s32[64,64]{1,0:T(8,128)}, u32[]{:S(2)}) copy-start(s32[64,64]{1,0:T(8,128)} %param.15) | copy-start | bytes 49156
  11.7 15.3 %collective-permute-start.8 = (bf16[96,1536]{1,0:T(8,128)(2,1)S(1)}, bf16[96,1536]{1,0:T(8,128)(2,1)S(1)}, u32[]{:S(2)}, u32[]{:S(2)}) collective-permute-start(bf16[96,1536]{1,0:T(8,128)(2,1)S(1)} %get-tuple-element.33), channel_id=1, source_target_pairs={{0,8},{8,0},{1,9},{9,1},{2,10},{10,2},{3,11},{11,3},{4,12},{12,4},... | collective-permute-start | bytes 884744 | tf_op jit(solution)/shard_map/ppermute | solution.py:27
  19.9 15.0 %collective-permute-start.4 = (bf16[96,1536]{1,0:T(8,128)(2,1)S(1)}, bf16[96,1536]{1,0:T(8,128)(2,1)S(1)}, u32[]{:S(2)}, u32[]{:S(2)}) collective-permute-start(bf16[96,1536]{1,0:T(8,128)(2,1)S(1)} %get-tuple-element.33), channel_id=1, source_target_pairs={{0,2},{2,0},{1,3},{3,1},{4,6},{6,4},{5,7},{7,5},{8,10},{10,8},{9,1... | collective-permute-start | bytes 884744 | tf_op jit(solution)/shard_map/ppermute | solution.py:27
  27.0 10.2 %collective-permute-start.2 = (bf16[2,768,128]{2,1,0:T(8,128)(2,1)}, bf16[2,768,128]{2,1,0:T(8,128)(2,1)S(1)}, u32[]{:S(2)}, u32[]{:S(2)}) collective-permute-start(bf16[2,768,128]{2,1,0:T(8,128)(2,1)} %get-tuple-element.34), channel_id=1, source_target_pairs={{0,4},{4,0},{1,5},{5,1},{2,6},{6,2},{3,7},{7,3},{8,12},{12,8},{9,1... | collective-permute-start | bytes 1179656 | tf_op jit(solution)/shard_map/ppermute | solution.py:27
  27.0 22.3 %copy-start.25 = (bf16[96,1536]{1,0:T(8,128)(2,1)}, bf16[96,1536]{1,0:T(8,128)(2,1)S(1)}, u32[]{:S(2)}) copy-start(bf16[96,1536]{1,0:T(8,128)(2,1)S(1)} %collective-permute-done.8.refs_8_) | copy-start | bytes 884740
  27.0 16.9 %collective-permute-start.9 = (bf16[96,1536]{1,0:T(8,128)(2,1)S(1)}, bf16[96,1536]{1,0:T(8,128)(2,1)S(1)}, u32[]{:S(2)}, u32[]{:S(2)}) collective-permute-start(bf16[96,1536]{1,0:T(8,128)(2,1)S(1)} %collective-permute-done.8.refs_8_), channel_id=1, source_target_pairs={{0,16},{16,0},{1,17},{17,1},{2,18},{18,2},{3,19},{19,3},{4,20},{20... | collective-permute-start | bytes 884744 | tf_op jit(solution)/shard_map/ppermute | solution.py:27
  34.9 14.5 %copy-start.26 = (bf16[96,1536]{1,0:T(8,128)(2,1)}, bf16[96,1536]{1,0:T(8,128)(2,1)S(1)}, u32[]{:S(2)}) copy-start(bf16[96,1536]{1,0:T(8,128)(2,1)S(1)} %collective-permute-done.4.refs_6_) | copy-start | bytes 884740
  34.9 9.0 %collective-permute-start.5 = (bf16[96,1536]{1,0:T(8,128)(2,1)S(1)}, bf16[96,1536]{1,0:T(8,128)(2,1)S(1)}, u32[]{:S(2)}, u32[]{:S(2)}) collective-permute-start(bf16[96,1536]{1,0:T(8,128)(2,1)S(1)} %collective-permute-done.4.refs_6_), channel_id=1, source_target_pairs={{0,16},{16,0},{1,17},{17,1},{2,18},{18,2},{3,19},{19,3},{4,20},{20... | collective-permute-start | bytes 884744 | tf_op jit(solution)/shard_map/ppermute | solution.py:27
  35.2 9.3 %collective-permute-start.11 = (bf16[96,1536]{1,0:T(8,128)(2,1)S(1)}, bf16[96,1536]{1,0:T(8,128)(2,1)S(1)}, u32[]{:S(2)}, u32[]{:S(2)}) collective-permute-start(bf16[96,1536]{1,0:T(8,128)(2,1)S(1)} %collective-permute-done.8.refs_8_), channel_id=1, source_target_pairs={{0,2},{2,0},{1,3},{3,1},{4,6},{6,4},{5,7},{7,5},{8,10},{10,8},{9,1... | collective-permute-start | bytes 884744 | tf_op jit(solution)/shard_map/ppermute | solution.py:27
  35.8 14.2 %collective-permute-start.7 = (bf16[2,768,128]{2,1,0:T(8,128)(2,1)}, bf16[2,768,128]{2,1,0:T(8,128)(2,1)S(1)}, u32[]{:S(2)}, u32[]{:S(2)}) collective-permute-start(bf16[2,768,128]{2,1,0:T(8,128)(2,1)} %get-tuple-element.31.refs_0_), channel_id=1, source_target_pairs={{0,4},{4,0},{1,5},{5,1},{2,6},{6,2},{3,7},{7,3},{8,12},{12,8},{9,1... | collective-permute-start | bytes 1179656 | tf_op jit(solution)/shard_map/ppermute | solution.py:27
  43.9 5.4 %copy-start.28 = (bf16[96,1536]{1,0:T(8,128)(2,1)}, bf16[96,1536]{1,0:T(8,128)(2,1)S(1)}, u32[]{:S(2)}) copy-start(bf16[96,1536]{1,0:T(8,128)(2,1)S(1)} %collective-permute-done.5.refs_7_) | copy-start | bytes 884740
  43.9 9.7 %collective-permute-start.6 = (bf16[2,768,128]{2,1,0:T(8,128)(2,1)}, bf16[2,768,128]{2,1,0:T(8,128)(2,1)S(1)}, u32[]{:S(2)}, u32[]{:S(2)}) collective-permute-start(bf16[2,768,128]{2,1,0:T(8,128)(2,1)} %get-tuple-element.34), channel_id=1, source_target_pairs={{0,1},{1,0},{2,3},{3,2},{4,5},{5,4},{6,7},{7,6},{8,9},{9,8},{10,11... | collective-permute-start | bytes 1179656 | tf_op jit(solution)/shard_map/ppermute | solution.py:27
  43.9 9.7 %collective-permute-start.10 = (bf16[2,768,128]{2,1,0:T(8,128)(2,1)S(1)}, bf16[2,768,128]{2,1,0:T(8,128)(2,1)S(1)}, u32[]{:S(2)}, u32[]{:S(2)}) collective-permute-start(bf16[2,768,128]{2,1,0:T(8,128)(2,1)S(1)} %collective-permute-done.2), channel_id=1, source_target_pairs={{0,1},{1,0},{2,3},{3,2},{4,5},{5,4},{6,7},{7,6},{8,9},{9,8},{10,11... | collective-permute-start | bytes 1179656 | tf_op jit(solution)/shard_map/ppermute | solution.py:27
  44.5 9.1 %collective-permute-start.12 = (bf16[96,1536]{1,0:T(8,128)(2,1)S(1)}, bf16[96,1536]{1,0:T(8,128)(2,1)S(1)}, u32[]{:S(2)}, u32[]{:S(2)}) collective-permute-start(bf16[96,1536]{1,0:T(8,128)(2,1)S(1)} %collective-permute-done.11.refs_10_), channel_id=1, source_target_pairs={{0,16},{16,0},{1,17},{17,1},{2,18},{18,2},{3,19},{19,3},{4,20},{20... | collective-permute-start | bytes 884744 | tf_op jit(solution)/shard_map/ppermute | solution.py:27
  60.7 2.6 %collective-permute-start.13 = (bf16[256,1536]{1,0:T(8,128)(2,1)}, bf16[256,1536]{1,0:T(8,128)(2,1)S(1)}, u32[]{:S(2)}, u32[]{:S(2)}) collective-permute-start(bf16[256,1536]{1,0:T(8,128)(2,1)} %get-tuple-element.37), channel_id=1, source_target_pairs={{0,1},{1,0},{2,3},{3,2},{4,5},{5,4},{6,7},{7,6},{8,9},{9,8},{10,11... | collective-permute-start | bytes 2359304 | tf_op jit(solution)/shard_map/ppermute | solution.py:27
  64.1 5.5 %collective-permute-start.14 = (bf16[768,1536]{1,0:T(8,128)(2,1)}, bf16[768,1536]{1,0:T(8,128)(2,1)}, u32[]{:S(2)}, u32[]{:S(2)}) collective-permute-start(bf16[768,1536]{1,0:T(8,128)(2,1)} %get-tuple-element.39.mine_ref), channel_id=1, source_target_pairs={{0,1},{1,0},{2,3},{3,2},{4,5},{5,4},{6,7},{7,6},{8,9},{9,8},{10,11... | collective-permute-start | bytes 7077896 | tf_op jit(solution)/shard_map/ppermute | solution.py:27
  68.8 7.0 %collective-permute-start.17 = (bf16[256,1536]{1,0:T(8,128)(2,1)}, bf16[256,1536]{1,0:T(8,128)(2,1)S(1)}, u32[]{:S(2)}, u32[]{:S(2)}) collective-permute-start(bf16[256,1536]{1,0:T(8,128)(2,1)} %attention.1.grad_ref.refs_4_), channel_id=1, source_target_pairs={{0,1},{1,0},{2,3},{3,2},{4,5},{5,4},{6,7},{7,6},{8,9},{9,8},{10,11... | collective-permute-start | bytes 2359304 | tf_op jit(solution)/shard_map/ppermute | solution.py:27
  75.7 23.0 %collective-permute-start.15 = (bf16[128,3072]{1,0:T(8,128)(2,1)S(1)}, bf16[128,3072]{1,0:T(8,128)(2,1)S(1)}, u32[]{:S(2)}, u32[]{:S(2)}) collective-permute-start(bf16[128,3072]{1,0:T(8,128)(2,1)S(1)} %get-tuple-element.41), channel_id=1, source_target_pairs={{0,4},{4,0},{1,5},{5,1},{2,6},{6,2},{3,7},{7,3},{8,12},{12,8},{9,1... | collective-permute-start | bytes 2359304 | tf_op jit(solution)/shard_map/ppermute | solution.py:27
  78.6 11.5 %collective-permute-start.18 = (bf16[96,1536]{1,0:T(8,128)(2,1)S(1)}, bf16[96,1536]{1,0:T(8,128)(2,1)S(1)}, u32[]{:S(2)}, u32[]{:S(2)}) collective-permute-start(bf16[96,1536]{1,0:T(8,128)(2,1)S(1)} %get-tuple-element.45), channel_id=1, source_target_pairs={{0,2},{2,0},{1,3},{3,1},{4,6},{6,4},{5,7},{7,5},{8,10},{10,8},{9,1... | collective-permute-start | bytes 884744 | tf_op jit(solution)/shard_map/ppermute | solution.py:27
  90.3 31.0 %collective-permute-start.23 = (bf16[96,1536]{1,0:T(8,128)(2,1)S(1)}, bf16[96,1536]{1,0:T(8,128)(2,1)S(1)}, u32[]{:S(2)}, u32[]{:S(2)}) collective-permute-start(bf16[96,1536]{1,0:T(8,128)(2,1)S(1)} %add_convert_fusion.3), channel_id=1, source_target_pairs={{0,8},{8,0},{1,9},{9,1},{2,10},{10,2},{3,11},{11,3},{4,12},{12,4},... | collective-permute-start | bytes 884744 | tf_op jit(solution)/shard_map/ppermute | solution.py:27
  98.7 19.6 %collective-permute-start.19 = (bf16[96,1536]{1,0:T(8,128)(2,1)S(1)}, bf16[96,1536]{1,0:T(8,128)(2,1)S(1)}, u32[]{:S(2)}, u32[]{:S(2)}) collective-permute-start(bf16[96,1536]{1,0:T(8,128)(2,1)S(1)} %get-tuple-element.46), channel_id=1, source_target_pairs={{0,2},{2,0},{1,3},{3,1},{4,6},{6,4},{5,7},{7,5},{8,10},{10,8},{9,1... | collective-permute-start | bytes 884744 | tf_op jit(solution)/shard_map/ppermute | solution.py:27
  104.0 30.9 %collective-permute-start.16 = (bf16[128,3072]{1,0:T(8,128)(2,1)S(1)}, bf16[128,3072]{1,0:T(8,128)(2,1)S(1)}, u32[]{:S(2)}, u32[]{:S(2)}) collective-permute-start(bf16[128,3072]{1,0:T(8,128)(2,1)S(1)} %add_convert_fusion), channel_id=1, source_target_pairs={{0,1},{1,2},{2,3},{3,4},{4,5},{5,6},{6,7},{7,8},{8,9},{9,10},{10,1... | collective-permute-start | bytes 2359304 | tf_op jit(solution)/shard_map/ppermute | solution.py:18
  118.3 8.4 %collective-permute-start.21 = (bf16[96,1536]{1,0:T(8,128)(2,1)S(1)}, bf16[96,1536]{1,0:T(8,128)(2,1)S(1)}, u32[]{:S(2)}, u32[]{:S(2)}) collective-permute-start(bf16[96,1536]{1,0:T(8,128)(2,1)S(1)} %get-tuple-element.52), channel_id=1, source_target_pairs={{0,2},{2,0},{1,3},{3,1},{4,6},{6,4},{5,7},{7,5},{8,10},{10,8},{9,1... | collective-permute-start | bytes 884744 | tf_op jit(solution)/shard_map/ppermute | solution.py:27
  120.9 14.0 %collective-permute-start.20 = (bf16[96,1536]{1,0:T(8,128)(2,1)S(1)}, bf16[96,1536]{1,0:T(8,128)(2,1)S(1)}, u32[]{:S(2)}, u32[]{:S(2)}) collective-permute-start(bf16[96,1536]{1,0:T(8,128)(2,1)S(1)} %add_convert_fusion.4), channel_id=1, source_target_pairs={{0,8},{8,0},{1,9},{9,1},{2,10},{10,2},{3,11},{11,3},{4,12},{12,4},... | collective-permute-start | bytes 884744 | tf_op jit(solution)/shard_map/ppermute | solution.py:27
  126.8 13.3 %collective-permute-start.24 = (bf16[96,1536]{1,0:T(8,128)(2,1)S(1)}, bf16[96,1536]{1,0:T(8,128)(2,1)S(1)}, u32[]{:S(2)}, u32[]{:S(2)}) collective-permute-start(bf16[96,1536]{1,0:T(8,128)(2,1)S(1)} %add_convert_fusion.2), channel_id=1, source_target_pairs={{0,4},{4,0},{1,5},{5,1},{2,6},{6,2},{3,7},{7,3},{8,12},{12,8},{9,1... | collective-permute-start | bytes 884744 | tf_op jit(solution)/shard_map/ppermute | solution.py:27
  126.9 13.3 %collective-permute-start.22 = (bf16[96,1536]{1,0:T(8,128)(2,1)S(1)}, bf16[96,1536]{1,0:T(8,128)(2,1)S(1)}, u32[]{:S(2)}, u32[]{:S(2)}) collective-permute-start(bf16[96,1536]{1,0:T(8,128)(2,1)S(1)} %get-tuple-element.53), channel_id=1, source_target_pairs={{0,2},{2,0},{1,3},{3,1},{4,6},{6,4},{5,7},{7,5},{8,10},{10,8},{9,1... | collective-permute-start | bytes 884744 | tf_op jit(solution)/shard_map/ppermute | solution.py:27
  (25 other events, 79.2 us)

commit v3 on v2

--- a/solution.py
+++ b/solution.py
@@ -410,10 +410,11 @@
 
     side_far_1 = swap(block(1, 1, 1), "side")
     arrived_back = swap(attended_other, "near")
-    side_far_0 = swap(after(block(1, 1, 0), (side_far_1, arrived_back)), "side")
+    side_far_0 = swap(after(block(1, 1, 0), side_far_1), "side")
+    side_far_0 = after(side_far_0, arrived_back)
     far_1 = swap((block(1, 0, 1).astype(f32) + side_far_1.astype(f32)).astype(bf16), "far")
     far_0 = swap(after((block(1, 0, 0).astype(f32) + side_far_0.astype(f32)).astype(bf16), side_far_1), "far")
-    side_1 = swap(after(block(0, 1, 1), side_far_0), "side")
+    side_1 = swap(after(block(0, 1, 1), (side_far_0, arrived_back)), "side")
     side_0 = swap(after(block(0, 1, 0), side_1), "side")
     total_1 = (block(0, 0, 1).astype(f32) + side_1.astype(f32) + far_1.astype(f32)).astype(bf16)
     theirs = swap(total_1, "near").astype(f32)

time: 144 us -> 142 us (0.986); the launches traced: 142 us -> 142 us
  starting transfers between devices: 33.8 us -> 31.4 us
  waiting for transfers between devices: 63.7 us -> 65.3 us
    ppermute x22, starting transfers between devices: 33.1 us -> 30.6 us  [swap(): return lax.ppermute(shard, axis, [(0, 1), (1, 0)])]
    ppermute x22, waiting for transfers between devices: 63.7 us -> 65.3 us  [swap(): return lax.ppermute(shard, axis, [(0, 1), (1, 0)])]
    unnamed x64 -> x60, local copies, waits for them, and re-layouts: 4.55 us -> 4.33 us
  transfers between devices with their start and end apart: 25 -> 25, of which waited for: 12 -> 11; matrix products, arithmetic and copies ran while one was open for 9% -> 10% of each run, Pallas kernels for 11% -> 11%
where the time goes in v3:
time: 142 us
  waiting for transfers between devices  65.3 us (46%)
  starting transfers between devices  31.4 us (22%)
  Pallas kernels  22.2 us (16%)
  local copies, waits for them, and re-layouts  9.56 us (7%)
  other arithmetic  6.35 us (4%)
  matrix products  5.81 us (4%)
    ppermute x22, waiting for transfers between devices, swap(): return lax.ppermute(shard, axis, [(0, 1), (1, 0)])  65.3 us
    ppermute x22, starting transfers between devices, swap(): return lax.ppermute(shard, axis, [(0, 1), (1, 0)])  30.6 us
    pallas_call x1, Pallas kernels, on_device(): kernel_call(products_kernel, (jax.ShapeDtypeStruct((2 * tile, 4 * part),...  6.09 us
    pallas_call x1, Pallas kernels, on_device(): kernel_call(outer_kernel, (jax.ShapeDtypeStruct((tile, 2 * width), f32),...  5 us
    pallas_call x1, Pallas kernels, on_device(): kernel_call(functools.partial(attention_kernel, area, head), jax.ShapeDty...  4.35 us
    unnamed x60, local copies, waits for them, and re-layouts  4.33 us
    pallas_call x1, Pallas kernels, on_device(): kernel_call(turned_rolls, (turned, turned), [smem, vmem] + [anywhere] * 4...  4.02 us
    dot_general x1, matrix products, picked(): jnp.dot(onehot, both, preferred_element_type=jnp.float32)  3.16 us
  transfers between devices with their start and end apart: 25, of which 11 were waited for; matrix products, arithmetic and copies ran while one was open for 10% of the time, Pallas kernels for 11%

profile of v3, /device:TPU:6, one launch (start us, length us, event | category | flops | bytes accessed | tf_op | source)
XLA Modules:
  0.0 141.8 jit_solution(1787487340068646260)
XLA Ops:
  0.7 1.3 fusion.81
  2.1 1.6 %collective-permute-start.3 = (bf16[96,1536]{1,0:T(8,128)(2,1)S(1)}, bf16[96,1536]{1,0:T(8,128)(2,1)S(1)}, u32[]{:S(2)}, u32[]{:S(2)}) collective-permute-start(bf16[96,1536]{1,0:T(8,128)(2,1)S(1)} %broadcast_select_fusion), channel_id=1, source_target_pairs={{0,4},{4,0},{1,5},{5,1},{2,6},{6,2},{3,7},{7,3},{8,12},{12,8},{9,1... | collective-permute-start | bytes 884744 | tf_op jit(solution)/shard_map/ppermute | solution.py:27
  6.1 4.8 %collective-permute-done.3.refs_5_ = bf16[96,1536]{1,0:T(8,128)(2,1)S(1)} collective-permute-done((bf16[96,1536]{1,0:T(8,128)(2,1)S(1)}, bf16[96,1536]{1,0:T(8,128)(2,1)S(1)}, u32[]{:S(2)}, u32[]{:S(2)}) %collective-permute-start.3) | collective-permute-done | bytes 294944 | tf_op jit(solution)/shard_map/ppermute | solution.py:27
  11.7 2.6 %collective-permute-start.8 = (bf16[96,1536]{1,0:T(8,128)(2,1)S(1)}, bf16[96,1536]{1,0:T(8,128)(2,1)S(1)}, u32[]{:S(2)}, u32[]{:S(2)}) collective-permute-start(bf16[96,1536]{1,0:T(8,128)(2,1)S(1)} %get-tuple-element.34), channel_id=1, source_target_pairs={{0,8},{8,0},{1,9},{9,1},{2,10},{10,2},{3,11},{11,3},{4,12},{12,4},... | collective-permute-start | bytes 884744 | tf_op jit(solution)/shard_map/ppermute | solution.py:27
  15.8 4.0 %turned_rolls.1 = (bf16[2,768,128]{2,1,0:T(8,128)(2,1)}, bf16[2,768,128]{2,1,0:T(8,128)(2,1)}) custom-call(s32[20]{0:T(128)} %concatenate.15.info_ref, f32[1,1536]{1,0:T(1,128)} %reshape.97.gain_ref, bf16[128,1536]{1,0:T(8,128)(2,1)} %bitcast.49, bf16[128,1536]{1,0:T(8,128)(2,1)} %copy-done.16, bf16[128,1536]{1,0:T(8,128)(2,1)} %bitcast.50, ...), custom_call_target="tpu_custom_call" | custom-call | flops 201326592 | bytes 3000000 | tf_op jit(solution)/shard_map/turned_rolls/pallas_call | solution.py:304
  19.9 7.2 %collective-permute-start.4 = (bf16[96,1536]{1,0:T(8,128)(2,1)S(1)}, bf16[96,1536]{1,0:T(8,128)(2,1)S(1)}, u32[]{:S(2)}, u32[]{:S(2)}) collective-permute-start(bf16[96,1536]{1,0:T(8,128)(2,1)S(1)} %get-tuple-element.34), channel_id=1, source_target_pairs={{0,2},{2,0},{1,3},{3,1},{4,6},{6,4},{5,7},{7,5},{8,10},{10,8},{9,1... | collective-permute-start | bytes 884744 | tf_op jit(solution)/shard_map/ppermute | solution.py:27
  27.6 7.2 %collective-permute-done.4.refs_6_ = bf16[96,1536]{1,0:T(8,128)(2,1)S(1)} collective-permute-done((bf16[96,1536]{1,0:T(8,128)(2,1)S(1)}, bf16[96,1536]{1,0:T(8,128)(2,1)S(1)}, u32[]{:S(2)}, u32[]{:S(2)}) %collective-permute-start.4) | collective-permute-done | bytes 294944 | tf_op jit(solution)/shard_map/ppermute | solution.py:27
  36.1 1.1 collective-permute-done.2
  37.3 6.6 %collective-permute-done.5.refs_7_ = bf16[96,1536]{1,0:T(8,128)(2,1)S(1)} collective-permute-done((bf16[96,1536]{1,0:T(8,128)(2,1)S(1)}, bf16[96,1536]{1,0:T(8,128)(2,1)S(1)}, u32[]{:S(2)}, u32[]{:S(2)}) %collective-permute-start.5) | collective-permute-done | bytes 294944 | tf_op jit(solution)/shard_map/ppermute | solution.py:27
  44.5 1.3 collective-permute-start.12
  45.8 2.6 %fusion.7 = f32[2,6,64,64]{3,1,2,0:T(8,128)S(1)} fusion(s32[64,64]{1,0:T(8,128)S(1)} %copy-done.29, pred[2,64,64]{2,1,0:T(8,128)(4,1)S(1)} %broadcast_compare_fusion, f32[2,225,6]{1,0,2:T(2,128)S(1)} %constant_dynamic-slice_fusion), kind=kOutput, calls=%fused_computation.9 | convolution fusion | flops 133681152 | bytes 231984 | tf_op jit(solution)/shard_map/qkr,lrh->lhqk/dot_general | solution.py:337
  48.5 0.9 copy.13
  50.0 3.6 %collective-permute-done.12.refs_11_ = bf16[96,1536]{1,0:T(8,128)(2,1)} collective-permute-done((bf16[96,1536]{1,0:T(8,128)(2,1)S(1)}, bf16[96,1536]{1,0:T(8,128)(2,1)}, u32[]{:S(2)}, u32[]{:S(2)}) %collective-permute-start.12) | collective-permute-done | bytes 294944 | tf_op jit(solution)/shard_map/ppermute | solution.py:27
  54.6 6.1 %products.1 = (f32[256,1536]{1,0:T(8,128)}, bf16[256,1536]{1,0:T(8,128)(2,1)}, bf16[768,1536]{1,0:T(8,128)(2,1)}) custom-call(s32[8]{0:T(128)} %stack.120.place_ref, bf16[2,768,128]{2,1,0:T(8,128)(2,1)} %get-tuple-element.32.refs_0_, bf16[2,768,128]{2,1,0:T(8,128)(2,1)} %copy-done.7, bf16[2,768,128]{2,1,0:T(8,128)(2,1)} %copy-done.5, ...), custom_call_target="tpu_custom_call" | custom-call | flops 1200000000 | bytes 9000000 | tf_op jit(solution)/shard_map/products/pallas_call | solution.py:345
  60.8 2.5 %collective-permute-done.13.came_ref = bf16[256,1536]{1,0:T(8,128)(2,1)S(1)} collective-permute-done((bf16[256,1536]{1,0:T(8,128)(2,1)}, bf16[256,1536]{1,0:T(8,128)(2,1)S(1)}, u32[]{:S(2)}, u32[]{:S(2)}) %collective-permute-start.13) | collective-permute-done | bytes 786464 | tf_op jit(solution)/shard_map/ppermute | solution.py:27
  64.1 4.3 %attention.1.grad_ref.refs_4_ = bf16[256,1536]{1,0:T(8,128)(2,1)} custom-call(f32[256,1536]{1,0:T(8,128)} %get-tuple-element.37.kept_ref, bf16[256,1536]{1,0:T(8,128)(2,1)} %copy-done.23, f32[2,3,128,64]{3,2,1,0:T(8,128)} %bitcast.52), custom_call_target="tpu_custom_call" | custom-call | flops 1000000000 | bytes 4000000 | tf_op jit(solution)/shard_map/attention/pallas_call | solution.py:365
  68.8 1.2 fusion.20
  70.2 1.1 copy-done.2
  71.3 5.0 %projections.1 = (f32[128,3072]{1,0:T(8,128)S(1)}, bf16[128,3072]{1,0:T(8,128)(2,1)S(1)}) custom-call(s32[16]{0:T(128)S(1)} %stack.111.place_ref, bf16[256,1536]{1,0:T(8,128)(2,1)S(1)} %copy-done.2, bf16[768,1536]{1,0:T(8,128)(2,1)S(1)} %copy-done.1, bf16[768,1536]{1,0:T(8,128)(2,1)} %collective-permute-done.14.theirs_ref), custom_call_target="tpu_custom_call" | custom-call | flops 1200000000 | bytes 8000000 | tf_op jit(solution)/shard_map/projections/pallas_call | solution.py:378
  76.5 2.7 %weight_gradient.1 = (bf16[96,1536]{1,0:T(8,128)(2,1)S(1)}, bf16[96,1536]{1,0:T(8,128)(2,1)S(1)}, bf16[96,1536]{1,0:T(8,128)(2,1)S(1)}, bf16[96,1536]{1,0:T(8,12...) custom-call(s32[1]{0:T(128)} %bitcast.34.near_ref, ...), custom_call_target="tpu_custom_call" | custom-call | flops 1200000000 | bytes 6000000 | tf_op jit(solution)/shard_map/weight_gradient/pallas_call | solution.py:392
  79.2 4.5 %collective-permute-start.18 = (bf16[96,1536]{1,0:T(8,128)(2,1)S(1)}, bf16[96,1536]{1,0:T(8,128)(2,1)S(1)}, u32[]{:S(2)}, u32[]{:S(2)}) collective-permute-start(bf16[96,1536]{1,0:T(8,128)(2,1)S(1)} %get-tuple-element.46), channel_id=1, source_target_pairs={{0,2},{2,0},{1,3},{3,1},{4,6},{6,4},{5,7},{7,5},{8,10},{10,8},{9,1... | collective-permute-start | bytes 884744 | tf_op jit(solution)/shard_map/ppermute | solution.py:27
  83.8 7.2 %collective-permute-done.18 = bf16[96,1536]{1,0:T(8,128)(2,1)S(1)} collective-permute-done((bf16[96,1536]{1,0:T(8,128)(2,1)S(1)}, bf16[96,1536]{1,0:T(8,128)(2,1)S(1)}, u32[]{:S(2)}, u32[]{:S(2)}) %collective-permute-start.18) | collective-permute-done | bytes 294944 | tf_op jit(solution)/shard_map/ppermute | solution.py:27
  91.0 1.7 %collective-permute-start.19 = (bf16[96,1536]{1,0:T(8,128)(2,1)S(1)}, bf16[96,1536]{1,0:T(8,128)(2,1)S(1)}, u32[]{:S(2)}, u32[]{:S(2)}) collective-permute-start(bf16[96,1536]{1,0:T(8,128)(2,1)S(1)} %get-tuple-element.47), channel_id=1, source_target_pairs={{0,2},{2,0},{1,3},{3,1},{4,6},{6,4},{5,7},{7,5},{8,10},{10,8},{9,1... | collective-permute-start | bytes 884744 | tf_op jit(solution)/shard_map/ppermute | solution.py:27
  92.8 3.4 %collective-permute-start.23 = (bf16[96,1536]{1,0:T(8,128)(2,1)S(1)}, bf16[96,1536]{1,0:T(8,128)(2,1)S(1)}, u32[]{:S(2)}, u32[]{:S(2)}) collective-permute-start(bf16[96,1536]{1,0:T(8,128)(2,1)S(1)} %add_convert_fusion.3), channel_id=1, source_target_pairs={{0,8},{8,0},{1,9},{9,1},{2,10},{10,2},{3,11},{11,3},{4,12},{12,4},... | collective-permute-start | bytes 884744 | tf_op jit(solution)/shard_map/ppermute | solution.py:27
  96.3 1.4 collective-permute-done.15
  97.9 1.5 %collective-permute-done.19 = bf16[96,1536]{1,0:T(8,128)(2,1)S(1)} collective-permute-done((bf16[96,1536]{1,0:T(8,128)(2,1)S(1)}, bf16[96,1536]{1,0:T(8,128)(2,1)S(1)}, u32[]{:S(2)}, u32[]{:S(2)}) %collective-permute-start.19) | collective-permute-done | bytes 294944 | tf_op jit(solution)/shard_map/ppermute | solution.py:27
  99.5 5.0 %collective-permute-start.21 = (bf16[96,1536]{1,0:T(8,128)(2,1)S(1)}, bf16[96,1536]{1,0:T(8,128)(2,1)S(1)}, u32[]{:S(2)}, u32[]{:S(2)}) collective-permute-start(bf16[96,1536]{1,0:T(8,128)(2,1)S(1)} %get-tuple-element.54), channel_id=1, source_target_pairs={{0,2},{2,0},{1,3},{3,1},{4,6},{6,4},{5,7},{7,5},{8,10},{10,8},{9,1... | collective-permute-start | bytes 884744 | tf_op jit(solution)/shard_map/ppermute | solution.py:27
  105.3 18.8 %collective-permute-done.23 = bf16[96,1536]{1,0:T(8,128)(2,1)S(1)} collective-permute-done((bf16[96,1536]{1,0:T(8,128)(2,1)S(1)}, bf16[96,1536]{1,0:T(8,128)(2,1)S(1)}, u32[]{:S(2)}, u32[]{:S(2)}) %collective-permute-start.23) | collective-permute-done | bytes 294944 | tf_op jit(solution)/shard_map/ppermute | solution.py:27
  125.0 10.4 %collective-permute-done.24 = bf16[96,1536]{1,0:T(8,128)(2,1)S(1)} collective-permute-done((bf16[96,1536]{1,0:T(8,128)(2,1)S(1)}, bf16[96,1536]{1,0:T(8,128)(2,1)S(1)}, u32[]{:S(2)}, u32[]{:S(2)}) %collective-permute-start.24) | collective-permute-done | bytes 294944 | tf_op jit(solution)/shard_map/ppermute | solution.py:27
  135.4 3.2 %convolution_convert_fusion = bf16[128,3072]{1,0:T(8,128)(2,1)S(1)} fusion(bf16[128,3072]{1,0:T(8,128)(2,1)S(1)} %add_convert_fusion, bf16[128,3072]{1,0:T(8,128)(2,1)S(1)} %collective-permute-done.16, s32[]{:T(128)} %bitcast.4, s32[]{:T(128)} %bitcast.3, s32[128]{0:T(128)S(1)} %get-tuple-element.89, s32[128]{0:T(128)S(1)} %get-tuple-element.91, ...), kind=kOutput, calls=%fused_computation.3 | convolution fusion | flops 206700544 | bytes 2362768 | tf_op jit(solution)/shard_map/dot_general | solution.py:52
  139.0 1.4 fusion.18
  140.7 1.1 broadcast_multiply_fusion
  (134 shorter events, 13.0 us)
Async XLA Ops:
  0.6 45.2 %copy-start = (f32[2,225,12]{1,0,2:T(2,128)S(1)}, f32[2,225,12]{1,0,2:T(2,128)}, u32[]{:S(2)}) copy-start(f32[2,225,12]{1,0,2:T(2,128)} %param.16) | copy-start | bytes 64804
  2.1 8.8 %collective-permute-start.3 = (bf16[96,1536]{1,0:T(8,128)(2,1)S(1)}, bf16[96,1536]{1,0:T(8,128)(2,1)S(1)}, u32[]{:S(2)}, u32[]{:S(2)}) collective-permute-start(bf16[96,1536]{1,0:T(8,128)(2,1)S(1)} %broadcast_select_fusion), channel_id=1, source_target_pairs={{0,4},{4,0},{1,5},{5,1},{2,6},{6,2},{3,7},{7,3},{8,12},{12,8},{9,1... | collective-permute-start | bytes 884744 | tf_op jit(solution)/shard_map/ppermute | solution.py:27
  4.1 10.3 %copy-start.11 = (bf16[2,8,8,1536]{3,2,1,0:T(8,128)(2,1)}, bf16[2,8,8,1536]{3,2,1,0:T(8,128)(2,1)S(1)}, u32[]{:S(2)}) copy-start(bf16[2,8,8,1536]{3,2,1,0:T(8,128)(2,1)S(1)} %get-tuple-element.64) | copy-start | bytes 1179652
  4.1 10.3 %collective-permute-start = (bf16[128,1536]{1,0:T(8,128)(2,1)S(1)}, bf16[128,1536]{1,0:T(8,128)(2,1)S(1)}, u32[]{:S(2)}, u32[]{:S(2)}) collective-permute-start(bf16[128,1536]{1,0:T(8,128)(2,1)S(1)} %bitcast.48), channel_id=1, source_target_pairs={{0,15},{1,0},{2,1},{3,2},{4,3},{5,4},{6,5},{7,6},{8,7},{9,8},{10,9... | collective-permute-start | bytes 1179656 | tf_op jit(solution)/shard_map/ppermute | solution.py:18
  4.1 10.2 %collective-permute-start.1 = (bf16[128,1536]{1,0:T(8,128)(2,1)S(1)}, bf16[128,1536]{1,0:T(8,128)(2,1)S(1)}, u32[]{:S(2)}, u32[]{:S(2)}) collective-permute-start(bf16[128,1536]{1,0:T(8,128)(2,1)S(1)} %bitcast.51), channel_id=1, source_target_pairs={{0,15},{1,0},{2,1},{3,2},{4,3},{5,4},{6,5},{7,6},{8,7},{9,8},{10,9... | collective-permute-start | bytes 1179656 | tf_op jit(solution)/shard_map/ppermute | solution.py:18
  10.9 9.0 %copy-start.18 = (bf16[96,1536]{1,0:T(8,128)(2,1)}, bf16[96,1536]{1,0:T(8,128)(2,1)S(1)}, u32[]{:S(2)}) copy-start(bf16[96,1536]{1,0:T(8,128)(2,1)S(1)} %collective-permute-done.3.refs_5_) | copy-start | bytes 884740
  11.7 34.1 %copy-start.29 = (s32[64,64]{1,0:T(8,128)S(1)}, s32[64,64]{1,0:T(8,128)}, u32[]{:S(2)}) copy-start(s32[64,64]{1,0:T(8,128)} %param.15) | copy-start | bytes 49156
  11.7 15.3 %collective-permute-start.8 = (bf16[96,1536]{1,0:T(8,128)(2,1)S(1)}, bf16[96,1536]{1,0:T(8,128)(2,1)S(1)}, u32[]{:S(2)}, u32[]{:S(2)}) collective-permute-start(bf16[96,1536]{1,0:T(8,128)(2,1)S(1)} %get-tuple-element.34), channel_id=1, source_target_pairs={{0,8},{8,0},{1,9},{9,1},{2,10},{10,2},{3,11},{11,3},{4,12},{12,4},... | collective-permute-start | bytes 884744 | tf_op jit(solution)/shard_map/ppermute | solution.py:27
  19.9 15.0 %collective-permute-start.4 = (bf16[96,1536]{1,0:T(8,128)(2,1)S(1)}, bf16[96,1536]{1,0:T(8,128)(2,1)S(1)}, u32[]{:S(2)}, u32[]{:S(2)}) collective-permute-start(bf16[96,1536]{1,0:T(8,128)(2,1)S(1)} %get-tuple-element.34), channel_id=1, source_target_pairs={{0,2},{2,0},{1,3},{3,1},{4,6},{6,4},{5,7},{7,5},{8,10},{10,8},{9,1... | collective-permute-start | bytes 884744 | tf_op jit(solution)/shard_map/ppermute | solution.py:27
  27.0 10.2 %collective-permute-start.2 = (bf16[2,768,128]{2,1,0:T(8,128)(2,1)}, bf16[2,768,128]{2,1,0:T(8,128)(2,1)S(1)}, u32[]{:S(2)}, u32[]{:S(2)}) collective-permute-start(bf16[2,768,128]{2,1,0:T(8,128)(2,1)} %get-tuple-element.35), channel_id=1, source_target_pairs={{0,4},{4,0},{1,5},{5,1},{2,6},{6,2},{3,7},{7,3},{8,12},{12,8},{9,1... | collective-permute-start | bytes 1179656 | tf_op jit(solution)/shard_map/ppermute | solution.py:27
  27.0 22.3 %copy-start.24 = (bf16[96,1536]{1,0:T(8,128)(2,1)}, bf16[96,1536]{1,0:T(8,128)(2,1)S(1)}, u32[]{:S(2)}) copy-start(bf16[96,1536]{1,0:T(8,128)(2,1)S(1)} %collective-permute-done.8.refs_8_) | copy-start | bytes 884740
  27.0 16.9 %collective-permute-start.9 = (bf16[96,1536]{1,0:T(8,128)(2,1)S(1)}, bf16[96,1536]{1,0:T(8,128)(2,1)S(1)}, u32[]{:S(2)}, u32[]{:S(2)}) collective-permute-start(bf16[96,1536]{1,0:T(8,128)(2,1)S(1)} %collective-permute-done.8.refs_8_), channel_id=1, source_target_pairs={{0,16},{16,0},{1,17},{17,1},{2,18},{18,2},{3,19},{19,3},{4,20},{20... | collective-permute-start | bytes 884744 | tf_op jit(solution)/shard_map/ppermute | solution.py:27
  34.9 14.5 %copy-start.25 = (bf16[96,1536]{1,0:T(8,128)(2,1)}, bf16[96,1536]{1,0:T(8,128)(2,1)S(1)}, u32[]{:S(2)}) copy-start(bf16[96,1536]{1,0:T(8,128)(2,1)S(1)} %collective-permute-done.4.refs_6_) | copy-start | bytes 884740
  34.9 9.0 %collective-permute-start.5 = (bf16[96,1536]{1,0:T(8,128)(2,1)S(1)}, bf16[96,1536]{1,0:T(8,128)(2,1)S(1)}, u32[]{:S(2)}, u32[]{:S(2)}) collective-permute-start(bf16[96,1536]{1,0:T(8,128)(2,1)S(1)} %collective-permute-done.4.refs_6_), channel_id=1, source_target_pairs={{0,16},{16,0},{1,17},{17,1},{2,18},{18,2},{3,19},{19,3},{4,20},{20... | collective-permute-start | bytes 884744 | tf_op jit(solution)/shard_map/ppermute | solution.py:27
  35.2 9.3 %collective-permute-start.11 = (bf16[96,1536]{1,0:T(8,128)(2,1)S(1)}, bf16[96,1536]{1,0:T(8,128)(2,1)S(1)}, u32[]{:S(2)}, u32[]{:S(2)}) collective-permute-start(bf16[96,1536]{1,0:T(8,128)(2,1)S(1)} %collective-permute-done.8.refs_8_), channel_id=1, source_target_pairs={{0,2},{2,0},{1,3},{3,1},{4,6},{6,4},{5,7},{7,5},{8,10},{10,8},{9,1... | collective-permute-start | bytes 884744 | tf_op jit(solution)/shard_map/ppermute | solution.py:27
  35.8 14.3 %collective-permute-start.7 = (bf16[2,768,128]{2,1,0:T(8,128)(2,1)}, bf16[2,768,128]{2,1,0:T(8,128)(2,1)S(1)}, u32[]{:S(2)}, u32[]{:S(2)}) collective-permute-start(bf16[2,768,128]{2,1,0:T(8,128)(2,1)} %get-tuple-element.32.refs_0_), channel_id=1, source_target_pairs={{0,4},{4,0},{1,5},{5,1},{2,6},{6,2},{3,7},{7,3},{8,12},{12,8},{9,1... | collective-permute-start | bytes 1179656 | tf_op jit(solution)/shard_map/ppermute | solution.py:27
  43.9 9.8 %collective-permute-start.6 = (bf16[2,768,128]{2,1,0:T(8,128)(2,1)}, bf16[2,768,128]{2,1,0:T(8,128)(2,1)S(1)}, u32[]{:S(2)}, u32[]{:S(2)}) collective-permute-start(bf16[2,768,128]{2,1,0:T(8,128)(2,1)} %get-tuple-element.35), channel_id=1, source_target_pairs={{0,1},{1,0},{2,3},{3,2},{4,5},{5,4},{6,7},{7,6},{8,9},{9,8},{10,11... | collective-permute-start | bytes 1179656 | tf_op jit(solution)/shard_map/ppermute | solution.py:27
  43.9 9.8 %collective-permute-start.10 = (bf16[2,768,128]{2,1,0:T(8,128)(2,1)S(1)}, bf16[2,768,128]{2,1,0:T(8,128)(2,1)S(1)}, u32[]{:S(2)}, u32[]{:S(2)}) collective-permute-start(bf16[2,768,128]{2,1,0:T(8,128)(2,1)S(1)} %collective-permute-done.2), channel_id=1, source_target_pairs={{0,1},{1,0},{2,3},{3,2},{4,5},{5,4},{6,7},{7,6},{8,9},{9,8},{10,11... | collective-permute-start | bytes 1179656 | tf_op jit(solution)/shard_map/ppermute | solution.py:27
  44.5 9.2 %collective-permute-start.12 = (bf16[96,1536]{1,0:T(8,128)(2,1)S(1)}, bf16[96,1536]{1,0:T(8,128)(2,1)}, u32[]{:S(2)}, u32[]{:S(2)}) collective-permute-start(bf16[96,1536]{1,0:T(8,128)(2,1)S(1)} %collective-permute-done.11.refs_10_), channel_id=1, source_target_pairs={{0,16},{16,0},{1,17},{17,1},{2,18},{18,2},{3,19},{19,3},{4,20},{20... | collective-permute-start | bytes 884744 | tf_op jit(solution)/shard_map/ppermute | solution.py:27
  60.7 2.6 %collective-permute-start.13 = (bf16[256,1536]{1,0:T(8,128)(2,1)}, bf16[256,1536]{1,0:T(8,128)(2,1)S(1)}, u32[]{:S(2)}, u32[]{:S(2)}) collective-permute-start(bf16[256,1536]{1,0:T(8,128)(2,1)} %get-tuple-element.38), channel_id=1, source_target_pairs={{0,1},{1,0},{2,3},{3,2},{4,5},{5,4},{6,7},{7,6},{8,9},{9,8},{10,11... | collective-permute-start | bytes 2359304 | tf_op jit(solution)/shard_map/ppermute | solution.py:27
  63.2 6.9 %collective-permute-start.14 = (bf16[768,1536]{1,0:T(8,128)(2,1)}, bf16[768,1536]{1,0:T(8,128)(2,1)}, u32[]{:S(2)}, u32[]{:S(2)}) collective-permute-start(bf16[768,1536]{1,0:T(8,128)(2,1)} %get-tuple-element.40.mine_ref), channel_id=1, source_target_pairs={{0,1},{1,0},{2,3},{3,2},{4,5},{5,4},{6,7},{7,6},{8,9},{9,8},{10,11... | collective-permute-start | bytes 7077896 | tf_op jit(solution)/shard_map/ppermute | solution.py:27
  64.1 6.0 %copy-start.1 = (bf16[768,1536]{1,0:T(8,128)(2,1)S(1)}, bf16[768,1536]{1,0:T(8,128)(2,1)}, u32[]{:S(2)}) copy-start(bf16[768,1536]{1,0:T(8,128)(2,1)} %get-tuple-element.40.mine_ref) | copy-start | bytes 7077892
  68.5 7.9 %collective-permute-start.17 = (bf16[256,1536]{1,0:T(8,128)(2,1)}, bf16[256,1536]{1,0:T(8,128)(2,1)S(1)}, u32[]{:S(2)}, u32[]{:S(2)}) collective-permute-start(bf16[256,1536]{1,0:T(8,128)(2,1)} %attention.1.grad_ref.refs_4_), channel_id=1, source_target_pairs={{0,1},{1,0},{2,3},{3,2},{4,5},{5,4},{6,7},{7,6},{8,9},{9,8},{10,11... | collective-permute-start | bytes 2359304 | tf_op jit(solution)/shard_map/ppermute | solution.py:27
  76.3 21.3 %collective-permute-start.15 = (bf16[128,3072]{1,0:T(8,128)(2,1)S(1)}, bf16[128,3072]{1,0:T(8,128)(2,1)S(1)}, u32[]{:S(2)}, u32[]{:S(2)}) collective-permute-start(bf16[128,3072]{1,0:T(8,128)(2,1)S(1)} %get-tuple-element.42), channel_id=1, source_target_pairs={{0,4},{4,0},{1,5},{5,1},{2,6},{6,2},{3,7},{7,3},{8,12},{12,8},{9,1... | collective-permute-start | bytes 2359304 | tf_op jit(solution)/shard_map/ppermute | solution.py:27
  79.2 11.8 %collective-permute-start.18 = (bf16[96,1536]{1,0:T(8,128)(2,1)S(1)}, bf16[96,1536]{1,0:T(8,128)(2,1)S(1)}, u32[]{:S(2)}, u32[]{:S(2)}) collective-permute-start(bf16[96,1536]{1,0:T(8,128)(2,1)S(1)} %get-tuple-element.46), channel_id=1, source_target_pairs={{0,2},{2,0},{1,3},{3,1},{4,6},{6,4},{5,7},{7,5},{8,10},{10,8},{9,1... | collective-permute-start | bytes 884744 | tf_op jit(solution)/shard_map/ppermute | solution.py:27
  91.0 8.5 %collective-permute-start.19 = (bf16[96,1536]{1,0:T(8,128)(2,1)S(1)}, bf16[96,1536]{1,0:T(8,128)(2,1)S(1)}, u32[]{:S(2)}, u32[]{:S(2)}) collective-permute-start(bf16[96,1536]{1,0:T(8,128)(2,1)S(1)} %get-tuple-element.47), channel_id=1, source_target_pairs={{0,2},{2,0},{1,3},{3,1},{4,6},{6,4},{5,7},{7,5},{8,10},{10,8},{9,1... | collective-permute-start | bytes 884744 | tf_op jit(solution)/shard_map/ppermute | solution.py:27
  92.8 31.3 %collective-permute-start.23 = (bf16[96,1536]{1,0:T(8,128)(2,1)S(1)}, bf16[96,1536]{1,0:T(8,128)(2,1)S(1)}, u32[]{:S(2)}, u32[]{:S(2)}) collective-permute-start(bf16[96,1536]{1,0:T(8,128)(2,1)S(1)} %add_convert_fusion.3), channel_id=1, source_target_pairs={{0,8},{8,0},{1,9},{9,1},{2,10},{10,2},{3,11},{11,3},{4,12},{12,4},... | collective-permute-start | bytes 884744 | tf_op jit(solution)/shard_map/ppermute | solution.py:27
  97.9 37.6 %collective-permute-start.16 = (bf16[128,3072]{1,0:T(8,128)(2,1)S(1)}, bf16[128,3072]{1,0:T(8,128)(2,1)S(1)}, u32[]{:S(2)}, u32[]{:S(2)}) collective-permute-start(bf16[128,3072]{1,0:T(8,128)(2,1)S(1)} %add_convert_fusion), channel_id=1, source_target_pairs={{0,1},{1,2},{2,3},{3,4},{4,5},{5,6},{6,7},{7,8},{8,9},{9,10},{10,1... | collective-permute-start | bytes 2359304 | tf_op jit(solution)/shard_map/ppermute | solution.py:18
  99.5 24.7 %collective-permute-start.21 = (bf16[96,1536]{1,0:T(8,128)(2,1)S(1)}, bf16[96,1536]{1,0:T(8,128)(2,1)S(1)}, u32[]{:S(2)}, u32[]{:S(2)}) collective-permute-start(bf16[96,1536]{1,0:T(8,128)(2,1)S(1)} %get-tuple-element.54), channel_id=1, source_target_pairs={{0,2},{2,0},{1,3},{3,1},{4,6},{6,4},{5,7},{7,5},{8,10},{10,8},{9,1... | collective-permute-start | bytes 884744 | tf_op jit(solution)/shard_map/ppermute | solution.py:27
  104.5 30.9 %collective-permute-start.20 = (bf16[96,1536]{1,0:T(8,128)(2,1)S(1)}, bf16[96,1536]{1,0:T(8,128)(2,1)S(1)}, u32[]{:S(2)}, u32[]{:S(2)}) collective-permute-start(bf16[96,1536]{1,0:T(8,128)(2,1)S(1)} %add_convert_fusion.4), channel_id=1, source_target_pairs={{0,8},{8,0},{1,9},{9,1},{2,10},{10,2},{3,11},{11,3},{4,12},{12,4},... | collective-permute-start | bytes 884744 | tf_op jit(solution)/shard_map/ppermute | solution.py:27
  124.3 11.1 %collective-permute-start.24 = (bf16[96,1536]{1,0:T(8,128)(2,1)S(1)}, bf16[96,1536]{1,0:T(8,128)(2,1)S(1)}, u32[]{:S(2)}, u32[]{:S(2)}) collective-permute-start(bf16[96,1536]{1,0:T(8,128)(2,1)S(1)} %add_convert_fusion.2), channel_id=1, source_target_pairs={{0,4},{4,0},{1,5},{5,1},{2,6},{6,2},{3,7},{7,3},{8,12},{12,8},{9,1... | collective-permute-start | bytes 884744 | tf_op jit(solution)/shard_map/ppermute | solution.py:27
  125.0 15.4 %collective-permute-start.22 = (bf16[96,1536]{1,0:T(8,128)(2,1)S(1)}, bf16[96,1536]{1,0:T(8,128)(2,1)S(1)}, u32[]{:S(2)}, u32[]{:S(2)}) collective-permute-start(bf16[96,1536]{1,0:T(8,128)(2,1)S(1)} %get-tuple-element.55), channel_id=1, source_target_pairs={{0,2},{2,0},{1,3},{3,1},{4,6},{6,4},{5,7},{7,5},{8,10},{10,8},{9,1... | collective-permute-start | bytes 884744 | tf_op jit(solution)/shard_map/ppermute | solution.py:27
  (23 other events, 74.1 us)

commit v4 on v3

--- a/solution.py
+++ b/solution.py
@@ -93,7 +93,7 @@
             center = rolled - jnp.mean(rolled, axis=-1, keepdims=True)
             spread = lax.rsqrt(jnp.mean(center * center, axis=-1, keepdims=True) + epsilon)
             rolled = center * spread * gain_ref[...]
-        turned_ref[...] = rolled.T.astype(jnp.bfloat16)
+        turned_ref[...] = rolled.astype(jnp.bfloat16).T
         for i in range(8):
             at = pl.ds(i * rows, rows)
             kept_ref[k, at, :] = turned_ref[pl.ds(pl.multiple_of(info_ref[4 + i] * rows, 16), rows), :]
@@ -110,7 +110,7 @@
 
 def products_kernel(place_ref, *refs):
     tiles, pieces = refs[:4], refs[4:12]
-    kept_ref, sent_ref, full_ref, tile_ref, w_ref, sems, out_sem = refs[12:]
+    kept_ref, sent_ref, full_ref, tile_ref, x_ref, w_ref, sems, out_sem = refs[12:]
     tile = tiles[0].shape[2]
     part = w_ref.shape[1] // 4
     copies = []
@@ -121,19 +121,19 @@
         copies.append(pltpu.make_async_copy(source, tile_ref.at[j], sems.at[8 + j]))
     for copy in copies:
         copy.start()
-    for copy in copies:
+    for j, at in enumerate((0, 2, 1, 3)):
+        copies[8 + j].wait()
+        for kind in range(2):
+            x_ref[kind, pl.ds(at * tile, tile), :] = tile_ref[j, kind].T
+    for copy in copies[:8]:
         copy.wait()
     out_copy = pltpu.make_async_copy(w_ref, full_ref, out_sem)
     out_copy.start()
-    for j in (1, 3, 0, 2):
-        rows = pl.ds(j // 2 * tile, tile)
-        for n in range(4):
-            cols = pl.ds(n * part, part)
-            product = down(tile_ref[j, n // 3], w_ref[:, cols])
-            if j % 2:
-                sent_ref[rows, cols] = product.astype(jnp.bfloat16)
-            else:
-                kept_ref[rows, cols] = product
+    for n in range(4):
+        cols = pl.ds(n * part, part)
+        product = jnp.dot(x_ref[n // 3], w_ref[:, cols], preferred_element_type=jnp.float32)
+        kept_ref[:, cols] = product[: 2 * tile]
+        sent_ref[:, cols] = product[2 * tile :].astype(jnp.bfloat16)
     out_copy.wait()
 
 
@@ -296,6 +296,7 @@
         below = picked(onehot_rows, stream, along_lat(stream, -1))
         below_cot = picked(onehot_rows, flat_cot, along_lat(flat_cot, -1))
         rows = zeros
+    moved, moved_cot = along_lon(below, -1), along_lon(below_cot, -1)
     info = jnp.concatenate(
         [jnp.stack([rows, shifts[:, 1]], axis=1).reshape(-1), jnp.stack(natural)]
     ).astype(jnp.int32)
@@ -314,15 +315,17 @@
         2 * 2 * 2 * tile * tile * width,
         3_000_000,
         "turned_rolls",
-    )(info, gain.reshape(1, -1), below, along_lon(below, -1), below_cot, along_lon(below_cot, -1))
-    half_side = swap(after(half_piece, own_turned), "side")
-    far_side = swap(across_far, "side")
-    side_grp, far_grp = swap(half_side, "grp"), swap(across_far, "grp")
+        24,
+    )(info, gain.reshape(1, -1), below, moved, below_cot, moved_cot)
+    mine_side = swap(after(mine, (moved, moved_cot)), "side")
+    across_far = after(across_far, mine_side)
+    far_side, far_grp = swap(across_far, "side"), swap(across_far, "grp")
+    came_side = swap(after(came, far_side), "side")
     pieces = [
         (mine, 0, 0, near),
         (came, 0, 0, 1 - near),
-        (half_side, 0, 1, held),
-        (side_grp, 0, 1, 1 - held),
+        (mine_side, 0, 1, near),
+        (came_side, 0, 1, 1 - near),
         (across_far, 1, 0, held),
         (far_grp, 1, 0, 1 - held),
         (far_side, 1, 1, held),
@@ -330,7 +333,7 @@
     ]
     places = jnp.stack([(1 - f) * 4 + (1 - s) * 2 + n for _, f, s, n in pieces]).astype(jnp.int32)
     own_near, sent_near = swap(own_turned, "near"), swap(sent_turned, "near")
-    tiles = [own_turned, swap(after(sent_turned, (sent_near, side_grp)), "core"), own_near, swap(after(sent_near, (far_grp, side_grp)), "core")]
+    tiles = [own_turned, swap(after(sent_turned, (sent_near, far_grp)), "core"), own_near, swap(after(sent_near, far_grp), "core")]
 
     onehot = (index_table[:, :, None] == jnp.arange(entries, dtype=jnp.int32)).astype(f32)
     own_table = lax.dynamic_slice_in_dim(bias_table, near * own_heads, own_heads, 2)
@@ -353,6 +356,7 @@
         (vmem, vmem, anywhere),
         [
             pltpu.VMEM((4, 2, half, tile), bf16),
+            pltpu.VMEM((2, 4 * tile, half), bf16),
             pltpu.VMEM((half, 4 * part), bf16),
             dma((12,)),
             dma,

time: 142 us -> 138 us (0.972)
  starting transfers between devices: 31.4 us -> 28.7 us
  waiting for transfers between devices: 65.3 us -> 67.5 us
  local copies, waits for them, and re-layouts: 9.56 us -> 7.46 us
    ppermute x22, starting transfers between devices: 30.6 us -> 28 us  [swap(): return lax.ppermute(shard, axis, [(0, 1), (1, 0)])]
    ppermute x22, waiting for transfers between devices: 65.3 us -> 67.5 us  [swap(): return lax.ppermute(shard, axis, [(0, 1), (1, 0)])]
    pallas_call x1, Pallas kernels: 4.02 us -> 2.41 us  [on_device(): kernel_call(turned_rolls, (turned, turned), [smem, vmem] + [anywhere] * 4...]
    unnamed x60 -> x46, local copies, waits for them, and re-layouts: 4.33 us -> 3.49 us
  transfers between devices with their start and end apart: 25 -> 25, of which waited for: 11 -> 12; matrix products, arithmetic and copies ran while one was open for 10% -> 9% of each run, Pallas kernels for 11% -> 11%
where the time goes in v4:
time: 138 us
  waiting for transfers between devices  67.5 us (49%)
  starting transfers between devices  28.7 us (21%)
  Pallas kernels  21.8 us (16%)
  local copies, waits for them, and re-layouts  7.46 us (5%)
  matrix products  5.76 us (4%)
  other arithmetic  5.29 us (4%)
    ppermute x22, waiting for transfers between devices, swap(): return lax.ppermute(shard, axis, [(0, 1), (1, 0)])  67.5 us
    ppermute x22, starting transfers between devices, swap(): return lax.ppermute(shard, axis, [(0, 1), (1, 0)])  28 us
    pallas_call x1, Pallas kernels, on_device(): kernel_call(products_kernel, (jax.ShapeDtypeStruct((2 * tile, 4 * part),...  6.32 us
    pallas_call x1, Pallas kernels, on_device(): kernel_call(outer_kernel, (jax.ShapeDtypeStruct((tile, 2 * width), f32),...  4.82 us
    pallas_call x1, Pallas kernels, on_device(): kernel_call(functools.partial(attention_kernel, area, head), jax.ShapeDty...  4.36 us
    pallas_call x1, Pallas kernels, on_device(): kernel_call(weights_kernel, [jax.ShapeDtypeStruct((own_rows, 4 * part), b...  3.88 us
    unnamed x46, local copies, waits for them, and re-layouts  3.49 us
    dot_general x1, matrix products, picked(): jnp.dot(onehot, both, preferred_element_type=jnp.float32)  3.12 us
  transfers between devices with their start and end apart: 25, of which 12 were waited for; matrix products, arithmetic and copies ran while one was open for 9% of the time, Pallas kernels for 11%

profile of v4, /device:TPU:6, one launch (start us, length us, event | category | flops | bytes accessed | tf_op | source)
XLA Modules:
  0.0 137.6 jit_solution(14282600324052247970)
XLA Ops:
  0.7 1.3 fusion.81
  2.0 1.6 %collective-permute-start.3 = (bf16[96,1536]{1,0:T(8,128)(2,1)S(1)}, bf16[96,1536]{1,0:T(8,128)(2,1)S(1)}, u32[]{:S(2)}, u32[]{:S(2)}) collective-permute-start(bf16[96,1536]{1,0:T(8,128)(2,1)S(1)} %broadcast_select_fusion), channel_id=1, source_target_pairs={{0,4},{4,0},{1,5},{5,1},{2,6},{6,2},{3,7},{7,3},{8,12},{12,8},{9,1... | collective-permute-start | bytes 884744 | tf_op jit(solution)/shard_map/ppermute | solution.py:27
  4.7 6.1 %collective-permute-done.3.refs_5_ = bf16[96,1536]{1,0:T(8,128)(2,1)S(1)} collective-permute-done((bf16[96,1536]{1,0:T(8,128)(2,1)S(1)}, bf16[96,1536]{1,0:T(8,128)(2,1)S(1)}, u32[]{:S(2)}, u32[]{:S(2)}) %collective-permute-start.3) | collective-permute-done | bytes 294944 | tf_op jit(solution)/shard_map/ppermute | solution.py:27
  10.9 0.8 broadcast_select_fusion.2
  11.7 2.6 %collective-permute-start.4 = (bf16[96,1536]{1,0:T(8,128)(2,1)}, bf16[96,1536]{1,0:T(8,128)(2,1)}, u32[]{:S(2)}, u32[]{:S(2)}) collective-permute-start(bf16[96,1536]{1,0:T(8,128)(2,1)} %get-tuple-element.69), channel_id=1, source_target_pairs={{0,8},{8,0},{1,9},{9,1},{2,10},{10,2},{3,11},{11,3},{4,12},{12,4},... | collective-permute-start | bytes 884744 | tf_op jit(solution)/shard_map/ppermute | solution.py:27
  14.3 7.8 %collective-permute-start.5 = (bf16[96,1536]{1,0:T(8,128)(2,1)S(1)}, bf16[96,1536]{1,0:T(8,128)(2,1)S(1)}, u32[]{:S(2)}, u32[]{:S(2)}) collective-permute-start(bf16[96,1536]{1,0:T(8,128)(2,1)S(1)} %get-tuple-element.36.refs_4_), channel_id=1, source_target_pairs={{0,2},{2,0},{1,3},{3,1},{4,6},{6,4},{5,7},{7,5},{8,10},{10,8},{9,1... | collective-permute-start | bytes 884744 | tf_op jit(solution)/shard_map/ppermute | solution.py:27
  22.3 2.4 %turned_rolls.1 = (bf16[2,768,128]{2,1,0:T(8,128)(2,1)S(1)}, bf16[2,768,128]{2,1,0:T(8,128)(2,1)S(1)}) custom-call(s32[20]{0:T(128)S(1)} %concatenate.15.info_ref, f32[1,1536]{1,0:T(1,128)S(1)} %reshape.97.gain_ref, bf16[128,1536]{1,0:T(8,128)(2,1)S(1)} %bitcast.49, bf16[128,1536]{1,0:T(8,128)(2,1)S(1)} %collective-permute-done.refs_1_, ...), custom_call_target="tpu_custom_call" | custom-call | flops 201326592 | bytes 3000000 | tf_op jit(solution)/shard_map/turned_rolls/pallas_call | solution.py:305
  24.8 2.4 %collective-permute-done.4.refs_8_ = bf16[96,1536]{1,0:T(8,128)(2,1)} collective-permute-done((bf16[96,1536]{1,0:T(8,128)(2,1)}, bf16[96,1536]{1,0:T(8,128)(2,1)}, u32[]{:S(2)}, u32[]{:S(2)}) %collective-permute-start.4) | collective-permute-done | bytes 294944 | tf_op jit(solution)/shard_map/ppermute | solution.py:27
  27.2 2.7 %collective-permute-done.5.refs_6_ = bf16[96,1536]{1,0:T(8,128)(2,1)S(1)} collective-permute-done((bf16[96,1536]{1,0:T(8,128)(2,1)S(1)}, bf16[96,1536]{1,0:T(8,128)(2,1)S(1)}, u32[]{:S(2)}, u32[]{:S(2)}) %collective-permute-start.5) | collective-permute-done | bytes 294944 | tf_op jit(solution)/shard_map/ppermute | solution.py:27
  31.0 3.2 %collective-permute-start.8 = (bf16[2,768,128]{2,1,0:T(8,128)(2,1)S(1)}, bf16[2,768,128]{2,1,0:T(8,128)(2,1)S(1)}, u32[]{:S(2)}, u32[]{:S(2)}) collective-permute-start(bf16[2,768,128]{2,1,0:T(8,128)(2,1)S(1)} %get-tuple-element.34.refs_0_), channel_id=1, source_target_pairs={{0,4},{4,0},{1,5},{5,1},{2,6},{6,2},{3,7},{7,3},{8,12},{12,8},{9,1... | collective-permute-start | bytes 1179656 | tf_op jit(solution)/shard_map/ppermute | solution.py:27
  34.2 2.3 %collective-permute-done.2 = bf16[2,768,128]{2,1,0:T(8,128)(2,1)} collective-permute-done((bf16[2,768,128]{2,1,0:T(8,128)(2,1)S(1)}, bf16[2,768,128]{2,1,0:T(8,128)(2,1)}, u32[]{:S(2)}, u32[]{:S(2)}) %collective-permute-start.2) | collective-permute-done | bytes 393248 | tf_op jit(solution)/shard_map/ppermute | solution.py:27
  36.4 2.8 %collective-permute-done.6.refs_9_ = bf16[96,1536]{1,0:T(8,128)(2,1)} collective-permute-done((bf16[96,1536]{1,0:T(8,128)(2,1)}, bf16[96,1536]{1,0:T(8,128)(2,1)}, u32[]{:S(2)}, u32[]{:S(2)}) %collective-permute-start.6) | collective-permute-done | bytes 294944 | tf_op jit(solution)/shard_map/ppermute | solution.py:27
  40.0 1.5 %collective-permute-start.12 = (bf16[96,1536]{1,0:T(8,128)(2,1)}, bf16[96,1536]{1,0:T(8,128)(2,1)}, u32[]{:S(2)}, u32[]{:S(2)}) collective-permute-start(bf16[96,1536]{1,0:T(8,128)(2,1)} %collective-permute-done.10.refs_10_), channel_id=1, source_target_pairs={{0,16},{16,0},{1,17},{17,1},{2,18},{18,2},{3,19},{19,3},{4,20},{20... | collective-permute-start | bytes 884744 | tf_op jit(solution)/shard_map/ppermute | solution.py:27
  41.5 2.6 %fusion.7 = f32[2,6,64,64]{3,1,2,0:T(8,128)S(1)} fusion(s32[64,64]{1,0:T(8,128)S(1)} %copy-done.22, pred[2,64,64]{2,1,0:T(8,128)(4,1)S(1)} %broadcast_compare_fusion, f32[2,225,6]{1,0,2:T(2,128)S(1)} %constant_dynamic-slice_fusion), kind=kOutput, calls=%fused_computation.9 | convolution fusion | flops 133681152 | bytes 231984 | tf_op jit(solution)/shard_map/qkr,lrh->lhqk/dot_general | solution.py:340
  44.2 0.8 copy.13
  45.7 3.3 %collective-permute-done.11.refs_7_ = bf16[96,1536]{1,0:T(8,128)(2,1)} collective-permute-done((bf16[96,1536]{1,0:T(8,128)(2,1)S(1)}, bf16[96,1536]{1,0:T(8,128)(2,1)}, u32[]{:S(2)}, u32[]{:S(2)}) %collective-permute-start.11) | collective-permute-done | bytes 294944 | tf_op jit(solution)/shard_map/ppermute | solution.py:27
  50.8 6.3 %products.1 = (f32[256,1536]{1,0:T(8,128)}, bf16[256,1536]{1,0:T(8,128)(2,1)}, bf16[768,1536]{1,0:T(8,128)(2,1)}) custom-call(s32[8]{0:T(128)} %stack.120.place_ref, bf16[2,768,128]{2,1,0:T(8,128)(2,1)} %copy-done.5, bf16[2,768,128]{2,1,0:T(8,128)(2,1)} %copy-done.9, bf16[2,768,128]{2,1,0:T(8,128)(2,1)} %copy-done.7, bf16[2,768,128]{2,1,0:T(8,128)(2,1)} %copy-done.11, ...), custom_call_target="tpu_custom_call" | custom-call | flops 1200000000 | bytes 9000000 | tf_op jit(solution)/shard_map/products/pallas_call | solution.py:348
  57.2 2.5 %collective-permute-done.13.came_ref = bf16[256,1536]{1,0:T(8,128)(2,1)S(1)} collective-permute-done((bf16[256,1536]{1,0:T(8,128)(2,1)}, bf16[256,1536]{1,0:T(8,128)(2,1)S(1)}, u32[]{:S(2)}, u32[]{:S(2)}) %collective-permute-start.13) | collective-permute-done | bytes 786464 | tf_op jit(solution)/shard_map/ppermute | solution.py:27
  60.6 4.4 %attention.1.grad_ref.refs_4_ = bf16[256,1536]{1,0:T(8,128)(2,1)} custom-call(f32[256,1536]{1,0:T(8,128)} %get-tuple-element.41.kept_ref, bf16[256,1536]{1,0:T(8,128)(2,1)} %copy-done.20, f32[2,3,128,64]{3,2,1,0:T(8,128)} %bitcast.52), custom_call_target="tpu_custom_call" | custom-call | flops 1000000000 | bytes 4000000 | tf_op jit(solution)/shard_map/attention/pallas_call | solution.py:369
  65.7 1.1 copy-done.3
  66.8 4.8 %projections.1 = (f32[128,3072]{1,0:T(8,128)S(1)}, bf16[128,3072]{1,0:T(8,128)(2,1)S(1)}) custom-call(s32[16]{0:T(128)S(1)} %stack.111.place_ref, bf16[256,1536]{1,0:T(8,128)(2,1)S(1)} %copy-done.3, bf16[768,1536]{1,0:T(8,128)(2,1)S(1)} %copy-done.1, bf16[768,1536]{1,0:T(8,128)(2,1)} %collective-permute-done.14.theirs_ref), custom_call_target="tpu_custom_call" | custom-call | flops 1200000000 | bytes 8000000 | tf_op jit(solution)/shard_map/projections/pallas_call | solution.py:382
  71.7 2.9 %collective-permute-start.15 = (bf16[128,3072]{1,0:T(8,128)(2,1)S(1)}, bf16[128,3072]{1,0:T(8,128)(2,1)S(1)}, u32[]{:S(2)}, u32[]{:S(2)}) collective-permute-start(bf16[128,3072]{1,0:T(8,128)(2,1)S(1)} %get-tuple-element.46), channel_id=1, source_target_pairs={{0,4},{4,0},{1,5},{5,1},{2,6},{6,2},{3,7},{7,3},{8,12},{12,8},{9,1... | collective-permute-start | bytes 2359304 | tf_op jit(solution)/shard_map/ppermute | solution.py:27
  74.6 3.9 %weight_gradient.1 = (bf16[96,1536]{1,0:T(8,128)(2,1)S(1)}, bf16[96,1536]{1,0:T(8,128)(2,1)S(1)}, bf16[96,1536]{1,0:T(8,128)(2,1)S(1)}, bf16[96,1536]{1,0:T(8,12...) custom-call(s32[1]{0:T(128)} %bitcast.34.near_ref, ...), custom_call_target="tpu_custom_call" | custom-call | flops 1200000000 | bytes 6000000 | tf_op jit(solution)/shard_map/weight_gradient/pallas_call | solution.py:396
  78.9 8.6 %collective-permute-done.18 = bf16[96,1536]{1,0:T(8,128)(2,1)S(1)} collective-permute-done((bf16[96,1536]{1,0:T(8,128)(2,1)S(1)}, bf16[96,1536]{1,0:T(8,128)(2,1)S(1)}, u32[]{:S(2)}, u32[]{:S(2)}) %collective-permute-start.18) | collective-permute-done | bytes 294944 | tf_op jit(solution)/shard_map/ppermute | solution.py:27
  87.9 3.5 %collective-permute-start.23 = (bf16[96,1536]{1,0:T(8,128)(2,1)S(1)}, bf16[96,1536]{1,0:T(8,128)(2,1)S(1)}, u32[]{:S(2)}, u32[]{:S(2)}) collective-permute-start(bf16[96,1536]{1,0:T(8,128)(2,1)S(1)} %add_convert_fusion.3), channel_id=1, source_target_pairs={{0,8},{8,0},{1,9},{9,1},{2,10},{10,2},{3,11},{11,3},{4,12},{12,4},... | collective-permute-start | bytes 884744 | tf_op jit(solution)/shard_map/ppermute | solution.py:27
  91.4 5.4 %collective-permute-done.15 = bf16[128,3072]{1,0:T(8,128)(2,1)S(1)} collective-permute-done((bf16[128,3072]{1,0:T(8,128)(2,1)S(1)}, bf16[128,3072]{1,0:T(8,128)(2,1)S(1)}, u32[]{:S(2)}, u32[]{:S(2)}) %collective-permute-start.15) | collective-permute-done | bytes 786464 | tf_op jit(solution)/shard_map/ppermute | solution.py:27
  97.2 2.3 %collective-permute-start.20 = (bf16[96,1536]{1,0:T(8,128)(2,1)S(1)}, bf16[96,1536]{1,0:T(8,128)(2,1)S(1)}, u32[]{:S(2)}, u32[]{:S(2)}) collective-permute-start(bf16[96,1536]{1,0:T(8,128)(2,1)S(1)} %add_convert_fusion.4), channel_id=1, source_target_pairs={{0,8},{8,0},{1,9},{9,1},{2,10},{10,2},{3,11},{11,3},{4,12},{12,4},... | collective-permute-start | bytes 884744 | tf_op jit(solution)/shard_map/ppermute | solution.py:27
  99.6 20.9 %collective-permute-done.23 = bf16[96,1536]{1,0:T(8,128)(2,1)S(1)} collective-permute-done((bf16[96,1536]{1,0:T(8,128)(2,1)S(1)}, bf16[96,1536]{1,0:T(8,128)(2,1)S(1)}, u32[]{:S(2)}, u32[]{:S(2)}) %collective-permute-start.23) | collective-permute-done | bytes 294944 | tf_op jit(solution)/shard_map/ppermute | solution.py:27
  121.2 10.0 %collective-permute-done.24 = bf16[96,1536]{1,0:T(8,128)(2,1)S(1)} collective-permute-done((bf16[96,1536]{1,0:T(8,128)(2,1)S(1)}, bf16[96,1536]{1,0:T(8,128)(2,1)S(1)}, u32[]{:S(2)}, u32[]{:S(2)}) %collective-permute-start.24) | collective-permute-done | bytes 294944 | tf_op jit(solution)/shard_map/ppermute | solution.py:27
  131.4 3.1 %convolution_convert_fusion = bf16[128,3072]{1,0:T(8,128)(2,1)S(1)} fusion(bf16[128,3072]{1,0:T(8,128)(2,1)S(1)} %add_convert_fusion, bf16[128,3072]{1,0:T(8,128)(2,1)S(1)} %collective-permute-done.16, s32[]{:T(128)} %bitcast.4, s32[]{:T(128)} %bitcast.3, s32[128]{0:T(128)S(1)} %get-tuple-element.93, s32[128]{0:T(128)S(1)} %get-tuple-element.95, ...), kind=kOutput, calls=%fused_computation.3 | convolution fusion | flops 206700544 | bytes 2362768 | tf_op jit(solution)/shard_map/dot_general | solution.py:52
  134.8 1.4 fusion.18
  136.5 1.1 broadcast_multiply_fusion
  (120 shorter events, 9.9 us)
Async XLA Ops:
  0.6 40.9 %copy-start = (f32[2,225,12]{1,0,2:T(2,128)S(1)}, f32[2,225,12]{1,0,2:T(2,128)}, u32[]{:S(2)}) copy-start(f32[2,225,12]{1,0,2:T(2,128)} %param.16) | copy-start | bytes 64804
  2.0 8.8 %collective-permute-start.3 = (bf16[96,1536]{1,0:T(8,128)(2,1)S(1)}, bf16[96,1536]{1,0:T(8,128)(2,1)S(1)}, u32[]{:S(2)}, u32[]{:S(2)}) collective-permute-start(bf16[96,1536]{1,0:T(8,128)(2,1)S(1)} %broadcast_select_fusion), channel_id=1, source_target_pairs={{0,4},{4,0},{1,5},{5,1},{2,6},{6,2},{3,7},{7,3},{8,12},{12,8},{9,1... | collective-permute-start | bytes 884744 | tf_op jit(solution)/shard_map/ppermute | solution.py:27
  3.9 18.3 %copy-start.19 = (s32[2,2]{1,0:T(2,128)S(1)}, s32[2,2]{1,0:T(2,128)}, u32[]{:S(2)}) copy-start(s32[2,2]{1,0:T(2,128)} %param.14) | copy-start | bytes 52
  3.9 18.4 %copy-start.16 = (f32[1536]{0:T(1024)S(1)}, f32[1536]{0:T(1024)}, u32[]{:S(2)}) copy-start(f32[1536]{0:T(1024)} %param.12) | copy-start | bytes 18436
  4.1 10.2 %collective-permute-start = (bf16[128,1536]{1,0:T(8,128)(2,1)S(1)}, bf16[128,1536]{1,0:T(8,128)(2,1)S(1)}, u32[]{:S(2)}, u32[]{:S(2)}) collective-permute-start(bf16[128,1536]{1,0:T(8,128)(2,1)S(1)} %bitcast.48), channel_id=1, source_target_pairs={{0,15},{1,0},{2,1},{3,2},{4,3},{5,4},{6,5},{7,6},{8,7},{9,8},{10,9... | collective-permute-start | bytes 1179656 | tf_op jit(solution)/shard_map/ppermute | solution.py:18
  4.1 10.2 %collective-permute-start.1 = (bf16[128,1536]{1,0:T(8,128)(2,1)S(1)}, bf16[128,1536]{1,0:T(8,128)(2,1)S(1)}, u32[]{:S(2)}, u32[]{:S(2)}) collective-permute-start(bf16[128,1536]{1,0:T(8,128)(2,1)S(1)} %bitcast.50), channel_id=1, source_target_pairs={{0,15},{1,0},{2,1},{3,2},{4,3},{5,4},{6,5},{7,6},{8,7},{9,8},{10,9... | collective-permute-start | bytes 1179656 | tf_op jit(solution)/shard_map/ppermute | solution.py:18
  10.9 29.0 %copy-start.14 = (bf16[96,1536]{1,0:T(8,128)(2,1)}, bf16[96,1536]{1,0:T(8,128)(2,1)S(1)}, u32[]{:S(2)}) copy-start(bf16[96,1536]{1,0:T(8,128)(2,1)S(1)} %collective-permute-done.3.refs_5_) | copy-start | bytes 884740
  11.7 32.5 %copy-start.15 = (bf16[96,1536]{1,0:T(8,128)(2,1)}, bf16[96,1536]{1,0:T(8,128)(2,1)S(1)}, u32[]{:S(2)}) copy-start(bf16[96,1536]{1,0:T(8,128)(2,1)S(1)} %get-tuple-element.36.refs_4_) | copy-start | bytes 884740
  11.7 29.8 %copy-start.22 = (s32[64,64]{1,0:T(8,128)S(1)}, s32[64,64]{1,0:T(8,128)}, u32[]{:S(2)}) copy-start(s32[64,64]{1,0:T(8,128)} %param.15) | copy-start | bytes 49156
  11.7 15.5 %collective-permute-start.4 = (bf16[96,1536]{1,0:T(8,128)(2,1)}, bf16[96,1536]{1,0:T(8,128)(2,1)}, u32[]{:S(2)}, u32[]{:S(2)}) collective-permute-start(bf16[96,1536]{1,0:T(8,128)(2,1)} %get-tuple-element.69), channel_id=1, source_target_pairs={{0,8},{8,0},{1,9},{9,1},{2,10},{10,2},{3,11},{11,3},{4,12},{12,4},... | collective-permute-start | bytes 884744 | tf_op jit(solution)/shard_map/ppermute | solution.py:27
  14.3 15.6 %collective-permute-start.5 = (bf16[96,1536]{1,0:T(8,128)(2,1)S(1)}, bf16[96,1536]{1,0:T(8,128)(2,1)S(1)}, u32[]{:S(2)}, u32[]{:S(2)}) collective-permute-start(bf16[96,1536]{1,0:T(8,128)(2,1)S(1)} %get-tuple-element.36.refs_4_), channel_id=1, source_target_pairs={{0,2},{2,0},{1,3},{3,1},{4,6},{6,4},{5,7},{7,5},{8,10},{10,8},{9,1... | collective-permute-start | bytes 884744 | tf_op jit(solution)/shard_map/ppermute | solution.py:27
  24.7 20.3 %copy-start.5 = (bf16[2,768,128]{2,1,0:T(8,128)(2,1)}, bf16[2,768,128]{2,1,0:T(8,128)(2,1)S(1)}, u32[]{:S(2)}) copy-start(bf16[2,768,128]{2,1,0:T(8,128)(2,1)S(1)} %get-tuple-element.34.refs_0_) | copy-start | bytes 1179652
  24.8 11.7 %collective-permute-start.2 = (bf16[2,768,128]{2,1,0:T(8,128)(2,1)S(1)}, bf16[2,768,128]{2,1,0:T(8,128)(2,1)}, u32[]{:S(2)}, u32[]{:S(2)}) collective-permute-start(bf16[2,768,128]{2,1,0:T(8,128)(2,1)S(1)} %get-tuple-element.38), channel_id=1, source_target_pairs={{0,4},{4,0},{1,5},{5,1},{2,6},{6,2},{3,7},{7,3},{8,12},{12,8},{9,1... | collective-permute-start | bytes 1179656 | tf_op jit(solution)/shard_map/ppermute | solution.py:27
  29.9 9.4 %collective-permute-start.6 = (bf16[96,1536]{1,0:T(8,128)(2,1)}, bf16[96,1536]{1,0:T(8,128)(2,1)}, u32[]{:S(2)}, u32[]{:S(2)}) collective-permute-start(bf16[96,1536]{1,0:T(8,128)(2,1)} %collective-permute-done.4.refs_8_), channel_id=1, source_target_pairs={{0,16},{16,0},{1,17},{17,1},{2,18},{18,2},{3,19},{19,3},{4,20},{20... | collective-permute-start | bytes 884744 | tf_op jit(solution)/shard_map/ppermute | solution.py:27
  30.2 9.7 %collective-permute-start.10 = (bf16[96,1536]{1,0:T(8,128)(2,1)}, bf16[96,1536]{1,0:T(8,128)(2,1)}, u32[]{:S(2)}, u32[]{:S(2)}) collective-permute-start(bf16[96,1536]{1,0:T(8,128)(2,1)} %collective-permute-done.4.refs_8_), channel_id=1, source_target_pairs={{0,2},{2,0},{1,3},{3,1},{4,6},{6,4},{5,7},{7,5},{8,10},{10,8},{9,1... | collective-permute-start | bytes 884744 | tf_op jit(solution)/shard_map/ppermute | solution.py:27
  31.0 14.7 %collective-permute-start.8 = (bf16[2,768,128]{2,1,0:T(8,128)(2,1)S(1)}, bf16[2,768,128]{2,1,0:T(8,128)(2,1)S(1)}, u32[]{:S(2)}, u32[]{:S(2)}) collective-permute-start(bf16[2,768,128]{2,1,0:T(8,128)(2,1)S(1)} %get-tuple-element.34.refs_0_), channel_id=1, source_target_pairs={{0,4},{4,0},{1,5},{5,1},{2,6},{6,2},{3,7},{7,3},{8,12},{12,8},{9,1... | collective-permute-start | bytes 1179656 | tf_op jit(solution)/shard_map/ppermute | solution.py:27
  39.3 10.0 %collective-permute-start.7 = (bf16[2,768,128]{2,1,0:T(8,128)(2,1)S(1)}, bf16[2,768,128]{2,1,0:T(8,128)(2,1)S(1)}, u32[]{:S(2)}, u32[]{:S(2)}) collective-permute-start(bf16[2,768,128]{2,1,0:T(8,128)(2,1)S(1)} %get-tuple-element.38), channel_id=1, source_target_pairs={{0,1},{1,0},{2,3},{3,2},{4,5},{5,4},{6,7},{7,6},{8,9},{9,8},{10,11... | collective-permute-start | bytes 1179656 | tf_op jit(solution)/shard_map/ppermute | solution.py:27
  39.3 10.0 %collective-permute-start.9 = (bf16[2,768,128]{2,1,0:T(8,128)(2,1)}, bf16[2,768,128]{2,1,0:T(8,128)(2,1)S(1)}, u32[]{:S(2)}, u32[]{:S(2)}) collective-permute-start(bf16[2,768,128]{2,1,0:T(8,128)(2,1)} %collective-permute-done.2), channel_id=1, source_target_pairs={{0,1},{1,0},{2,3},{3,2},{4,5},{5,4},{6,7},{7,6},{8,9},{9,8},{10,11... | collective-permute-start | bytes 1179656 | tf_op jit(solution)/shard_map/ppermute | solution.py:27
  39.9 9.1 %collective-permute-start.11 = (bf16[96,1536]{1,0:T(8,128)(2,1)S(1)}, bf16[96,1536]{1,0:T(8,128)(2,1)}, u32[]{:S(2)}, u32[]{:S(2)}) collective-permute-start(bf16[96,1536]{1,0:T(8,128)(2,1)S(1)} %collective-permute-done.3.refs_5_), channel_id=1, source_target_pairs={{0,2},{2,0},{1,3},{3,1},{4,6},{6,4},{5,7},{7,5},{8,10},{10,8},{9,1... | collective-permute-start | bytes 884744 | tf_op jit(solution)/shard_map/ppermute | solution.py:27
  40.0 9.3 %collective-permute-start.12 = (bf16[96,1536]{1,0:T(8,128)(2,1)}, bf16[96,1536]{1,0:T(8,128)(2,1)}, u32[]{:S(2)}, u32[]{:S(2)}) collective-permute-start(bf16[96,1536]{1,0:T(8,128)(2,1)} %collective-permute-done.10.refs_10_), channel_id=1, source_target_pairs={{0,16},{16,0},{1,17},{17,1},{2,18},{18,2},{3,19},{19,3},{4,20},{20... | collective-permute-start | bytes 884744 | tf_op jit(solution)/shard_map/ppermute | solution.py:27
  57.2 2.6 %collective-permute-start.13 = (bf16[256,1536]{1,0:T(8,128)(2,1)}, bf16[256,1536]{1,0:T(8,128)(2,1)S(1)}, u32[]{:S(2)}, u32[]{:S(2)}) collective-permute-start(bf16[256,1536]{1,0:T(8,128)(2,1)} %get-tuple-element.42), channel_id=1, source_target_pairs={{0,1},{1,0},{2,3},{3,2},{4,5},{5,4},{6,7},{7,6},{8,9},{9,8},{10,11... | collective-permute-start | bytes 2359304 | tf_op jit(solution)/shard_map/ppermute | solution.py:27
  59.7 5.9 %collective-permute-start.14 = (bf16[768,1536]{1,0:T(8,128)(2,1)}, bf16[768,1536]{1,0:T(8,128)(2,1)}, u32[]{:S(2)}, u32[]{:S(2)}) collective-permute-start(bf16[768,1536]{1,0:T(8,128)(2,1)} %get-tuple-element.44.mine_ref), channel_id=1, source_target_pairs={{0,1},{1,0},{2,3},{3,2},{4,5},{5,4},{6,7},{7,6},{8,9},{9,8},{10,11... | collective-permute-start | bytes 7077896 | tf_op jit(solution)/shard_map/ppermute | solution.py:27
  65.0 9.6 %collective-permute-start.17 = (bf16[256,1536]{1,0:T(8,128)(2,1)}, bf16[256,1536]{1,0:T(8,128)(2,1)}, u32[]{:S(2)}, u32[]{:S(2)}) collective-permute-start(bf16[256,1536]{1,0:T(8,128)(2,1)} %attention.1.grad_ref.refs_4_), channel_id=1, source_target_pairs={{0,1},{1,0},{2,3},{3,2},{4,5},{5,4},{6,7},{7,6},{8,9},{9,8},{10,11... | collective-permute-start | bytes 2359304 | tf_op jit(solution)/shard_map/ppermute | solution.py:27
  71.7 25.2 %collective-permute-start.15 = (bf16[128,3072]{1,0:T(8,128)(2,1)S(1)}, bf16[128,3072]{1,0:T(8,128)(2,1)S(1)}, u32[]{:S(2)}, u32[]{:S(2)}) collective-permute-start(bf16[128,3072]{1,0:T(8,128)(2,1)S(1)} %get-tuple-element.46), channel_id=1, source_target_pairs={{0,4},{4,0},{1,5},{5,1},{2,6},{6,2},{3,7},{7,3},{8,12},{12,8},{9,1... | collective-permute-start | bytes 2359304 | tf_op jit(solution)/shard_map/ppermute | solution.py:27
  78.5 9.1 %collective-permute-start.18 = (bf16[96,1536]{1,0:T(8,128)(2,1)S(1)}, bf16[96,1536]{1,0:T(8,128)(2,1)S(1)}, u32[]{:S(2)}, u32[]{:S(2)}) collective-permute-start(bf16[96,1536]{1,0:T(8,128)(2,1)S(1)} %get-tuple-element.50), channel_id=1, source_target_pairs={{0,2},{2,0},{1,3},{3,1},{4,6},{6,4},{5,7},{7,5},{8,10},{10,8},{9,1... | collective-permute-start | bytes 884744 | tf_op jit(solution)/shard_map/ppermute | solution.py:27
  87.5 9.6 %collective-permute-start.19 = (bf16[96,1536]{1,0:T(8,128)(2,1)S(1)}, bf16[96,1536]{1,0:T(8,128)(2,1)S(1)}, u32[]{:S(2)}, u32[]{:S(2)}) collective-permute-start(bf16[96,1536]{1,0:T(8,128)(2,1)S(1)} %get-tuple-element.51), channel_id=1, source_target_pairs={{0,2},{2,0},{1,3},{3,1},{4,6},{6,4},{5,7},{7,5},{8,10},{10,8},{9,1... | collective-permute-start | bytes 884744 | tf_op jit(solution)/shard_map/ppermute | solution.py:27
  87.9 32.5 %collective-permute-start.23 = (bf16[96,1536]{1,0:T(8,128)(2,1)S(1)}, bf16[96,1536]{1,0:T(8,128)(2,1)S(1)}, u32[]{:S(2)}, u32[]{:S(2)}) collective-permute-start(bf16[96,1536]{1,0:T(8,128)(2,1)S(1)} %add_convert_fusion.3), channel_id=1, source_target_pairs={{0,8},{8,0},{1,9},{9,1},{2,10},{10,2},{3,11},{11,3},{4,12},{12,4},... | collective-permute-start | bytes 884744 | tf_op jit(solution)/shard_map/ppermute | solution.py:27
  97.0 34.4 %collective-permute-start.16 = (bf16[128,3072]{1,0:T(8,128)(2,1)S(1)}, bf16[128,3072]{1,0:T(8,128)(2,1)S(1)}, u32[]{:S(2)}, u32[]{:S(2)}) collective-permute-start(bf16[128,3072]{1,0:T(8,128)(2,1)S(1)} %add_convert_fusion), channel_id=1, source_target_pairs={{0,1},{1,2},{2,3},{3,4},{4,5},{5,6},{6,7},{7,8},{8,9},{9,10},{10,1... | collective-permute-start | bytes 2359304 | tf_op jit(solution)/shard_map/ppermute | solution.py:18
  97.1 23.4 %collective-permute-start.21 = (bf16[96,1536]{1,0:T(8,128)(2,1)S(1)}, bf16[96,1536]{1,0:T(8,128)(2,1)S(1)}, u32[]{:S(2)}, u32[]{:S(2)}) collective-permute-start(bf16[96,1536]{1,0:T(8,128)(2,1)S(1)} %get-tuple-element.58), channel_id=1, source_target_pairs={{0,2},{2,0},{1,3},{3,1},{4,6},{6,4},{5,7},{7,5},{8,10},{10,8},{9,1... | collective-permute-start | bytes 884744 | tf_op jit(solution)/shard_map/ppermute | solution.py:27
  97.2 34.1 %collective-permute-start.20 = (bf16[96,1536]{1,0:T(8,128)(2,1)S(1)}, bf16[96,1536]{1,0:T(8,128)(2,1)S(1)}, u32[]{:S(2)}, u32[]{:S(2)}) collective-permute-start(bf16[96,1536]{1,0:T(8,128)(2,1)S(1)} %add_convert_fusion.4), channel_id=1, source_target_pairs={{0,8},{8,0},{1,9},{9,1},{2,10},{10,2},{3,11},{11,3},{4,12},{12,4},... | collective-permute-start | bytes 884744 | tf_op jit(solution)/shard_map/ppermute | solution.py:27
  120.6 10.7 %collective-permute-start.24 = (bf16[96,1536]{1,0:T(8,128)(2,1)S(1)}, bf16[96,1536]{1,0:T(8,128)(2,1)S(1)}, u32[]{:S(2)}, u32[]{:S(2)}) collective-permute-start(bf16[96,1536]{1,0:T(8,128)(2,1)S(1)} %add_convert_fusion.2), channel_id=1, source_target_pairs={{0,4},{4,0},{1,5},{5,1},{2,6},{6,2},{3,7},{7,3},{8,12},{12,8},{9,1... | collective-permute-start | bytes 884744 | tf_op jit(solution)/shard_map/ppermute | solution.py:27
  121.2 14.9 %collective-permute-start.22 = (bf16[96,1536]{1,0:T(8,128)(2,1)S(1)}, bf16[96,1536]{1,0:T(8,128)(2,1)S(1)}, u32[]{:S(2)}, u32[]{:S(2)}) collective-permute-start(bf16[96,1536]{1,0:T(8,128)(2,1)S(1)} %get-tuple-element.59), channel_id=1, source_target_pairs={{0,2},{2,0},{1,3},{3,1},{4,6},{6,4},{5,7},{7,5},{8,10},{10,8},{9,1... | collective-permute-start | bytes 884744 | tf_op jit(solution)/shard_map/ppermute | solution.py:27
  (16 other events, 63.2 us)

commit v5 on v4

--- a/solution.py
+++ b/solution.py
@@ -417,14 +417,14 @@
     side_far_0 = swap(after(block(1, 1, 0), side_far_1), "side")
     side_far_0 = after(side_far_0, arrived_back)
     far_1 = swap((block(1, 0, 1).astype(f32) + side_far_1.astype(f32)).astype(bf16), "far")
-    far_0 = swap(after((block(1, 0, 0).astype(f32) + side_far_0.astype(f32)).astype(bf16), side_far_1), "far")
+    far_0 = swap(after((block(1, 0, 0).astype(f32) + side_far_0.astype(f32)).astype(bf16), far_1), "far")
     side_1 = swap(after(block(0, 1, 1), (side_far_0, arrived_back)), "side")
     side_0 = swap(after(block(0, 1, 0), side_1), "side")
     total_1 = (block(0, 0, 1).astype(f32) + side_1.astype(f32) + far_1.astype(f32)).astype(bf16)
     theirs = swap(total_1, "near").astype(f32)
 
     back = (attended_own + arrived_back.astype(f32)).astype(jnp.bfloat16)
-    back = roll_back(back, shifts, levels, side, far_0)
+    back = after(roll_back(back, shifts, levels, side, far_1), far_0)
     output = (values + back[:, :width].astype(f32)).astype(jnp.bfloat16)
     scaled = center * spread
     upstream = back[:, width:].astype(f32) * gain

time: 138 us -> 136 us (0.986)
  the two profiles are of different devices: /device:TPU:6 before, /device:TPU:0 now
where the time goes in v5:
time: 136 us; the launch traced here: 135 us
  waiting for transfers between devices  62.3 us (46%)
  starting transfers between devices  32.6 us (24%)
  Pallas kernels  19.7 us (14%)
  local copies, waits for them, and re-layouts  7.52 us (6%)
  matrix products  6.92 us (5%)
  other arithmetic  5.31 us (4%)
    ppermute x22, waiting for transfers between devices, swap(): return lax.ppermute(shard, axis, [(0, 1), (1, 0)])  55 us
    ppermute x22, starting transfers between devices, swap(): return lax.ppermute(shard, axis, [(0, 1), (1, 0)])  29 us
    ppermute x3, waiting for transfers between devices, along_lon(): lax.ppermute(shard, LON, [(i, (i + by) % count) for i in range(count)])  7.32 us
    pallas_call x1, Pallas kernels, on_device(): kernel_call(products_kernel, (jax.ShapeDtypeStruct((2 * tile, 4 * part),...  6.32 us
    pallas_call x1, Pallas kernels, on_device(): kernel_call(functools.partial(attention_kernel, area, head), jax.ShapeDty...  4.35 us
    dot_general x1, matrix products, picked(): jnp.dot(onehot, both, preferred_element_type=jnp.float32)  4.27 us
    pallas_call x1, Pallas kernels, on_device(): kernel_call(outer_kernel, (jax.ShapeDtypeStruct((tile, 2 * width), f32),...  3.83 us
    ppermute x3, starting transfers between devices, along_lon(): lax.ppermute(shard, LON, [(i, (i + by) % count) for i in range(count)])  3.64 us
  transfers between devices with their start and end apart: 25, of which 16 were waited for; matrix products, arithmetic and copies ran while one was open for 10% of the time, Pallas kernels for 10%

profile of v5, /device:TPU:0, one launch (start us, length us, event | category | flops | bytes accessed | tf_op | source)
XLA Modules:
  0.0 135.3 jit_solution(5226048272331641729)
XLA Ops:
  2.0 3.1 %collective-permute-start.3 = (bf16[96,1536]{1,0:T(8,128)(2,1)S(1)}, bf16[96,1536]{1,0:T(8,128)(2,1)S(1)}, u32[]{:S(2)}, u32[]{:S(2)}) collective-permute-start(bf16[96,1536]{1,0:T(8,128)(2,1)S(1)} %broadcast_select_fusion), channel_id=1, source_target_pairs={{0,4},{4,0},{1,5},{5,1},{2,6},{6,2},{3,7},{7,3},{8,12},{12,8},{9,1... | collective-permute-start | bytes 884744 | tf_op jit(solution)/shard_map/ppermute | solution.py:27
  5.5 2.6 %collective-permute-start = (bf16[128,1536]{1,0:T(8,128)(2,1)S(1)}, bf16[128,1536]{1,0:T(8,128)(2,1)S(1)}, u32[]{:S(2)}, u32[]{:S(2)}) collective-permute-start(bf16[128,1536]{1,0:T(8,128)(2,1)S(1)} %bitcast.48), channel_id=1, source_target_pairs={{0,15},{1,0},{2,1},{3,2},{4,3},{5,4},{6,5},{7,6},{8,7},{9,8},{10,9... | collective-permute-start | bytes 1179656 | tf_op jit(solution)/shard_map/ppermute | solution.py:18
  9.1 3.1 %collective-permute-done.3.refs_5_ = bf16[96,1536]{1,0:T(8,128)(2,1)S(1)} collective-permute-done((bf16[96,1536]{1,0:T(8,128)(2,1)S(1)}, bf16[96,1536]{1,0:T(8,128)(2,1)S(1)}, u32[]{:S(2)}, u32[]{:S(2)}) %collective-permute-start.3) | collective-permute-done | bytes 294944 | tf_op jit(solution)/shard_map/ppermute | solution.py:27
  13.0 2.8 %collective-permute-start.4 = (bf16[96,1536]{1,0:T(8,128)(2,1)}, bf16[96,1536]{1,0:T(8,128)(2,1)}, u32[]{:S(2)}, u32[]{:S(2)}) collective-permute-start(bf16[96,1536]{1,0:T(8,128)(2,1)} %get-tuple-element.71), channel_id=1, source_target_pairs={{0,8},{8,0},{1,9},{9,1},{2,10},{10,2},{3,11},{11,3},{4,12},{12,4},... | collective-permute-start | bytes 884744 | tf_op jit(solution)/shard_map/ppermute | solution.py:27
  16.1 7.0 %collective-permute-done.1.refs_3_ = bf16[128,1536]{1,0:T(8,128)(2,1)S(1)} collective-permute-done((bf16[128,1536]{1,0:T(8,128)(2,1)S(1)}, bf16[128,1536]{1,0:T(8,128)(2,1)S(1)}, u32[]{:S(2)}, u32[]{:S(2)}) %collective-permute-start.1) | collective-permute-done | bytes 393248 | tf_op jit(solution)/shard_map/ppermute | solution.py:18
  23.3 2.4 %turned_rolls.1 = (bf16[2,768,128]{2,1,0:T(8,128)(2,1)S(1)}, bf16[2,768,128]{2,1,0:T(8,128)(2,1)S(1)}) custom-call(s32[20]{0:T(128)S(1)} %concatenate.15.info_ref, f32[1,1536]{1,0:T(1,128)S(1)} %reshape.97.gain_ref, bf16[128,1536]{1,0:T(8,128)(2,1)S(1)} %bitcast.49, bf16[128,1536]{1,0:T(8,128)(2,1)S(1)} %collective-permute-done.refs_1_, ...), custom_call_target="tpu_custom_call" | custom-call | flops 201326592 | bytes 3000000 | tf_op jit(solution)/shard_map/turned_rolls/pallas_call | solution.py:305
  25.8 5.2 %collective-permute-done.4.refs_8_ = bf16[96,1536]{1,0:T(8,128)(2,1)} collective-permute-done((bf16[96,1536]{1,0:T(8,128)(2,1)}, bf16[96,1536]{1,0:T(8,128)(2,1)}, u32[]{:S(2)}, u32[]{:S(2)}) %collective-permute-start.4) | collective-permute-done | bytes 294944 | tf_op jit(solution)/shard_map/ppermute | solution.py:27
  31.0 1.7 %collective-permute-start.6 = (bf16[96,1536]{1,0:T(8,128)(2,1)}, bf16[96,1536]{1,0:T(8,128)(2,1)}, u32[]{:S(2)}, u32[]{:S(2)}) collective-permute-start(bf16[96,1536]{1,0:T(8,128)(2,1)} %collective-permute-done.4.refs_8_), channel_id=1, source_target_pairs={{0,16},{16,0},{1,17},{17,1},{2,18},{18,2},{3,19},{19,3},{4,20},{20... | collective-permute-start | bytes 884744 | tf_op jit(solution)/shard_map/ppermute | solution.py:27
  32.7 1.8 %collective-permute-start.10 = (bf16[96,1536]{1,0:T(8,128)(2,1)}, bf16[96,1536]{1,0:T(8,128)(2,1)}, u32[]{:S(2)}, u32[]{:S(2)}) collective-permute-start(bf16[96,1536]{1,0:T(8,128)(2,1)} %collective-permute-done.4.refs_8_), channel_id=1, source_target_pairs={{0,2},{2,0},{1,3},{3,1},{4,6},{6,4},{5,7},{7,5},{8,10},{10,8},{9,1... | collective-permute-start | bytes 884744 | tf_op jit(solution)/shard_map/ppermute | solution.py:27
  36.1 3.2 %collective-permute-done.2 = bf16[2,768,128]{2,1,0:T(8,128)(2,1)} collective-permute-done((bf16[2,768,128]{2,1,0:T(8,128)(2,1)S(1)}, bf16[2,768,128]{2,1,0:T(8,128)(2,1)}, u32[]{:S(2)}, u32[]{:S(2)}) %collective-permute-start.2) | collective-permute-done | bytes 393248 | tf_op jit(solution)/shard_map/ppermute | solution.py:27
  40.0 1.9 %collective-permute-done.10.refs_10_ = bf16[96,1536]{1,0:T(8,128)(2,1)} collective-permute-done((bf16[96,1536]{1,0:T(8,128)(2,1)}, bf16[96,1536]{1,0:T(8,128)(2,1)}, u32[]{:S(2)}, u32[]{:S(2)}) %collective-permute-start.10) | collective-permute-done | bytes 294944 | tf_op jit(solution)/shard_map/ppermute | solution.py:27
  41.9 1.7 %collective-permute-start.11 = (bf16[96,1536]{1,0:T(8,128)(2,1)S(1)}, bf16[96,1536]{1,0:T(8,128)(2,1)}, u32[]{:S(2)}, u32[]{:S(2)}) collective-permute-start(bf16[96,1536]{1,0:T(8,128)(2,1)S(1)} %collective-permute-done.3.refs_5_), channel_id=1, source_target_pairs={{0,2},{2,0},{1,3},{3,1},{4,6},{6,4},{5,7},{7,5},{8,10},{10,8},{9,1... | collective-permute-start | bytes 884744 | tf_op jit(solution)/shard_map/ppermute | solution.py:27
  44.4 2.6 %fusion.7 = f32[2,6,64,64]{3,1,2,0:T(8,128)S(1)} fusion(s32[64,64]{1,0:T(8,128)S(1)} %copy-done.21, pred[2,64,64]{2,1,0:T(8,128)(4,1)S(1)} %broadcast_compare_fusion, f32[2,225,6]{1,0,2:T(2,128)S(1)} %constant_dynamic-slice_fusion), kind=kOutput, calls=%fused_computation.9 | convolution fusion | flops 133681152 | bytes 231984 | tf_op jit(solution)/shard_map/qkr,lrh->lhqk/dot_general | solution.py:340
  50.0 1.7 %collective-permute-done.12.refs_11_ = bf16[96,1536]{1,0:T(8,128)(2,1)} collective-permute-done((bf16[96,1536]{1,0:T(8,128)(2,1)}, bf16[96,1536]{1,0:T(8,128)(2,1)}, u32[]{:S(2)}, u32[]{:S(2)}) %collective-permute-start.12) | collective-permute-done | bytes 294944 | tf_op jit(solution)/shard_map/ppermute | solution.py:27
  53.2 6.3 %products.1 = (f32[256,1536]{1,0:T(8,128)}, bf16[256,1536]{1,0:T(8,128)(2,1)}, bf16[768,1536]{1,0:T(8,128)(2,1)}) custom-call(s32[8]{0:T(128)} %stack.120.place_ref, bf16[2,768,128]{2,1,0:T(8,128)(2,1)} %copy-done.4, bf16[2,768,128]{2,1,0:T(8,128)(2,1)} %copy-done.8, bf16[2,768,128]{2,1,0:T(8,128)(2,1)} %copy-done.6, bf16[2,768,128]{2,1,0:T(8,128)(2,1)} %copy-done.10, ...), custom_call_target="tpu_custom_call" | custom-call | flops 1200000000 | bytes 9000000 | tf_op jit(solution)/shard_map/products/pallas_call | solution.py:348
  59.6 2.5 %collective-permute-done.13.came_ref = bf16[256,1536]{1,0:T(8,128)(2,1)S(1)} collective-permute-done((bf16[256,1536]{1,0:T(8,128)(2,1)}, bf16[256,1536]{1,0:T(8,128)(2,1)S(1)}, u32[]{:S(2)}, u32[]{:S(2)}) %collective-permute-start.13) | collective-permute-done | bytes 786464 | tf_op jit(solution)/shard_map/ppermute | solution.py:27
  63.2 4.3 %attention.1.grad_ref.refs_4_ = bf16[256,1536]{1,0:T(8,128)(2,1)} custom-call(f32[256,1536]{1,0:T(8,128)} %get-tuple-element.42.kept_ref, bf16[256,1536]{1,0:T(8,128)(2,1)} %copy-done.19, f32[2,3,128,64]{3,2,1,0:T(8,128)} %bitcast.52), custom_call_target="tpu_custom_call" | custom-call | flops 1000000000 | bytes 4000000 | tf_op jit(solution)/shard_map/attention/pallas_call | solution.py:369
  69.9 3.8 %projections.1 = (f32[128,3072]{1,0:T(8,128)S(1)}, bf16[128,3072]{1,0:T(8,128)(2,1)S(1)}) custom-call(s32[16]{0:T(128)S(1)} %stack.111.place_ref, bf16[256,1536]{1,0:T(8,128)(2,1)S(1)} %copy-done.3, bf16[768,1536]{1,0:T(8,128)(2,1)S(1)} %copy-done.1, bf16[768,1536]{1,0:T(8,128)(2,1)S(1)} %collective-permute-done.14.theirs_ref), custom_call_target="tpu_custom_call" | custom-call | flops 1200000000 | bytes 8000000 | tf_op jit(solution)/shard_map/projections/pallas_call | solution.py:382
  73.7 1.8 %collective-permute-start.15 = (bf16[128,3072]{1,0:T(8,128)(2,1)S(1)}, bf16[128,3072]{1,0:T(8,128)(2,1)S(1)}, u32[]{:S(2)}, u32[]{:S(2)}) collective-permute-start(bf16[128,3072]{1,0:T(8,128)(2,1)S(1)} %get-tuple-element.47), channel_id=1, source_target_pairs={{0,4},{4,0},{1,5},{5,1},{2,6},{6,2},{3,7},{7,3},{8,12},{12,8},{9,1... | collective-permute-start | bytes 2359304 | tf_op jit(solution)/shard_map/ppermute | solution.py:27
  75.6 2.7 %weight_gradient.1 = (bf16[96,1536]{1,0:T(8,128)(2,1)S(1)}, bf16[96,1536]{1,0:T(8,128)(2,1)S(1)}, bf16[96,1536]{1,0:T(8,128)(2,1)S(1)}, bf16[96,1536]{1,0:T(8,12...) custom-call(s32[1]{0:T(128)} %bitcast.34.near_ref, ...), custom_call_target="tpu_custom_call" | custom-call | flops 1200000000 | bytes 6000000 | tf_op jit(solution)/shard_map/weight_gradient/pallas_call | solution.py:396
  78.3 1.7 %collective-permute-start.18 = (bf16[96,1536]{1,0:T(8,128)(2,1)S(1)}, bf16[96,1536]{1,0:T(8,128)(2,1)S(1)}, u32[]{:S(2)}, u32[]{:S(2)}) collective-permute-start(bf16[96,1536]{1,0:T(8,128)(2,1)S(1)} %get-tuple-element.50), channel_id=1, source_target_pairs={{0,2},{2,0},{1,3},{3,1},{4,6},{6,4},{5,7},{7,5},{8,10},{10,8},{9,1... | collective-permute-start | bytes 884744 | tf_op jit(solution)/shard_map/ppermute | solution.py:27
  80.1 7.1 %collective-permute-done.18 = bf16[96,1536]{1,0:T(8,128)(2,1)S(1)} collective-permute-done((bf16[96,1536]{1,0:T(8,128)(2,1)S(1)}, bf16[96,1536]{1,0:T(8,128)(2,1)S(1)}, u32[]{:S(2)}, u32[]{:S(2)}) %collective-permute-start.18) | collective-permute-done | bytes 294944 | tf_op jit(solution)/shard_map/ppermute | solution.py:27
  87.2 1.7 %collective-permute-start.20 = (bf16[96,1536]{1,0:T(8,128)(2,1)S(1)}, bf16[96,1536]{1,0:T(8,128)(2,1)S(1)}, u32[]{:S(2)}, u32[]{:S(2)}) collective-permute-start(bf16[96,1536]{1,0:T(8,128)(2,1)S(1)} %get-tuple-element.54), channel_id=1, source_target_pairs={{0,2},{2,0},{1,3},{3,1},{4,6},{6,4},{5,7},{7,5},{8,10},{10,8},{9,1... | collective-permute-start | bytes 884744 | tf_op jit(solution)/shard_map/ppermute | solution.py:27
  88.9 3.4 %collective-permute-start.19 = (bf16[96,1536]{1,0:T(8,128)(2,1)S(1)}, bf16[96,1536]{1,0:T(8,128)(2,1)S(1)}, u32[]{:S(2)}, u32[]{:S(2)}) collective-permute-start(bf16[96,1536]{1,0:T(8,128)(2,1)S(1)} %add_convert_fusion.4), channel_id=1, source_target_pairs={{0,8},{8,0},{1,9},{9,1},{2,10},{10,2},{3,11},{11,3},{4,12},{12,4},... | collective-permute-start | bytes 884744 | tf_op jit(solution)/shard_map/ppermute | solution.py:27
  92.4 2.7 %collective-permute-done.20 = bf16[96,1536]{1,0:T(8,128)(2,1)S(1)} collective-permute-done((bf16[96,1536]{1,0:T(8,128)(2,1)S(1)}, bf16[96,1536]{1,0:T(8,128)(2,1)S(1)}, u32[]{:S(2)}, u32[]{:S(2)}) %collective-permute-start.20) | collective-permute-done | bytes 294944 | tf_op jit(solution)/shard_map/ppermute | solution.py:27
  95.1 2.7 %collective-permute-done.15 = bf16[128,3072]{1,0:T(8,128)(2,1)S(1)} collective-permute-done((bf16[128,3072]{1,0:T(8,128)(2,1)S(1)}, bf16[128,3072]{1,0:T(8,128)(2,1)S(1)}, u32[]{:S(2)}, u32[]{:S(2)}) %collective-permute-start.15) | collective-permute-done | bytes 786464 | tf_op jit(solution)/shard_map/ppermute | solution.py:27
  97.7 3.0 %collective-permute-start.22 = (bf16[96,1536]{1,0:T(8,128)(2,1)S(1)}, bf16[96,1536]{1,0:T(8,128)(2,1)S(1)}, u32[]{:S(2)}, u32[]{:S(2)}) collective-permute-start(bf16[96,1536]{1,0:T(8,128)(2,1)S(1)} %get-tuple-element.61), channel_id=1, source_target_pairs={{0,2},{2,0},{1,3},{3,1},{4,6},{6,4},{5,7},{7,5},{8,10},{10,8},{9,1... | collective-permute-start | bytes 884744 | tf_op jit(solution)/shard_map/ppermute | solution.py:27
  100.9 3.7 %collective-permute-done.19 = bf16[96,1536]{1,0:T(8,128)(2,1)S(1)} collective-permute-done((bf16[96,1536]{1,0:T(8,128)(2,1)S(1)}, bf16[96,1536]{1,0:T(8,128)(2,1)S(1)}, u32[]{:S(2)}, u32[]{:S(2)}) %collective-permute-start.19) | collective-permute-done | bytes 294944 | tf_op jit(solution)/shard_map/ppermute | solution.py:27
  104.6 11.3 %collective-permute-done.22 = bf16[96,1536]{1,0:T(8,128)(2,1)S(1)} collective-permute-done((bf16[96,1536]{1,0:T(8,128)(2,1)S(1)}, bf16[96,1536]{1,0:T(8,128)(2,1)S(1)}, u32[]{:S(2)}, u32[]{:S(2)}) %collective-permute-start.22) | collective-permute-done | bytes 294944 | tf_op jit(solution)/shard_map/ppermute | solution.py:27
  116.2 2.9 %collective-permute-start.21 = (bf16[96,1536]{1,0:T(8,128)(2,1)S(1)}, bf16[96,1536]{1,0:T(8,128)(2,1)S(1)}, u32[]{:S(2)}, u32[]{:S(2)}) collective-permute-start(bf16[96,1536]{1,0:T(8,128)(2,1)S(1)} %add_convert_fusion.3), channel_id=1, source_target_pairs={{0,8},{8,0},{1,9},{9,1},{2,10},{10,2},{3,11},{11,3},{4,12},{12,4},... | collective-permute-start | bytes 884744 | tf_op jit(solution)/shard_map/ppermute | solution.py:27
  119.3 8.5 %collective-permute-done.24 = bf16[96,1536]{1,0:T(8,128)(2,1)S(1)} collective-permute-done((bf16[96,1536]{1,0:T(8,128)(2,1)S(1)}, bf16[96,1536]{1,0:T(8,128)(2,1)S(1)}, u32[]{:S(2)}, u32[]{:S(2)}) %collective-permute-start.24) | collective-permute-done | bytes 294944 | tf_op jit(solution)/shard_map/ppermute | solution.py:27
  127.9 4.3 %convolution_convert_fusion = bf16[128,3072]{1,0:T(8,128)(2,1)S(1)} fusion(bf16[128,3072]{1,0:T(8,128)(2,1)S(1)} %add_convert_fusion, bf16[128,3072]{1,0:T(8,128)(2,1)} %collective-permute-done.16, s32[]{:T(128)} %bitcast.4, s32[]{:T(128)} %bitcast.3, s32[128]{0:T(128)S(1)} %get-tuple-element.95, s32[128]{0:T(128)S(1)} %get-tuple-element.97, s32[]{:T(128)} %bitcast.2, ...), kind=kOutput, calls=%fused_computation.3 | convolution fusion | flops 206700544 | bytes 2362768 | tf_op jit(solution)/shard_map/dot_general | solution.py:52
  (118 shorter events, 19.1 us)
Async XLA Ops:
  0.6 43.8 %copy-start = (f32[2,225,12]{1,0,2:T(2,128)S(1)}, f32[2,225,12]{1,0,2:T(2,128)}, u32[]{:S(2)}) copy-start(f32[2,225,12]{1,0,2:T(2,128)} %param.16) | copy-start | bytes 64804
  2.0 10.1 %collective-permute-start.3 = (bf16[96,1536]{1,0:T(8,128)(2,1)S(1)}, bf16[96,1536]{1,0:T(8,128)(2,1)S(1)}, u32[]{:S(2)}, u32[]{:S(2)}) collective-permute-start(bf16[96,1536]{1,0:T(8,128)(2,1)S(1)} %broadcast_select_fusion), channel_id=1, source_target_pairs={{0,4},{4,0},{1,5},{5,1},{2,6},{6,2},{3,7},{7,3},{8,12},{12,8},{9,1... | collective-permute-start | bytes 884744 | tf_op jit(solution)/shard_map/ppermute | solution.py:27
  5.3 17.8 %copy-start.18 = (s32[2,2]{1,0:T(2,128)S(1)}, s32[2,2]{1,0:T(2,128)}, u32[]{:S(2)}) copy-start(s32[2,2]{1,0:T(2,128)} %param.14) | copy-start | bytes 52
  5.3 17.8 %copy-start.15 = (f32[1536]{0:T(1024)S(1)}, f32[1536]{0:T(1024)}, u32[]{:S(2)}) copy-start(f32[1536]{0:T(1024)} %param.12) | copy-start | bytes 18436
  5.5 10.6 %collective-permute-start = (bf16[128,1536]{1,0:T(8,128)(2,1)S(1)}, bf16[128,1536]{1,0:T(8,128)(2,1)S(1)}, u32[]{:S(2)}, u32[]{:S(2)}) collective-permute-start(bf16[128,1536]{1,0:T(8,128)(2,1)S(1)} %bitcast.48), channel_id=1, source_target_pairs={{0,15},{1,0},{2,1},{3,2},{4,3},{5,4},{6,5},{7,6},{8,7},{9,8},{10,9... | collective-permute-start | bytes 1179656 | tf_op jit(solution)/shard_map/ppermute | solution.py:18
  8.1 14.9 %collective-permute-start.1 = (bf16[128,1536]{1,0:T(8,128)(2,1)S(1)}, bf16[128,1536]{1,0:T(8,128)(2,1)S(1)}, u32[]{:S(2)}, u32[]{:S(2)}) collective-permute-start(bf16[128,1536]{1,0:T(8,128)(2,1)S(1)} %bitcast.50), channel_id=1, source_target_pairs={{0,15},{1,0},{2,1},{3,2},{4,3},{5,4},{6,5},{7,6},{8,7},{9,8},{10,9... | collective-permute-start | bytes 1179656 | tf_op jit(solution)/shard_map/ppermute | solution.py:18
  12.1 29.7 %copy-start.13 = (bf16[96,1536]{1,0:T(8,128)(2,1)}, bf16[96,1536]{1,0:T(8,128)(2,1)S(1)}, u32[]{:S(2)}) copy-start(bf16[96,1536]{1,0:T(8,128)(2,1)S(1)} %collective-permute-done.3.refs_5_) | copy-start | bytes 884740
  13.0 34.1 %copy-start.14 = (bf16[96,1536]{1,0:T(8,128)(2,1)}, bf16[96,1536]{1,0:T(8,128)(2,1)S(1)}, u32[]{:S(2)}) copy-start(bf16[96,1536]{1,0:T(8,128)(2,1)S(1)} %get-tuple-element.37.refs_4_) | copy-start | bytes 884740
  13.0 31.4 %copy-start.21 = (s32[64,64]{1,0:T(8,128)S(1)}, s32[64,64]{1,0:T(8,128)}, u32[]{:S(2)}) copy-start(s32[64,64]{1,0:T(8,128)} %param.15) | copy-start | bytes 49156
  13.0 17.9 %collective-permute-start.4 = (bf16[96,1536]{1,0:T(8,128)(2,1)}, bf16[96,1536]{1,0:T(8,128)(2,1)}, u32[]{:S(2)}, u32[]{:S(2)}) collective-permute-start(bf16[96,1536]{1,0:T(8,128)(2,1)} %get-tuple-element.71), channel_id=1, source_target_pairs={{0,8},{8,0},{1,9},{9,1},{2,10},{10,2},{3,11},{11,3},{4,12},{12,4},... | collective-permute-start | bytes 884744 | tf_op jit(solution)/shard_map/ppermute | solution.py:27
  23.1 7.9 %collective-permute-start.5 = (bf16[96,1536]{1,0:T(8,128)(2,1)S(1)}, bf16[96,1536]{1,0:T(8,128)(2,1)S(1)}, u32[]{:S(2)}, u32[]{:S(2)}) collective-permute-start(bf16[96,1536]{1,0:T(8,128)(2,1)S(1)} %get-tuple-element.37.refs_4_), channel_id=1, source_target_pairs={{0,2},{2,0},{1,3},{3,1},{4,6},{6,4},{5,7},{7,5},{8,10},{10,8},{9,1... | collective-permute-start | bytes 884744 | tf_op jit(solution)/shard_map/ppermute | solution.py:27
  25.7 22.3 %copy-start.4 = (bf16[2,768,128]{2,1,0:T(8,128)(2,1)}, bf16[2,768,128]{2,1,0:T(8,128)(2,1)S(1)}, u32[]{:S(2)}) copy-start(bf16[2,768,128]{2,1,0:T(8,128)(2,1)S(1)} %get-tuple-element.35.refs_0_) | copy-start | bytes 1179652
  25.7 13.6 %collective-permute-start.2 = (bf16[2,768,128]{2,1,0:T(8,128)(2,1)S(1)}, bf16[2,768,128]{2,1,0:T(8,128)(2,1)}, u32[]{:S(2)}, u32[]{:S(2)}) collective-permute-start(bf16[2,768,128]{2,1,0:T(8,128)(2,1)S(1)} %get-tuple-element.39), channel_id=1, source_target_pairs={{0,4},{4,0},{1,5},{5,1},{2,6},{6,2},{3,7},{7,3},{8,12},{12,8},{9,1... | collective-permute-start | bytes 1179656 | tf_op jit(solution)/shard_map/ppermute | solution.py:27
  31.0 8.4 %collective-permute-start.6 = (bf16[96,1536]{1,0:T(8,128)(2,1)}, bf16[96,1536]{1,0:T(8,128)(2,1)}, u32[]{:S(2)}, u32[]{:S(2)}) collective-permute-start(bf16[96,1536]{1,0:T(8,128)(2,1)} %collective-permute-done.4.refs_8_), channel_id=1, source_target_pairs={{0,16},{16,0},{1,17},{17,1},{2,18},{18,2},{3,19},{19,3},{4,20},{20... | collective-permute-start | bytes 884744 | tf_op jit(solution)/shard_map/ppermute | solution.py:27
  32.7 9.1 %collective-permute-start.10 = (bf16[96,1536]{1,0:T(8,128)(2,1)}, bf16[96,1536]{1,0:T(8,128)(2,1)}, u32[]{:S(2)}, u32[]{:S(2)}) collective-permute-start(bf16[96,1536]{1,0:T(8,128)(2,1)} %collective-permute-done.4.refs_8_), channel_id=1, source_target_pairs={{0,2},{2,0},{1,3},{3,1},{4,6},{6,4},{5,7},{7,5},{8,10},{10,8},{9,1... | collective-permute-start | bytes 884744 | tf_op jit(solution)/shard_map/ppermute | solution.py:27
  34.8 13.7 %collective-permute-start.8 = (bf16[2,768,128]{2,1,0:T(8,128)(2,1)S(1)}, bf16[2,768,128]{2,1,0:T(8,128)(2,1)S(1)}, u32[]{:S(2)}, u32[]{:S(2)}) collective-permute-start(bf16[2,768,128]{2,1,0:T(8,128)(2,1)S(1)} %get-tuple-element.35.refs_0_), channel_id=1, source_target_pairs={{0,4},{4,0},{1,5},{5,1},{2,6},{6,2},{3,7},{7,3},{8,12},{12,8},{9,1... | collective-permute-start | bytes 1179656 | tf_op jit(solution)/shard_map/ppermute | solution.py:27
  39.4 12.2 %collective-permute-start.7 = (bf16[2,768,128]{2,1,0:T(8,128)(2,1)S(1)}, bf16[2,768,128]{2,1,0:T(8,128)(2,1)S(1)}, u32[]{:S(2)}, u32[]{:S(2)}) collective-permute-start(bf16[2,768,128]{2,1,0:T(8,128)(2,1)S(1)} %get-tuple-element.39), channel_id=1, source_target_pairs={{0,1},{1,0},{2,3},{3,2},{4,5},{5,4},{6,7},{7,6},{8,9},{9,8},{10,11... | collective-permute-start | bytes 1179656 | tf_op jit(solution)/shard_map/ppermute | solution.py:27
  39.4 12.2 %collective-permute-start.9 = (bf16[2,768,128]{2,1,0:T(8,128)(2,1)}, bf16[2,768,128]{2,1,0:T(8,128)(2,1)S(1)}, u32[]{:S(2)}, u32[]{:S(2)}) collective-permute-start(bf16[2,768,128]{2,1,0:T(8,128)(2,1)} %collective-permute-done.2), channel_id=1, source_target_pairs={{0,1},{1,0},{2,3},{3,2},{4,5},{5,4},{6,7},{7,6},{8,9},{9,8},{10,11... | collective-permute-start | bytes 1179656 | tf_op jit(solution)/shard_map/ppermute | solution.py:27
  41.9 8.1 %collective-permute-start.11 = (bf16[96,1536]{1,0:T(8,128)(2,1)S(1)}, bf16[96,1536]{1,0:T(8,128)(2,1)}, u32[]{:S(2)}, u32[]{:S(2)}) collective-permute-start(bf16[96,1536]{1,0:T(8,128)(2,1)S(1)} %collective-permute-done.3.refs_5_), channel_id=1, source_target_pairs={{0,2},{2,0},{1,3},{3,1},{4,6},{6,4},{5,7},{7,5},{8,10},{10,8},{9,1... | collective-permute-start | bytes 884744 | tf_op jit(solution)/shard_map/ppermute | solution.py:27
  43.6 8.0 %collective-permute-start.12 = (bf16[96,1536]{1,0:T(8,128)(2,1)}, bf16[96,1536]{1,0:T(8,128)(2,1)}, u32[]{:S(2)}, u32[]{:S(2)}) collective-permute-start(bf16[96,1536]{1,0:T(8,128)(2,1)} %collective-permute-done.10.refs_10_), channel_id=1, source_target_pairs={{0,16},{16,0},{1,17},{17,1},{2,18},{18,2},{3,19},{19,3},{4,20},{20... | collective-permute-start | bytes 884744 | tf_op jit(solution)/shard_map/ppermute | solution.py:27
  59.5 2.6 %collective-permute-start.13 = (bf16[256,1536]{1,0:T(8,128)(2,1)}, bf16[256,1536]{1,0:T(8,128)(2,1)S(1)}, u32[]{:S(2)}, u32[]{:S(2)}) collective-permute-start(bf16[256,1536]{1,0:T(8,128)(2,1)} %get-tuple-element.43), channel_id=1, source_target_pairs={{0,1},{1,0},{2,3},{3,2},{4,5},{5,4},{6,7},{7,6},{8,9},{9,8},{10,11... | collective-permute-start | bytes 2359304 | tf_op jit(solution)/shard_map/ppermute | solution.py:27
  62.9 5.8 %collective-permute-start.14 = (bf16[768,1536]{1,0:T(8,128)(2,1)}, bf16[768,1536]{1,0:T(8,128)(2,1)S(1)}, u32[]{:S(2)}, u32[]{:S(2)}) collective-permute-start(bf16[768,1536]{1,0:T(8,128)(2,1)} %get-tuple-element.45.mine_ref), channel_id=1, source_target_pairs={{0,1},{1,0},{2,3},{3,2},{4,5},{5,4},{6,7},{7,6},{8,9},{9,8},{10,11... | collective-permute-start | bytes 7077896 | tf_op jit(solution)/shard_map/ppermute | solution.py:27
  67.5 8.0 %collective-permute-start.17 = (bf16[256,1536]{1,0:T(8,128)(2,1)}, bf16[256,1536]{1,0:T(8,128)(2,1)S(1)}, u32[]{:S(2)}, u32[]{:S(2)}) collective-permute-start(bf16[256,1536]{1,0:T(8,128)(2,1)} %attention.1.grad_ref.refs_4_), channel_id=1, source_target_pairs={{0,1},{1,0},{2,3},{3,2},{4,5},{5,4},{6,7},{7,6},{8,9},{9,8},{10,11... | collective-permute-start | bytes 2359304 | tf_op jit(solution)/shard_map/ppermute | solution.py:27
  73.7 24.0 %collective-permute-start.15 = (bf16[128,3072]{1,0:T(8,128)(2,1)S(1)}, bf16[128,3072]{1,0:T(8,128)(2,1)S(1)}, u32[]{:S(2)}, u32[]{:S(2)}) collective-permute-start(bf16[128,3072]{1,0:T(8,128)(2,1)S(1)} %get-tuple-element.47), channel_id=1, source_target_pairs={{0,4},{4,0},{1,5},{5,1},{2,6},{6,2},{3,7},{7,3},{8,12},{12,8},{9,1... | collective-permute-start | bytes 2359304 | tf_op jit(solution)/shard_map/ppermute | solution.py:27
  78.3 8.8 %collective-permute-start.18 = (bf16[96,1536]{1,0:T(8,128)(2,1)S(1)}, bf16[96,1536]{1,0:T(8,128)(2,1)S(1)}, u32[]{:S(2)}, u32[]{:S(2)}) collective-permute-start(bf16[96,1536]{1,0:T(8,128)(2,1)S(1)} %get-tuple-element.50), channel_id=1, source_target_pairs={{0,2},{2,0},{1,3},{3,1},{4,6},{6,4},{5,7},{7,5},{8,10},{10,8},{9,1... | collective-permute-start | bytes 884744 | tf_op jit(solution)/shard_map/ppermute | solution.py:27
  87.2 7.9 %collective-permute-start.20 = (bf16[96,1536]{1,0:T(8,128)(2,1)S(1)}, bf16[96,1536]{1,0:T(8,128)(2,1)S(1)}, u32[]{:S(2)}, u32[]{:S(2)}) collective-permute-start(bf16[96,1536]{1,0:T(8,128)(2,1)S(1)} %get-tuple-element.54), channel_id=1, source_target_pairs={{0,2},{2,0},{1,3},{3,1},{4,6},{6,4},{5,7},{7,5},{8,10},{10,8},{9,1... | collective-permute-start | bytes 884744 | tf_op jit(solution)/shard_map/ppermute | solution.py:27
  88.9 15.7 %collective-permute-start.19 = (bf16[96,1536]{1,0:T(8,128)(2,1)S(1)}, bf16[96,1536]{1,0:T(8,128)(2,1)S(1)}, u32[]{:S(2)}, u32[]{:S(2)}) collective-permute-start(bf16[96,1536]{1,0:T(8,128)(2,1)S(1)} %add_convert_fusion.4), channel_id=1, source_target_pairs={{0,8},{8,0},{1,9},{9,1},{2,10},{10,2},{3,11},{11,3},{4,12},{12,4},... | collective-permute-start | bytes 884744 | tf_op jit(solution)/shard_map/ppermute | solution.py:27
  97.7 18.2 %collective-permute-start.22 = (bf16[96,1536]{1,0:T(8,128)(2,1)S(1)}, bf16[96,1536]{1,0:T(8,128)(2,1)S(1)}, u32[]{:S(2)}, u32[]{:S(2)}) collective-permute-start(bf16[96,1536]{1,0:T(8,128)(2,1)S(1)} %get-tuple-element.61), channel_id=1, source_target_pairs={{0,2},{2,0},{1,3},{3,1},{4,6},{6,4},{5,7},{7,5},{8,10},{10,8},{9,1... | collective-permute-start | bytes 884744 | tf_op jit(solution)/shard_map/ppermute | solution.py:27
  100.9 27.0 %collective-permute-start.16 = (bf16[128,3072]{1,0:T(8,128)(2,1)S(1)}, bf16[128,3072]{1,0:T(8,128)(2,1)}, u32[]{:S(2)}, u32[]{:S(2)}) collective-permute-start(bf16[128,3072]{1,0:T(8,128)(2,1)S(1)} %add_convert_fusion), channel_id=1, source_target_pairs={{0,1},{1,2},{2,3},{3,4},{4,5},{5,6},{6,7},{7,8},{8,9},{9,10},{10,1... | collective-permute-start | bytes 2359304 | tf_op jit(solution)/shard_map/ppermute | solution.py:18
  116.0 11.8 %collective-permute-start.24 = (bf16[96,1536]{1,0:T(8,128)(2,1)S(1)}, bf16[96,1536]{1,0:T(8,128)(2,1)S(1)}, u32[]{:S(2)}, u32[]{:S(2)}) collective-permute-start(bf16[96,1536]{1,0:T(8,128)(2,1)S(1)} %add_convert_fusion.2), channel_id=1, source_target_pairs={{0,4},{4,0},{1,5},{5,1},{2,6},{6,2},{3,7},{7,3},{8,12},{12,8},{9,1... | collective-permute-start | bytes 884744 | tf_op jit(solution)/shard_map/ppermute | solution.py:27
  116.2 16.0 %collective-permute-start.21 = (bf16[96,1536]{1,0:T(8,128)(2,1)S(1)}, bf16[96,1536]{1,0:T(8,128)(2,1)S(1)}, u32[]{:S(2)}, u32[]{:S(2)}) collective-permute-start(bf16[96,1536]{1,0:T(8,128)(2,1)S(1)} %add_convert_fusion.3), channel_id=1, source_target_pairs={{0,8},{8,0},{1,9},{9,1},{2,10},{10,2},{3,11},{11,3},{4,12},{12,4},... | collective-permute-start | bytes 884744 | tf_op jit(solution)/shard_map/ppermute | solution.py:27
  119.3 14.6 %collective-permute-start.23 = (bf16[96,1536]{1,0:T(8,128)(2,1)S(1)}, bf16[96,1536]{1,0:T(8,128)(2,1)S(1)}, u32[]{:S(2)}, u32[]{:S(2)}) collective-permute-start(bf16[96,1536]{1,0:T(8,128)(2,1)S(1)} %get-tuple-element.62), channel_id=1, source_target_pairs={{0,2},{2,0},{1,3},{3,1},{4,6},{6,4},{5,7},{7,5},{8,10},{10,8},{9,1... | collective-permute-start | bytes 884744 | tf_op jit(solution)/shard_map/ppermute | solution.py:27
  (15 other events, 58.3 us)

commit v6 on v5

--- a/solution.py
+++ b/solution.py
@@ -132,7 +132,7 @@
     for n in range(4):
         cols = pl.ds(n * part, part)
         product = jnp.dot(x_ref[n // 3], w_ref[:, cols], preferred_element_type=jnp.float32)
-        kept_ref[:, cols] = product[: 2 * tile]
+        kept_ref[:, cols] = product[: 2 * tile].astype(jnp.bfloat16)
         sent_ref[:, cols] = product[2 * tile :].astype(jnp.bfloat16)
     out_copy.wait()
 
@@ -157,7 +157,7 @@
     def view(w, p, n):
         return pl.ds(w * area, area), pl.ds(n * part + p * 2 * head, 2 * head)
 
-    qkv_ref[...] = (kept_ref[...] + came_ref[...].astype(jnp.float32)).astype(jnp.bfloat16)
+    qkv_ref[...] = (kept_ref[...].astype(jnp.float32) + came_ref[...].astype(jnp.float32)).astype(jnp.bfloat16)
     for g, w, p in groups:
         scores_ref[g] = across(stacked(qkv_ref[view(w, p, 0)]), qkv_ref[view(w, p, 1)])
         toward_ref[g] = across(stacked(qkv_ref[view(w, p, 3)]), qkv_ref[view(w, p, 2)])
@@ -320,7 +320,7 @@
     mine_side = swap(after(mine, (moved, moved_cot)), "side")
     across_far = after(across_far, mine_side)
     far_side, far_grp = swap(across_far, "side"), swap(across_far, "grp")
-    came_side = swap(after(came, far_side), "side")
+    came_side = swap(after(came, far_grp), "side")
     pieces = [
         (mine, 0, 0, near),
         (came, 0, 0, 1 - near),
@@ -348,7 +348,7 @@
     kept, sent, w_mine = kernel_call(
         products_kernel,
         (
-            jax.ShapeDtypeStruct((2 * tile, 4 * part), f32),
+            jax.ShapeDtypeStruct((2 * tile, 4 * part), bf16),
             jax.ShapeDtypeStruct((2 * tile, 4 * part), bf16),
             jax.ShapeDtypeStruct((half, 4 * part), bf16),
         ),
@@ -415,10 +415,9 @@
     side_far_1 = swap(block(1, 1, 1), "side")
     arrived_back = swap(attended_other, "near")
     side_far_0 = swap(after(block(1, 1, 0), side_far_1), "side")
-    side_far_0 = after(side_far_0, arrived_back)
     far_1 = swap((block(1, 0, 1).astype(f32) + side_far_1.astype(f32)).astype(bf16), "far")
-    far_0 = swap(after((block(1, 0, 0).astype(f32) + side_far_0.astype(f32)).astype(bf16), far_1), "far")
-    side_1 = swap(after(block(0, 1, 1), (side_far_0, arrived_back)), "side")
+    far_0 = swap(after((block(1, 0, 0).astype(f32) + side_far_0.astype(f32)).astype(bf16), (far_1, arrived_back)), "far")
+    side_1 = swap(after(block(0, 1, 1), side_far_0), "side")
     side_0 = swap(after(block(0, 1, 0), side_1), "side")
     total_1 = (block(0, 0, 1).astype(f32) + side_1.astype(f32) + far_1.astype(f32)).astype(bf16)
     theirs = swap(total_1, "near").astype(f32)

time: 136 us -> 129 us (0.949)
  the two profiles are of different devices: /device:TPU:0 before, /device:TPU:6 now
where the time goes in v6:
time: 129 us
  waiting for transfers between devices  62.3 us (48%)
  starting transfers between devices  26.8 us (21%)
  Pallas kernels  19.2 us (15%)
  local copies, waits for them, and re-layouts  7.6 us (6%)
  matrix products  6.87 us (5%)
  other arithmetic  5.29 us (4%)
    ppermute x22, waiting for transfers between devices, swap(): return lax.ppermute(shard, axis, [(0, 1), (1, 0)])  62.3 us
    ppermute x22, starting transfers between devices, swap(): return lax.ppermute(shard, axis, [(0, 1), (1, 0)])  26.1 us
    pallas_call x1, Pallas kernels, on_device(): kernel_call(products_kernel, (jax.ShapeDtypeStruct((2 * tile, 4 * part),...  6.07 us
    dot_general x1, matrix products, picked(): jnp.dot(onehot, both, preferred_element_type=jnp.float32)  4.22 us
    pallas_call x1, Pallas kernels, on_device(): kernel_call(functools.partial(attention_kernel, area, head), jax.ShapeDty...  4.13 us
    pallas_call x1, Pallas kernels, on_device(): kernel_call(outer_kernel, (jax.ShapeDtypeStruct((tile, 2 * width), f32),...  3.82 us
    unnamed x44, local copies, waits for them, and re-layouts  3.62 us
    pallas_call x1, Pallas kernels, on_device(): kernel_call(weights_kernel, [jax.ShapeDtypeStruct((own_rows, 4 * part), b...  2.75 us
  transfers between devices with their start and end apart: 25, of which 13 were waited for; matrix products, arithmetic and copies ran while one was open for 10% of the time, Pallas kernels for 10%

profile of v6, /device:TPU:6, one launch (start us, length us, event | category | flops | bytes accessed | tf_op | source)
XLA Modules:
  0.0 129.2 jit_solution(15530123487231889618)
XLA Ops:
  0.7 1.3 fusion.81
  2.0 1.6 %collective-permute-start.3 = (bf16[96,1536]{1,0:T(8,128)(2,1)S(1)}, bf16[96,1536]{1,0:T(8,128)(2,1)S(1)}, u32[]{:S(2)}, u32[]{:S(2)}) collective-permute-start(bf16[96,1536]{1,0:T(8,128)(2,1)S(1)} %broadcast_select_fusion), channel_id=1, source_target_pairs={{0,4},{4,0},{1,5},{5,1},{2,6},{6,2},{3,7},{7,3},{8,12},{12,8},{9,1... | collective-permute-start | bytes 884744 | tf_op jit(solution)/shard_map/ppermute | solution.py:27
  4.7 6.1 %collective-permute-done.3.refs_5_ = bf16[96,1536]{1,0:T(8,128)(2,1)S(1)} collective-permute-done((bf16[96,1536]{1,0:T(8,128)(2,1)S(1)}, bf16[96,1536]{1,0:T(8,128)(2,1)S(1)}, u32[]{:S(2)}, u32[]{:S(2)}) %collective-permute-start.3) | collective-permute-done | bytes 294944 | tf_op jit(solution)/shard_map/ppermute | solution.py:27
  10.9 0.8 broadcast_select_fusion.2
  11.7 2.6 %collective-permute-start.4 = (bf16[96,1536]{1,0:T(8,128)(2,1)}, bf16[96,1536]{1,0:T(8,128)(2,1)}, u32[]{:S(2)}, u32[]{:S(2)}) collective-permute-start(bf16[96,1536]{1,0:T(8,128)(2,1)} %get-tuple-element.69), channel_id=1, source_target_pairs={{0,8},{8,0},{1,9},{9,1},{2,10},{10,2},{3,11},{11,3},{4,12},{12,4},... | collective-permute-start | bytes 884744 | tf_op jit(solution)/shard_map/ppermute | solution.py:27
  14.3 7.8 %collective-permute-start.5 = (bf16[96,1536]{1,0:T(8,128)(2,1)S(1)}, bf16[96,1536]{1,0:T(8,128)(2,1)S(1)}, u32[]{:S(2)}, u32[]{:S(2)}) collective-permute-start(bf16[96,1536]{1,0:T(8,128)(2,1)S(1)} %get-tuple-element.36.refs_4_), channel_id=1, source_target_pairs={{0,2},{2,0},{1,3},{3,1},{4,6},{6,4},{5,7},{7,5},{8,10},{10,8},{9,1... | collective-permute-start | bytes 884744 | tf_op jit(solution)/shard_map/ppermute | solution.py:27
  22.3 2.4 %turned_rolls.1 = (bf16[2,768,128]{2,1,0:T(8,128)(2,1)S(1)}, bf16[2,768,128]{2,1,0:T(8,128)(2,1)S(1)}) custom-call(s32[20]{0:T(128)S(1)} %concatenate.15.info_ref, f32[1,1536]{1,0:T(1,128)S(1)} %reshape.97.gain_ref, bf16[128,1536]{1,0:T(8,128)(2,1)S(1)} %bitcast.49, bf16[128,1536]{1,0:T(8,128)(2,1)S(1)} %collective-permute-done.refs_1_, ...), custom_call_target="tpu_custom_call" | custom-call | flops 201326592 | bytes 3000000 | tf_op jit(solution)/shard_map/turned_rolls/pallas_call | solution.py:305
  24.8 2.3 %collective-permute-done.4.refs_8_ = bf16[96,1536]{1,0:T(8,128)(2,1)} collective-permute-done((bf16[96,1536]{1,0:T(8,128)(2,1)}, bf16[96,1536]{1,0:T(8,128)(2,1)}, u32[]{:S(2)}, u32[]{:S(2)}) %collective-permute-start.4) | collective-permute-done | bytes 294944 | tf_op jit(solution)/shard_map/ppermute | solution.py:27
  27.2 2.7 %collective-permute-done.5.refs_6_ = bf16[96,1536]{1,0:T(8,128)(2,1)S(1)} collective-permute-done((bf16[96,1536]{1,0:T(8,128)(2,1)S(1)}, bf16[96,1536]{1,0:T(8,128)(2,1)S(1)}, u32[]{:S(2)}, u32[]{:S(2)}) %collective-permute-start.5) | collective-permute-done | bytes 294944 | tf_op jit(solution)/shard_map/ppermute | solution.py:27
  31.0 3.2 %collective-permute-start.8 = (bf16[2,768,128]{2,1,0:T(8,128)(2,1)S(1)}, bf16[2,768,128]{2,1,0:T(8,128)(2,1)S(1)}, u32[]{:S(2)}, u32[]{:S(2)}) collective-permute-start(bf16[2,768,128]{2,1,0:T(8,128)(2,1)S(1)} %get-tuple-element.34.refs_0_), channel_id=1, source_target_pairs={{0,4},{4,0},{1,5},{5,1},{2,6},{6,2},{3,7},{7,3},{8,12},{12,8},{9,1... | collective-permute-start | bytes 1179656 | tf_op jit(solution)/shard_map/ppermute | solution.py:27
  34.2 2.3 %collective-permute-done.2 = bf16[2,768,128]{2,1,0:T(8,128)(2,1)} collective-permute-done((bf16[2,768,128]{2,1,0:T(8,128)(2,1)S(1)}, bf16[2,768,128]{2,1,0:T(8,128)(2,1)}, u32[]{:S(2)}, u32[]{:S(2)}) %collective-permute-start.2) | collective-permute-done | bytes 393248 | tf_op jit(solution)/shard_map/ppermute | solution.py:27
  36.4 2.8 %collective-permute-done.6.refs_9_ = bf16[96,1536]{1,0:T(8,128)(2,1)} collective-permute-done((bf16[96,1536]{1,0:T(8,128)(2,1)}, bf16[96,1536]{1,0:T(8,128)(2,1)}, u32[]{:S(2)}, u32[]{:S(2)}) %collective-permute-start.6) | collective-permute-done | bytes 294944 | tf_op jit(solution)/shard_map/ppermute | solution.py:27
  40.0 1.2 collective-permute-start.12
  41.2 2.6 %fusion.7 = f32[2,6,64,64]{3,1,2,0:T(8,128)S(1)} fusion(s32[64,64]{1,0:T(8,128)S(1)} %copy-done.21, pred[2,64,64]{2,1,0:T(8,128)(4,1)S(1)} %broadcast_compare_fusion, f32[2,225,6]{1,0,2:T(2,128)S(1)} %constant_dynamic-slice_fusion), kind=kOutput, calls=%fused_computation.9 | convolution fusion | flops 133681152 | bytes 231984 | tf_op jit(solution)/shard_map/qkr,lrh->lhqk/dot_general | solution.py:340
  45.4 3.6 %collective-permute-done.10.refs_7_ = bf16[96,1536]{1,0:T(8,128)(2,1)} collective-permute-done((bf16[96,1536]{1,0:T(8,128)(2,1)S(1)}, bf16[96,1536]{1,0:T(8,128)(2,1)}, u32[]{:S(2)}, u32[]{:S(2)}) %collective-permute-start.10) | collective-permute-done | bytes 294944 | tf_op jit(solution)/shard_map/ppermute | solution.py:27
  50.8 6.1 %products.1 = (bf16[256,1536]{1,0:T(8,128)(2,1)}, bf16[256,1536]{1,0:T(8,128)(2,1)}, bf16[768,1536]{1,0:T(8,128)(2,1)}) custom-call(s32[8]{0:T(128)} %stack.120.place_ref, bf16[2,768,128]{2,1,0:T(8,128)(2,1)} %copy-done.4, bf16[2,768,128]{2,1,0:T(8,128)(2,1)} %copy-done.10, bf16[2,768,128]{2,1,0:T(8,128)(2,1)} %copy-done.6, bf16[2,768,128]{2,1,0:T(8,128)(2,1)} %copy-done.8, ...), custom_call_target="tpu_custom_call" | custom-call | flops 1200000000 | bytes 9000000 | tf_op jit(solution)/shard_map/products/pallas_call | solution.py:348
  57.0 2.5 %collective-permute-done.13.came_ref = bf16[256,1536]{1,0:T(8,128)(2,1)S(1)} collective-permute-done((bf16[256,1536]{1,0:T(8,128)(2,1)}, bf16[256,1536]{1,0:T(8,128)(2,1)S(1)}, u32[]{:S(2)}, u32[]{:S(2)}) %collective-permute-start.13) | collective-permute-done | bytes 786464 | tf_op jit(solution)/shard_map/ppermute | solution.py:27
  59.5 0.9 copy-done.19
  60.6 4.1 %attention.1.grad_ref.refs_4_ = bf16[256,1536]{1,0:T(8,128)(2,1)} custom-call(bf16[256,1536]{1,0:T(8,128)(2,1)} %get-tuple-element.41.kept_ref, bf16[256,1536]{1,0:T(8,128)(2,1)} %copy-done.19, f32[2,3,128,64]{3,2,1,0:T(8,128)} %bitcast.52), custom_call_target="tpu_custom_call" | custom-call | flops 1000000000 | bytes 4000000 | tf_op jit(solution)/shard_map/attention/pallas_call | solution.py:369
  66.0 1.1 copy-done.3
  67.1 3.8 %projections.1 = (f32[128,3072]{1,0:T(8,128)S(1)}, bf16[128,3072]{1,0:T(8,128)(2,1)S(1)}) custom-call(s32[16]{0:T(128)S(1)} %stack.111.place_ref, bf16[256,1536]{1,0:T(8,128)(2,1)S(1)} %copy-done.3, bf16[768,1536]{1,0:T(8,128)(2,1)S(1)} %copy-done.1, bf16[768,1536]{1,0:T(8,128)(2,1)S(1)} %collective-permute-done.14.theirs_ref), custom_call_target="tpu_custom_call" | custom-call | flops 1200000000 | bytes 8000000 | tf_op jit(solution)/shard_map/projections/pallas_call | solution.py:382
  71.0 2.8 %collective-permute-start.15 = (bf16[128,3072]{1,0:T(8,128)(2,1)S(1)}, bf16[128,3072]{1,0:T(8,128)(2,1)S(1)}, u32[]{:S(2)}, u32[]{:S(2)}) collective-permute-start(bf16[128,3072]{1,0:T(8,128)(2,1)S(1)} %get-tuple-element.46), channel_id=1, source_target_pairs={{0,4},{4,0},{1,5},{5,1},{2,6},{6,2},{3,7},{7,3},{8,12},{12,8},{9,1... | collective-permute-start | bytes 2359304 | tf_op jit(solution)/shard_map/ppermute | solution.py:27
  73.8 2.7 %weight_gradient.1 = (bf16[96,1536]{1,0:T(8,128)(2,1)S(1)}, bf16[96,1536]{1,0:T(8,128)(2,1)S(1)}, bf16[96,1536]{1,0:T(8,128)(2,1)S(1)}, bf16[96,1536]{1,0:T(8,12...) custom-call(s32[1]{0:T(128)} %bitcast.34.near_ref, ...), custom_call_target="tpu_custom_call" | custom-call | flops 1200000000 | bytes 6000000 | tf_op jit(solution)/shard_map/weight_gradient/pallas_call | solution.py:396
  77.0 8.4 %collective-permute-done.18 = bf16[96,1536]{1,0:T(8,128)(2,1)S(1)} collective-permute-done((bf16[96,1536]{1,0:T(8,128)(2,1)S(1)}, bf16[96,1536]{1,0:T(8,128)(2,1)S(1)}, u32[]{:S(2)}, u32[]{:S(2)}) %collective-permute-start.18) | collective-permute-done | bytes 294944 | tf_op jit(solution)/shard_map/ppermute | solution.py:27
  85.9 3.4 %collective-permute-start.19 = (bf16[96,1536]{1,0:T(8,128)(2,1)S(1)}, bf16[96,1536]{1,0:T(8,128)(2,1)S(1)}, u32[]{:S(2)}, u32[]{:S(2)}) collective-permute-start(bf16[96,1536]{1,0:T(8,128)(2,1)S(1)} %add_convert_fusion.4), channel_id=1, source_target_pairs={{0,8},{8,0},{1,9},{9,1},{2,10},{10,2},{3,11},{11,3},{4,12},{12,4},... | collective-permute-start | bytes 884744 | tf_op jit(solution)/shard_map/ppermute | solution.py:27
  89.3 4.0 %collective-permute-done.20 = bf16[96,1536]{1,0:T(8,128)(2,1)S(1)} collective-permute-done((bf16[96,1536]{1,0:T(8,128)(2,1)S(1)}, bf16[96,1536]{1,0:T(8,128)(2,1)S(1)}, u32[]{:S(2)}, u32[]{:S(2)}) %collective-permute-start.20) | collective-permute-done | bytes 294944 | tf_op jit(solution)/shard_map/ppermute | solution.py:27
  93.7 3.6 %collective-permute-done.15 = bf16[128,3072]{1,0:T(8,128)(2,1)S(1)} collective-permute-done((bf16[128,3072]{1,0:T(8,128)(2,1)S(1)}, bf16[128,3072]{1,0:T(8,128)(2,1)S(1)}, u32[]{:S(2)}, u32[]{:S(2)}) %collective-permute-start.15) | collective-permute-done | bytes 786464 | tf_op jit(solution)/shard_map/ppermute | solution.py:27
  97.5 13.0 %collective-permute-done.19 = bf16[96,1536]{1,0:T(8,128)(2,1)S(1)} collective-permute-done((bf16[96,1536]{1,0:T(8,128)(2,1)S(1)}, bf16[96,1536]{1,0:T(8,128)(2,1)S(1)}, u32[]{:S(2)}, u32[]{:S(2)}) %collective-permute-start.19) | collective-permute-done | bytes 294944 | tf_op jit(solution)/shard_map/ppermute | solution.py:27
  111.2 10.5 %collective-permute-done.24 = bf16[96,1536]{1,0:T(8,128)(2,1)S(1)} collective-permute-done((bf16[96,1536]{1,0:T(8,128)(2,1)S(1)}, bf16[96,1536]{1,0:T(8,128)(2,1)S(1)}, u32[]{:S(2)}, u32[]{:S(2)}) %collective-permute-start.24) | collective-permute-done | bytes 294944 | tf_op jit(solution)/shard_map/ppermute | solution.py:27
  121.7 4.2 %convolution_convert_fusion = bf16[128,3072]{1,0:T(8,128)(2,1)S(1)} fusion(bf16[128,3072]{1,0:T(8,128)(2,1)S(1)} %add_convert_fusion, bf16[128,3072]{1,0:T(8,128)(2,1)} %collective-permute-done.16, s32[]{:T(128)} %bitcast.4, s32[]{:T(128)} %bitcast.3, s32[128]{0:T(128)S(1)} %get-tuple-element.93, s32[128]{0:T(128)S(1)} %get-tuple-element.95, s32[]{:T(128)} %bitcast.2, ...), kind=kOutput, calls=%fused_computation.3 | convolution fusion | flops 206700544 | bytes 2362768 | tf_op jit(solution)/shard_map/dot_general | solution.py:52
  126.3 1.4 %fusion.18 = (bf16[128,1536]{1,0:T(8,128)(2,1)}, bf16[128,1536]{1,0:T(8,128)(2,1)}) fusion(f32[128]{0:T(128)S(1)} %broadcast_multiply_fusion.2, f32[128]{0:T(128)S(1)} %div.55, f32[128]{0:T(128)S(1)} %broadcast_multiply_fusion.3, f32[1536]{0:T(1024)S(1)} %copy-done.15, f32[128]{0:T(128)S(1)} %rsqrt.12, bf16[128,3072]{1,0:T(8,128)(2,1)S(1)} %convolution_convert_fusion, ...), kind=kLoop, calls=%fused_computation.22 | loop fusion | flops 2949120 | bytes 2367488 | tf_op jit(solution)/shard_map/convert_element_type | solution.py:435
  128.0 1.1 broadcast_multiply_fusion
  (118 shorter events, 10.7 us)
Async XLA Ops:
  0.6 40.6 %copy-start = (f32[2,225,12]{1,0,2:T(2,128)S(1)}, f32[2,225,12]{1,0,2:T(2,128)}, u32[]{:S(2)}) copy-start(f32[2,225,12]{1,0,2:T(2,128)} %param.16) | copy-start | bytes 64804
  2.0 8.8 %collective-permute-start.3 = (bf16[96,1536]{1,0:T(8,128)(2,1)S(1)}, bf16[96,1536]{1,0:T(8,128)(2,1)S(1)}, u32[]{:S(2)}, u32[]{:S(2)}) collective-permute-start(bf16[96,1536]{1,0:T(8,128)(2,1)S(1)} %broadcast_select_fusion), channel_id=1, source_target_pairs={{0,4},{4,0},{1,5},{5,1},{2,6},{6,2},{3,7},{7,3},{8,12},{12,8},{9,1... | collective-permute-start | bytes 884744 | tf_op jit(solution)/shard_map/ppermute | solution.py:27
  3.9 18.3 %copy-start.18 = (s32[2,2]{1,0:T(2,128)S(1)}, s32[2,2]{1,0:T(2,128)}, u32[]{:S(2)}) copy-start(s32[2,2]{1,0:T(2,128)} %param.14) | copy-start | bytes 52
  3.9 18.4 %copy-start.15 = (f32[1536]{0:T(1024)S(1)}, f32[1536]{0:T(1024)}, u32[]{:S(2)}) copy-start(f32[1536]{0:T(1024)} %param.12) | copy-start | bytes 18436
  4.1 10.2 %collective-permute-start = (bf16[128,1536]{1,0:T(8,128)(2,1)S(1)}, bf16[128,1536]{1,0:T(8,128)(2,1)S(1)}, u32[]{:S(2)}, u32[]{:S(2)}) collective-permute-start(bf16[128,1536]{1,0:T(8,128)(2,1)S(1)} %bitcast.48), channel_id=1, source_target_pairs={{0,15},{1,0},{2,1},{3,2},{4,3},{5,4},{6,5},{7,6},{8,7},{9,8},{10,9... | collective-permute-start | bytes 1179656 | tf_op jit(solution)/shard_map/ppermute | solution.py:18
  4.1 10.2 %collective-permute-start.1 = (bf16[128,1536]{1,0:T(8,128)(2,1)S(1)}, bf16[128,1536]{1,0:T(8,128)(2,1)S(1)}, u32[]{:S(2)}, u32[]{:S(2)}) collective-permute-start(bf16[128,1536]{1,0:T(8,128)(2,1)S(1)} %bitcast.50), channel_id=1, source_target_pairs={{0,15},{1,0},{2,1},{3,2},{4,3},{5,4},{6,5},{7,6},{8,7},{9,8},{10,9... | collective-permute-start | bytes 1179656 | tf_op jit(solution)/shard_map/ppermute | solution.py:18
  10.9 29.0 %copy-start.13 = (bf16[96,1536]{1,0:T(8,128)(2,1)}, bf16[96,1536]{1,0:T(8,128)(2,1)S(1)}, u32[]{:S(2)}) copy-start(bf16[96,1536]{1,0:T(8,128)(2,1)S(1)} %collective-permute-done.3.refs_5_) | copy-start | bytes 884740
  11.7 32.2 %copy-start.14 = (bf16[96,1536]{1,0:T(8,128)(2,1)}, bf16[96,1536]{1,0:T(8,128)(2,1)S(1)}, u32[]{:S(2)}) copy-start(bf16[96,1536]{1,0:T(8,128)(2,1)S(1)} %get-tuple-element.36.refs_4_) | copy-start | bytes 884740
  11.7 29.5 %copy-start.21 = (s32[64,64]{1,0:T(8,128)S(1)}, s32[64,64]{1,0:T(8,128)}, u32[]{:S(2)}) copy-start(s32[64,64]{1,0:T(8,128)} %param.15) | copy-start | bytes 49156
  11.7 15.5 %collective-permute-start.4 = (bf16[96,1536]{1,0:T(8,128)(2,1)}, bf16[96,1536]{1,0:T(8,128)(2,1)}, u32[]{:S(2)}, u32[]{:S(2)}) collective-permute-start(bf16[96,1536]{1,0:T(8,128)(2,1)} %get-tuple-element.69), channel_id=1, source_target_pairs={{0,8},{8,0},{1,9},{9,1},{2,10},{10,2},{3,11},{11,3},{4,12},{12,4},... | collective-permute-start | bytes 884744 | tf_op jit(solution)/shard_map/ppermute | solution.py:27
  14.3 15.6 %collective-permute-start.5 = (bf16[96,1536]{1,0:T(8,128)(2,1)S(1)}, bf16[96,1536]{1,0:T(8,128)(2,1)S(1)}, u32[]{:S(2)}, u32[]{:S(2)}) collective-permute-start(bf16[96,1536]{1,0:T(8,128)(2,1)S(1)} %get-tuple-element.36.refs_4_), channel_id=1, source_target_pairs={{0,2},{2,0},{1,3},{3,1},{4,6},{6,4},{5,7},{7,5},{8,10},{10,8},{9,1... | collective-permute-start | bytes 884744 | tf_op jit(solution)/shard_map/ppermute | solution.py:27
  24.7 20.0 %copy-start.4 = (bf16[2,768,128]{2,1,0:T(8,128)(2,1)}, bf16[2,768,128]{2,1,0:T(8,128)(2,1)S(1)}, u32[]{:S(2)}) copy-start(bf16[2,768,128]{2,1,0:T(8,128)(2,1)S(1)} %get-tuple-element.34.refs_0_) | copy-start | bytes 1179652
  24.8 11.7 %collective-permute-start.2 = (bf16[2,768,128]{2,1,0:T(8,128)(2,1)S(1)}, bf16[2,768,128]{2,1,0:T(8,128)(2,1)}, u32[]{:S(2)}, u32[]{:S(2)}) collective-permute-start(bf16[2,768,128]{2,1,0:T(8,128)(2,1)S(1)} %get-tuple-element.38), channel_id=1, source_target_pairs={{0,4},{4,0},{1,5},{5,1},{2,6},{6,2},{3,7},{7,3},{8,12},{12,8},{9,1... | collective-permute-start | bytes 1179656 | tf_op jit(solution)/shard_map/ppermute | solution.py:27
  29.9 9.4 %collective-permute-start.6 = (bf16[96,1536]{1,0:T(8,128)(2,1)}, bf16[96,1536]{1,0:T(8,128)(2,1)}, u32[]{:S(2)}, u32[]{:S(2)}) collective-permute-start(bf16[96,1536]{1,0:T(8,128)(2,1)} %collective-permute-done.4.refs_8_), channel_id=1, source_target_pairs={{0,16},{16,0},{1,17},{17,1},{2,18},{18,2},{3,19},{19,3},{4,20},{20... | collective-permute-start | bytes 884744 | tf_op jit(solution)/shard_map/ppermute | solution.py:27
  30.2 9.7 %collective-permute-start.11 = (bf16[96,1536]{1,0:T(8,128)(2,1)}, bf16[96,1536]{1,0:T(8,128)(2,1)}, u32[]{:S(2)}, u32[]{:S(2)}) collective-permute-start(bf16[96,1536]{1,0:T(8,128)(2,1)} %collective-permute-done.4.refs_8_), channel_id=1, source_target_pairs={{0,2},{2,0},{1,3},{3,1},{4,6},{6,4},{5,7},{7,5},{8,10},{10,8},{9,1... | collective-permute-start | bytes 884744 | tf_op jit(solution)/shard_map/ppermute | solution.py:27
  31.0 14.4 %collective-permute-start.8 = (bf16[2,768,128]{2,1,0:T(8,128)(2,1)S(1)}, bf16[2,768,128]{2,1,0:T(8,128)(2,1)S(1)}, u32[]{:S(2)}, u32[]{:S(2)}) collective-permute-start(bf16[2,768,128]{2,1,0:T(8,128)(2,1)S(1)} %get-tuple-element.34.refs_0_), channel_id=1, source_target_pairs={{0,4},{4,0},{1,5},{5,1},{2,6},{6,2},{3,7},{7,3},{8,12},{12,8},{9,1... | collective-permute-start | bytes 1179656 | tf_op jit(solution)/shard_map/ppermute | solution.py:27
  39.3 10.0 %collective-permute-start.9 = (bf16[2,768,128]{2,1,0:T(8,128)(2,1)}, bf16[2,768,128]{2,1,0:T(8,128)(2,1)S(1)}, u32[]{:S(2)}, u32[]{:S(2)}) collective-permute-start(bf16[2,768,128]{2,1,0:T(8,128)(2,1)} %collective-permute-done.2), channel_id=1, source_target_pairs={{0,1},{1,0},{2,3},{3,2},{4,5},{5,4},{6,7},{7,6},{8,9},{9,8},{10,11... | collective-permute-start | bytes 1179656 | tf_op jit(solution)/shard_map/ppermute | solution.py:27
  39.3 10.0 %collective-permute-start.7 = (bf16[2,768,128]{2,1,0:T(8,128)(2,1)S(1)}, bf16[2,768,128]{2,1,0:T(8,128)(2,1)S(1)}, u32[]{:S(2)}, u32[]{:S(2)}) collective-permute-start(bf16[2,768,128]{2,1,0:T(8,128)(2,1)S(1)} %get-tuple-element.38), channel_id=1, source_target_pairs={{0,1},{1,0},{2,3},{3,2},{4,5},{5,4},{6,7},{7,6},{8,9},{9,8},{10,11... | collective-permute-start | bytes 1179656 | tf_op jit(solution)/shard_map/ppermute | solution.py:27
  39.9 9.1 %collective-permute-start.10 = (bf16[96,1536]{1,0:T(8,128)(2,1)S(1)}, bf16[96,1536]{1,0:T(8,128)(2,1)}, u32[]{:S(2)}, u32[]{:S(2)}) collective-permute-start(bf16[96,1536]{1,0:T(8,128)(2,1)S(1)} %collective-permute-done.3.refs_5_), channel_id=1, source_target_pairs={{0,2},{2,0},{1,3},{3,1},{4,6},{6,4},{5,7},{7,5},{8,10},{10,8},{9,1... | collective-permute-start | bytes 884744 | tf_op jit(solution)/shard_map/ppermute | solution.py:27
  40.0 9.3 %collective-permute-start.12 = (bf16[96,1536]{1,0:T(8,128)(2,1)}, bf16[96,1536]{1,0:T(8,128)(2,1)}, u32[]{:S(2)}, u32[]{:S(2)}) collective-permute-start(bf16[96,1536]{1,0:T(8,128)(2,1)} %collective-permute-done.11.refs_10_), channel_id=1, source_target_pairs={{0,16},{16,0},{1,17},{17,1},{2,18},{18,2},{3,19},{19,3},{4,20},{20... | collective-permute-start | bytes 884744 | tf_op jit(solution)/shard_map/ppermute | solution.py:27
  56.9 2.6 %collective-permute-start.13 = (bf16[256,1536]{1,0:T(8,128)(2,1)}, bf16[256,1536]{1,0:T(8,128)(2,1)S(1)}, u32[]{:S(2)}, u32[]{:S(2)}) collective-permute-start(bf16[256,1536]{1,0:T(8,128)(2,1)} %get-tuple-element.42), channel_id=1, source_target_pairs={{0,1},{1,0},{2,3},{3,2},{4,5},{5,4},{6,7},{7,6},{8,9},{9,8},{10,11... | collective-permute-start | bytes 2359304 | tf_op jit(solution)/shard_map/ppermute | solution.py:27
  60.4 5.6 %collective-permute-start.14 = (bf16[768,1536]{1,0:T(8,128)(2,1)}, bf16[768,1536]{1,0:T(8,128)(2,1)S(1)}, u32[]{:S(2)}, u32[]{:S(2)}) collective-permute-start(bf16[768,1536]{1,0:T(8,128)(2,1)} %get-tuple-element.44.mine_ref), channel_id=1, source_target_pairs={{0,1},{1,0},{2,3},{3,2},{4,5},{5,4},{6,7},{7,6},{8,9},{9,8},{10,11... | collective-permute-start | bytes 7077896 | tf_op jit(solution)/shard_map/ppermute | solution.py:27
  64.7 9.1 %collective-permute-start.17 = (bf16[256,1536]{1,0:T(8,128)(2,1)}, bf16[256,1536]{1,0:T(8,128)(2,1)S(1)}, u32[]{:S(2)}, u32[]{:S(2)}) collective-permute-start(bf16[256,1536]{1,0:T(8,128)(2,1)} %attention.1.grad_ref.refs_4_), channel_id=1, source_target_pairs={{0,1},{1,0},{2,3},{3,2},{4,5},{5,4},{6,7},{7,6},{8,9},{9,8},{10,11... | collective-permute-start | bytes 2359304 | tf_op jit(solution)/shard_map/ppermute | solution.py:27
  71.0 26.3 %collective-permute-start.15 = (bf16[128,3072]{1,0:T(8,128)(2,1)S(1)}, bf16[128,3072]{1,0:T(8,128)(2,1)S(1)}, u32[]{:S(2)}, u32[]{:S(2)}) collective-permute-start(bf16[128,3072]{1,0:T(8,128)(2,1)S(1)} %get-tuple-element.46), channel_id=1, source_target_pairs={{0,4},{4,0},{1,5},{5,1},{2,6},{6,2},{3,7},{7,3},{8,12},{12,8},{9,1... | collective-permute-start | bytes 2359304 | tf_op jit(solution)/shard_map/ppermute | solution.py:27
  76.6 8.8 %collective-permute-start.18 = (bf16[96,1536]{1,0:T(8,128)(2,1)S(1)}, bf16[96,1536]{1,0:T(8,128)(2,1)S(1)}, u32[]{:S(2)}, u32[]{:S(2)}) collective-permute-start(bf16[96,1536]{1,0:T(8,128)(2,1)S(1)} %get-tuple-element.49), channel_id=1, source_target_pairs={{0,2},{2,0},{1,3},{3,1},{4,6},{6,4},{5,7},{7,5},{8,10},{10,8},{9,1... | collective-permute-start | bytes 884744 | tf_op jit(solution)/shard_map/ppermute | solution.py:27
  85.4 7.9 %collective-permute-start.20 = (bf16[96,1536]{1,0:T(8,128)(2,1)S(1)}, bf16[96,1536]{1,0:T(8,128)(2,1)S(1)}, u32[]{:S(2)}, u32[]{:S(2)}) collective-permute-start(bf16[96,1536]{1,0:T(8,128)(2,1)S(1)} %get-tuple-element.53), channel_id=1, source_target_pairs={{0,2},{2,0},{1,3},{3,1},{4,6},{6,4},{5,7},{7,5},{8,10},{10,8},{9,1... | collective-permute-start | bytes 884744 | tf_op jit(solution)/shard_map/ppermute | solution.py:27
  85.9 24.7 %collective-permute-start.19 = (bf16[96,1536]{1,0:T(8,128)(2,1)S(1)}, bf16[96,1536]{1,0:T(8,128)(2,1)S(1)}, u32[]{:S(2)}, u32[]{:S(2)}) collective-permute-start(bf16[96,1536]{1,0:T(8,128)(2,1)S(1)} %add_convert_fusion.4), channel_id=1, source_target_pairs={{0,8},{8,0},{1,9},{9,1},{2,10},{10,2},{3,11},{11,3},{4,12},{12,4},... | collective-permute-start | bytes 884744 | tf_op jit(solution)/shard_map/ppermute | solution.py:27
  93.3 17.2 %collective-permute-start.22 = (bf16[96,1536]{1,0:T(8,128)(2,1)S(1)}, bf16[96,1536]{1,0:T(8,128)(2,1)S(1)}, u32[]{:S(2)}, u32[]{:S(2)}) collective-permute-start(bf16[96,1536]{1,0:T(8,128)(2,1)S(1)} %get-tuple-element.59), channel_id=1, source_target_pairs={{0,2},{2,0},{1,3},{3,1},{4,6},{6,4},{5,7},{7,5},{8,10},{10,8},{9,1... | collective-permute-start | bytes 884744 | tf_op jit(solution)/shard_map/ppermute | solution.py:27
  97.4 24.3 %collective-permute-start.16 = (bf16[128,3072]{1,0:T(8,128)(2,1)S(1)}, bf16[128,3072]{1,0:T(8,128)(2,1)}, u32[]{:S(2)}, u32[]{:S(2)}) collective-permute-start(bf16[128,3072]{1,0:T(8,128)(2,1)S(1)} %add_convert_fusion), channel_id=1, source_target_pairs={{0,1},{1,2},{2,3},{3,4},{4,5},{5,6},{6,7},{7,8},{8,9},{9,10},{10,1... | collective-permute-start | bytes 2359304 | tf_op jit(solution)/shard_map/ppermute | solution.py:18
  110.7 11.0 %collective-permute-start.24 = (bf16[96,1536]{1,0:T(8,128)(2,1)S(1)}, bf16[96,1536]{1,0:T(8,128)(2,1)S(1)}, u32[]{:S(2)}, u32[]{:S(2)}) collective-permute-start(bf16[96,1536]{1,0:T(8,128)(2,1)S(1)} %add_convert_fusion.2), channel_id=1, source_target_pairs={{0,4},{4,0},{1,5},{5,1},{2,6},{6,2},{3,7},{7,3},{8,12},{12,8},{9,1... | collective-permute-start | bytes 884744 | tf_op jit(solution)/shard_map/ppermute | solution.py:27
  110.8 15.2 %collective-permute-start.21 = (bf16[96,1536]{1,0:T(8,128)(2,1)S(1)}, bf16[96,1536]{1,0:T(8,128)(2,1)S(1)}, u32[]{:S(2)}, u32[]{:S(2)}) collective-permute-start(bf16[96,1536]{1,0:T(8,128)(2,1)S(1)} %add_convert_fusion.3), channel_id=1, source_target_pairs={{0,8},{8,0},{1,9},{9,1},{2,10},{10,2},{3,11},{11,3},{4,12},{12,4},... | collective-permute-start | bytes 884744 | tf_op jit(solution)/shard_map/ppermute | solution.py:27
  111.1 16.6 %collective-permute-start.23 = (bf16[96,1536]{1,0:T(8,128)(2,1)S(1)}, bf16[96,1536]{1,0:T(8,128)(2,1)S(1)}, u32[]{:S(2)}, u32[]{:S(2)}) collective-permute-start(bf16[96,1536]{1,0:T(8,128)(2,1)S(1)} %get-tuple-element.60), channel_id=1, source_target_pairs={{0,2},{2,0},{1,3},{3,1},{4,6},{6,4},{5,7},{7,5},{8,10},{10,8},{9,1... | collective-permute-start | bytes 884744 | tf_op jit(solution)/shard_map/ppermute | solution.py:27
  (15 other events, 51.9 us)

commit v7 on v6

--- a/solution.py
+++ b/solution.py
@@ -119,7 +119,7 @@
         copies.append(pltpu.make_async_copy(piece, w_ref.at[rows, :], sems.at[i]))
     for j, source in enumerate(tiles):
         copies.append(pltpu.make_async_copy(source, tile_ref.at[j], sems.at[8 + j]))
-    for copy in copies:
+    for copy in copies[8:] + copies[:8]:
         copy.start()
     for j, at in enumerate((0, 2, 1, 3)):
         copies[8 + j].wait()
@@ -379,20 +379,6 @@
     )(kept, crossed, bias)
     w_theirs = swap(after(w_mine, crossed), "core")
     grad_theirs = swap(grad, "core")
-    attended_own, attended_other = kernel_call(
-        outer_kernel,
-        (
-            jax.ShapeDtypeStruct((tile, 2 * width), f32),
-            jax.ShapeDtypeStruct((tile, 2 * width), bf16),
-        ),
-        [smem, vmem, anywhere, anywhere],
-        (vmem, vmem),
-        [pltpu.VMEM((width, 4 * part), bf16), dma((16,))],
-        1_200_000_000,
-        8_000_000,
-        "projections",
-        24,
-    )(jnp.stack(natural).astype(jnp.int32), grad, w_mine, w_theirs)
     blocks = kernel_call(
         weights_kernel,
         [jax.ShapeDtypeStruct((own_rows, 4 * part), bf16)] * 8,
@@ -407,12 +393,26 @@
         6_000_000,
         "weight_gradient",
         24,
-    )(after(near.astype(jnp.int32).reshape(1), attended_other), *tiles, grad, grad_theirs)
+    )(near.astype(jnp.int32).reshape(1), *tiles, grad, grad_theirs)
 
     def block(f, s, n):
         return blocks[((1 - f) * 2 + 1 - s) * 2 + 1 - n]
 
-    side_far_1 = swap(block(1, 1, 1), "side")
+    attended_own, attended_other = kernel_call(
+        outer_kernel,
+        (
+            jax.ShapeDtypeStruct((tile, 2 * width), f32),
+            jax.ShapeDtypeStruct((tile, 2 * width), bf16),
+        ),
+        [smem, vmem, anywhere, anywhere],
+        (vmem, vmem),
+        [pltpu.VMEM((width, 4 * part), bf16), dma((16,))],
+        1_200_000_000,
+        8_000_000,
+        "projections",
+        24,
+    )(after(jnp.stack(natural).astype(jnp.int32), blocks[0]), grad, w_mine, w_theirs)
+    side_far_1 = after(swap(block(1, 1, 1), "side"), attended_other)
     arrived_back = swap(attended_other, "near")
     side_far_0 = swap(after(block(1, 1, 0), side_far_1), "side")
     far_1 = swap((block(1, 0, 1).astype(f32) + side_far_1.astype(f32)).astype(bf16), "far")

time: 129 us -> 136 us (1.054); the launches traced: 129 us -> 134 us
  starting transfers between devices: 26.8 us -> 34.6 us
  waiting for transfers between devices: 62.3 us -> 60.9 us
    ppermute x22, starting transfers between devices: 26.1 us -> 33.9 us  [swap(): return lax.ppermute(shard, axis, [(0, 1), (1, 0)])]
    ppermute x22, waiting for transfers between devices: 62.3 us -> 60.9 us  [swap(): return lax.ppermute(shard, axis, [(0, 1), (1, 0)])]
    unnamed x44 -> x48, local copies, waits for them, and re-layouts: 3.62 us -> 3.63 us
  transfers between devices with their start and end apart: 25 -> 25, of which waited for: 13 -> 12; matrix products, arithmetic and copies ran while one was open for 10% -> 9% of each run, Pallas kernels for 10% -> 10%
where the time goes in v7:
time: 136 us; the launch traced here: 134 us
  waiting for transfers between devices  60.9 us (45%)
  starting transfers between devices  34.6 us (25%)
  Pallas kernels  18.8 us (14%)
  local copies, waits for them, and re-layouts  7.55 us (6%)
  matrix products  6.85 us (5%)
  other arithmetic  4.58 us (3%)
    ppermute x22, waiting for transfers between devices, swap(): return lax.ppermute(shard, axis, [(0, 1), (1, 0)])  60.9 us
    ppermute x22, starting transfers between devices, swap(): return lax.ppermute(shard, axis, [(0, 1), (1, 0)])  33.9 us
    pallas_call x1, Pallas kernels, on_device(): kernel_call(products_kernel, (jax.ShapeDtypeStruct((2 * tile, 4 * part),...  5.79 us
    dot_general x1, matrix products, picked(): jnp.dot(onehot, both, preferred_element_type=jnp.float32)  4.2 us
    pallas_call x1, Pallas kernels, on_device(): kernel_call(functools.partial(attention_kernel, area, head), jax.ShapeDty...  4.09 us
    pallas_call x1, Pallas kernels, on_device(): kernel_call(outer_kernel, (jax.ShapeDtypeStruct((tile, 2 * width), f32),...  3.83 us
    unnamed x48, local copies, waits for them, and re-layouts  3.63 us
    pallas_call x1, Pallas kernels, on_device(): kernel_call(weights_kernel, [jax.ShapeDtypeStruct((own_rows, 4 * part), b...  2.73 us
  transfers between devices with their start and end apart: 25, of which 12 were waited for; matrix products, arithmetic and copies ran while one was open for 9% of the time, Pallas kernels for 10%

profile of v7, /device:TPU:6, one launch (start us, length us, event | category | flops | bytes accessed | tf_op | source)
XLA Modules:
  0.0 134.5 jit_solution(17106312818462716040)
XLA Ops:
  0.7 1.3 fusion.81
  2.0 1.6 %collective-permute-start.3 = (bf16[96,1536]{1,0:T(8,128)(2,1)S(1)}, bf16[96,1536]{1,0:T(8,128)(2,1)S(1)}, u32[]{:S(2)}, u32[]{:S(2)}) collective-permute-start(bf16[96,1536]{1,0:T(8,128)(2,1)S(1)} %broadcast_select_fusion), channel_id=1, source_target_pairs={{0,4},{4,0},{1,5},{5,1},{2,6},{6,2},{3,7},{7,3},{8,12},{12,8},{9,1... | collective-permute-start | bytes 884744 | tf_op jit(solution)/shard_map/ppermute | solution.py:27
  4.7 6.2 %collective-permute-done.3.refs_5_ = bf16[96,1536]{1,0:T(8,128)(2,1)S(1)} collective-permute-done((bf16[96,1536]{1,0:T(8,128)(2,1)S(1)}, bf16[96,1536]{1,0:T(8,128)(2,1)S(1)}, u32[]{:S(2)}, u32[]{:S(2)}) %collective-permute-start.3) | collective-permute-done | bytes 294944 | tf_op jit(solution)/shard_map/ppermute | solution.py:27
  11.0 2.7 %collective-permute-start.4 = (bf16[96,1536]{1,0:T(8,128)(2,1)S(1)}, bf16[96,1536]{1,0:T(8,128)(2,1)}, u32[]{:S(2)}, u32[]{:S(2)}) collective-permute-start(bf16[96,1536]{1,0:T(8,128)(2,1)S(1)} %get-tuple-element.71), channel_id=1, source_target_pairs={{0,8},{8,0},{1,9},{9,1},{2,10},{10,2},{3,11},{11,3},{4,12},{12,4},... | collective-permute-start | bytes 884744 | tf_op jit(solution)/shard_map/ppermute | solution.py:27
  13.7 8.5 %collective-permute-start.5 = (bf16[96,1536]{1,0:T(8,128)(2,1)S(1)}, bf16[96,1536]{1,0:T(8,128)(2,1)}, u32[]{:S(2)}, u32[]{:S(2)}) collective-permute-start(bf16[96,1536]{1,0:T(8,128)(2,1)S(1)} %get-tuple-element.36.refs_4_), channel_id=1, source_target_pairs={{0,2},{2,0},{1,3},{3,1},{4,6},{6,4},{5,7},{7,5},{8,10},{10,8},{9,1... | collective-permute-start | bytes 884744 | tf_op jit(solution)/shard_map/ppermute | solution.py:27
  22.3 2.4 %turned_rolls.1 = (bf16[2,768,128]{2,1,0:T(8,128)(2,1)S(1)}, bf16[2,768,128]{2,1,0:T(8,128)(2,1)S(1)}) custom-call(s32[20]{0:T(128)S(1)} %concatenate.15.info_ref, f32[1,1536]{1,0:T(1,128)S(1)} %reshape.97.gain_ref, bf16[128,1536]{1,0:T(8,128)(2,1)S(1)} %bitcast.49, bf16[128,1536]{1,0:T(8,128)(2,1)S(1)} %collective-permute-done.refs_1_, ...), custom_call_target="tpu_custom_call" | custom-call | flops 201326592 | bytes 3000000 | tf_op jit(solution)/shard_map/turned_rolls/pallas_call | solution.py:305
  24.8 1.4 %collective-permute-done.4.refs_8_ = bf16[96,1536]{1,0:T(8,128)(2,1)} collective-permute-done((bf16[96,1536]{1,0:T(8,128)(2,1)S(1)}, bf16[96,1536]{1,0:T(8,128)(2,1)}, u32[]{:S(2)}, u32[]{:S(2)}) %collective-permute-start.4) | collective-permute-done | bytes 294944 | tf_op jit(solution)/shard_map/ppermute | solution.py:27
  26.3 2.9 %collective-permute-done.5.refs_6_ = bf16[96,1536]{1,0:T(8,128)(2,1)} collective-permute-done((bf16[96,1536]{1,0:T(8,128)(2,1)S(1)}, bf16[96,1536]{1,0:T(8,128)(2,1)}, u32[]{:S(2)}, u32[]{:S(2)}) %collective-permute-start.5) | collective-permute-done | bytes 294944 | tf_op jit(solution)/shard_map/ppermute | solution.py:27
  31.7 2.3 %collective-permute-start.8 = (bf16[2,768,128]{2,1,0:T(8,128)(2,1)S(1)}, bf16[2,768,128]{2,1,0:T(8,128)(2,1)S(1)}, u32[]{:S(2)}, u32[]{:S(2)}) collective-permute-start(bf16[2,768,128]{2,1,0:T(8,128)(2,1)S(1)} %get-tuple-element.34.refs_0_), channel_id=1, source_target_pairs={{0,4},{4,0},{1,5},{5,1},{2,6},{6,2},{3,7},{7,3},{8,12},{12,8},{9,1... | collective-permute-start | bytes 1179656 | tf_op jit(solution)/shard_map/ppermute | solution.py:27
  34.0 2.9 %collective-permute-done.2 = bf16[2,768,128]{2,1,0:T(8,128)(2,1)} collective-permute-done((bf16[2,768,128]{2,1,0:T(8,128)(2,1)S(1)}, bf16[2,768,128]{2,1,0:T(8,128)(2,1)}, u32[]{:S(2)}, u32[]{:S(2)}) %collective-permute-start.2) | collective-permute-done | bytes 393248 | tf_op jit(solution)/shard_map/ppermute | solution.py:27
  36.9 2.5 %collective-permute-done.6.refs_9_ = bf16[96,1536]{1,0:T(8,128)(2,1)} collective-permute-done((bf16[96,1536]{1,0:T(8,128)(2,1)}, bf16[96,1536]{1,0:T(8,128)(2,1)}, u32[]{:S(2)}, u32[]{:S(2)}) %collective-permute-start.6) | collective-permute-done | bytes 294944 | tf_op jit(solution)/shard_map/ppermute | solution.py:27
  41.4 2.6 %fusion.7 = f32[2,6,64,64]{3,1,2,0:T(8,128)S(1)} fusion(s32[64,64]{1,0:T(8,128)S(1)} %copy-done.23, pred[2,64,64]{2,1,0:T(8,128)(4,1)S(1)} %broadcast_compare_fusion, f32[2,225,6]{1,0,2:T(2,128)S(1)} %constant_dynamic-slice_fusion), kind=kOutput, calls=%fused_computation.9 | convolution fusion | flops 133681152 | bytes 231984 | tf_op jit(solution)/shard_map/qkr,lrh->lhqk/dot_general | solution.py:340
  45.5 4.1 %collective-permute-done.12.refs_11_ = bf16[96,1536]{1,0:T(8,128)(2,1)} collective-permute-done((bf16[96,1536]{1,0:T(8,128)(2,1)}, bf16[96,1536]{1,0:T(8,128)(2,1)}, u32[]{:S(2)}, u32[]{:S(2)}) %collective-permute-start.12) | collective-permute-done | bytes 294944 | tf_op jit(solution)/shard_map/ppermute | solution.py:27
  51.1 5.8 %products.1 = (bf16[256,1536]{1,0:T(8,128)(2,1)}, bf16[256,1536]{1,0:T(8,128)(2,1)}, bf16[768,1536]{1,0:T(8,128)(2,1)}) custom-call(s32[8]{0:T(128)} %stack.120.place_ref, bf16[2,768,128]{2,1,0:T(8,128)(2,1)} %copy-done.5, bf16[2,768,128]{2,1,0:T(8,128)(2,1)} %copy-done.9, bf16[2,768,128]{2,1,0:T(8,128)(2,1)} %copy-done.7, bf16[2,768,128]{2,1,0:T(8,128)(2,1)} %copy-done.11, ...), custom_call_target="tpu_custom_call" | custom-call | flops 1200000000 | bytes 9000000 | tf_op jit(solution)/shard_map/products/pallas_call | solution.py:348
  56.9 2.5 %collective-permute-done.13.came_ref = bf16[256,1536]{1,0:T(8,128)(2,1)S(1)} collective-permute-done((bf16[256,1536]{1,0:T(8,128)(2,1)}, bf16[256,1536]{1,0:T(8,128)(2,1)S(1)}, u32[]{:S(2)}, u32[]{:S(2)}) %collective-permute-start.13) | collective-permute-done | bytes 786464 | tf_op jit(solution)/shard_map/ppermute | solution.py:27
  60.6 4.1 %attention.1.refs_4_.grad_ref = bf16[256,1536]{1,0:T(8,128)(2,1)} custom-call(bf16[256,1536]{1,0:T(8,128)(2,1)} %get-tuple-element.42.kept_ref, bf16[256,1536]{1,0:T(8,128)(2,1)} %copy-done.22, f32[2,3,128,64]{3,2,1,0:T(8,128)} %bitcast.52), custom_call_target="tpu_custom_call" | custom-call | flops 1000000000 | bytes 4000000 | tf_op jit(solution)/shard_map/attention/pallas_call | solution.py:369
  65.9 1.3 collective-permute-done.14.refs_5_
  68.3 2.7 %weight_gradient.1 = (bf16[96,1536]{1,0:T(8,128)(2,1)S(1)}, bf16[96,1536]{1,0:T(8,128)(2,1)S(1)}, bf16[96,1536]{1,0:T(8,128)(2,1)S(1)}, bf16[96,1536]{1,0:T(8,12...) custom-call(s32[1]{0:T(128)} %bitcast.21.near_ref, ...), custom_call_target="tpu_custom_call" | custom-call | flops 1200000000 | bytes 6000000 | tf_op jit(solution)/shard_map/weight_gradient/pallas_call | solution.py:382
  71.1 1.7 %collective-permute-start.18 = (bf16[96,1536]{1,0:T(8,128)(2,1)S(1)}, bf16[96,1536]{1,0:T(8,128)(2,1)S(1)}, u32[]{:S(2)}, u32[]{:S(2)}) collective-permute-start(bf16[96,1536]{1,0:T(8,128)(2,1)S(1)} %get-tuple-element.44), channel_id=1, source_target_pairs={{0,2},{2,0},{1,3},{3,1},{4,6},{6,4},{5,7},{7,5},{8,10},{10,8},{9,1... | collective-permute-start | bytes 884744 | tf_op jit(solution)/shard_map/ppermute | solution.py:27
  72.8 3.8 %projections.1 = (f32[128,3072]{1,0:T(8,128)S(1)}, bf16[128,3072]{1,0:T(8,128)(2,1)S(1)}) custom-call(s32[16]{0:T(128)S(1)} %stack.111.place_ref, bf16[256,1536]{1,0:T(8,128)(2,1)S(1)} %copy-done.4, bf16[768,1536]{1,0:T(8,128)(2,1)S(1)} %copy-done.1, bf16[768,1536]{1,0:T(8,128)(2,1)S(1)} %collective-permute-done.15.theirs_ref), custom_call_target="tpu_custom_call" | custom-call | flops 1200000000 | bytes 8000000 | tf_op jit(solution)/shard_map/projections/pallas_call | solution.py:401
  77.9 2.5 %collective-permute-done.18 = bf16[96,1536]{1,0:T(8,128)(2,1)S(1)} collective-permute-done((bf16[96,1536]{1,0:T(8,128)(2,1)S(1)}, bf16[96,1536]{1,0:T(8,128)(2,1)S(1)}, u32[]{:S(2)}, u32[]{:S(2)}) %collective-permute-start.18) | collective-permute-done | bytes 294944 | tf_op jit(solution)/shard_map/ppermute | solution.py:27
  80.4 1.7 %collective-permute-start.20 = (bf16[96,1536]{1,0:T(8,128)(2,1)S(1)}, bf16[96,1536]{1,0:T(8,128)(2,1)S(1)}, u32[]{:S(2)}, u32[]{:S(2)}) collective-permute-start(bf16[96,1536]{1,0:T(8,128)(2,1)S(1)} %get-tuple-element.55), channel_id=1, source_target_pairs={{0,2},{2,0},{1,3},{3,1},{4,6},{6,4},{5,7},{7,5},{8,10},{10,8},{9,1... | collective-permute-start | bytes 884744 | tf_op jit(solution)/shard_map/ppermute | solution.py:27
  82.2 1.4 %collective-permute-start.19 = (bf16[96,1536]{1,0:T(8,128)(2,1)S(1)}, bf16[96,1536]{1,0:T(8,128)(2,1)S(1)}, u32[]{:S(2)}, u32[]{:S(2)}) collective-permute-start(bf16[96,1536]{1,0:T(8,128)(2,1)S(1)} %add_convert_fusion.4), channel_id=1, source_target_pairs={{0,8},{8,0},{1,9},{9,1},{2,10},{10,2},{3,11},{11,3},{4,12},{12,4},... | collective-permute-start | bytes 884744 | tf_op jit(solution)/shard_map/ppermute | solution.py:27
  83.6 5.3 %collective-permute-done.20 = bf16[96,1536]{1,0:T(8,128)(2,1)S(1)} collective-permute-done((bf16[96,1536]{1,0:T(8,128)(2,1)S(1)}, bf16[96,1536]{1,0:T(8,128)(2,1)S(1)}, u32[]{:S(2)}, u32[]{:S(2)}) %collective-permute-start.20) | collective-permute-done | bytes 294944 | tf_op jit(solution)/shard_map/ppermute | solution.py:27
  88.9 1.7 %collective-permute-start.22 = (bf16[96,1536]{1,0:T(8,128)(2,1)S(1)}, bf16[96,1536]{1,0:T(8,128)(2,1)S(1)}, u32[]{:S(2)}, u32[]{:S(2)}) collective-permute-start(bf16[96,1536]{1,0:T(8,128)(2,1)S(1)} %get-tuple-element.61), channel_id=1, source_target_pairs={{0,2},{2,0},{1,3},{3,1},{4,6},{6,4},{5,7},{7,5},{8,10},{10,8},{9,1... | collective-permute-start | bytes 884744 | tf_op jit(solution)/shard_map/ppermute | solution.py:27
  90.6 12.0 %collective-permute-done.16 = bf16[128,3072]{1,0:T(8,128)(2,1)S(1)} collective-permute-done((bf16[128,3072]{1,0:T(8,128)(2,1)S(1)}, bf16[128,3072]{1,0:T(8,128)(2,1)S(1)}, u32[]{:S(2)}, u32[]{:S(2)}) %collective-permute-start.16) | collective-permute-done | bytes 786464 | tf_op jit(solution)/shard_map/ppermute | solution.py:27
  103.0 2.7 %collective-permute-start.24 = (bf16[96,1536]{1,0:T(8,128)(2,1)S(1)}, bf16[96,1536]{1,0:T(8,128)(2,1)S(1)}, u32[]{:S(2)}, u32[]{:S(2)}) collective-permute-start(bf16[96,1536]{1,0:T(8,128)(2,1)S(1)} %add_convert_fusion.2), channel_id=1, source_target_pairs={{0,4},{4,0},{1,5},{5,1},{2,6},{6,2},{3,7},{7,3},{8,12},{12,8},{9,1... | collective-permute-start | bytes 884744 | tf_op jit(solution)/shard_map/ppermute | solution.py:27
  105.7 2.1 %collective-permute-start.21 = (bf16[96,1536]{1,0:T(8,128)(2,1)S(1)}, bf16[96,1536]{1,0:T(8,128)(2,1)S(1)}, u32[]{:S(2)}, u32[]{:S(2)}) collective-permute-start(bf16[96,1536]{1,0:T(8,128)(2,1)S(1)} %add_convert_fusion.3), channel_id=1, source_target_pairs={{0,8},{8,0},{1,9},{9,1},{2,10},{10,2},{3,11},{11,3},{4,12},{12,4},... | collective-permute-start | bytes 884744 | tf_op jit(solution)/shard_map/ppermute | solution.py:27
  108.0 1.7 %collective-permute-start.23 = (bf16[96,1536]{1,0:T(8,128)(2,1)S(1)}, bf16[96,1536]{1,0:T(8,128)(2,1)S(1)}, u32[]{:S(2)}, u32[]{:S(2)}) collective-permute-start(bf16[96,1536]{1,0:T(8,128)(2,1)S(1)} %copy-done.14), channel_id=1, source_target_pairs={{0,2},{2,0},{1,3},{3,1},{4,6},{6,4},{5,7},{7,5},{8,10},{10,8},{9,1... | collective-permute-start | bytes 884744 | tf_op jit(solution)/shard_map/ppermute | solution.py:27
  109.7 17.3 %collective-permute-done.24 = bf16[96,1536]{1,0:T(8,128)(2,1)S(1)} collective-permute-done((bf16[96,1536]{1,0:T(8,128)(2,1)S(1)}, bf16[96,1536]{1,0:T(8,128)(2,1)S(1)}, u32[]{:S(2)}, u32[]{:S(2)}) %collective-permute-start.24) | collective-permute-done | bytes 294944 | tf_op jit(solution)/shard_map/ppermute | solution.py:27
  127.1 4.2 %convolution_convert_fusion = bf16[128,3072]{1,0:T(8,128)(2,1)S(1)} fusion(bf16[128,3072]{1,0:T(8,128)(2,1)S(1)} %add_convert_fusion, bf16[128,3072]{1,0:T(8,128)(2,1)} %collective-permute-done.17, s32[]{:T(128)} %bitcast.4, s32[]{:T(128)} %bitcast.3, s32[128]{0:T(128)S(1)} %get-tuple-element.95, s32[128]{0:T(128)S(1)} %get-tuple-element.97, s32[]{:T(128)} %bitcast.2, ...), kind=kOutput, calls=%fused_computation.3 | convolution fusion | flops 206700544 | bytes 2362768 | tf_op jit(solution)/shard_map/dot_general | solution.py:52
  131.7 1.4 %fusion.18 = (bf16[128,1536]{1,0:T(8,128)(2,1)}, bf16[128,1536]{1,0:T(8,128)(2,1)}) fusion(f32[128]{0:T(128)S(1)} %broadcast_multiply_fusion.2, f32[128]{0:T(128)S(1)} %div.55, f32[128]{0:T(128)S(1)} %broadcast_multiply_fusion.3, f32[1536]{0:T(1024)S(1)} %copy-done.18, f32[128]{0:T(128)S(1)} %rsqrt.12, bf16[128,3072]{1,0:T(8,128)(2,1)S(1)} %convolution_convert_fusion, ...), kind=kLoop, calls=%fused_computation.22 | loop fusion | flops 2949120 | bytes 2367488 | tf_op jit(solution)/shard_map/convert_element_type | solution.py:435
  (122 shorter events, 16.1 us)
Async XLA Ops:
  0.6 40.7 %copy-start = (f32[2,225,12]{1,0,2:T(2,128)S(1)}, f32[2,225,12]{1,0,2:T(2,128)}, u32[]{:S(2)}) copy-start(f32[2,225,12]{1,0,2:T(2,128)} %param.16) | copy-start | bytes 64804
  2.0 8.8 %collective-permute-start.3 = (bf16[96,1536]{1,0:T(8,128)(2,1)S(1)}, bf16[96,1536]{1,0:T(8,128)(2,1)S(1)}, u32[]{:S(2)}, u32[]{:S(2)}) collective-permute-start(bf16[96,1536]{1,0:T(8,128)(2,1)S(1)} %broadcast_select_fusion), channel_id=1, source_target_pairs={{0,4},{4,0},{1,5},{5,1},{2,6},{6,2},{3,7},{7,3},{8,12},{12,8},{9,1... | collective-permute-start | bytes 884744 | tf_op jit(solution)/shard_map/ppermute | solution.py:27
  3.9 18.3 %copy-start.21 = (s32[2,2]{1,0:T(2,128)S(1)}, s32[2,2]{1,0:T(2,128)}, u32[]{:S(2)}) copy-start(s32[2,2]{1,0:T(2,128)} %param.14) | copy-start | bytes 52
  3.9 18.4 %copy-start.18 = (f32[1536]{0:T(1024)S(1)}, f32[1536]{0:T(1024)}, u32[]{:S(2)}) copy-start(f32[1536]{0:T(1024)} %param.12) | copy-start | bytes 18436
  4.0 9.6 %collective-permute-start = (bf16[128,1536]{1,0:T(8,128)(2,1)S(1)}, bf16[128,1536]{1,0:T(8,128)(2,1)S(1)}, u32[]{:S(2)}, u32[]{:S(2)}) collective-permute-start(bf16[128,1536]{1,0:T(8,128)(2,1)S(1)} %bitcast.48), channel_id=1, source_target_pairs={{0,15},{1,0},{2,1},{3,2},{4,3},{5,4},{6,5},{7,6},{8,7},{9,8},{10,9... | collective-permute-start | bytes 1179656 | tf_op jit(solution)/shard_map/ppermute | solution.py:18
  4.1 9.6 %collective-permute-start.1 = (bf16[128,1536]{1,0:T(8,128)(2,1)S(1)}, bf16[128,1536]{1,0:T(8,128)(2,1)S(1)}, u32[]{:S(2)}, u32[]{:S(2)}) collective-permute-start(bf16[128,1536]{1,0:T(8,128)(2,1)S(1)} %bitcast.50), channel_id=1, source_target_pairs={{0,15},{1,0},{2,1},{3,2},{4,3},{5,4},{6,5},{7,6},{8,7},{9,8},{10,9... | collective-permute-start | bytes 1179656 | tf_op jit(solution)/shard_map/ppermute | solution.py:18
  10.9 29.1 %copy-start.16 = (bf16[96,1536]{1,0:T(8,128)(2,1)}, bf16[96,1536]{1,0:T(8,128)(2,1)S(1)}, u32[]{:S(2)}) copy-start(bf16[96,1536]{1,0:T(8,128)(2,1)S(1)} %collective-permute-done.3.refs_5_) | copy-start | bytes 884740
  11.0 33.0 %copy-start.17 = (bf16[96,1536]{1,0:T(8,128)(2,1)}, bf16[96,1536]{1,0:T(8,128)(2,1)S(1)}, u32[]{:S(2)}) copy-start(bf16[96,1536]{1,0:T(8,128)(2,1)S(1)} %get-tuple-element.36.refs_4_) | copy-start | bytes 884740
  11.0 30.4 %copy-start.23 = (s32[64,64]{1,0:T(8,128)S(1)}, s32[64,64]{1,0:T(8,128)}, u32[]{:S(2)}) copy-start(s32[64,64]{1,0:T(8,128)} %param.15) | copy-start | bytes 49156
  11.0 15.3 %collective-permute-start.4 = (bf16[96,1536]{1,0:T(8,128)(2,1)S(1)}, bf16[96,1536]{1,0:T(8,128)(2,1)}, u32[]{:S(2)}, u32[]{:S(2)}) collective-permute-start(bf16[96,1536]{1,0:T(8,128)(2,1)S(1)} %get-tuple-element.71), channel_id=1, source_target_pairs={{0,8},{8,0},{1,9},{9,1},{2,10},{10,2},{3,11},{11,3},{4,12},{12,4},... | collective-permute-start | bytes 884744 | tf_op jit(solution)/shard_map/ppermute | solution.py:27
  13.7 15.6 %collective-permute-start.5 = (bf16[96,1536]{1,0:T(8,128)(2,1)S(1)}, bf16[96,1536]{1,0:T(8,128)(2,1)}, u32[]{:S(2)}, u32[]{:S(2)}) collective-permute-start(bf16[96,1536]{1,0:T(8,128)(2,1)S(1)} %get-tuple-element.36.refs_4_), channel_id=1, source_target_pairs={{0,2},{2,0},{1,3},{3,1},{4,6},{6,4},{5,7},{7,5},{8,10},{10,8},{9,1... | collective-permute-start | bytes 884744 | tf_op jit(solution)/shard_map/ppermute | solution.py:27
  24.7 20.1 %copy-start.5 = (bf16[2,768,128]{2,1,0:T(8,128)(2,1)}, bf16[2,768,128]{2,1,0:T(8,128)(2,1)S(1)}, u32[]{:S(2)}) copy-start(bf16[2,768,128]{2,1,0:T(8,128)(2,1)S(1)} %get-tuple-element.34.refs_0_) | copy-start | bytes 1179652
  24.8 12.2 %collective-permute-start.2 = (bf16[2,768,128]{2,1,0:T(8,128)(2,1)S(1)}, bf16[2,768,128]{2,1,0:T(8,128)(2,1)}, u32[]{:S(2)}, u32[]{:S(2)}) collective-permute-start(bf16[2,768,128]{2,1,0:T(8,128)(2,1)S(1)} %get-tuple-element.38), channel_id=1, source_target_pairs={{0,4},{4,0},{1,5},{5,1},{2,6},{6,2},{3,7},{7,3},{8,12},{12,8},{9,1... | collective-permute-start | bytes 1179656 | tf_op jit(solution)/shard_map/ppermute | solution.py:27
  29.2 10.2 %collective-permute-start.6 = (bf16[96,1536]{1,0:T(8,128)(2,1)}, bf16[96,1536]{1,0:T(8,128)(2,1)}, u32[]{:S(2)}, u32[]{:S(2)}) collective-permute-start(bf16[96,1536]{1,0:T(8,128)(2,1)} %collective-permute-done.4.refs_8_), channel_id=1, source_target_pairs={{0,16},{16,0},{1,17},{17,1},{2,18},{18,2},{3,19},{19,3},{4,20},{20... | collective-permute-start | bytes 884744 | tf_op jit(solution)/shard_map/ppermute | solution.py:27
  30.4 10.0 %collective-permute-start.11 = (bf16[96,1536]{1,0:T(8,128)(2,1)}, bf16[96,1536]{1,0:T(8,128)(2,1)}, u32[]{:S(2)}, u32[]{:S(2)}) collective-permute-start(bf16[96,1536]{1,0:T(8,128)(2,1)} %collective-permute-done.4.refs_8_), channel_id=1, source_target_pairs={{0,2},{2,0},{1,3},{3,1},{4,6},{6,4},{5,7},{7,5},{8,10},{10,8},{9,1... | collective-permute-start | bytes 884744 | tf_op jit(solution)/shard_map/ppermute | solution.py:27
  31.7 13.7 %collective-permute-start.8 = (bf16[2,768,128]{2,1,0:T(8,128)(2,1)S(1)}, bf16[2,768,128]{2,1,0:T(8,128)(2,1)S(1)}, u32[]{:S(2)}, u32[]{:S(2)}) collective-permute-start(bf16[2,768,128]{2,1,0:T(8,128)(2,1)S(1)} %get-tuple-element.34.refs_0_), channel_id=1, source_target_pairs={{0,4},{4,0},{1,5},{5,1},{2,6},{6,2},{3,7},{7,3},{8,12},{12,8},{9,1... | collective-permute-start | bytes 1179656 | tf_op jit(solution)/shard_map/ppermute | solution.py:27
  39.4 10.1 %collective-permute-start.7 = (bf16[2,768,128]{2,1,0:T(8,128)(2,1)S(1)}, bf16[2,768,128]{2,1,0:T(8,128)(2,1)S(1)}, u32[]{:S(2)}, u32[]{:S(2)}) collective-permute-start(bf16[2,768,128]{2,1,0:T(8,128)(2,1)S(1)} %get-tuple-element.38), channel_id=1, source_target_pairs={{0,1},{1,0},{2,3},{3,2},{4,5},{5,4},{6,7},{7,6},{8,9},{9,8},{10,11... | collective-permute-start | bytes 1179656 | tf_op jit(solution)/shard_map/ppermute | solution.py:27
  39.5 10.0 %collective-permute-start.9 = (bf16[2,768,128]{2,1,0:T(8,128)(2,1)}, bf16[2,768,128]{2,1,0:T(8,128)(2,1)S(1)}, u32[]{:S(2)}, u32[]{:S(2)}) collective-permute-start(bf16[2,768,128]{2,1,0:T(8,128)(2,1)} %collective-permute-done.2), channel_id=1, source_target_pairs={{0,1},{1,0},{2,3},{3,2},{4,5},{5,4},{6,7},{7,6},{8,9},{9,8},{10,11... | collective-permute-start | bytes 1179656 | tf_op jit(solution)/shard_map/ppermute | solution.py:27
  40.0 9.5 %collective-permute-start.10 = (bf16[96,1536]{1,0:T(8,128)(2,1)S(1)}, bf16[96,1536]{1,0:T(8,128)(2,1)}, u32[]{:S(2)}, u32[]{:S(2)}) collective-permute-start(bf16[96,1536]{1,0:T(8,128)(2,1)S(1)} %collective-permute-done.3.refs_5_), channel_id=1, source_target_pairs={{0,2},{2,0},{1,3},{3,1},{4,6},{6,4},{5,7},{7,5},{8,10},{10,8},{9,1... | collective-permute-start | bytes 884744 | tf_op jit(solution)/shard_map/ppermute | solution.py:27
  40.5 9.1 %collective-permute-start.12 = (bf16[96,1536]{1,0:T(8,128)(2,1)}, bf16[96,1536]{1,0:T(8,128)(2,1)}, u32[]{:S(2)}, u32[]{:S(2)}) collective-permute-start(bf16[96,1536]{1,0:T(8,128)(2,1)} %collective-permute-done.11.refs_10_), channel_id=1, source_target_pairs={{0,16},{16,0},{1,17},{17,1},{2,18},{18,2},{3,19},{19,3},{4,20},{20... | collective-permute-start | bytes 884744 | tf_op jit(solution)/shard_map/ppermute | solution.py:27
  56.9 2.6 %collective-permute-start.13 = (bf16[256,1536]{1,0:T(8,128)(2,1)}, bf16[256,1536]{1,0:T(8,128)(2,1)S(1)}, u32[]{:S(2)}, u32[]{:S(2)}) collective-permute-start(bf16[256,1536]{1,0:T(8,128)(2,1)} %get-tuple-element.43), channel_id=1, source_target_pairs={{0,1},{1,0},{2,3},{3,2},{4,5},{5,4},{6,7},{7,6},{8,9},{9,8},{10,11... | collective-permute-start | bytes 2359304 | tf_op jit(solution)/shard_map/ppermute | solution.py:27
  60.3 12.5 %collective-permute-start.15 = (bf16[768,1536]{1,0:T(8,128)(2,1)}, bf16[768,1536]{1,0:T(8,128)(2,1)S(1)}, u32[]{:S(2)}, u32[]{:S(2)}) collective-permute-start(bf16[768,1536]{1,0:T(8,128)(2,1)} %get-tuple-element.47.mine_ref), channel_id=1, source_target_pairs={{0,1},{1,0},{2,3},{3,2},{4,5},{5,4},{6,7},{7,6},{8,9},{9,8},{10,11... | collective-permute-start | bytes 7077896 | tf_op jit(solution)/shard_map/ppermute | solution.py:27
  64.7 2.5 %collective-permute-start.14 = (bf16[256,1536]{1,0:T(8,128)(2,1)}, bf16[256,1536]{1,0:T(8,128)(2,1)S(1)}, u32[]{:S(2)}, u32[]{:S(2)}) collective-permute-start(bf16[256,1536]{1,0:T(8,128)(2,1)} %attention.1.refs_4_.grad_ref), channel_id=1, source_target_pairs={{0,1},{1,0},{2,3},{3,2},{4,5},{5,4},{6,7},{7,6},{8,9},{9,8},{10,11... | collective-permute-start | bytes 2359304 | tf_op jit(solution)/shard_map/ppermute | solution.py:27
  71.1 9.3 %collective-permute-start.18 = (bf16[96,1536]{1,0:T(8,128)(2,1)S(1)}, bf16[96,1536]{1,0:T(8,128)(2,1)S(1)}, u32[]{:S(2)}, u32[]{:S(2)}) collective-permute-start(bf16[96,1536]{1,0:T(8,128)(2,1)S(1)} %get-tuple-element.44), channel_id=1, source_target_pairs={{0,2},{2,0},{1,3},{3,1},{4,6},{6,4},{5,7},{7,5},{8,10},{10,8},{9,1... | collective-permute-start | bytes 884744 | tf_op jit(solution)/shard_map/ppermute | solution.py:27
  76.7 25.9 %collective-permute-start.16 = (bf16[128,3072]{1,0:T(8,128)(2,1)S(1)}, bf16[128,3072]{1,0:T(8,128)(2,1)S(1)}, u32[]{:S(2)}, u32[]{:S(2)}) collective-permute-start(bf16[128,3072]{1,0:T(8,128)(2,1)S(1)} %get-tuple-element.49), channel_id=1, source_target_pairs={{0,4},{4,0},{1,5},{5,1},{2,6},{6,2},{3,7},{7,3},{8,12},{12,8},{9,1... | collective-permute-start | bytes 2359304 | tf_op jit(solution)/shard_map/ppermute | solution.py:27
  80.4 8.5 %collective-permute-start.20 = (bf16[96,1536]{1,0:T(8,128)(2,1)S(1)}, bf16[96,1536]{1,0:T(8,128)(2,1)S(1)}, u32[]{:S(2)}, u32[]{:S(2)}) collective-permute-start(bf16[96,1536]{1,0:T(8,128)(2,1)S(1)} %get-tuple-element.55), channel_id=1, source_target_pairs={{0,2},{2,0},{1,3},{3,1},{4,6},{6,4},{5,7},{7,5},{8,10},{10,8},{9,1... | collective-permute-start | bytes 884744 | tf_op jit(solution)/shard_map/ppermute | solution.py:27
  82.2 20.7 %collective-permute-start.19 = (bf16[96,1536]{1,0:T(8,128)(2,1)S(1)}, bf16[96,1536]{1,0:T(8,128)(2,1)S(1)}, u32[]{:S(2)}, u32[]{:S(2)}) collective-permute-start(bf16[96,1536]{1,0:T(8,128)(2,1)S(1)} %add_convert_fusion.4), channel_id=1, source_target_pairs={{0,8},{8,0},{1,9},{9,1},{2,10},{10,2},{3,11},{11,3},{4,12},{12,4},... | collective-permute-start | bytes 884744 | tf_op jit(solution)/shard_map/ppermute | solution.py:27
  88.9 13.9 %collective-permute-start.22 = (bf16[96,1536]{1,0:T(8,128)(2,1)S(1)}, bf16[96,1536]{1,0:T(8,128)(2,1)S(1)}, u32[]{:S(2)}, u32[]{:S(2)}) collective-permute-start(bf16[96,1536]{1,0:T(8,128)(2,1)S(1)} %get-tuple-element.61), channel_id=1, source_target_pairs={{0,2},{2,0},{1,3},{3,1},{4,6},{6,4},{5,7},{7,5},{8,10},{10,8},{9,1... | collective-permute-start | bytes 884744 | tf_op jit(solution)/shard_map/ppermute | solution.py:27
  102.8 24.3 %collective-permute-start.17 = (bf16[128,3072]{1,0:T(8,128)(2,1)S(1)}, bf16[128,3072]{1,0:T(8,128)(2,1)}, u32[]{:S(2)}, u32[]{:S(2)}) collective-permute-start(bf16[128,3072]{1,0:T(8,128)(2,1)S(1)} %add_convert_fusion), channel_id=1, source_target_pairs={{0,1},{1,2},{2,3},{3,4},{4,5},{5,6},{6,7},{7,8},{8,9},{9,10},{10,1... | collective-permute-start | bytes 2359304 | tf_op jit(solution)/shard_map/ppermute | solution.py:18
  103.0 24.1 %collective-permute-start.24 = (bf16[96,1536]{1,0:T(8,128)(2,1)S(1)}, bf16[96,1536]{1,0:T(8,128)(2,1)S(1)}, u32[]{:S(2)}, u32[]{:S(2)}) collective-permute-start(bf16[96,1536]{1,0:T(8,128)(2,1)S(1)} %add_convert_fusion.2), channel_id=1, source_target_pairs={{0,4},{4,0},{1,5},{5,1},{2,6},{6,2},{3,7},{7,3},{8,12},{12,8},{9,1... | collective-permute-start | bytes 884744 | tf_op jit(solution)/shard_map/ppermute | solution.py:27
  105.7 25.6 %collective-permute-start.21 = (bf16[96,1536]{1,0:T(8,128)(2,1)S(1)}, bf16[96,1536]{1,0:T(8,128)(2,1)S(1)}, u32[]{:S(2)}, u32[]{:S(2)}) collective-permute-start(bf16[96,1536]{1,0:T(8,128)(2,1)S(1)} %add_convert_fusion.3), channel_id=1, source_target_pairs={{0,8},{8,0},{1,9},{9,1},{2,10},{10,2},{3,11},{11,3},{4,12},{12,4},... | collective-permute-start | bytes 884744 | tf_op jit(solution)/shard_map/ppermute | solution.py:27
  108.0 25.0 %collective-permute-start.23 = (bf16[96,1536]{1,0:T(8,128)(2,1)S(1)}, bf16[96,1536]{1,0:T(8,128)(2,1)S(1)}, u32[]{:S(2)}, u32[]{:S(2)}) collective-permute-start(bf16[96,1536]{1,0:T(8,128)(2,1)S(1)} %copy-done.14), channel_id=1, source_target_pairs={{0,2},{2,0},{1,3},{3,1},{4,6},{6,4},{5,7},{7,5},{8,10},{10,8},{9,1... | collective-permute-start | bytes 884744 | tf_op jit(solution)/shard_map/ppermute | solution.py:27
  (17 other events, 65.3 us)

commit v8 on v6

--- a/solution.py
+++ b/solution.py
@@ -119,7 +119,7 @@
         copies.append(pltpu.make_async_copy(piece, w_ref.at[rows, :], sems.at[i]))
     for j, source in enumerate(tiles):
         copies.append(pltpu.make_async_copy(source, tile_ref.at[j], sems.at[8 + j]))
-    for copy in copies:
+    for copy in copies[8:] + copies[:8]:
         copy.start()
     for j, at in enumerate((0, 2, 1, 3)):
         copies[8 + j].wait()
@@ -208,8 +208,9 @@
         out_ref[...] = sum_ref[pl.ds(pl.multiple_of((i // 2 * 2 + wanted) * rows, 16), rows), :]
 
 
-def outer_kernel(place_ref, grad_ref, mine_ref, theirs_ref, own_ref, other_ref, w_ref, sems):
-    tile = own_ref.shape[0]
+def outer_kernel(place_ref, grad_ref, mine_ref, theirs_ref, *refs):
+    own_refs, other_refs, (w_ref, sems) = refs[:2], refs[2:4], refs[4:]
+    tile = own_refs[0].shape[0]
     width = w_ref.shape[0]
     rows = width // 16
     part = w_ref.shape[1] // 4
@@ -227,9 +228,8 @@
         at = pl.ds(n * step, step)
         for k, w_cols in enumerate((pl.ds(3 * part, part), pl.ds(0, 3 * part))):
             product = across(grad_ref[:, w_cols], w_ref[at, w_cols])
-            cols = pl.ds(k * width + n * step, step)
-            own_ref[:, cols] = product[:tile]
-            other_ref[:, cols] = product[tile:].astype(jnp.bfloat16)
+            own_refs[k][:, at] = product[:tile]
+            other_refs[k][:, at] = product[tile:].astype(jnp.bfloat16)
 
 
 def after(value, earlier):
@@ -379,14 +379,11 @@
     )(kept, crossed, bias)
     w_theirs = swap(after(w_mine, crossed), "core")
     grad_theirs = swap(grad, "core")
-    attended_own, attended_other = kernel_call(
+    attended_own, grad_own, attended_other, grad_other = kernel_call(
         outer_kernel,
-        (
-            jax.ShapeDtypeStruct((tile, 2 * width), f32),
-            jax.ShapeDtypeStruct((tile, 2 * width), bf16),
-        ),
+        (jax.ShapeDtypeStruct((tile, width), f32),) * 2 + (jax.ShapeDtypeStruct((tile, width), bf16),) * 2,
         [smem, vmem, anywhere, anywhere],
-        (vmem, vmem),
+        (vmem,) * 4,
         [pltpu.VMEM((width, 4 * part), bf16), dma((16,))],
         1_200_000_000,
         8_000_000,
@@ -407,14 +404,15 @@
         6_000_000,
         "weight_gradient",
         24,
-    )(after(near.astype(jnp.int32).reshape(1), attended_other), *tiles, grad, grad_theirs)
+    )(after(near.astype(jnp.int32).reshape(1), grad_other), *tiles, grad, grad_theirs)
 
     def block(f, s, n):
         return blocks[((1 - f) * 2 + 1 - s) * 2 + 1 - n]
 
-    side_far_1 = swap(block(1, 1, 1), "side")
-    arrived_back = swap(attended_other, "near")
-    side_far_0 = swap(after(block(1, 1, 0), side_far_1), "side")
+    arrived_first = swap(attended_other, "near")
+    side_far_1 = after(swap(block(1, 1, 1), "side"), arrived_first)
+    arrived_back = swap(grad_other, "near")
+    side_far_0 = swap(after(block(1, 1, 0), (side_far_1, arrived_first)), "side")
     far_1 = swap((block(1, 0, 1).astype(f32) + side_far_1.astype(f32)).astype(bf16), "far")
     far_0 = swap(after((block(1, 0, 0).astype(f32) + side_far_0.astype(f32)).astype(bf16), (far_1, arrived_back)), "far")
     side_1 = swap(after(block(0, 1, 1), side_far_0), "side")
@@ -422,11 +420,12 @@
     total_1 = (block(0, 0, 1).astype(f32) + side_1.astype(f32) + far_1.astype(f32)).astype(bf16)
     theirs = swap(total_1, "near").astype(f32)
 
-    back = (attended_own + arrived_back.astype(f32)).astype(jnp.bfloat16)
-    back = after(roll_back(back, shifts, levels, side, far_1), far_0)
-    output = (values + back[:, :width].astype(f32)).astype(jnp.bfloat16)
+    first_back = roll_back((attended_own + arrived_first.astype(f32)).astype(bf16), shifts, levels, side, ())
+    output = (values + first_back.astype(f32)).astype(bf16)
+    back = roll_back((grad_own + arrived_back.astype(f32)).astype(bf16), shifts, levels, side, (theirs, output))
+    back = after(back, far_0)
     scaled = center * spread
-    upstream = back[:, width:].astype(f32) * gain
+    upstream = back.astype(f32) * gain
     grad_stream = spread * (
         upstream
         - jnp.mean(upstream, axis=-1, keepdims=True)

time: 129 us -> 138 us (1.070)
  the two profiles are of different devices: /device:TPU:6 before, /device:TPU:0 now
where the time goes in v8:
time: 138 us
  waiting for transfers between devices  57.8 us (42%)
  starting transfers between devices  35.4 us (26%)
  Pallas kernels  21 us (15%)
  matrix products  9.42 us (7%)
  local copies, waits for them, and re-layouts  7.64 us (6%)
  other arithmetic  5.09 us (4%)
    ppermute x23, waiting for transfers between devices, swap(): return lax.ppermute(shard, axis, [(0, 1), (1, 0)])  50.5 us
    ppermute x23, starting transfers between devices, swap(): return lax.ppermute(shard, axis, [(0, 1), (1, 0)])  31.5 us
    ppermute x4, waiting for transfers between devices, along_lon(): lax.ppermute(shard, LON, [(i, (i + by) % count) for i in range(count)])  7.34 us
    dot_general x2, matrix products, picked(): jnp.dot(onehot, both, preferred_element_type=jnp.float32)  6.77 us
    pallas_call x1, Pallas kernels, on_device(): kernel_call(products_kernel, (jax.ShapeDtypeStruct((2 * tile, 4 * part),...  5.79 us
    pallas_call x1, Pallas kernels, on_device(): kernel_call(outer_kernel, (jax.ShapeDtypeStruct((tile, width), f32),) * 2...  4.82 us
    pallas_call x1, Pallas kernels, on_device(): kernel_call(functools.partial(attention_kernel, area, head), jax.ShapeDty...  4.14 us
    ppermute x4, starting transfers between devices, along_lon(): lax.ppermute(shard, LON, [(i, (i + by) % count) for i in range(count)])  3.9 us
  transfers between devices with their start and end apart: 27, of which 14 were waited for; matrix products, arithmetic and copies ran while one was open for 11% of the time, Pallas kernels for 11%

profile of v8, /device:TPU:0, one launch (start us, length us, event | category | flops | bytes accessed | tf_op | source)
XLA Modules:
  0.0 137.5 jit_solution(7295402295405176169)
XLA Ops:
  2.0 3.1 %collective-permute-start.3 = (bf16[96,1536]{1,0:T(8,128)(2,1)S(1)}, bf16[96,1536]{1,0:T(8,128)(2,1)S(1)}, u32[]{:S(2)}, u32[]{:S(2)}) collective-permute-start(bf16[96,1536]{1,0:T(8,128)(2,1)S(1)} %broadcast_select_fusion), channel_id=1, source_target_pairs={{0,4},{4,0},{1,5},{5,1},{2,6},{6,2},{3,7},{7,3},{8,12},{12,8},{9,1... | collective-permute-start | bytes 884744 | tf_op jit(solution)/shard_map/ppermute | solution.py:27
  5.5 2.6 %collective-permute-start = (bf16[128,1536]{1,0:T(8,128)(2,1)S(1)}, bf16[128,1536]{1,0:T(8,128)(2,1)S(1)}, u32[]{:S(2)}, u32[]{:S(2)}) collective-permute-start(bf16[128,1536]{1,0:T(8,128)(2,1)S(1)} %bitcast.47), channel_id=1, source_target_pairs={{0,15},{1,0},{2,1},{3,2},{4,3},{5,4},{6,5},{7,6},{8,7},{9,8},{10,9... | collective-permute-start | bytes 1179656 | tf_op jit(solution)/shard_map/ppermute | solution.py:18
  9.1 3.1 %collective-permute-done.3.refs_5_ = bf16[96,1536]{1,0:T(8,128)(2,1)S(1)} collective-permute-done((bf16[96,1536]{1,0:T(8,128)(2,1)S(1)}, bf16[96,1536]{1,0:T(8,128)(2,1)S(1)}, u32[]{:S(2)}, u32[]{:S(2)}) %collective-permute-start.3) | collective-permute-done | bytes 294944 | tf_op jit(solution)/shard_map/ppermute | solution.py:27
  13.0 2.8 %collective-permute-start.4 = (bf16[96,1536]{1,0:T(8,128)(2,1)}, bf16[96,1536]{1,0:T(8,128)(2,1)}, u32[]{:S(2)}, u32[]{:S(2)}) collective-permute-start(bf16[96,1536]{1,0:T(8,128)(2,1)} %get-tuple-element.75), channel_id=1, source_target_pairs={{0,8},{8,0},{1,9},{9,1},{2,10},{10,2},{3,11},{11,3},{4,12},{12,4},... | collective-permute-start | bytes 884744 | tf_op jit(solution)/shard_map/ppermute | solution.py:27
  16.1 6.9 %collective-permute-done.1.refs_3_ = bf16[128,1536]{1,0:T(8,128)(2,1)S(1)} collective-permute-done((bf16[128,1536]{1,0:T(8,128)(2,1)S(1)}, bf16[128,1536]{1,0:T(8,128)(2,1)S(1)}, u32[]{:S(2)}, u32[]{:S(2)}) %collective-permute-start.1) | collective-permute-done | bytes 393248 | tf_op jit(solution)/shard_map/ppermute | solution.py:18
  23.3 2.4 %turned_rolls.1 = (bf16[2,768,128]{2,1,0:T(8,128)(2,1)S(1)}, bf16[2,768,128]{2,1,0:T(8,128)(2,1)S(1)}) custom-call(s32[20]{0:T(128)S(1)} %concatenate.18.info_ref, f32[1,1536]{1,0:T(1,128)S(1)} %reshape.97.gain_ref, bf16[128,1536]{1,0:T(8,128)(2,1)S(1)} %bitcast.48, bf16[128,1536]{1,0:T(8,128)(2,1)S(1)} %collective-permute-done.refs_1_, ...), custom_call_target="tpu_custom_call" | custom-call | flops 201326592 | bytes 3000000 | tf_op jit(solution)/shard_map/turned_rolls/pallas_call | solution.py:305
  25.8 5.2 %collective-permute-done.4.refs_8_ = bf16[96,1536]{1,0:T(8,128)(2,1)} collective-permute-done((bf16[96,1536]{1,0:T(8,128)(2,1)}, bf16[96,1536]{1,0:T(8,128)(2,1)}, u32[]{:S(2)}, u32[]{:S(2)}) %collective-permute-start.4) | collective-permute-done | bytes 294944 | tf_op jit(solution)/shard_map/ppermute | solution.py:27
  31.0 1.7 %collective-permute-start.6 = (bf16[96,1536]{1,0:T(8,128)(2,1)}, bf16[96,1536]{1,0:T(8,128)(2,1)}, u32[]{:S(2)}, u32[]{:S(2)}) collective-permute-start(bf16[96,1536]{1,0:T(8,128)(2,1)} %collective-permute-done.4.refs_8_), channel_id=1, source_target_pairs={{0,16},{16,0},{1,17},{17,1},{2,18},{18,2},{3,19},{19,3},{4,20},{20... | collective-permute-start | bytes 884744 | tf_op jit(solution)/shard_map/ppermute | solution.py:27
  32.7 1.8 %collective-permute-start.11 = (bf16[96,1536]{1,0:T(8,128)(2,1)}, bf16[96,1536]{1,0:T(8,128)(2,1)}, u32[]{:S(2)}, u32[]{:S(2)}) collective-permute-start(bf16[96,1536]{1,0:T(8,128)(2,1)} %collective-permute-done.4.refs_8_), channel_id=1, source_target_pairs={{0,2},{2,0},{1,3},{3,1},{4,6},{6,4},{5,7},{7,5},{8,10},{10,8},{9,1... | collective-permute-start | bytes 884744 | tf_op jit(solution)/shard_map/ppermute | solution.py:27
  36.1 3.2 %collective-permute-done.2 = bf16[2,768,128]{2,1,0:T(8,128)(2,1)} collective-permute-done((bf16[2,768,128]{2,1,0:T(8,128)(2,1)S(1)}, bf16[2,768,128]{2,1,0:T(8,128)(2,1)}, u32[]{:S(2)}, u32[]{:S(2)}) %collective-permute-start.2) | collective-permute-done | bytes 393248 | tf_op jit(solution)/shard_map/ppermute | solution.py:27
  40.0 2.7 %collective-permute-start.10 = (bf16[96,1536]{1,0:T(8,128)(2,1)S(1)}, bf16[96,1536]{1,0:T(8,128)(2,1)}, u32[]{:S(2)}, u32[]{:S(2)}) collective-permute-start(bf16[96,1536]{1,0:T(8,128)(2,1)S(1)} %collective-permute-done.3.refs_5_), channel_id=1, source_target_pairs={{0,2},{2,0},{1,3},{3,1},{4,6},{6,4},{5,7},{7,5},{8,10},{10,8},{9,1... | collective-permute-start | bytes 884744 | tf_op jit(solution)/shard_map/ppermute | solution.py:27
  42.7 1.7 %collective-permute-start.12 = (bf16[96,1536]{1,0:T(8,128)(2,1)}, bf16[96,1536]{1,0:T(8,128)(2,1)}, u32[]{:S(2)}, u32[]{:S(2)}) collective-permute-start(bf16[96,1536]{1,0:T(8,128)(2,1)} %collective-permute-done.11.refs_10_), channel_id=1, source_target_pairs={{0,16},{16,0},{1,17},{17,1},{2,18},{18,2},{3,19},{19,3},{4,20},{20... | collective-permute-start | bytes 884744 | tf_op jit(solution)/shard_map/ppermute | solution.py:27
  44.4 2.6 %fusion.7 = f32[2,6,64,64]{3,1,2,0:T(8,128)S(1)} fusion(s32[64,64]{1,0:T(8,128)S(1)} %copy-done.22, pred[2,64,64]{2,1,0:T(8,128)(4,1)S(1)} %broadcast_compare_fusion, f32[2,225,6]{1,0,2:T(2,128)S(1)} %constant_dynamic-slice_fusion), kind=kOutput, calls=%fused_computation.9 | convolution fusion | flops 133681152 | bytes 231984 | tf_op jit(solution)/shard_map/qkr,lrh->lhqk/dot_general | solution.py:340
  50.0 1.7 %collective-permute-done.12.refs_11_ = bf16[96,1536]{1,0:T(8,128)(2,1)} collective-permute-done((bf16[96,1536]{1,0:T(8,128)(2,1)}, bf16[96,1536]{1,0:T(8,128)(2,1)}, u32[]{:S(2)}, u32[]{:S(2)}) %collective-permute-start.12) | collective-permute-done | bytes 294944 | tf_op jit(solution)/shard_map/ppermute | solution.py:27
  53.1 5.8 %products.1 = (bf16[256,1536]{1,0:T(8,128)(2,1)}, bf16[256,1536]{1,0:T(8,128)(2,1)}, bf16[768,1536]{1,0:T(8,128)(2,1)}) custom-call(s32[8]{0:T(128)} %stack.120.place_ref, bf16[2,768,128]{2,1,0:T(8,128)(2,1)} %copy-done.5, bf16[2,768,128]{2,1,0:T(8,128)(2,1)} %copy-done.11, bf16[2,768,128]{2,1,0:T(8,128)(2,1)} %copy-done.7, bf16[2,768,128]{2,1,0:T(8,128)(2,1)} %copy-done.9, ...), custom_call_target="tpu_custom_call" | custom-call | flops 1200000000 | bytes 9000000 | tf_op jit(solution)/shard_map/products/pallas_call | solution.py:348
  59.0 2.5 %collective-permute-done.13.came_ref = bf16[256,1536]{1,0:T(8,128)(2,1)S(1)} collective-permute-done((bf16[256,1536]{1,0:T(8,128)(2,1)}, bf16[256,1536]{1,0:T(8,128)(2,1)S(1)}, u32[]{:S(2)}, u32[]{:S(2)}) %collective-permute-start.13) | collective-permute-done | bytes 786464 | tf_op jit(solution)/shard_map/ppermute | solution.py:27
  62.8 4.1 %attention.1.grad_ref.refs_4_ = bf16[256,1536]{1,0:T(8,128)(2,1)} custom-call(bf16[256,1536]{1,0:T(8,128)(2,1)} %get-tuple-element.44.kept_ref, bf16[256,1536]{1,0:T(8,128)(2,1)} %copy-done.20, f32[2,3,128,64]{3,2,1,0:T(8,128)} %bitcast.52), custom_call_target="tpu_custom_call" | custom-call | flops 1000000000 | bytes 4000000 | tf_op jit(solution)/shard_map/attention/pallas_call | solution.py:369
  68.9 4.8 %projections.1 = (f32[128,1536]{1,0:T(8,128)S(1)}, f32[128,1536]{1,0:T(8,128)S(1)}, bf16[128,1536]{1,0:T(8,128)(2,1)S(1)}, bf16[128,1536]{1,0:T(8,128)(2,1)S(1)}) custom-call(s32[16]{0:T(128)S(1)} %stack.111.place_ref, bf16[256,1536]{1,0:T(8,128)(2,1)S(1)} %copy-done.3, bf16[768,1536]{1,0:T(8,128)(2,1)S(1)} %copy-done.1, ...), custom_call_target="tpu_custom_call" | custom-call | flops 1200000000 | bytes 8000000 | tf_op jit(solution)/shard_map/projections/pallas_call | solution.py:382
  73.7 1.8 %collective-permute-start.15 = (bf16[128,1536]{1,0:T(8,128)(2,1)S(1)}, bf16[128,1536]{1,0:T(8,128)(2,1)S(1)}, u32[]{:S(2)}, u32[]{:S(2)}) collective-permute-start(bf16[128,1536]{1,0:T(8,128)(2,1)S(1)} %get-tuple-element.49), channel_id=1, source_target_pairs={{0,4},{4,0},{1,5},{5,1},{2,6},{6,2},{3,7},{7,3},{8,12},{12,8},{9,1... | collective-permute-start | bytes 1179656 | tf_op jit(solution)/shard_map/ppermute | solution.py:27
  75.5 3.9 %weight_gradient.1 = (bf16[96,1536]{1,0:T(8,128)(2,1)S(1)}, bf16[96,1536]{1,0:T(8,128)(2,1)S(1)}, bf16[96,1536]{1,0:T(8,128)(2,1)S(1)}, bf16[96,1536]{1,0:T(8,12...) custom-call(s32[1]{0:T(128)} %bitcast.35.near_ref, ...), custom_call_target="tpu_custom_call" | custom-call | flops 1200000000 | bytes 6000000 | tf_op jit(solution)/shard_map/weight_gradient/pallas_call | solution.py:393
  79.4 1.7 %collective-permute-start.20 = (bf16[96,1536]{1,0:T(8,128)(2,1)S(1)}, bf16[96,1536]{1,0:T(8,128)(2,1)S(1)}, u32[]{:S(2)}, u32[]{:S(2)}) collective-permute-start(bf16[96,1536]{1,0:T(8,128)(2,1)S(1)} %get-tuple-element.56), channel_id=1, source_target_pairs={{0,2},{2,0},{1,3},{3,1},{4,6},{6,4},{5,7},{7,5},{8,10},{10,8},{9,1... | collective-permute-start | bytes 884744 | tf_op jit(solution)/shard_map/ppermute | solution.py:27
  81.8 6.5 %collective-permute-done.20 = bf16[96,1536]{1,0:T(8,128)(2,1)S(1)} collective-permute-done((bf16[96,1536]{1,0:T(8,128)(2,1)S(1)}, bf16[96,1536]{1,0:T(8,128)(2,1)S(1)}, u32[]{:S(2)}, u32[]{:S(2)}) %collective-permute-start.20) | collective-permute-done | bytes 294944 | tf_op jit(solution)/shard_map/ppermute | solution.py:27
  88.3 1.7 %collective-permute-start.21 = (bf16[96,1536]{1,0:T(8,128)(2,1)S(1)}, bf16[96,1536]{1,0:T(8,128)(2,1)S(1)}, u32[]{:S(2)}, u32[]{:S(2)}) collective-permute-start(bf16[96,1536]{1,0:T(8,128)(2,1)S(1)} %get-tuple-element.58), channel_id=1, source_target_pairs={{0,2},{2,0},{1,3},{3,1},{4,6},{6,4},{5,7},{7,5},{8,10},{10,8},{9,1... | collective-permute-start | bytes 884744 | tf_op jit(solution)/shard_map/ppermute | solution.py:27
  90.0 3.4 %collective-permute-start.23 = (bf16[96,1536]{1,0:T(8,128)(2,1)S(1)}, bf16[96,1536]{1,0:T(8,128)(2,1)S(1)}, u32[]{:S(2)}, u32[]{:S(2)}) collective-permute-start(bf16[96,1536]{1,0:T(8,128)(2,1)S(1)} %add_convert_fusion.5), channel_id=1, source_target_pairs={{0,8},{8,0},{1,9},{9,1},{2,10},{10,2},{3,11},{11,3},{4,12},{12,4},... | collective-permute-start | bytes 884744 | tf_op jit(solution)/shard_map/ppermute | solution.py:27
  93.4 2.8 %collective-permute-done.17 = bf16[128,1536]{1,0:T(8,128)(2,1)S(1)} collective-permute-done((bf16[128,1536]{1,0:T(8,128)(2,1)S(1)}, bf16[128,1536]{1,0:T(8,128)(2,1)S(1)}, u32[]{:S(2)}, u32[]{:S(2)}) %collective-permute-start.17) | collective-permute-done | bytes 393248 | tf_op jit(solution)/shard_map/ppermute | solution.py:27
  96.6 3.4 %collective-permute-start.22 = (bf16[96,1536]{1,0:T(8,128)(2,1)S(1)}, bf16[96,1536]{1,0:T(8,128)(2,1)S(1)}, u32[]{:S(2)}, u32[]{:S(2)}) collective-permute-start(bf16[96,1536]{1,0:T(8,128)(2,1)S(1)} %get-tuple-element.59), channel_id=1, source_target_pairs={{0,2},{2,0},{1,3},{3,1},{4,6},{6,4},{5,7},{7,5},{8,10},{10,8},{9,1... | collective-permute-start | bytes 884744 | tf_op jit(solution)/shard_map/ppermute | solution.py:27
  100.1 5.6 %collective-permute-done.23 = bf16[96,1536]{1,0:T(8,128)(2,1)S(1)} collective-permute-done((bf16[96,1536]{1,0:T(8,128)(2,1)S(1)}, bf16[96,1536]{1,0:T(8,128)(2,1)S(1)}, u32[]{:S(2)}, u32[]{:S(2)}) %collective-permute-start.23) | collective-permute-done | bytes 294944 | tf_op jit(solution)/shard_map/ppermute | solution.py:27
  105.7 9.4 %collective-permute-done.22 = bf16[96,1536]{1,0:T(8,128)(2,1)S(1)} collective-permute-done((bf16[96,1536]{1,0:T(8,128)(2,1)S(1)}, bf16[96,1536]{1,0:T(8,128)(2,1)S(1)}, u32[]{:S(2)}, u32[]{:S(2)}) %collective-permute-start.22) | collective-permute-done | bytes 294944 | tf_op jit(solution)/shard_map/ppermute | solution.py:27
  115.4 3.2 %collective-permute-start.25 = (bf16[96,1536]{1,0:T(8,128)(2,1)S(1)}, bf16[96,1536]{1,0:T(8,128)(2,1)S(1)}, u32[]{:S(2)}, u32[]{:S(2)}) collective-permute-start(bf16[96,1536]{1,0:T(8,128)(2,1)S(1)} %add_convert_fusion.3), channel_id=1, source_target_pairs={{0,8},{8,0},{1,9},{9,1},{2,10},{10,2},{3,11},{11,3},{4,12},{12,4},... | collective-permute-start | bytes 884744 | tf_op jit(solution)/shard_map/ppermute | solution.py:27
  118.6 3.8 %fusion.5 = bf16[128,1536]{1,0:T(8,128)(2,1)} fusion(bf16[128,1536]{1,0:T(8,128)(2,1)S(1)} %bitcast.49, bf16[128,1536]{1,0:T(8,128)(2,1)S(1)} %add_convert_fusion.1, bf16[128,1536]{1,0:T(8,128)(2,1)S(1)} %collective-permute-done.16, s32[]{:T(128)} %bitcast.4, s32[]{:T(128)} %bitcast.3, s32[128]{0:T(128)S(1)} %get-tuple-element.97, ...), kind=kOutput, calls=%fused_computation.7 | convolution fusion | flops 105054208 | bytes 1576336 | tf_op jit(solution)/shard_map/dot_general | solution.py:52
  122.3 9.1 %collective-permute-done.24 = bf16[96,1536]{1,0:T(8,128)(2,1)S(1)} collective-permute-done((bf16[96,1536]{1,0:T(8,128)(2,1)S(1)}, bf16[96,1536]{1,0:T(8,128)(2,1)S(1)}, u32[]{:S(2)}, u32[]{:S(2)}) %collective-permute-start.24) | collective-permute-done | bytes 294944 | tf_op jit(solution)/shard_map/ppermute | solution.py:27
  131.5 3.0 %convolution_convert_fusion = bf16[128,1536]{1,0:T(8,128)(2,1)S(1)} fusion(bf16[128,1536]{1,0:T(8,128)(2,1)S(1)} %add_convert_fusion, bf16[128,1536]{1,0:T(8,128)(2,1)S(1)} %collective-permute-done.18, s32[]{:T(128)} %bitcast.4, s32[]{:T(128)} %bitcast.3, s32[128]{0:T(128)S(1)} %get-tuple-element.97, s32[128]{0:T(128)S(1)} %get-tuple-element.99, ...), kind=kOutput, calls=%fused_computation.3 | convolution fusion | flops 104267776 | bytes 1183120 | tf_op jit(solution)/shard_map/dot_general | solution.py:52
  (126 shorter events, 18.5 us)
Async XLA Ops:
  0.6 43.8 %copy-start = (f32[2,225,12]{1,0,2:T(2,128)S(1)}, f32[2,225,12]{1,0,2:T(2,128)}, u32[]{:S(2)}) copy-start(f32[2,225,12]{1,0,2:T(2,128)} %param.16) | copy-start | bytes 64804
  2.0 10.1 %collective-permute-start.3 = (bf16[96,1536]{1,0:T(8,128)(2,1)S(1)}, bf16[96,1536]{1,0:T(8,128)(2,1)S(1)}, u32[]{:S(2)}, u32[]{:S(2)}) collective-permute-start(bf16[96,1536]{1,0:T(8,128)(2,1)S(1)} %broadcast_select_fusion), channel_id=1, source_target_pairs={{0,4},{4,0},{1,5},{5,1},{2,6},{6,2},{3,7},{7,3},{8,12},{12,8},{9,1... | collective-permute-start | bytes 884744 | tf_op jit(solution)/shard_map/ppermute | solution.py:27
  5.5 10.6 %collective-permute-start = (bf16[128,1536]{1,0:T(8,128)(2,1)S(1)}, bf16[128,1536]{1,0:T(8,128)(2,1)S(1)}, u32[]{:S(2)}, u32[]{:S(2)}) collective-permute-start(bf16[128,1536]{1,0:T(8,128)(2,1)S(1)} %bitcast.47), channel_id=1, source_target_pairs={{0,15},{1,0},{2,1},{3,2},{4,3},{5,4},{6,5},{7,6},{8,7},{9,8},{10,9... | collective-permute-start | bytes 1179656 | tf_op jit(solution)/shard_map/ppermute | solution.py:18
  8.1 14.9 %collective-permute-start.1 = (bf16[128,1536]{1,0:T(8,128)(2,1)S(1)}, bf16[128,1536]{1,0:T(8,128)(2,1)S(1)}, u32[]{:S(2)}, u32[]{:S(2)}) collective-permute-start(bf16[128,1536]{1,0:T(8,128)(2,1)S(1)} %bitcast.50), channel_id=1, source_target_pairs={{0,15},{1,0},{2,1},{3,2},{4,3},{5,4},{6,5},{7,6},{8,7},{9,8},{10,9... | collective-permute-start | bytes 1179656 | tf_op jit(solution)/shard_map/ppermute | solution.py:18
  12.1 27.9 %copy-start.14 = (bf16[96,1536]{1,0:T(8,128)(2,1)}, bf16[96,1536]{1,0:T(8,128)(2,1)S(1)}, u32[]{:S(2)}) copy-start(bf16[96,1536]{1,0:T(8,128)(2,1)S(1)} %collective-permute-done.3.refs_5_) | copy-start | bytes 884740
  13.0 34.1 %copy-start.15 = (bf16[96,1536]{1,0:T(8,128)(2,1)}, bf16[96,1536]{1,0:T(8,128)(2,1)S(1)}, u32[]{:S(2)}) copy-start(bf16[96,1536]{1,0:T(8,128)(2,1)S(1)} %get-tuple-element.39.refs_4_) | copy-start | bytes 884740
  13.0 31.5 %copy-start.22 = (s32[64,64]{1,0:T(8,128)S(1)}, s32[64,64]{1,0:T(8,128)}, u32[]{:S(2)}) copy-start(s32[64,64]{1,0:T(8,128)} %param.15) | copy-start | bytes 49156
  13.0 18.0 %collective-permute-start.4 = (bf16[96,1536]{1,0:T(8,128)(2,1)}, bf16[96,1536]{1,0:T(8,128)(2,1)}, u32[]{:S(2)}, u32[]{:S(2)}) collective-permute-start(bf16[96,1536]{1,0:T(8,128)(2,1)} %get-tuple-element.75), channel_id=1, source_target_pairs={{0,8},{8,0},{1,9},{9,1},{2,10},{10,2},{3,11},{11,3},{4,12},{12,4},... | collective-permute-start | bytes 884744 | tf_op jit(solution)/shard_map/ppermute | solution.py:27
  23.1 7.9 %collective-permute-start.5 = (bf16[96,1536]{1,0:T(8,128)(2,1)S(1)}, bf16[96,1536]{1,0:T(8,128)(2,1)S(1)}, u32[]{:S(2)}, u32[]{:S(2)}) collective-permute-start(bf16[96,1536]{1,0:T(8,128)(2,1)S(1)} %get-tuple-element.39.refs_4_), channel_id=1, source_target_pairs={{0,2},{2,0},{1,3},{3,1},{4,6},{6,4},{5,7},{7,5},{8,10},{10,8},{9,1... | collective-permute-start | bytes 884744 | tf_op jit(solution)/shard_map/ppermute | solution.py:27
  25.7 22.2 %copy-start.5 = (bf16[2,768,128]{2,1,0:T(8,128)(2,1)}, bf16[2,768,128]{2,1,0:T(8,128)(2,1)S(1)}, u32[]{:S(2)}) copy-start(bf16[2,768,128]{2,1,0:T(8,128)(2,1)S(1)} %get-tuple-element.37.refs_0_) | copy-start | bytes 1179652
  25.7 13.6 %collective-permute-start.2 = (bf16[2,768,128]{2,1,0:T(8,128)(2,1)S(1)}, bf16[2,768,128]{2,1,0:T(8,128)(2,1)}, u32[]{:S(2)}, u32[]{:S(2)}) collective-permute-start(bf16[2,768,128]{2,1,0:T(8,128)(2,1)S(1)} %get-tuple-element.41), channel_id=1, source_target_pairs={{0,4},{4,0},{1,5},{5,1},{2,6},{6,2},{3,7},{7,3},{8,12},{12,8},{9,1... | collective-permute-start | bytes 1179656 | tf_op jit(solution)/shard_map/ppermute | solution.py:27
  31.0 8.5 %collective-permute-start.6 = (bf16[96,1536]{1,0:T(8,128)(2,1)}, bf16[96,1536]{1,0:T(8,128)(2,1)}, u32[]{:S(2)}, u32[]{:S(2)}) collective-permute-start(bf16[96,1536]{1,0:T(8,128)(2,1)} %collective-permute-done.4.refs_8_), channel_id=1, source_target_pairs={{0,16},{16,0},{1,17},{17,1},{2,18},{18,2},{3,19},{19,3},{4,20},{20... | collective-permute-start | bytes 884744 | tf_op jit(solution)/shard_map/ppermute | solution.py:27
  32.7 9.9 %collective-permute-start.11 = (bf16[96,1536]{1,0:T(8,128)(2,1)}, bf16[96,1536]{1,0:T(8,128)(2,1)}, u32[]{:S(2)}, u32[]{:S(2)}) collective-permute-start(bf16[96,1536]{1,0:T(8,128)(2,1)} %collective-permute-done.4.refs_8_), channel_id=1, source_target_pairs={{0,2},{2,0},{1,3},{3,1},{4,6},{6,4},{5,7},{7,5},{8,10},{10,8},{9,1... | collective-permute-start | bytes 884744 | tf_op jit(solution)/shard_map/ppermute | solution.py:27
  34.8 13.8 %collective-permute-start.8 = (bf16[2,768,128]{2,1,0:T(8,128)(2,1)S(1)}, bf16[2,768,128]{2,1,0:T(8,128)(2,1)S(1)}, u32[]{:S(2)}, u32[]{:S(2)}) collective-permute-start(bf16[2,768,128]{2,1,0:T(8,128)(2,1)S(1)} %get-tuple-element.37.refs_0_), channel_id=1, source_target_pairs={{0,4},{4,0},{1,5},{5,1},{2,6},{6,2},{3,7},{7,3},{8,12},{12,8},{9,1... | collective-permute-start | bytes 1179656 | tf_op jit(solution)/shard_map/ppermute | solution.py:27
  39.4 12.2 %collective-permute-start.9 = (bf16[2,768,128]{2,1,0:T(8,128)(2,1)}, bf16[2,768,128]{2,1,0:T(8,128)(2,1)S(1)}, u32[]{:S(2)}, u32[]{:S(2)}) collective-permute-start(bf16[2,768,128]{2,1,0:T(8,128)(2,1)} %collective-permute-done.2), channel_id=1, source_target_pairs={{0,1},{1,0},{2,3},{3,2},{4,5},{5,4},{6,7},{7,6},{8,9},{9,8},{10,11... | collective-permute-start | bytes 1179656 | tf_op jit(solution)/shard_map/ppermute | solution.py:27
  39.4 12.2 %collective-permute-start.7 = (bf16[2,768,128]{2,1,0:T(8,128)(2,1)S(1)}, bf16[2,768,128]{2,1,0:T(8,128)(2,1)S(1)}, u32[]{:S(2)}, u32[]{:S(2)}) collective-permute-start(bf16[2,768,128]{2,1,0:T(8,128)(2,1)S(1)} %get-tuple-element.41), channel_id=1, source_target_pairs={{0,1},{1,0},{2,3},{3,2},{4,5},{5,4},{6,7},{7,6},{8,9},{9,8},{10,11... | collective-permute-start | bytes 1179656 | tf_op jit(solution)/shard_map/ppermute | solution.py:27
  40.0 9.9 %collective-permute-start.10 = (bf16[96,1536]{1,0:T(8,128)(2,1)S(1)}, bf16[96,1536]{1,0:T(8,128)(2,1)}, u32[]{:S(2)}, u32[]{:S(2)}) collective-permute-start(bf16[96,1536]{1,0:T(8,128)(2,1)S(1)} %collective-permute-done.3.refs_5_), channel_id=1, source_target_pairs={{0,2},{2,0},{1,3},{3,1},{4,6},{6,4},{5,7},{7,5},{8,10},{10,8},{9,1... | collective-permute-start | bytes 884744 | tf_op jit(solution)/shard_map/ppermute | solution.py:27
  42.7 9.0 %collective-permute-start.12 = (bf16[96,1536]{1,0:T(8,128)(2,1)}, bf16[96,1536]{1,0:T(8,128)(2,1)}, u32[]{:S(2)}, u32[]{:S(2)}) collective-permute-start(bf16[96,1536]{1,0:T(8,128)(2,1)} %collective-permute-done.11.refs_10_), channel_id=1, source_target_pairs={{0,16},{16,0},{1,17},{17,1},{2,18},{18,2},{3,19},{19,3},{4,20},{20... | collective-permute-start | bytes 884744 | tf_op jit(solution)/shard_map/ppermute | solution.py:27
  58.9 2.6 %collective-permute-start.13 = (bf16[256,1536]{1,0:T(8,128)(2,1)}, bf16[256,1536]{1,0:T(8,128)(2,1)S(1)}, u32[]{:S(2)}, u32[]{:S(2)}) collective-permute-start(bf16[256,1536]{1,0:T(8,128)(2,1)} %get-tuple-element.45), channel_id=1, source_target_pairs={{0,1},{1,0},{2,3},{3,2},{4,5},{5,4},{6,7},{7,6},{8,9},{9,8},{10,11... | collective-permute-start | bytes 2359304 | tf_op jit(solution)/shard_map/ppermute | solution.py:27
  62.4 5.2 %collective-permute-start.14 = (bf16[768,1536]{1,0:T(8,128)(2,1)}, bf16[768,1536]{1,0:T(8,128)(2,1)}, u32[]{:S(2)}, u32[]{:S(2)}) collective-permute-start(bf16[768,1536]{1,0:T(8,128)(2,1)} %get-tuple-element.47.mine_ref), channel_id=1, source_target_pairs={{0,1},{1,0},{2,3},{3,2},{4,5},{5,4},{6,7},{7,6},{8,9},{9,8},{10,11... | collective-permute-start | bytes 7077896 | tf_op jit(solution)/shard_map/ppermute | solution.py:27
  66.9 8.6 %collective-permute-start.19 = (bf16[256,1536]{1,0:T(8,128)(2,1)}, bf16[256,1536]{1,0:T(8,128)(2,1)}, u32[]{:S(2)}, u32[]{:S(2)}) collective-permute-start(bf16[256,1536]{1,0:T(8,128)(2,1)} %attention.1.grad_ref.refs_4_), channel_id=1, source_target_pairs={{0,1},{1,0},{2,3},{3,2},{4,5},{5,4},{6,7},{7,6},{8,9},{9,8},{10,11... | collective-permute-start | bytes 2359304 | tf_op jit(solution)/shard_map/ppermute | solution.py:27
  73.7 14.6 %collective-permute-start.15 = (bf16[128,1536]{1,0:T(8,128)(2,1)S(1)}, bf16[128,1536]{1,0:T(8,128)(2,1)S(1)}, u32[]{:S(2)}, u32[]{:S(2)}) collective-permute-start(bf16[128,1536]{1,0:T(8,128)(2,1)S(1)} %get-tuple-element.49), channel_id=1, source_target_pairs={{0,4},{4,0},{1,5},{5,1},{2,6},{6,2},{3,7},{7,3},{8,12},{12,8},{9,1... | collective-permute-start | bytes 1179656 | tf_op jit(solution)/shard_map/ppermute | solution.py:27
  79.4 8.8 %collective-permute-start.20 = (bf16[96,1536]{1,0:T(8,128)(2,1)S(1)}, bf16[96,1536]{1,0:T(8,128)(2,1)S(1)}, u32[]{:S(2)}, u32[]{:S(2)}) collective-permute-start(bf16[96,1536]{1,0:T(8,128)(2,1)S(1)} %get-tuple-element.56), channel_id=1, source_target_pairs={{0,2},{2,0},{1,3},{3,1},{4,6},{6,4},{5,7},{7,5},{8,10},{10,8},{9,1... | collective-permute-start | bytes 884744 | tf_op jit(solution)/shard_map/ppermute | solution.py:27
  81.8 14.5 %collective-permute-start.17 = (bf16[128,1536]{1,0:T(8,128)(2,1)S(1)}, bf16[128,1536]{1,0:T(8,128)(2,1)S(1)}, u32[]{:S(2)}, u32[]{:S(2)}) collective-permute-start(bf16[128,1536]{1,0:T(8,128)(2,1)S(1)} %get-tuple-element.51), channel_id=1, source_target_pairs={{0,4},{4,0},{1,5},{5,1},{2,6},{6,2},{3,7},{7,3},{8,12},{12,8},{9,1... | collective-permute-start | bytes 1179656 | tf_op jit(solution)/shard_map/ppermute | solution.py:27
  88.3 8.3 %collective-permute-start.21 = (bf16[96,1536]{1,0:T(8,128)(2,1)S(1)}, bf16[96,1536]{1,0:T(8,128)(2,1)S(1)}, u32[]{:S(2)}, u32[]{:S(2)}) collective-permute-start(bf16[96,1536]{1,0:T(8,128)(2,1)S(1)} %get-tuple-element.58), channel_id=1, source_target_pairs={{0,2},{2,0},{1,3},{3,1},{4,6},{6,4},{5,7},{7,5},{8,10},{10,8},{9,1... | collective-permute-start | bytes 884744 | tf_op jit(solution)/shard_map/ppermute | solution.py:27
  90.0 15.7 %collective-permute-start.23 = (bf16[96,1536]{1,0:T(8,128)(2,1)S(1)}, bf16[96,1536]{1,0:T(8,128)(2,1)S(1)}, u32[]{:S(2)}, u32[]{:S(2)}) collective-permute-start(bf16[96,1536]{1,0:T(8,128)(2,1)S(1)} %add_convert_fusion.5), channel_id=1, source_target_pairs={{0,8},{8,0},{1,9},{9,1},{2,10},{10,2},{3,11},{11,3},{4,12},{12,4},... | collective-permute-start | bytes 884744 | tf_op jit(solution)/shard_map/ppermute | solution.py:27
  96.3 35.2 %collective-permute-start.18 = (bf16[128,1536]{1,0:T(8,128)(2,1)S(1)}, bf16[128,1536]{1,0:T(8,128)(2,1)S(1)}, u32[]{:S(2)}, u32[]{:S(2)}) collective-permute-start(bf16[128,1536]{1,0:T(8,128)(2,1)S(1)} %add_convert_fusion), channel_id=1, source_target_pairs={{0,1},{1,2},{2,3},{3,4},{4,5},{5,6},{6,7},{7,8},{8,9},{9,10},{10,1... | collective-permute-start | bytes 1179656 | tf_op jit(solution)/shard_map/ppermute | solution.py:18
  96.6 18.6 %collective-permute-start.22 = (bf16[96,1536]{1,0:T(8,128)(2,1)S(1)}, bf16[96,1536]{1,0:T(8,128)(2,1)S(1)}, u32[]{:S(2)}, u32[]{:S(2)}) collective-permute-start(bf16[96,1536]{1,0:T(8,128)(2,1)S(1)} %get-tuple-element.59), channel_id=1, source_target_pairs={{0,2},{2,0},{1,3},{3,1},{4,6},{6,4},{5,7},{7,5},{8,10},{10,8},{9,1... | collective-permute-start | bytes 884744 | tf_op jit(solution)/shard_map/ppermute | solution.py:27
  100.0 18.6 %collective-permute-start.16 = (bf16[128,1536]{1,0:T(8,128)(2,1)S(1)}, bf16[128,1536]{1,0:T(8,128)(2,1)S(1)}, u32[]{:S(2)}, u32[]{:S(2)}) collective-permute-start(bf16[128,1536]{1,0:T(8,128)(2,1)S(1)} %add_convert_fusion.1), channel_id=1, source_target_pairs={{0,1},{1,2},{2,3},{3,4},{4,5},{5,6},{6,7},{7,8},{8,9},{9,10},{10,1... | collective-permute-start | bytes 1179656 | tf_op jit(solution)/shard_map/ppermute | solution.py:18
  115.2 16.2 %collective-permute-start.24 = (bf16[96,1536]{1,0:T(8,128)(2,1)S(1)}, bf16[96,1536]{1,0:T(8,128)(2,1)S(1)}, u32[]{:S(2)}, u32[]{:S(2)}) collective-permute-start(bf16[96,1536]{1,0:T(8,128)(2,1)S(1)} %add_convert_fusion.4), channel_id=1, source_target_pairs={{0,4},{4,0},{1,5},{5,1},{2,6},{6,2},{3,7},{7,3},{8,12},{12,8},{9,1... | collective-permute-start | bytes 884744 | tf_op jit(solution)/shard_map/ppermute | solution.py:27
  115.4 19.1 %collective-permute-start.25 = (bf16[96,1536]{1,0:T(8,128)(2,1)S(1)}, bf16[96,1536]{1,0:T(8,128)(2,1)S(1)}, u32[]{:S(2)}, u32[]{:S(2)}) collective-permute-start(bf16[96,1536]{1,0:T(8,128)(2,1)S(1)} %add_convert_fusion.3), channel_id=1, source_target_pairs={{0,8},{8,0},{1,9},{9,1},{2,10},{10,2},{3,11},{11,3},{4,12},{12,4},... | collective-permute-start | bytes 884744 | tf_op jit(solution)/shard_map/ppermute | solution.py:27
  122.3 13.7 %collective-permute-start.26 = (bf16[96,1536]{1,0:T(8,128)(2,1)S(1)}, bf16[96,1536]{1,0:T(8,128)(2,1)S(1)}, u32[]{:S(2)}, u32[]{:S(2)}) collective-permute-start(bf16[96,1536]{1,0:T(8,128)(2,1)S(1)} %get-tuple-element.67), channel_id=1, source_target_pairs={{0,2},{2,0},{1,3},{3,1},{4,6},{6,4},{5,7},{7,5},{8,10},{10,8},{9,1... | collective-permute-start | bytes 884744 | tf_op jit(solution)/shard_map/ppermute | solution.py:27
  (18 other events, 103.9 us)

commit v9 on v6

--- a/solution.py
+++ b/solution.py
@@ -119,7 +119,7 @@
         copies.append(pltpu.make_async_copy(piece, w_ref.at[rows, :], sems.at[i]))
     for j, source in enumerate(tiles):
         copies.append(pltpu.make_async_copy(source, tile_ref.at[j], sems.at[8 + j]))
-    for copy in copies:
+    for copy in copies[8:] + copies[:8]:
         copy.start()
     for j, at in enumerate((0, 2, 1, 3)):
         copies[8 + j].wait()
@@ -423,7 +423,7 @@
     theirs = swap(total_1, "near").astype(f32)
 
     back = (attended_own + arrived_back.astype(f32)).astype(jnp.bfloat16)
-    back = after(roll_back(back, shifts, levels, side, far_1), far_0)
+    back = after(roll_back(after(back, far_1), shifts, levels, side, ()), far_0)
     output = (values + back[:, :width].astype(f32)).astype(jnp.bfloat16)
     scaled = center * spread
     upstream = back[:, width:].astype(f32) * gain

time: 129 us -> 134 us (1.039)
  starting transfers between devices: 26.8 us -> 31.6 us
    ppermute x22, starting transfers between devices: 26.1 us -> 31 us  [swap(): return lax.ppermute(shard, axis, [(0, 1), (1, 0)])]
where the time goes in v9:
time: 134 us; the launch traced here: 133 us
  waiting for transfers between devices  62.1 us (46%)
  starting transfers between devices  31.6 us (24%)
  Pallas kernels  18.9 us (14%)
  local copies, waits for them, and re-layouts  7.6 us (6%)
  matrix products  6.87 us (5%)
  other arithmetic  5.29 us (4%)
    ppermute x22, waiting for transfers between devices, swap(): return lax.ppermute(shard, axis, [(0, 1), (1, 0)])  62.1 us
    ppermute x22, starting transfers between devices, swap(): return lax.ppermute(shard, axis, [(0, 1), (1, 0)])  31 us
    pallas_call x1, Pallas kernels, on_device(): kernel_call(products_kernel, (jax.ShapeDtypeStruct((2 * tile, 4 * part),...  5.78 us
    dot_general x1, matrix products, picked(): jnp.dot(onehot, both, preferred_element_type=jnp.float32)  4.22 us
    pallas_call x1, Pallas kernels, on_device(): kernel_call(functools.partial(attention_kernel, area, head), jax.ShapeDty...  4.12 us
    pallas_call x1, Pallas kernels, on_device(): kernel_call(outer_kernel, (jax.ShapeDtypeStruct((tile, 2 * width), f32),...  3.83 us
    unnamed x44, local copies, waits for them, and re-layouts  3.62 us
    pallas_call x1, Pallas kernels, on_device(): kernel_call(weights_kernel, [jax.ShapeDtypeStruct((own_rows, 4 * part), b...  2.75 us
  transfers between devices with their start and end apart: 25, of which 13 were waited for; matrix products, arithmetic and copies ran while one was open for 10% of the time, Pallas kernels for 10%

profile of v9, /device:TPU:6, one launch (start us, length us, event | category | flops | bytes accessed | tf_op | source)
XLA Modules:
  0.0 133.4 jit_solution(10767394209872995173)
XLA Ops:
  0.7 1.3 fusion.81
  2.0 1.6 %collective-permute-start.3 = (bf16[96,1536]{1,0:T(8,128)(2,1)S(1)}, bf16[96,1536]{1,0:T(8,128)(2,1)S(1)}, u32[]{:S(2)}, u32[]{:S(2)}) collective-permute-start(bf16[96,1536]{1,0:T(8,128)(2,1)S(1)} %broadcast_select_fusion), channel_id=1, source_target_pairs={{0,4},{4,0},{1,5},{5,1},{2,6},{6,2},{3,7},{7,3},{8,12},{12,8},{9,1... | collective-permute-start | bytes 884744 | tf_op jit(solution)/shard_map/ppermute | solution.py:27
  4.7 6.1 %collective-permute-done.3.refs_5_ = bf16[96,1536]{1,0:T(8,128)(2,1)S(1)} collective-permute-done((bf16[96,1536]{1,0:T(8,128)(2,1)S(1)}, bf16[96,1536]{1,0:T(8,128)(2,1)S(1)}, u32[]{:S(2)}, u32[]{:S(2)}) %collective-permute-start.3) | collective-permute-done | bytes 294944 | tf_op jit(solution)/shard_map/ppermute | solution.py:27
  11.7 2.6 %collective-permute-start.4 = (bf16[96,1536]{1,0:T(8,128)(2,1)}, bf16[96,1536]{1,0:T(8,128)(2,1)}, u32[]{:S(2)}, u32[]{:S(2)}) collective-permute-start(bf16[96,1536]{1,0:T(8,128)(2,1)} %get-tuple-element.69), channel_id=1, source_target_pairs={{0,8},{8,0},{1,9},{9,1},{2,10},{10,2},{3,11},{11,3},{4,12},{12,4},... | collective-permute-start | bytes 884744 | tf_op jit(solution)/shard_map/ppermute | solution.py:27
  14.3 7.8 %collective-permute-start.5 = (bf16[96,1536]{1,0:T(8,128)(2,1)S(1)}, bf16[96,1536]{1,0:T(8,128)(2,1)S(1)}, u32[]{:S(2)}, u32[]{:S(2)}) collective-permute-start(bf16[96,1536]{1,0:T(8,128)(2,1)S(1)} %get-tuple-element.36.refs_4_), channel_id=1, source_target_pairs={{0,2},{2,0},{1,3},{3,1},{4,6},{6,4},{5,7},{7,5},{8,10},{10,8},{9,1... | collective-permute-start | bytes 884744 | tf_op jit(solution)/shard_map/ppermute | solution.py:27
  22.3 2.4 %turned_rolls.1 = (bf16[2,768,128]{2,1,0:T(8,128)(2,1)S(1)}, bf16[2,768,128]{2,1,0:T(8,128)(2,1)S(1)}) custom-call(s32[20]{0:T(128)S(1)} %concatenate.15.info_ref, f32[1,1536]{1,0:T(1,128)S(1)} %reshape.97.gain_ref, bf16[128,1536]{1,0:T(8,128)(2,1)S(1)} %bitcast.49, bf16[128,1536]{1,0:T(8,128)(2,1)S(1)} %collective-permute-done.refs_1_, ...), custom_call_target="tpu_custom_call" | custom-call | flops 201326592 | bytes 3000000 | tf_op jit(solution)/shard_map/turned_rolls/pallas_call | solution.py:305
  24.8 2.3 %collective-permute-done.4.refs_8_ = bf16[96,1536]{1,0:T(8,128)(2,1)} collective-permute-done((bf16[96,1536]{1,0:T(8,128)(2,1)}, bf16[96,1536]{1,0:T(8,128)(2,1)}, u32[]{:S(2)}, u32[]{:S(2)}) %collective-permute-start.4) | collective-permute-done | bytes 294944 | tf_op jit(solution)/shard_map/ppermute | solution.py:27
  27.2 2.7 %collective-permute-done.5.refs_6_ = bf16[96,1536]{1,0:T(8,128)(2,1)S(1)} collective-permute-done((bf16[96,1536]{1,0:T(8,128)(2,1)S(1)}, bf16[96,1536]{1,0:T(8,128)(2,1)S(1)}, u32[]{:S(2)}, u32[]{:S(2)}) %collective-permute-start.5) | collective-permute-done | bytes 294944 | tf_op jit(solution)/shard_map/ppermute | solution.py:27
  31.0 3.2 %collective-permute-start.8 = (bf16[2,768,128]{2,1,0:T(8,128)(2,1)S(1)}, bf16[2,768,128]{2,1,0:T(8,128)(2,1)S(1)}, u32[]{:S(2)}, u32[]{:S(2)}) collective-permute-start(bf16[2,768,128]{2,1,0:T(8,128)(2,1)S(1)} %get-tuple-element.34.refs_0_), channel_id=1, source_target_pairs={{0,4},{4,0},{1,5},{5,1},{2,6},{6,2},{3,7},{7,3},{8,12},{12,8},{9,1... | collective-permute-start | bytes 1179656 | tf_op jit(solution)/shard_map/ppermute | solution.py:27
  34.2 2.3 %collective-permute-done.2 = bf16[2,768,128]{2,1,0:T(8,128)(2,1)} collective-permute-done((bf16[2,768,128]{2,1,0:T(8,128)(2,1)S(1)}, bf16[2,768,128]{2,1,0:T(8,128)(2,1)}, u32[]{:S(2)}, u32[]{:S(2)}) %collective-permute-start.2) | collective-permute-done | bytes 393248 | tf_op jit(solution)/shard_map/ppermute | solution.py:27
  36.4 2.8 %collective-permute-done.6.refs_9_ = bf16[96,1536]{1,0:T(8,128)(2,1)} collective-permute-done((bf16[96,1536]{1,0:T(8,128)(2,1)}, bf16[96,1536]{1,0:T(8,128)(2,1)}, u32[]{:S(2)}, u32[]{:S(2)}) %collective-permute-start.6) | collective-permute-done | bytes 294944 | tf_op jit(solution)/shard_map/ppermute | solution.py:27
  40.0 1.2 collective-permute-start.12
  41.2 2.6 %fusion.7 = f32[2,6,64,64]{3,1,2,0:T(8,128)S(1)} fusion(s32[64,64]{1,0:T(8,128)S(1)} %copy-done.21, pred[2,64,64]{2,1,0:T(8,128)(4,1)S(1)} %broadcast_compare_fusion, f32[2,225,6]{1,0,2:T(2,128)S(1)} %constant_dynamic-slice_fusion), kind=kOutput, calls=%fused_computation.9 | convolution fusion | flops 133681152 | bytes 231984 | tf_op jit(solution)/shard_map/qkr,lrh->lhqk/dot_general | solution.py:340
  45.4 3.6 %collective-permute-done.10.refs_7_ = bf16[96,1536]{1,0:T(8,128)(2,1)} collective-permute-done((bf16[96,1536]{1,0:T(8,128)(2,1)S(1)}, bf16[96,1536]{1,0:T(8,128)(2,1)}, u32[]{:S(2)}, u32[]{:S(2)}) %collective-permute-start.10) | collective-permute-done | bytes 294944 | tf_op jit(solution)/shard_map/ppermute | solution.py:27
  50.8 5.8 %products.1 = (bf16[256,1536]{1,0:T(8,128)(2,1)}, bf16[256,1536]{1,0:T(8,128)(2,1)}, bf16[768,1536]{1,0:T(8,128)(2,1)}) custom-call(s32[8]{0:T(128)} %stack.120.place_ref, bf16[2,768,128]{2,1,0:T(8,128)(2,1)} %copy-done.4, bf16[2,768,128]{2,1,0:T(8,128)(2,1)} %copy-done.10, bf16[2,768,128]{2,1,0:T(8,128)(2,1)} %copy-done.6, bf16[2,768,128]{2,1,0:T(8,128)(2,1)} %copy-done.8, ...), custom_call_target="tpu_custom_call" | custom-call | flops 1200000000 | bytes 9000000 | tf_op jit(solution)/shard_map/products/pallas_call | solution.py:348
  56.7 2.5 %collective-permute-done.13.came_ref = bf16[256,1536]{1,0:T(8,128)(2,1)S(1)} collective-permute-done((bf16[256,1536]{1,0:T(8,128)(2,1)}, bf16[256,1536]{1,0:T(8,128)(2,1)S(1)}, u32[]{:S(2)}, u32[]{:S(2)}) %collective-permute-start.13) | collective-permute-done | bytes 786464 | tf_op jit(solution)/shard_map/ppermute | solution.py:27
  60.3 4.1 %attention.1.grad_ref.refs_4_ = bf16[256,1536]{1,0:T(8,128)(2,1)} custom-call(bf16[256,1536]{1,0:T(8,128)(2,1)} %get-tuple-element.41.kept_ref, bf16[256,1536]{1,0:T(8,128)(2,1)} %copy-done.19, f32[2,3,128,64]{3,2,1,0:T(8,128)} %bitcast.52), custom_call_target="tpu_custom_call" | custom-call | flops 1000000000 | bytes 4000000 | tf_op jit(solution)/shard_map/attention/pallas_call | solution.py:369
  65.7 1.1 copy-done.3
  66.8 3.8 %projections.1 = (f32[128,3072]{1,0:T(8,128)S(1)}, bf16[128,3072]{1,0:T(8,128)(2,1)S(1)}) custom-call(s32[16]{0:T(128)S(1)} %stack.111.place_ref, bf16[256,1536]{1,0:T(8,128)(2,1)S(1)} %copy-done.3, bf16[768,1536]{1,0:T(8,128)(2,1)S(1)} %copy-done.1, bf16[768,1536]{1,0:T(8,128)(2,1)S(1)} %collective-permute-done.14.theirs_ref), custom_call_target="tpu_custom_call" | custom-call | flops 1200000000 | bytes 8000000 | tf_op jit(solution)/shard_map/projections/pallas_call | solution.py:382
  70.7 2.8 %collective-permute-start.15 = (bf16[128,3072]{1,0:T(8,128)(2,1)S(1)}, bf16[128,3072]{1,0:T(8,128)(2,1)S(1)}, u32[]{:S(2)}, u32[]{:S(2)}) collective-permute-start(bf16[128,3072]{1,0:T(8,128)(2,1)S(1)} %get-tuple-element.46), channel_id=1, source_target_pairs={{0,4},{4,0},{1,5},{5,1},{2,6},{6,2},{3,7},{7,3},{8,12},{12,8},{9,1... | collective-permute-start | bytes 2359304 | tf_op jit(solution)/shard_map/ppermute | solution.py:27
  73.5 2.7 %weight_gradient.1 = (bf16[96,1536]{1,0:T(8,128)(2,1)S(1)}, bf16[96,1536]{1,0:T(8,128)(2,1)S(1)}, bf16[96,1536]{1,0:T(8,128)(2,1)S(1)}, bf16[96,1536]{1,0:T(8,12...) custom-call(s32[1]{0:T(128)} %bitcast.34.near_ref, ...), custom_call_target="tpu_custom_call" | custom-call | flops 1200000000 | bytes 6000000 | tf_op jit(solution)/shard_map/weight_gradient/pallas_call | solution.py:396
  76.7 8.4 %collective-permute-done.17 = bf16[96,1536]{1,0:T(8,128)(2,1)S(1)} collective-permute-done((bf16[96,1536]{1,0:T(8,128)(2,1)S(1)}, bf16[96,1536]{1,0:T(8,128)(2,1)S(1)}, u32[]{:S(2)}, u32[]{:S(2)}) %collective-permute-start.17) | collective-permute-done | bytes 294944 | tf_op jit(solution)/shard_map/ppermute | solution.py:27
  85.6 3.4 %collective-permute-start.18 = (bf16[96,1536]{1,0:T(8,128)(2,1)S(1)}, bf16[96,1536]{1,0:T(8,128)(2,1)S(1)}, u32[]{:S(2)}, u32[]{:S(2)}) collective-permute-start(bf16[96,1536]{1,0:T(8,128)(2,1)S(1)} %add_convert_fusion.4), channel_id=1, source_target_pairs={{0,8},{8,0},{1,9},{9,1},{2,10},{10,2},{3,11},{11,3},{4,12},{12,4},... | collective-permute-start | bytes 884744 | tf_op jit(solution)/shard_map/ppermute | solution.py:27
  89.0 4.0 %collective-permute-done.20 = bf16[96,1536]{1,0:T(8,128)(2,1)S(1)} collective-permute-done((bf16[96,1536]{1,0:T(8,128)(2,1)S(1)}, bf16[96,1536]{1,0:T(8,128)(2,1)S(1)}, u32[]{:S(2)}, u32[]{:S(2)}) %collective-permute-start.20) | collective-permute-done | bytes 294944 | tf_op jit(solution)/shard_map/ppermute | solution.py:27
  93.4 3.6 %collective-permute-done.15 = bf16[128,3072]{1,0:T(8,128)(2,1)S(1)} collective-permute-done((bf16[128,3072]{1,0:T(8,128)(2,1)S(1)}, bf16[128,3072]{1,0:T(8,128)(2,1)S(1)}, u32[]{:S(2)}, u32[]{:S(2)}) %collective-permute-start.15) | collective-permute-done | bytes 786464 | tf_op jit(solution)/shard_map/ppermute | solution.py:27
  97.1 4.1 %collective-permute-done.18 = bf16[96,1536]{1,0:T(8,128)(2,1)S(1)} collective-permute-done((bf16[96,1536]{1,0:T(8,128)(2,1)S(1)}, bf16[96,1536]{1,0:T(8,128)(2,1)S(1)}, u32[]{:S(2)}, u32[]{:S(2)}) %collective-permute-start.18) | collective-permute-done | bytes 294944 | tf_op jit(solution)/shard_map/ppermute | solution.py:27
  101.5 3.3 %collective-permute-start.21 = (bf16[96,1536]{1,0:T(8,128)(2,1)S(1)}, bf16[96,1536]{1,0:T(8,128)(2,1)S(1)}, u32[]{:S(2)}, u32[]{:S(2)}) collective-permute-start(bf16[96,1536]{1,0:T(8,128)(2,1)S(1)} %add_convert_fusion.3), channel_id=1, source_target_pairs={{0,8},{8,0},{1,9},{9,1},{2,10},{10,2},{3,11},{11,3},{4,12},{12,4},... | collective-permute-start | bytes 884744 | tf_op jit(solution)/shard_map/ppermute | solution.py:27
  105.0 1.7 %collective-permute-start.23 = (bf16[96,1536]{1,0:T(8,128)(2,1)S(1)}, bf16[96,1536]{1,0:T(8,128)(2,1)S(1)}, u32[]{:S(2)}, u32[]{:S(2)}) collective-permute-start(bf16[96,1536]{1,0:T(8,128)(2,1)S(1)} %get-tuple-element.60), channel_id=1, source_target_pairs={{0,2},{2,0},{1,3},{3,1},{4,6},{6,4},{5,7},{7,5},{8,10},{10,8},{9,1... | collective-permute-start | bytes 884744 | tf_op jit(solution)/shard_map/ppermute | solution.py:27
  106.8 19.2 %collective-permute-done.24 = bf16[96,1536]{1,0:T(8,128)(2,1)S(1)} collective-permute-done((bf16[96,1536]{1,0:T(8,128)(2,1)S(1)}, bf16[96,1536]{1,0:T(8,128)(2,1)S(1)}, u32[]{:S(2)}, u32[]{:S(2)}) %collective-permute-start.24) | collective-permute-done | bytes 294944 | tf_op jit(solution)/shard_map/ppermute | solution.py:27
  126.0 4.2 %convolution_convert_fusion = bf16[128,3072]{1,0:T(8,128)(2,1)S(1)} fusion(bf16[128,3072]{1,0:T(8,128)(2,1)S(1)} %add_convert_fusion, bf16[128,3072]{1,0:T(8,128)(2,1)} %collective-permute-done.19, s32[]{:T(128)} %bitcast.4, s32[]{:T(128)} %bitcast.3, s32[128]{0:T(128)S(1)} %get-tuple-element.93, s32[128]{0:T(128)S(1)} %get-tuple-element.95, s32[]{:T(128)} %bitcast.2, ...), kind=kOutput, calls=%fused_computation.3 | convolution fusion | flops 206700544 | bytes 2362768 | tf_op jit(solution)/shard_map/dot_general | solution.py:52
  130.6 1.4 %fusion.18 = (bf16[128,1536]{1,0:T(8,128)(2,1)}, bf16[128,1536]{1,0:T(8,128)(2,1)}) fusion(f32[128]{0:T(128)S(1)} %broadcast_multiply_fusion.2, f32[128]{0:T(128)S(1)} %div.55, f32[128]{0:T(128)S(1)} %broadcast_multiply_fusion.3, f32[1536]{0:T(1024)S(1)} %copy-done.15, f32[128]{0:T(128)S(1)} %rsqrt.12, bf16[128,3072]{1,0:T(8,128)(2,1)S(1)} %convolution_convert_fusion, ...), kind=kLoop, calls=%fused_computation.22 | loop fusion | flops 2949120 | bytes 2367488 | tf_op jit(solution)/shard_map/convert_element_type | solution.py:435
  132.3 1.1 broadcast_multiply_fusion
  (118 shorter events, 12.2 us)
Async XLA Ops:
  0.6 40.6 %copy-start = (f32[2,225,12]{1,0,2:T(2,128)S(1)}, f32[2,225,12]{1,0,2:T(2,128)}, u32[]{:S(2)}) copy-start(f32[2,225,12]{1,0,2:T(2,128)} %param.16) | copy-start | bytes 64804
  2.0 8.8 %collective-permute-start.3 = (bf16[96,1536]{1,0:T(8,128)(2,1)S(1)}, bf16[96,1536]{1,0:T(8,128)(2,1)S(1)}, u32[]{:S(2)}, u32[]{:S(2)}) collective-permute-start(bf16[96,1536]{1,0:T(8,128)(2,1)S(1)} %broadcast_select_fusion), channel_id=1, source_target_pairs={{0,4},{4,0},{1,5},{5,1},{2,6},{6,2},{3,7},{7,3},{8,12},{12,8},{9,1... | collective-permute-start | bytes 884744 | tf_op jit(solution)/shard_map/ppermute | solution.py:27
  3.9 18.3 %copy-start.18 = (s32[2,2]{1,0:T(2,128)S(1)}, s32[2,2]{1,0:T(2,128)}, u32[]{:S(2)}) copy-start(s32[2,2]{1,0:T(2,128)} %param.14) | copy-start | bytes 52
  3.9 18.4 %copy-start.15 = (f32[1536]{0:T(1024)S(1)}, f32[1536]{0:T(1024)}, u32[]{:S(2)}) copy-start(f32[1536]{0:T(1024)} %param.12) | copy-start | bytes 18436
  4.1 10.2 %collective-permute-start = (bf16[128,1536]{1,0:T(8,128)(2,1)S(1)}, bf16[128,1536]{1,0:T(8,128)(2,1)S(1)}, u32[]{:S(2)}, u32[]{:S(2)}) collective-permute-start(bf16[128,1536]{1,0:T(8,128)(2,1)S(1)} %bitcast.48), channel_id=1, source_target_pairs={{0,15},{1,0},{2,1},{3,2},{4,3},{5,4},{6,5},{7,6},{8,7},{9,8},{10,9... | collective-permute-start | bytes 1179656 | tf_op jit(solution)/shard_map/ppermute | solution.py:18
  4.1 10.2 %collective-permute-start.1 = (bf16[128,1536]{1,0:T(8,128)(2,1)S(1)}, bf16[128,1536]{1,0:T(8,128)(2,1)S(1)}, u32[]{:S(2)}, u32[]{:S(2)}) collective-permute-start(bf16[128,1536]{1,0:T(8,128)(2,1)S(1)} %bitcast.50), channel_id=1, source_target_pairs={{0,15},{1,0},{2,1},{3,2},{4,3},{5,4},{6,5},{7,6},{8,7},{9,8},{10,9... | collective-permute-start | bytes 1179656 | tf_op jit(solution)/shard_map/ppermute | solution.py:18
  10.9 29.0 %copy-start.13 = (bf16[96,1536]{1,0:T(8,128)(2,1)}, bf16[96,1536]{1,0:T(8,128)(2,1)S(1)}, u32[]{:S(2)}) copy-start(bf16[96,1536]{1,0:T(8,128)(2,1)S(1)} %collective-permute-done.3.refs_5_) | copy-start | bytes 884740
  11.7 32.2 %copy-start.14 = (bf16[96,1536]{1,0:T(8,128)(2,1)}, bf16[96,1536]{1,0:T(8,128)(2,1)S(1)}, u32[]{:S(2)}) copy-start(bf16[96,1536]{1,0:T(8,128)(2,1)S(1)} %get-tuple-element.36.refs_4_) | copy-start | bytes 884740
  11.7 29.5 %copy-start.21 = (s32[64,64]{1,0:T(8,128)S(1)}, s32[64,64]{1,0:T(8,128)}, u32[]{:S(2)}) copy-start(s32[64,64]{1,0:T(8,128)} %param.15) | copy-start | bytes 49156
  11.7 15.5 %collective-permute-start.4 = (bf16[96,1536]{1,0:T(8,128)(2,1)}, bf16[96,1536]{1,0:T(8,128)(2,1)}, u32[]{:S(2)}, u32[]{:S(2)}) collective-permute-start(bf16[96,1536]{1,0:T(8,128)(2,1)} %get-tuple-element.69), channel_id=1, source_target_pairs={{0,8},{8,0},{1,9},{9,1},{2,10},{10,2},{3,11},{11,3},{4,12},{12,4},... | collective-permute-start | bytes 884744 | tf_op jit(solution)/shard_map/ppermute | solution.py:27
  14.3 15.6 %collective-permute-start.5 = (bf16[96,1536]{1,0:T(8,128)(2,1)S(1)}, bf16[96,1536]{1,0:T(8,128)(2,1)S(1)}, u32[]{:S(2)}, u32[]{:S(2)}) collective-permute-start(bf16[96,1536]{1,0:T(8,128)(2,1)S(1)} %get-tuple-element.36.refs_4_), channel_id=1, source_target_pairs={{0,2},{2,0},{1,3},{3,1},{4,6},{6,4},{5,7},{7,5},{8,10},{10,8},{9,1... | collective-permute-start | bytes 884744 | tf_op jit(solution)/shard_map/ppermute | solution.py:27
  24.7 20.0 %copy-start.4 = (bf16[2,768,128]{2,1,0:T(8,128)(2,1)}, bf16[2,768,128]{2,1,0:T(8,128)(2,1)S(1)}, u32[]{:S(2)}) copy-start(bf16[2,768,128]{2,1,0:T(8,128)(2,1)S(1)} %get-tuple-element.34.refs_0_) | copy-start | bytes 1179652
  24.8 11.7 %collective-permute-start.2 = (bf16[2,768,128]{2,1,0:T(8,128)(2,1)S(1)}, bf16[2,768,128]{2,1,0:T(8,128)(2,1)}, u32[]{:S(2)}, u32[]{:S(2)}) collective-permute-start(bf16[2,768,128]{2,1,0:T(8,128)(2,1)S(1)} %get-tuple-element.38), channel_id=1, source_target_pairs={{0,4},{4,0},{1,5},{5,1},{2,6},{6,2},{3,7},{7,3},{8,12},{12,8},{9,1... | collective-permute-start | bytes 1179656 | tf_op jit(solution)/shard_map/ppermute | solution.py:27
  29.9 9.4 %collective-permute-start.6 = (bf16[96,1536]{1,0:T(8,128)(2,1)}, bf16[96,1536]{1,0:T(8,128)(2,1)}, u32[]{:S(2)}, u32[]{:S(2)}) collective-permute-start(bf16[96,1536]{1,0:T(8,128)(2,1)} %collective-permute-done.4.refs_8_), channel_id=1, source_target_pairs={{0,16},{16,0},{1,17},{17,1},{2,18},{18,2},{3,19},{19,3},{4,20},{20... | collective-permute-start | bytes 884744 | tf_op jit(solution)/shard_map/ppermute | solution.py:27
  30.2 9.7 %collective-permute-start.11 = (bf16[96,1536]{1,0:T(8,128)(2,1)}, bf16[96,1536]{1,0:T(8,128)(2,1)}, u32[]{:S(2)}, u32[]{:S(2)}) collective-permute-start(bf16[96,1536]{1,0:T(8,128)(2,1)} %collective-permute-done.4.refs_8_), channel_id=1, source_target_pairs={{0,2},{2,0},{1,3},{3,1},{4,6},{6,4},{5,7},{7,5},{8,10},{10,8},{9,1... | collective-permute-start | bytes 884744 | tf_op jit(solution)/shard_map/ppermute | solution.py:27
  31.0 14.4 %collective-permute-start.8 = (bf16[2,768,128]{2,1,0:T(8,128)(2,1)S(1)}, bf16[2,768,128]{2,1,0:T(8,128)(2,1)S(1)}, u32[]{:S(2)}, u32[]{:S(2)}) collective-permute-start(bf16[2,768,128]{2,1,0:T(8,128)(2,1)S(1)} %get-tuple-element.34.refs_0_), channel_id=1, source_target_pairs={{0,4},{4,0},{1,5},{5,1},{2,6},{6,2},{3,7},{7,3},{8,12},{12,8},{9,1... | collective-permute-start | bytes 1179656 | tf_op jit(solution)/shard_map/ppermute | solution.py:27
  39.3 10.0 %collective-permute-start.9 = (bf16[2,768,128]{2,1,0:T(8,128)(2,1)}, bf16[2,768,128]{2,1,0:T(8,128)(2,1)S(1)}, u32[]{:S(2)}, u32[]{:S(2)}) collective-permute-start(bf16[2,768,128]{2,1,0:T(8,128)(2,1)} %collective-permute-done.2), channel_id=1, source_target_pairs={{0,1},{1,0},{2,3},{3,2},{4,5},{5,4},{6,7},{7,6},{8,9},{9,8},{10,11... | collective-permute-start | bytes 1179656 | tf_op jit(solution)/shard_map/ppermute | solution.py:27
  39.3 10.0 %collective-permute-start.7 = (bf16[2,768,128]{2,1,0:T(8,128)(2,1)S(1)}, bf16[2,768,128]{2,1,0:T(8,128)(2,1)S(1)}, u32[]{:S(2)}, u32[]{:S(2)}) collective-permute-start(bf16[2,768,128]{2,1,0:T(8,128)(2,1)S(1)} %get-tuple-element.38), channel_id=1, source_target_pairs={{0,1},{1,0},{2,3},{3,2},{4,5},{5,4},{6,7},{7,6},{8,9},{9,8},{10,11... | collective-permute-start | bytes 1179656 | tf_op jit(solution)/shard_map/ppermute | solution.py:27
  39.9 9.1 %collective-permute-start.10 = (bf16[96,1536]{1,0:T(8,128)(2,1)S(1)}, bf16[96,1536]{1,0:T(8,128)(2,1)}, u32[]{:S(2)}, u32[]{:S(2)}) collective-permute-start(bf16[96,1536]{1,0:T(8,128)(2,1)S(1)} %collective-permute-done.3.refs_5_), channel_id=1, source_target_pairs={{0,2},{2,0},{1,3},{3,1},{4,6},{6,4},{5,7},{7,5},{8,10},{10,8},{9,1... | collective-permute-start | bytes 884744 | tf_op jit(solution)/shard_map/ppermute | solution.py:27
  40.0 9.3 %collective-permute-start.12 = (bf16[96,1536]{1,0:T(8,128)(2,1)}, bf16[96,1536]{1,0:T(8,128)(2,1)}, u32[]{:S(2)}, u32[]{:S(2)}) collective-permute-start(bf16[96,1536]{1,0:T(8,128)(2,1)} %collective-permute-done.11.refs_10_), channel_id=1, source_target_pairs={{0,16},{16,0},{1,17},{17,1},{2,18},{18,2},{3,19},{19,3},{4,20},{20... | collective-permute-start | bytes 884744 | tf_op jit(solution)/shard_map/ppermute | solution.py:27
  56.6 2.6 %collective-permute-start.13 = (bf16[256,1536]{1,0:T(8,128)(2,1)}, bf16[256,1536]{1,0:T(8,128)(2,1)S(1)}, u32[]{:S(2)}, u32[]{:S(2)}) collective-permute-start(bf16[256,1536]{1,0:T(8,128)(2,1)} %get-tuple-element.42), channel_id=1, source_target_pairs={{0,1},{1,0},{2,3},{3,2},{4,5},{5,4},{6,7},{7,6},{8,9},{9,8},{10,11... | collective-permute-start | bytes 2359304 | tf_op jit(solution)/shard_map/ppermute | solution.py:27
  60.1 5.6 %collective-permute-start.14 = (bf16[768,1536]{1,0:T(8,128)(2,1)}, bf16[768,1536]{1,0:T(8,128)(2,1)S(1)}, u32[]{:S(2)}, u32[]{:S(2)}) collective-permute-start(bf16[768,1536]{1,0:T(8,128)(2,1)} %get-tuple-element.44.mine_ref), channel_id=1, source_target_pairs={{0,1},{1,0},{2,3},{3,2},{4,5},{5,4},{6,7},{7,6},{8,9},{9,8},{10,11... | collective-permute-start | bytes 7077896 | tf_op jit(solution)/shard_map/ppermute | solution.py:27
  64.4 9.1 %collective-permute-start.16 = (bf16[256,1536]{1,0:T(8,128)(2,1)}, bf16[256,1536]{1,0:T(8,128)(2,1)S(1)}, u32[]{:S(2)}, u32[]{:S(2)}) collective-permute-start(bf16[256,1536]{1,0:T(8,128)(2,1)} %attention.1.grad_ref.refs_4_), channel_id=1, source_target_pairs={{0,1},{1,0},{2,3},{3,2},{4,5},{5,4},{6,7},{7,6},{8,9},{9,8},{10,11... | collective-permute-start | bytes 2359304 | tf_op jit(solution)/shard_map/ppermute | solution.py:27
  70.7 26.3 %collective-permute-start.15 = (bf16[128,3072]{1,0:T(8,128)(2,1)S(1)}, bf16[128,3072]{1,0:T(8,128)(2,1)S(1)}, u32[]{:S(2)}, u32[]{:S(2)}) collective-permute-start(bf16[128,3072]{1,0:T(8,128)(2,1)S(1)} %get-tuple-element.46), channel_id=1, source_target_pairs={{0,4},{4,0},{1,5},{5,1},{2,6},{6,2},{3,7},{7,3},{8,12},{12,8},{9,1... | collective-permute-start | bytes 2359304 | tf_op jit(solution)/shard_map/ppermute | solution.py:27
  76.3 8.8 %collective-permute-start.17 = (bf16[96,1536]{1,0:T(8,128)(2,1)S(1)}, bf16[96,1536]{1,0:T(8,128)(2,1)S(1)}, u32[]{:S(2)}, u32[]{:S(2)}) collective-permute-start(bf16[96,1536]{1,0:T(8,128)(2,1)S(1)} %get-tuple-element.49), channel_id=1, source_target_pairs={{0,2},{2,0},{1,3},{3,1},{4,6},{6,4},{5,7},{7,5},{8,10},{10,8},{9,1... | collective-permute-start | bytes 884744 | tf_op jit(solution)/shard_map/ppermute | solution.py:27
  85.1 7.9 %collective-permute-start.20 = (bf16[96,1536]{1,0:T(8,128)(2,1)S(1)}, bf16[96,1536]{1,0:T(8,128)(2,1)S(1)}, u32[]{:S(2)}, u32[]{:S(2)}) collective-permute-start(bf16[96,1536]{1,0:T(8,128)(2,1)S(1)} %get-tuple-element.53), channel_id=1, source_target_pairs={{0,2},{2,0},{1,3},{3,1},{4,6},{6,4},{5,7},{7,5},{8,10},{10,8},{9,1... | collective-permute-start | bytes 884744 | tf_op jit(solution)/shard_map/ppermute | solution.py:27
  85.6 15.7 %collective-permute-start.18 = (bf16[96,1536]{1,0:T(8,128)(2,1)S(1)}, bf16[96,1536]{1,0:T(8,128)(2,1)S(1)}, u32[]{:S(2)}, u32[]{:S(2)}) collective-permute-start(bf16[96,1536]{1,0:T(8,128)(2,1)S(1)} %add_convert_fusion.4), channel_id=1, source_target_pairs={{0,8},{8,0},{1,9},{9,1},{2,10},{10,2},{3,11},{11,3},{4,12},{12,4},... | collective-permute-start | bytes 884744 | tf_op jit(solution)/shard_map/ppermute | solution.py:27
  93.0 8.2 %collective-permute-start.22 = (bf16[96,1536]{1,0:T(8,128)(2,1)S(1)}, bf16[96,1536]{1,0:T(8,128)(2,1)S(1)}, u32[]{:S(2)}, u32[]{:S(2)}) collective-permute-start(bf16[96,1536]{1,0:T(8,128)(2,1)S(1)} %get-tuple-element.59), channel_id=1, source_target_pairs={{0,2},{2,0},{1,3},{3,1},{4,6},{6,4},{5,7},{7,5},{8,10},{10,8},{9,1... | collective-permute-start | bytes 884744 | tf_op jit(solution)/shard_map/ppermute | solution.py:27
  101.3 24.8 %collective-permute-start.19 = (bf16[128,3072]{1,0:T(8,128)(2,1)S(1)}, bf16[128,3072]{1,0:T(8,128)(2,1)}, u32[]{:S(2)}, u32[]{:S(2)}) collective-permute-start(bf16[128,3072]{1,0:T(8,128)(2,1)S(1)} %add_convert_fusion), channel_id=1, source_target_pairs={{0,1},{1,2},{2,3},{3,4},{4,5},{5,6},{6,7},{7,8},{8,9},{9,10},{10,1... | collective-permute-start | bytes 2359304 | tf_op jit(solution)/shard_map/ppermute | solution.py:18
  101.4 24.6 %collective-permute-start.24 = (bf16[96,1536]{1,0:T(8,128)(2,1)S(1)}, bf16[96,1536]{1,0:T(8,128)(2,1)S(1)}, u32[]{:S(2)}, u32[]{:S(2)}) collective-permute-start(bf16[96,1536]{1,0:T(8,128)(2,1)S(1)} %add_convert_fusion.2), channel_id=1, source_target_pairs={{0,4},{4,0},{1,5},{5,1},{2,6},{6,2},{3,7},{7,3},{8,12},{12,8},{9,1... | collective-permute-start | bytes 884744 | tf_op jit(solution)/shard_map/ppermute | solution.py:27
  101.5 28.7 %collective-permute-start.21 = (bf16[96,1536]{1,0:T(8,128)(2,1)S(1)}, bf16[96,1536]{1,0:T(8,128)(2,1)S(1)}, u32[]{:S(2)}, u32[]{:S(2)}) collective-permute-start(bf16[96,1536]{1,0:T(8,128)(2,1)S(1)} %add_convert_fusion.3), channel_id=1, source_target_pairs={{0,8},{8,0},{1,9},{9,1},{2,10},{10,2},{3,11},{11,3},{4,12},{12,4},... | collective-permute-start | bytes 884744 | tf_op jit(solution)/shard_map/ppermute | solution.py:27
  105.0 26.9 %collective-permute-start.23 = (bf16[96,1536]{1,0:T(8,128)(2,1)S(1)}, bf16[96,1536]{1,0:T(8,128)(2,1)S(1)}, u32[]{:S(2)}, u32[]{:S(2)}) collective-permute-start(bf16[96,1536]{1,0:T(8,128)(2,1)S(1)} %get-tuple-element.60), channel_id=1, source_target_pairs={{0,2},{2,0},{1,3},{3,1},{4,6},{6,4},{5,7},{7,5},{8,10},{10,8},{9,1... | collective-permute-start | bytes 884744 | tf_op jit(solution)/shard_map/ppermute | solution.py:27
  (15 other events, 51.9 us)

commit v10 on v9

--- a/solution.py
+++ b/solution.py
@@ -420,10 +420,12 @@
     side_1 = swap(after(block(0, 1, 1), side_far_0), "side")
     side_0 = swap(after(block(0, 1, 0), side_1), "side")
     total_1 = (block(0, 0, 1).astype(f32) + side_1.astype(f32) + far_1.astype(f32)).astype(bf16)
-    theirs = swap(total_1, "near").astype(f32)
+    theirs = swap(total_1, "near")
 
     back = (attended_own + arrived_back.astype(f32)).astype(jnp.bfloat16)
-    back = after(roll_back(after(back, far_1), shifts, levels, side, ()), far_0)
+    back = roll_back(back, shifts, levels, side, far_1)
+    theirs = after(theirs, back).astype(f32)
+    back = after(back, (far_0, theirs))
     output = (values + back[:, :width].astype(f32)).astype(jnp.bfloat16)
     scaled = center * spread
     upstream = back[:, width:].astype(f32) * gain

time: 134 us -> 130 us (0.970)
  starting transfers between devices: 31.6 us -> 26.7 us
  waiting for transfers between devices: 62.1 us -> 63.5 us
    ppermute x22, starting transfers between devices: 31 us -> 26 us  [swap(): return lax.ppermute(shard, axis, [(0, 1), (1, 0)])]
    ppermute x22, waiting for transfers between devices: 62.1 us -> 63.5 us  [swap(): return lax.ppermute(shard, axis, [(0, 1), (1, 0)])]
where the time goes in v10:
time: 130 us
  waiting for transfers between devices  63.5 us (49%)
  starting transfers between devices  26.7 us (21%)
  Pallas kernels  18.9 us (15%)
  local copies, waits for them, and re-layouts  7.6 us (6%)
  matrix products  6.87 us (5%)
  other arithmetic  5.28 us (4%)
    ppermute x22, waiting for transfers between devices, swap(): return lax.ppermute(shard, axis, [(0, 1), (1, 0)])  63.5 us
    ppermute x22, starting transfers between devices, swap(): return lax.ppermute(shard, axis, [(0, 1), (1, 0)])  26 us
    pallas_call x1, Pallas kernels, on_device(): kernel_call(products_kernel, (jax.ShapeDtypeStruct((2 * tile, 4 * part),...  5.78 us
    dot_general x1, matrix products, picked(): jnp.dot(onehot, both, preferred_element_type=jnp.float32)  4.22 us
    pallas_call x1, Pallas kernels, on_device(): kernel_call(functools.partial(attention_kernel, area, head), jax.ShapeDty...  4.12 us
    pallas_call x1, Pallas kernels, on_device(): kernel_call(outer_kernel, (jax.ShapeDtypeStruct((tile, 2 * width), f32),...  3.83 us
    unnamed x44, local copies, waits for them, and re-layouts  3.62 us
    pallas_call x1, Pallas kernels, on_device(): kernel_call(weights_kernel, [jax.ShapeDtypeStruct((own_rows, 4 * part), b...  2.75 us
  transfers between devices with their start and end apart: 25, of which 13 were waited for; matrix products, arithmetic and copies ran while one was open for 10% of the time, Pallas kernels for 10%

profile of v10, /device:TPU:6, one launch (start us, length us, event | category | flops | bytes accessed | tf_op | source)
XLA Modules:
  0.0 130.0 jit_solution(11223435597402070392)
XLA Ops:
  0.7 1.3 fusion.81
  2.0 1.6 %collective-permute-start.3 = (bf16[96,1536]{1,0:T(8,128)(2,1)S(1)}, bf16[96,1536]{1,0:T(8,128)(2,1)S(1)}, u32[]{:S(2)}, u32[]{:S(2)}) collective-permute-start(bf16[96,1536]{1,0:T(8,128)(2,1)S(1)} %broadcast_select_fusion), channel_id=1, source_target_pairs={{0,4},{4,0},{1,5},{5,1},{2,6},{6,2},{3,7},{7,3},{8,12},{12,8},{9,1... | collective-permute-start | bytes 884744 | tf_op jit(solution)/shard_map/ppermute | solution.py:27
  4.7 6.1 %collective-permute-done.3.refs_5_ = bf16[96,1536]{1,0:T(8,128)(2,1)S(1)} collective-permute-done((bf16[96,1536]{1,0:T(8,128)(2,1)S(1)}, bf16[96,1536]{1,0:T(8,128)(2,1)S(1)}, u32[]{:S(2)}, u32[]{:S(2)}) %collective-permute-start.3) | collective-permute-done | bytes 294944 | tf_op jit(solution)/shard_map/ppermute | solution.py:27
  10.9 0.8 broadcast_select_fusion.2
  11.7 2.6 %collective-permute-start.4 = (bf16[96,1536]{1,0:T(8,128)(2,1)}, bf16[96,1536]{1,0:T(8,128)(2,1)}, u32[]{:S(2)}, u32[]{:S(2)}) collective-permute-start(bf16[96,1536]{1,0:T(8,128)(2,1)} %get-tuple-element.71), channel_id=1, source_target_pairs={{0,8},{8,0},{1,9},{9,1},{2,10},{10,2},{3,11},{11,3},{4,12},{12,4},... | collective-permute-start | bytes 884744 | tf_op jit(solution)/shard_map/ppermute | solution.py:27
  14.3 7.8 %collective-permute-start.5 = (bf16[96,1536]{1,0:T(8,128)(2,1)S(1)}, bf16[96,1536]{1,0:T(8,128)(2,1)S(1)}, u32[]{:S(2)}, u32[]{:S(2)}) collective-permute-start(bf16[96,1536]{1,0:T(8,128)(2,1)S(1)} %get-tuple-element.37.refs_4_), channel_id=1, source_target_pairs={{0,2},{2,0},{1,3},{3,1},{4,6},{6,4},{5,7},{7,5},{8,10},{10,8},{9,1... | collective-permute-start | bytes 884744 | tf_op jit(solution)/shard_map/ppermute | solution.py:27
  22.3 2.4 %turned_rolls.1 = (bf16[2,768,128]{2,1,0:T(8,128)(2,1)S(1)}, bf16[2,768,128]{2,1,0:T(8,128)(2,1)S(1)}) custom-call(s32[20]{0:T(128)S(1)} %concatenate.15.info_ref, f32[1,1536]{1,0:T(1,128)S(1)} %reshape.97.gain_ref, bf16[128,1536]{1,0:T(8,128)(2,1)S(1)} %bitcast.49, bf16[128,1536]{1,0:T(8,128)(2,1)S(1)} %collective-permute-done.refs_1_, ...), custom_call_target="tpu_custom_call" | custom-call | flops 201326592 | bytes 3000000 | tf_op jit(solution)/shard_map/turned_rolls/pallas_call | solution.py:305
  24.8 2.3 %collective-permute-done.4.refs_8_ = bf16[96,1536]{1,0:T(8,128)(2,1)} collective-permute-done((bf16[96,1536]{1,0:T(8,128)(2,1)}, bf16[96,1536]{1,0:T(8,128)(2,1)}, u32[]{:S(2)}, u32[]{:S(2)}) %collective-permute-start.4) | collective-permute-done | bytes 294944 | tf_op jit(solution)/shard_map/ppermute | solution.py:27
  27.2 2.7 %collective-permute-done.5.refs_6_ = bf16[96,1536]{1,0:T(8,128)(2,1)S(1)} collective-permute-done((bf16[96,1536]{1,0:T(8,128)(2,1)S(1)}, bf16[96,1536]{1,0:T(8,128)(2,1)S(1)}, u32[]{:S(2)}, u32[]{:S(2)}) %collective-permute-start.5) | collective-permute-done | bytes 294944 | tf_op jit(solution)/shard_map/ppermute | solution.py:27
  31.0 3.2 %collective-permute-start.8 = (bf16[2,768,128]{2,1,0:T(8,128)(2,1)S(1)}, bf16[2,768,128]{2,1,0:T(8,128)(2,1)S(1)}, u32[]{:S(2)}, u32[]{:S(2)}) collective-permute-start(bf16[2,768,128]{2,1,0:T(8,128)(2,1)S(1)} %get-tuple-element.35.refs_0_), channel_id=1, source_target_pairs={{0,4},{4,0},{1,5},{5,1},{2,6},{6,2},{3,7},{7,3},{8,12},{12,8},{9,1... | collective-permute-start | bytes 1179656 | tf_op jit(solution)/shard_map/ppermute | solution.py:27
  34.2 2.3 %collective-permute-done.2 = bf16[2,768,128]{2,1,0:T(8,128)(2,1)} collective-permute-done((bf16[2,768,128]{2,1,0:T(8,128)(2,1)S(1)}, bf16[2,768,128]{2,1,0:T(8,128)(2,1)}, u32[]{:S(2)}, u32[]{:S(2)}) %collective-permute-start.2) | collective-permute-done | bytes 393248 | tf_op jit(solution)/shard_map/ppermute | solution.py:27
  36.4 2.8 %collective-permute-done.6.refs_9_ = bf16[96,1536]{1,0:T(8,128)(2,1)} collective-permute-done((bf16[96,1536]{1,0:T(8,128)(2,1)}, bf16[96,1536]{1,0:T(8,128)(2,1)}, u32[]{:S(2)}, u32[]{:S(2)}) %collective-permute-start.6) | collective-permute-done | bytes 294944 | tf_op jit(solution)/shard_map/ppermute | solution.py:27
  40.0 1.2 collective-permute-start.12
  41.2 2.6 %fusion.7 = f32[2,6,64,64]{3,1,2,0:T(8,128)S(1)} fusion(s32[64,64]{1,0:T(8,128)S(1)} %copy-done.21, pred[2,64,64]{2,1,0:T(8,128)(4,1)S(1)} %broadcast_compare_fusion, f32[2,225,6]{1,0,2:T(2,128)S(1)} %constant_dynamic-slice_fusion), kind=kOutput, calls=%fused_computation.9 | convolution fusion | flops 133681152 | bytes 231984 | tf_op jit(solution)/shard_map/qkr,lrh->lhqk/dot_general | solution.py:340
  45.4 3.6 %collective-permute-done.10.refs_7_ = bf16[96,1536]{1,0:T(8,128)(2,1)} collective-permute-done((bf16[96,1536]{1,0:T(8,128)(2,1)S(1)}, bf16[96,1536]{1,0:T(8,128)(2,1)}, u32[]{:S(2)}, u32[]{:S(2)}) %collective-permute-start.10) | collective-permute-done | bytes 294944 | tf_op jit(solution)/shard_map/ppermute | solution.py:27
  50.8 5.8 %products.1 = (bf16[256,1536]{1,0:T(8,128)(2,1)}, bf16[256,1536]{1,0:T(8,128)(2,1)}, bf16[768,1536]{1,0:T(8,128)(2,1)}) custom-call(s32[8]{0:T(128)} %stack.120.place_ref, bf16[2,768,128]{2,1,0:T(8,128)(2,1)} %copy-done.4, bf16[2,768,128]{2,1,0:T(8,128)(2,1)} %copy-done.10, bf16[2,768,128]{2,1,0:T(8,128)(2,1)} %copy-done.6, bf16[2,768,128]{2,1,0:T(8,128)(2,1)} %copy-done.8, ...), custom_call_target="tpu_custom_call" | custom-call | flops 1200000000 | bytes 9000000 | tf_op jit(solution)/shard_map/products/pallas_call | solution.py:348
  56.7 2.5 %collective-permute-done.13.came_ref = bf16[256,1536]{1,0:T(8,128)(2,1)S(1)} collective-permute-done((bf16[256,1536]{1,0:T(8,128)(2,1)}, bf16[256,1536]{1,0:T(8,128)(2,1)S(1)}, u32[]{:S(2)}, u32[]{:S(2)}) %collective-permute-start.13) | collective-permute-done | bytes 786464 | tf_op jit(solution)/shard_map/ppermute | solution.py:27
  59.2 0.9 copy-done.19
  60.3 4.1 %attention.1.grad_ref.refs_4_ = bf16[256,1536]{1,0:T(8,128)(2,1)} custom-call(bf16[256,1536]{1,0:T(8,128)(2,1)} %get-tuple-element.42.kept_ref, bf16[256,1536]{1,0:T(8,128)(2,1)} %copy-done.19, f32[2,3,128,64]{3,2,1,0:T(8,128)} %bitcast.52), custom_call_target="tpu_custom_call" | custom-call | flops 1000000000 | bytes 4000000 | tf_op jit(solution)/shard_map/attention/pallas_call | solution.py:369
  65.7 1.1 copy-done.3
  66.8 3.8 %projections.1 = (f32[128,3072]{1,0:T(8,128)S(1)}, bf16[128,3072]{1,0:T(8,128)(2,1)S(1)}) custom-call(s32[16]{0:T(128)S(1)} %stack.111.place_ref, bf16[256,1536]{1,0:T(8,128)(2,1)S(1)} %copy-done.3, bf16[768,1536]{1,0:T(8,128)(2,1)S(1)} %copy-done.1, bf16[768,1536]{1,0:T(8,128)(2,1)S(1)} %collective-permute-done.14.theirs_ref), custom_call_target="tpu_custom_call" | custom-call | flops 1200000000 | bytes 8000000 | tf_op jit(solution)/shard_map/projections/pallas_call | solution.py:382
  70.7 2.8 %collective-permute-start.15 = (bf16[128,3072]{1,0:T(8,128)(2,1)S(1)}, bf16[128,3072]{1,0:T(8,128)(2,1)S(1)}, u32[]{:S(2)}, u32[]{:S(2)}) collective-permute-start(bf16[128,3072]{1,0:T(8,128)(2,1)S(1)} %get-tuple-element.47), channel_id=1, source_target_pairs={{0,4},{4,0},{1,5},{5,1},{2,6},{6,2},{3,7},{7,3},{8,12},{12,8},{9,1... | collective-permute-start | bytes 2359304 | tf_op jit(solution)/shard_map/ppermute | solution.py:27
  73.5 2.7 %weight_gradient.1 = (bf16[96,1536]{1,0:T(8,128)(2,1)S(1)}, bf16[96,1536]{1,0:T(8,128)(2,1)S(1)}, bf16[96,1536]{1,0:T(8,128)(2,1)S(1)}, bf16[96,1536]{1,0:T(8,12...) custom-call(s32[1]{0:T(128)} %bitcast.34.near_ref, ...), custom_call_target="tpu_custom_call" | custom-call | flops 1200000000 | bytes 6000000 | tf_op jit(solution)/shard_map/weight_gradient/pallas_call | solution.py:396
  76.7 8.4 %collective-permute-done.18 = bf16[96,1536]{1,0:T(8,128)(2,1)S(1)} collective-permute-done((bf16[96,1536]{1,0:T(8,128)(2,1)S(1)}, bf16[96,1536]{1,0:T(8,128)(2,1)S(1)}, u32[]{:S(2)}, u32[]{:S(2)}) %collective-permute-start.18) | collective-permute-done | bytes 294944 | tf_op jit(solution)/shard_map/ppermute | solution.py:27
  85.6 3.4 %collective-permute-start.19 = (bf16[96,1536]{1,0:T(8,128)(2,1)S(1)}, bf16[96,1536]{1,0:T(8,128)(2,1)S(1)}, u32[]{:S(2)}, u32[]{:S(2)}) collective-permute-start(bf16[96,1536]{1,0:T(8,128)(2,1)S(1)} %add_convert_fusion.4), channel_id=1, source_target_pairs={{0,8},{8,0},{1,9},{9,1},{2,10},{10,2},{3,11},{11,3},{4,12},{12,4},... | collective-permute-start | bytes 884744 | tf_op jit(solution)/shard_map/ppermute | solution.py:27
  89.0 4.0 %collective-permute-done.20 = bf16[96,1536]{1,0:T(8,128)(2,1)S(1)} collective-permute-done((bf16[96,1536]{1,0:T(8,128)(2,1)S(1)}, bf16[96,1536]{1,0:T(8,128)(2,1)S(1)}, u32[]{:S(2)}, u32[]{:S(2)}) %collective-permute-start.20) | collective-permute-done | bytes 294944 | tf_op jit(solution)/shard_map/ppermute | solution.py:27
  93.4 3.6 %collective-permute-done.15 = bf16[128,3072]{1,0:T(8,128)(2,1)S(1)} collective-permute-done((bf16[128,3072]{1,0:T(8,128)(2,1)S(1)}, bf16[128,3072]{1,0:T(8,128)(2,1)S(1)}, u32[]{:S(2)}, u32[]{:S(2)}) %collective-permute-start.15) | collective-permute-done | bytes 786464 | tf_op jit(solution)/shard_map/ppermute | solution.py:27
  97.3 19.4 %collective-permute-done.19 = bf16[96,1536]{1,0:T(8,128)(2,1)S(1)} collective-permute-done((bf16[96,1536]{1,0:T(8,128)(2,1)S(1)}, bf16[96,1536]{1,0:T(8,128)(2,1)S(1)}, u32[]{:S(2)}, u32[]{:S(2)}) %collective-permute-start.19) | collective-permute-done | bytes 294944 | tf_op jit(solution)/shard_map/ppermute | solution.py:27
  117.1 4.2 %convolution_convert_fusion = bf16[128,3072]{1,0:T(8,128)(2,1)S(1)} fusion(bf16[128,3072]{1,0:T(8,128)(2,1)S(1)} %add_convert_fusion, bf16[128,3072]{1,0:T(8,128)(2,1)} %collective-permute-done.16, s32[]{:T(128)} %bitcast.4, s32[]{:T(128)} %bitcast.3, s32[128]{0:T(128)S(1)} %get-tuple-element.95, s32[128]{0:T(128)S(1)} %get-tuple-element.97, s32[]{:T(128)} %bitcast.2, ...), kind=kOutput, calls=%fused_computation.3 | convolution fusion | flops 206700544 | bytes 2362768 | tf_op jit(solution)/shard_map/dot_general | solution.py:52
  121.4 5.4 %collective-permute-done.23 = bf16[96,1536]{1,0:T(8,128)(2,1)S(1)} collective-permute-done((bf16[96,1536]{1,0:T(8,128)(2,1)S(1)}, bf16[96,1536]{1,0:T(8,128)(2,1)S(1)}, u32[]{:S(2)}, u32[]{:S(2)}) %collective-permute-start.23) | collective-permute-done | bytes 294944 | tf_op jit(solution)/shard_map/ppermute | solution.py:27
  127.1 1.4 %fusion.18 = (bf16[128,1536]{1,0:T(8,128)(2,1)}, bf16[128,1536]{1,0:T(8,128)(2,1)}) fusion(f32[128]{0:T(128)S(1)} %broadcast_multiply_fusion.2, f32[128]{0:T(128)S(1)} %div.55, f32[128]{0:T(128)S(1)} %broadcast_multiply_fusion.3, f32[1536]{0:T(1024)S(1)} %copy-done.15, f32[128]{0:T(128)S(1)} %rsqrt.12, bf16[128,3072]{1,0:T(8,128)(2,1)S(1)} %convolution_convert_fusion, ...), kind=kLoop, calls=%fused_computation.22 | loop fusion | flops 2949120 | bytes 2367488 | tf_op jit(solution)/shard_map/convert_element_type | solution.py:437
  128.8 1.1 broadcast_multiply_fusion
  (118 shorter events, 10.6 us)
Async XLA Ops:
  0.6 40.6 %copy-start = (f32[2,225,12]{1,0,2:T(2,128)S(1)}, f32[2,225,12]{1,0,2:T(2,128)}, u32[]{:S(2)}) copy-start(f32[2,225,12]{1,0,2:T(2,128)} %param.16) | copy-start | bytes 64804
  2.0 8.8 %collective-permute-start.3 = (bf16[96,1536]{1,0:T(8,128)(2,1)S(1)}, bf16[96,1536]{1,0:T(8,128)(2,1)S(1)}, u32[]{:S(2)}, u32[]{:S(2)}) collective-permute-start(bf16[96,1536]{1,0:T(8,128)(2,1)S(1)} %broadcast_select_fusion), channel_id=1, source_target_pairs={{0,4},{4,0},{1,5},{5,1},{2,6},{6,2},{3,7},{7,3},{8,12},{12,8},{9,1... | collective-permute-start | bytes 884744 | tf_op jit(solution)/shard_map/ppermute | solution.py:27
  3.9 18.3 %copy-start.18 = (s32[2,2]{1,0:T(2,128)S(1)}, s32[2,2]{1,0:T(2,128)}, u32[]{:S(2)}) copy-start(s32[2,2]{1,0:T(2,128)} %param.14) | copy-start | bytes 52
  3.9 18.4 %copy-start.15 = (f32[1536]{0:T(1024)S(1)}, f32[1536]{0:T(1024)}, u32[]{:S(2)}) copy-start(f32[1536]{0:T(1024)} %param.12) | copy-start | bytes 18436
  4.1 10.2 %collective-permute-start = (bf16[128,1536]{1,0:T(8,128)(2,1)S(1)}, bf16[128,1536]{1,0:T(8,128)(2,1)S(1)}, u32[]{:S(2)}, u32[]{:S(2)}) collective-permute-start(bf16[128,1536]{1,0:T(8,128)(2,1)S(1)} %bitcast.48), channel_id=1, source_target_pairs={{0,15},{1,0},{2,1},{3,2},{4,3},{5,4},{6,5},{7,6},{8,7},{9,8},{10,9... | collective-permute-start | bytes 1179656 | tf_op jit(solution)/shard_map/ppermute | solution.py:18
  4.1 10.2 %collective-permute-start.1 = (bf16[128,1536]{1,0:T(8,128)(2,1)S(1)}, bf16[128,1536]{1,0:T(8,128)(2,1)S(1)}, u32[]{:S(2)}, u32[]{:S(2)}) collective-permute-start(bf16[128,1536]{1,0:T(8,128)(2,1)S(1)} %bitcast.50), channel_id=1, source_target_pairs={{0,15},{1,0},{2,1},{3,2},{4,3},{5,4},{6,5},{7,6},{8,7},{9,8},{10,9... | collective-permute-start | bytes 1179656 | tf_op jit(solution)/shard_map/ppermute | solution.py:18
  10.9 29.0 %copy-start.13 = (bf16[96,1536]{1,0:T(8,128)(2,1)}, bf16[96,1536]{1,0:T(8,128)(2,1)S(1)}, u32[]{:S(2)}) copy-start(bf16[96,1536]{1,0:T(8,128)(2,1)S(1)} %collective-permute-done.3.refs_5_) | copy-start | bytes 884740
  11.7 32.2 %copy-start.14 = (bf16[96,1536]{1,0:T(8,128)(2,1)}, bf16[96,1536]{1,0:T(8,128)(2,1)S(1)}, u32[]{:S(2)}) copy-start(bf16[96,1536]{1,0:T(8,128)(2,1)S(1)} %get-tuple-element.37.refs_4_) | copy-start | bytes 884740
  11.7 29.5 %copy-start.21 = (s32[64,64]{1,0:T(8,128)S(1)}, s32[64,64]{1,0:T(8,128)}, u32[]{:S(2)}) copy-start(s32[64,64]{1,0:T(8,128)} %param.15) | copy-start | bytes 49156
  11.7 15.5 %collective-permute-start.4 = (bf16[96,1536]{1,0:T(8,128)(2,1)}, bf16[96,1536]{1,0:T(8,128)(2,1)}, u32[]{:S(2)}, u32[]{:S(2)}) collective-permute-start(bf16[96,1536]{1,0:T(8,128)(2,1)} %get-tuple-element.71), channel_id=1, source_target_pairs={{0,8},{8,0},{1,9},{9,1},{2,10},{10,2},{3,11},{11,3},{4,12},{12,4},... | collective-permute-start | bytes 884744 | tf_op jit(solution)/shard_map/ppermute | solution.py:27
  14.3 15.6 %collective-permute-start.5 = (bf16[96,1536]{1,0:T(8,128)(2,1)S(1)}, bf16[96,1536]{1,0:T(8,128)(2,1)S(1)}, u32[]{:S(2)}, u32[]{:S(2)}) collective-permute-start(bf16[96,1536]{1,0:T(8,128)(2,1)S(1)} %get-tuple-element.37.refs_4_), channel_id=1, source_target_pairs={{0,2},{2,0},{1,3},{3,1},{4,6},{6,4},{5,7},{7,5},{8,10},{10,8},{9,1... | collective-permute-start | bytes 884744 | tf_op jit(solution)/shard_map/ppermute | solution.py:27
  24.7 20.0 %copy-start.4 = (bf16[2,768,128]{2,1,0:T(8,128)(2,1)}, bf16[2,768,128]{2,1,0:T(8,128)(2,1)S(1)}, u32[]{:S(2)}) copy-start(bf16[2,768,128]{2,1,0:T(8,128)(2,1)S(1)} %get-tuple-element.35.refs_0_) | copy-start | bytes 1179652
  24.8 11.7 %collective-permute-start.2 = (bf16[2,768,128]{2,1,0:T(8,128)(2,1)S(1)}, bf16[2,768,128]{2,1,0:T(8,128)(2,1)}, u32[]{:S(2)}, u32[]{:S(2)}) collective-permute-start(bf16[2,768,128]{2,1,0:T(8,128)(2,1)S(1)} %get-tuple-element.39), channel_id=1, source_target_pairs={{0,4},{4,0},{1,5},{5,1},{2,6},{6,2},{3,7},{7,3},{8,12},{12,8},{9,1... | collective-permute-start | bytes 1179656 | tf_op jit(solution)/shard_map/ppermute | solution.py:27
  29.9 9.4 %collective-permute-start.6 = (bf16[96,1536]{1,0:T(8,128)(2,1)}, bf16[96,1536]{1,0:T(8,128)(2,1)}, u32[]{:S(2)}, u32[]{:S(2)}) collective-permute-start(bf16[96,1536]{1,0:T(8,128)(2,1)} %collective-permute-done.4.refs_8_), channel_id=1, source_target_pairs={{0,16},{16,0},{1,17},{17,1},{2,18},{18,2},{3,19},{19,3},{4,20},{20... | collective-permute-start | bytes 884744 | tf_op jit(solution)/shard_map/ppermute | solution.py:27
  30.2 9.7 %collective-permute-start.11 = (bf16[96,1536]{1,0:T(8,128)(2,1)}, bf16[96,1536]{1,0:T(8,128)(2,1)}, u32[]{:S(2)}, u32[]{:S(2)}) collective-permute-start(bf16[96,1536]{1,0:T(8,128)(2,1)} %collective-permute-done.4.refs_8_), channel_id=1, source_target_pairs={{0,2},{2,0},{1,3},{3,1},{4,6},{6,4},{5,7},{7,5},{8,10},{10,8},{9,1... | collective-permute-start | bytes 884744 | tf_op jit(solution)/shard_map/ppermute | solution.py:27
  31.0 14.4 %collective-permute-start.8 = (bf16[2,768,128]{2,1,0:T(8,128)(2,1)S(1)}, bf16[2,768,128]{2,1,0:T(8,128)(2,1)S(1)}, u32[]{:S(2)}, u32[]{:S(2)}) collective-permute-start(bf16[2,768,128]{2,1,0:T(8,128)(2,1)S(1)} %get-tuple-element.35.refs_0_), channel_id=1, source_target_pairs={{0,4},{4,0},{1,5},{5,1},{2,6},{6,2},{3,7},{7,3},{8,12},{12,8},{9,1... | collective-permute-start | bytes 1179656 | tf_op jit(solution)/shard_map/ppermute | solution.py:27
  39.3 10.0 %collective-permute-start.9 = (bf16[2,768,128]{2,1,0:T(8,128)(2,1)}, bf16[2,768,128]{2,1,0:T(8,128)(2,1)S(1)}, u32[]{:S(2)}, u32[]{:S(2)}) collective-permute-start(bf16[2,768,128]{2,1,0:T(8,128)(2,1)} %collective-permute-done.2), channel_id=1, source_target_pairs={{0,1},{1,0},{2,3},{3,2},{4,5},{5,4},{6,7},{7,6},{8,9},{9,8},{10,11... | collective-permute-start | bytes 1179656 | tf_op jit(solution)/shard_map/ppermute | solution.py:27
  39.3 10.0 %collective-permute-start.7 = (bf16[2,768,128]{2,1,0:T(8,128)(2,1)S(1)}, bf16[2,768,128]{2,1,0:T(8,128)(2,1)S(1)}, u32[]{:S(2)}, u32[]{:S(2)}) collective-permute-start(bf16[2,768,128]{2,1,0:T(8,128)(2,1)S(1)} %get-tuple-element.39), channel_id=1, source_target_pairs={{0,1},{1,0},{2,3},{3,2},{4,5},{5,4},{6,7},{7,6},{8,9},{9,8},{10,11... | collective-permute-start | bytes 1179656 | tf_op jit(solution)/shard_map/ppermute | solution.py:27
  39.9 9.1 %collective-permute-start.10 = (bf16[96,1536]{1,0:T(8,128)(2,1)S(1)}, bf16[96,1536]{1,0:T(8,128)(2,1)}, u32[]{:S(2)}, u32[]{:S(2)}) collective-permute-start(bf16[96,1536]{1,0:T(8,128)(2,1)S(1)} %collective-permute-done.3.refs_5_), channel_id=1, source_target_pairs={{0,2},{2,0},{1,3},{3,1},{4,6},{6,4},{5,7},{7,5},{8,10},{10,8},{9,1... | collective-permute-start | bytes 884744 | tf_op jit(solution)/shard_map/ppermute | solution.py:27
  40.0 9.3 %collective-permute-start.12 = (bf16[96,1536]{1,0:T(8,128)(2,1)}, bf16[96,1536]{1,0:T(8,128)(2,1)}, u32[]{:S(2)}, u32[]{:S(2)}) collective-permute-start(bf16[96,1536]{1,0:T(8,128)(2,1)} %collective-permute-done.11.refs_10_), channel_id=1, source_target_pairs={{0,16},{16,0},{1,17},{17,1},{2,18},{18,2},{3,19},{19,3},{4,20},{20... | collective-permute-start | bytes 884744 | tf_op jit(solution)/shard_map/ppermute | solution.py:27
  56.6 2.6 %collective-permute-start.13 = (bf16[256,1536]{1,0:T(8,128)(2,1)}, bf16[256,1536]{1,0:T(8,128)(2,1)S(1)}, u32[]{:S(2)}, u32[]{:S(2)}) collective-permute-start(bf16[256,1536]{1,0:T(8,128)(2,1)} %get-tuple-element.43), channel_id=1, source_target_pairs={{0,1},{1,0},{2,3},{3,2},{4,5},{5,4},{6,7},{7,6},{8,9},{9,8},{10,11... | collective-permute-start | bytes 2359304 | tf_op jit(solution)/shard_map/ppermute | solution.py:27
  60.1 5.6 %collective-permute-start.14 = (bf16[768,1536]{1,0:T(8,128)(2,1)}, bf16[768,1536]{1,0:T(8,128)(2,1)S(1)}, u32[]{:S(2)}, u32[]{:S(2)}) collective-permute-start(bf16[768,1536]{1,0:T(8,128)(2,1)} %get-tuple-element.45.mine_ref), channel_id=1, source_target_pairs={{0,1},{1,0},{2,3},{3,2},{4,5},{5,4},{6,7},{7,6},{8,9},{9,8},{10,11... | collective-permute-start | bytes 7077896 | tf_op jit(solution)/shard_map/ppermute | solution.py:27
  64.4 9.1 %collective-permute-start.17 = (bf16[256,1536]{1,0:T(8,128)(2,1)}, bf16[256,1536]{1,0:T(8,128)(2,1)S(1)}, u32[]{:S(2)}, u32[]{:S(2)}) collective-permute-start(bf16[256,1536]{1,0:T(8,128)(2,1)} %attention.1.grad_ref.refs_4_), channel_id=1, source_target_pairs={{0,1},{1,0},{2,3},{3,2},{4,5},{5,4},{6,7},{7,6},{8,9},{9,8},{10,11... | collective-permute-start | bytes 2359304 | tf_op jit(solution)/shard_map/ppermute | solution.py:27
  70.7 26.3 %collective-permute-start.15 = (bf16[128,3072]{1,0:T(8,128)(2,1)S(1)}, bf16[128,3072]{1,0:T(8,128)(2,1)S(1)}, u32[]{:S(2)}, u32[]{:S(2)}) collective-permute-start(bf16[128,3072]{1,0:T(8,128)(2,1)S(1)} %get-tuple-element.47), channel_id=1, source_target_pairs={{0,4},{4,0},{1,5},{5,1},{2,6},{6,2},{3,7},{7,3},{8,12},{12,8},{9,1... | collective-permute-start | bytes 2359304 | tf_op jit(solution)/shard_map/ppermute | solution.py:27
  76.3 8.8 %collective-permute-start.18 = (bf16[96,1536]{1,0:T(8,128)(2,1)S(1)}, bf16[96,1536]{1,0:T(8,128)(2,1)S(1)}, u32[]{:S(2)}, u32[]{:S(2)}) collective-permute-start(bf16[96,1536]{1,0:T(8,128)(2,1)S(1)} %get-tuple-element.50), channel_id=1, source_target_pairs={{0,2},{2,0},{1,3},{3,1},{4,6},{6,4},{5,7},{7,5},{8,10},{10,8},{9,1... | collective-permute-start | bytes 884744 | tf_op jit(solution)/shard_map/ppermute | solution.py:27
  85.1 7.9 %collective-permute-start.20 = (bf16[96,1536]{1,0:T(8,128)(2,1)S(1)}, bf16[96,1536]{1,0:T(8,128)(2,1)S(1)}, u32[]{:S(2)}, u32[]{:S(2)}) collective-permute-start(bf16[96,1536]{1,0:T(8,128)(2,1)S(1)} %get-tuple-element.54), channel_id=1, source_target_pairs={{0,2},{2,0},{1,3},{3,1},{4,6},{6,4},{5,7},{7,5},{8,10},{10,8},{9,1... | collective-permute-start | bytes 884744 | tf_op jit(solution)/shard_map/ppermute | solution.py:27
  85.6 31.1 %collective-permute-start.19 = (bf16[96,1536]{1,0:T(8,128)(2,1)S(1)}, bf16[96,1536]{1,0:T(8,128)(2,1)S(1)}, u32[]{:S(2)}, u32[]{:S(2)}) collective-permute-start(bf16[96,1536]{1,0:T(8,128)(2,1)S(1)} %add_convert_fusion.4), channel_id=1, source_target_pairs={{0,8},{8,0},{1,9},{9,1},{2,10},{10,2},{3,11},{11,3},{4,12},{12,4},... | collective-permute-start | bytes 884744 | tf_op jit(solution)/shard_map/ppermute | solution.py:27
  93.0 23.6 %collective-permute-start.22 = (bf16[96,1536]{1,0:T(8,128)(2,1)S(1)}, bf16[96,1536]{1,0:T(8,128)(2,1)S(1)}, u32[]{:S(2)}, u32[]{:S(2)}) collective-permute-start(bf16[96,1536]{1,0:T(8,128)(2,1)S(1)} %get-tuple-element.58), channel_id=1, source_target_pairs={{0,2},{2,0},{1,3},{3,1},{4,6},{6,4},{5,7},{7,5},{8,10},{10,8},{9,1... | collective-permute-start | bytes 884744 | tf_op jit(solution)/shard_map/ppermute | solution.py:27
  97.1 20.0 %collective-permute-start.16 = (bf16[128,3072]{1,0:T(8,128)(2,1)S(1)}, bf16[128,3072]{1,0:T(8,128)(2,1)}, u32[]{:S(2)}, u32[]{:S(2)}) collective-permute-start(bf16[128,3072]{1,0:T(8,128)(2,1)S(1)} %add_convert_fusion), channel_id=1, source_target_pairs={{0,1},{1,2},{2,3},{3,4},{4,5},{5,6},{6,7},{7,8},{8,9},{9,10},{10,1... | collective-permute-start | bytes 2359304 | tf_op jit(solution)/shard_map/ppermute | solution.py:18
  116.7 10.1 %collective-permute-start.21 = (bf16[96,1536]{1,0:T(8,128)(2,1)S(1)}, bf16[96,1536]{1,0:T(8,128)(2,1)S(1)}, u32[]{:S(2)}, u32[]{:S(2)}) collective-permute-start(bf16[96,1536]{1,0:T(8,128)(2,1)S(1)} %add_convert_fusion.3), channel_id=1, source_target_pairs={{0,8},{8,0},{1,9},{9,1},{2,10},{10,2},{3,11},{11,3},{4,12},{12,4},... | collective-permute-start | bytes 884744 | tf_op jit(solution)/shard_map/ppermute | solution.py:27
  116.8 9.9 %collective-permute-start.23 = (bf16[96,1536]{1,0:T(8,128)(2,1)S(1)}, bf16[96,1536]{1,0:T(8,128)(2,1)S(1)}, u32[]{:S(2)}, u32[]{:S(2)}) collective-permute-start(bf16[96,1536]{1,0:T(8,128)(2,1)S(1)} %add_convert_fusion.2), channel_id=1, source_target_pairs={{0,4},{4,0},{1,5},{5,1},{2,6},{6,2},{3,7},{7,3},{8,12},{12,8},{9,1... | collective-permute-start | bytes 884744 | tf_op jit(solution)/shard_map/ppermute | solution.py:27
  117.1 11.4 %collective-permute-start.24 = (bf16[96,1536]{1,0:T(8,128)(2,1)S(1)}, bf16[96,1536]{1,0:T(8,128)(2,1)S(1)}, u32[]{:S(2)}, u32[]{:S(2)}) collective-permute-start(bf16[96,1536]{1,0:T(8,128)(2,1)S(1)} %get-tuple-element.63), channel_id=1, source_target_pairs={{0,2},{2,0},{1,3},{3,1},{4,6},{6,4},{5,7},{7,5},{8,10},{10,8},{9,1... | collective-permute-start | bytes 884744 | tf_op jit(solution)/shard_map/ppermute | solution.py:27
  (15 other events, 51.9 us)

commit v11 on v9

--- a/solution.py
+++ b/solution.py
@@ -423,7 +423,7 @@
     theirs = swap(total_1, "near").astype(f32)
 
     back = (attended_own + arrived_back.astype(f32)).astype(jnp.bfloat16)
-    back = after(roll_back(after(back, far_1), shifts, levels, side, ()), far_0)
+    back = after(roll_back(back, shifts, levels, side, far_1), far_0)
     output = (values + back[:, :width].astype(f32)).astype(jnp.bfloat16)
     scaled = center * spread
     upstream = back[:, width:].astype(f32) * gain

time: 134 us -> 129 us (0.963)
  starting transfers between devices: 31.6 us -> 26.8 us
    ppermute x22, starting transfers between devices: 31 us -> 26.1 us  [swap(): return lax.ppermute(shard, axis, [(0, 1), (1, 0)])]
where the time goes in v11:
time: 129 us
  waiting for transfers between devices  62.3 us (48%)
  starting transfers between devices  26.8 us (21%)
  Pallas kernels  18.9 us (15%)
  local copies, waits for them, and re-layouts  7.6 us (6%)
  matrix products  6.87 us (5%)
  other arithmetic  5.29 us (4%)
    ppermute x22, waiting for transfers between devices, swap(): return lax.ppermute(shard, axis, [(0, 1), (1, 0)])  62.3 us
    ppermute x22, starting transfers between devices, swap(): return lax.ppermute(shard, axis, [(0, 1), (1, 0)])  26.1 us
    pallas_call x1, Pallas kernels, on_device(): kernel_call(products_kernel, (jax.ShapeDtypeStruct((2 * tile, 4 * part),...  5.78 us
    dot_general x1, matrix products, picked(): jnp.dot(onehot, both, preferred_element_type=jnp.float32)  4.22 us
    pallas_call x1, Pallas kernels, on_device(): kernel_call(functools.partial(attention_kernel, area, head), jax.ShapeDty...  4.12 us
    pallas_call x1, Pallas kernels, on_device(): kernel_call(outer_kernel, (jax.ShapeDtypeStruct((tile, 2 * width), f32),...  3.83 us
    unnamed x44, local copies, waits for them, and re-layouts  3.62 us
    pallas_call x1, Pallas kernels, on_device(): kernel_call(weights_kernel, [jax.ShapeDtypeStruct((own_rows, 4 * part), b...  2.75 us
  transfers between devices with their start and end apart: 25, of which 13 were waited for; matrix products, arithmetic and copies ran while one was open for 10% of the time, Pallas kernels for 10%

profile of v11, /device:TPU:6, one launch (start us, length us, event | category | flops | bytes accessed | tf_op | source)
XLA Modules:
  0.0 128.9 jit_solution(7011730010271917608)
XLA Ops:
  0.7 1.3 fusion.81
  2.0 1.6 %collective-permute-start.3 = (bf16[96,1536]{1,0:T(8,128)(2,1)S(1)}, bf16[96,1536]{1,0:T(8,128)(2,1)S(1)}, u32[]{:S(2)}, u32[]{:S(2)}) collective-permute-start(bf16[96,1536]{1,0:T(8,128)(2,1)S(1)} %broadcast_select_fusion), channel_id=1, source_target_pairs={{0,4},{4,0},{1,5},{5,1},{2,6},{6,2},{3,7},{7,3},{8,12},{12,8},{9,1... | collective-permute-start | bytes 884744 | tf_op jit(solution)/shard_map/ppermute | solution.py:27
  4.7 6.1 %collective-permute-done.3.refs_5_ = bf16[96,1536]{1,0:T(8,128)(2,1)S(1)} collective-permute-done((bf16[96,1536]{1,0:T(8,128)(2,1)S(1)}, bf16[96,1536]{1,0:T(8,128)(2,1)S(1)}, u32[]{:S(2)}, u32[]{:S(2)}) %collective-permute-start.3) | collective-permute-done | bytes 294944 | tf_op jit(solution)/shard_map/ppermute | solution.py:27
  10.9 0.8 broadcast_select_fusion.2
  11.7 2.6 %collective-permute-start.4 = (bf16[96,1536]{1,0:T(8,128)(2,1)}, bf16[96,1536]{1,0:T(8,128)(2,1)}, u32[]{:S(2)}, u32[]{:S(2)}) collective-permute-start(bf16[96,1536]{1,0:T(8,128)(2,1)} %get-tuple-element.69), channel_id=1, source_target_pairs={{0,8},{8,0},{1,9},{9,1},{2,10},{10,2},{3,11},{11,3},{4,12},{12,4},... | collective-permute-start | bytes 884744 | tf_op jit(solution)/shard_map/ppermute | solution.py:27
  14.3 7.8 %collective-permute-start.5 = (bf16[96,1536]{1,0:T(8,128)(2,1)S(1)}, bf16[96,1536]{1,0:T(8,128)(2,1)S(1)}, u32[]{:S(2)}, u32[]{:S(2)}) collective-permute-start(bf16[96,1536]{1,0:T(8,128)(2,1)S(1)} %get-tuple-element.36.refs_4_), channel_id=1, source_target_pairs={{0,2},{2,0},{1,3},{3,1},{4,6},{6,4},{5,7},{7,5},{8,10},{10,8},{9,1... | collective-permute-start | bytes 884744 | tf_op jit(solution)/shard_map/ppermute | solution.py:27
  22.3 2.4 %turned_rolls.1 = (bf16[2,768,128]{2,1,0:T(8,128)(2,1)S(1)}, bf16[2,768,128]{2,1,0:T(8,128)(2,1)S(1)}) custom-call(s32[20]{0:T(128)S(1)} %concatenate.15.info_ref, f32[1,1536]{1,0:T(1,128)S(1)} %reshape.97.gain_ref, bf16[128,1536]{1,0:T(8,128)(2,1)S(1)} %bitcast.49, bf16[128,1536]{1,0:T(8,128)(2,1)S(1)} %collective-permute-done.refs_1_, ...), custom_call_target="tpu_custom_call" | custom-call | flops 201326592 | bytes 3000000 | tf_op jit(solution)/shard_map/turned_rolls/pallas_call | solution.py:305
  24.8 2.3 %collective-permute-done.4.refs_8_ = bf16[96,1536]{1,0:T(8,128)(2,1)} collective-permute-done((bf16[96,1536]{1,0:T(8,128)(2,1)}, bf16[96,1536]{1,0:T(8,128)(2,1)}, u32[]{:S(2)}, u32[]{:S(2)}) %collective-permute-start.4) | collective-permute-done | bytes 294944 | tf_op jit(solution)/shard_map/ppermute | solution.py:27
  27.2 2.7 %collective-permute-done.5.refs_6_ = bf16[96,1536]{1,0:T(8,128)(2,1)S(1)} collective-permute-done((bf16[96,1536]{1,0:T(8,128)(2,1)S(1)}, bf16[96,1536]{1,0:T(8,128)(2,1)S(1)}, u32[]{:S(2)}, u32[]{:S(2)}) %collective-permute-start.5) | collective-permute-done | bytes 294944 | tf_op jit(solution)/shard_map/ppermute | solution.py:27
  31.0 3.2 %collective-permute-start.8 = (bf16[2,768,128]{2,1,0:T(8,128)(2,1)S(1)}, bf16[2,768,128]{2,1,0:T(8,128)(2,1)S(1)}, u32[]{:S(2)}, u32[]{:S(2)}) collective-permute-start(bf16[2,768,128]{2,1,0:T(8,128)(2,1)S(1)} %get-tuple-element.34.refs_0_), channel_id=1, source_target_pairs={{0,4},{4,0},{1,5},{5,1},{2,6},{6,2},{3,7},{7,3},{8,12},{12,8},{9,1... | collective-permute-start | bytes 1179656 | tf_op jit(solution)/shard_map/ppermute | solution.py:27
  34.2 2.3 %collective-permute-done.2 = bf16[2,768,128]{2,1,0:T(8,128)(2,1)} collective-permute-done((bf16[2,768,128]{2,1,0:T(8,128)(2,1)S(1)}, bf16[2,768,128]{2,1,0:T(8,128)(2,1)}, u32[]{:S(2)}, u32[]{:S(2)}) %collective-permute-start.2) | collective-permute-done | bytes 393248 | tf_op jit(solution)/shard_map/ppermute | solution.py:27
  36.4 2.8 %collective-permute-done.6.refs_9_ = bf16[96,1536]{1,0:T(8,128)(2,1)} collective-permute-done((bf16[96,1536]{1,0:T(8,128)(2,1)}, bf16[96,1536]{1,0:T(8,128)(2,1)}, u32[]{:S(2)}, u32[]{:S(2)}) %collective-permute-start.6) | collective-permute-done | bytes 294944 | tf_op jit(solution)/shard_map/ppermute | solution.py:27
  40.0 1.2 collective-permute-start.12
  41.2 2.6 %fusion.7 = f32[2,6,64,64]{3,1,2,0:T(8,128)S(1)} fusion(s32[64,64]{1,0:T(8,128)S(1)} %copy-done.21, pred[2,64,64]{2,1,0:T(8,128)(4,1)S(1)} %broadcast_compare_fusion, f32[2,225,6]{1,0,2:T(2,128)S(1)} %constant_dynamic-slice_fusion), kind=kOutput, calls=%fused_computation.9 | convolution fusion | flops 133681152 | bytes 231984 | tf_op jit(solution)/shard_map/qkr,lrh->lhqk/dot_general | solution.py:340
  45.4 3.6 %collective-permute-done.10.refs_7_ = bf16[96,1536]{1,0:T(8,128)(2,1)} collective-permute-done((bf16[96,1536]{1,0:T(8,128)(2,1)S(1)}, bf16[96,1536]{1,0:T(8,128)(2,1)}, u32[]{:S(2)}, u32[]{:S(2)}) %collective-permute-start.10) | collective-permute-done | bytes 294944 | tf_op jit(solution)/shard_map/ppermute | solution.py:27
  50.8 5.8 %products.1 = (bf16[256,1536]{1,0:T(8,128)(2,1)}, bf16[256,1536]{1,0:T(8,128)(2,1)}, bf16[768,1536]{1,0:T(8,128)(2,1)}) custom-call(s32[8]{0:T(128)} %stack.120.place_ref, bf16[2,768,128]{2,1,0:T(8,128)(2,1)} %copy-done.4, bf16[2,768,128]{2,1,0:T(8,128)(2,1)} %copy-done.10, bf16[2,768,128]{2,1,0:T(8,128)(2,1)} %copy-done.6, bf16[2,768,128]{2,1,0:T(8,128)(2,1)} %copy-done.8, ...), custom_call_target="tpu_custom_call" | custom-call | flops 1200000000 | bytes 9000000 | tf_op jit(solution)/shard_map/products/pallas_call | solution.py:348
  56.7 2.5 %collective-permute-done.13.came_ref = bf16[256,1536]{1,0:T(8,128)(2,1)S(1)} collective-permute-done((bf16[256,1536]{1,0:T(8,128)(2,1)}, bf16[256,1536]{1,0:T(8,128)(2,1)S(1)}, u32[]{:S(2)}, u32[]{:S(2)}) %collective-permute-start.13) | collective-permute-done | bytes 786464 | tf_op jit(solution)/shard_map/ppermute | solution.py:27
  59.2 0.9 copy-done.19
  60.3 4.1 %attention.1.grad_ref.refs_4_ = bf16[256,1536]{1,0:T(8,128)(2,1)} custom-call(bf16[256,1536]{1,0:T(8,128)(2,1)} %get-tuple-element.41.kept_ref, bf16[256,1536]{1,0:T(8,128)(2,1)} %copy-done.19, f32[2,3,128,64]{3,2,1,0:T(8,128)} %bitcast.52), custom_call_target="tpu_custom_call" | custom-call | flops 1000000000 | bytes 4000000 | tf_op jit(solution)/shard_map/attention/pallas_call | solution.py:369
  65.7 1.1 copy-done.3
  66.8 3.8 %projections.1 = (f32[128,3072]{1,0:T(8,128)S(1)}, bf16[128,3072]{1,0:T(8,128)(2,1)S(1)}) custom-call(s32[16]{0:T(128)S(1)} %stack.111.place_ref, bf16[256,1536]{1,0:T(8,128)(2,1)S(1)} %copy-done.3, bf16[768,1536]{1,0:T(8,128)(2,1)S(1)} %copy-done.1, bf16[768,1536]{1,0:T(8,128)(2,1)S(1)} %collective-permute-done.14.theirs_ref), custom_call_target="tpu_custom_call" | custom-call | flops 1200000000 | bytes 8000000 | tf_op jit(solution)/shard_map/projections/pallas_call | solution.py:382
  70.7 2.8 %collective-permute-start.15 = (bf16[128,3072]{1,0:T(8,128)(2,1)S(1)}, bf16[128,3072]{1,0:T(8,128)(2,1)S(1)}, u32[]{:S(2)}, u32[]{:S(2)}) collective-permute-start(bf16[128,3072]{1,0:T(8,128)(2,1)S(1)} %get-tuple-element.46), channel_id=1, source_target_pairs={{0,4},{4,0},{1,5},{5,1},{2,6},{6,2},{3,7},{7,3},{8,12},{12,8},{9,1... | collective-permute-start | bytes 2359304 | tf_op jit(solution)/shard_map/ppermute | solution.py:27
  73.5 2.7 %weight_gradient.1 = (bf16[96,1536]{1,0:T(8,128)(2,1)S(1)}, bf16[96,1536]{1,0:T(8,128)(2,1)S(1)}, bf16[96,1536]{1,0:T(8,128)(2,1)S(1)}, bf16[96,1536]{1,0:T(8,12...) custom-call(s32[1]{0:T(128)} %bitcast.34.near_ref, ...), custom_call_target="tpu_custom_call" | custom-call | flops 1200000000 | bytes 6000000 | tf_op jit(solution)/shard_map/weight_gradient/pallas_call | solution.py:396
  76.7 8.4 %collective-permute-done.18 = bf16[96,1536]{1,0:T(8,128)(2,1)S(1)} collective-permute-done((bf16[96,1536]{1,0:T(8,128)(2,1)S(1)}, bf16[96,1536]{1,0:T(8,128)(2,1)S(1)}, u32[]{:S(2)}, u32[]{:S(2)}) %collective-permute-start.18) | collective-permute-done | bytes 294944 | tf_op jit(solution)/shard_map/ppermute | solution.py:27
  85.6 3.4 %collective-permute-start.19 = (bf16[96,1536]{1,0:T(8,128)(2,1)S(1)}, bf16[96,1536]{1,0:T(8,128)(2,1)S(1)}, u32[]{:S(2)}, u32[]{:S(2)}) collective-permute-start(bf16[96,1536]{1,0:T(8,128)(2,1)S(1)} %add_convert_fusion.4), channel_id=1, source_target_pairs={{0,8},{8,0},{1,9},{9,1},{2,10},{10,2},{3,11},{11,3},{4,12},{12,4},... | collective-permute-start | bytes 884744 | tf_op jit(solution)/shard_map/ppermute | solution.py:27
  89.0 4.0 %collective-permute-done.20 = bf16[96,1536]{1,0:T(8,128)(2,1)S(1)} collective-permute-done((bf16[96,1536]{1,0:T(8,128)(2,1)S(1)}, bf16[96,1536]{1,0:T(8,128)(2,1)S(1)}, u32[]{:S(2)}, u32[]{:S(2)}) %collective-permute-start.20) | collective-permute-done | bytes 294944 | tf_op jit(solution)/shard_map/ppermute | solution.py:27
  93.4 3.6 %collective-permute-done.15 = bf16[128,3072]{1,0:T(8,128)(2,1)S(1)} collective-permute-done((bf16[128,3072]{1,0:T(8,128)(2,1)S(1)}, bf16[128,3072]{1,0:T(8,128)(2,1)S(1)}, u32[]{:S(2)}, u32[]{:S(2)}) %collective-permute-start.15) | collective-permute-done | bytes 786464 | tf_op jit(solution)/shard_map/ppermute | solution.py:27
  97.2 13.1 %collective-permute-done.19 = bf16[96,1536]{1,0:T(8,128)(2,1)S(1)} collective-permute-done((bf16[96,1536]{1,0:T(8,128)(2,1)S(1)}, bf16[96,1536]{1,0:T(8,128)(2,1)S(1)}, u32[]{:S(2)}, u32[]{:S(2)}) %collective-permute-start.19) | collective-permute-done | bytes 294944 | tf_op jit(solution)/shard_map/ppermute | solution.py:27
  110.9 10.5 %collective-permute-done.24 = bf16[96,1536]{1,0:T(8,128)(2,1)S(1)} collective-permute-done((bf16[96,1536]{1,0:T(8,128)(2,1)S(1)}, bf16[96,1536]{1,0:T(8,128)(2,1)S(1)}, u32[]{:S(2)}, u32[]{:S(2)}) %collective-permute-start.24) | collective-permute-done | bytes 294944 | tf_op jit(solution)/shard_map/ppermute | solution.py:27
  121.5 4.2 %convolution_convert_fusion = bf16[128,3072]{1,0:T(8,128)(2,1)S(1)} fusion(bf16[128,3072]{1,0:T(8,128)(2,1)S(1)} %add_convert_fusion, bf16[128,3072]{1,0:T(8,128)(2,1)} %collective-permute-done.16, s32[]{:T(128)} %bitcast.4, s32[]{:T(128)} %bitcast.3, s32[128]{0:T(128)S(1)} %get-tuple-element.93, s32[128]{0:T(128)S(1)} %get-tuple-element.95, s32[]{:T(128)} %bitcast.2, ...), kind=kOutput, calls=%fused_computation.3 | convolution fusion | flops 206700544 | bytes 2362768 | tf_op jit(solution)/shard_map/dot_general | solution.py:52
  126.0 1.4 %fusion.18 = (bf16[128,1536]{1,0:T(8,128)(2,1)}, bf16[128,1536]{1,0:T(8,128)(2,1)}) fusion(f32[128]{0:T(128)S(1)} %broadcast_multiply_fusion.2, f32[128]{0:T(128)S(1)} %div.55, f32[128]{0:T(128)S(1)} %broadcast_multiply_fusion.3, f32[1536]{0:T(1024)S(1)} %copy-done.15, f32[128]{0:T(128)S(1)} %rsqrt.12, bf16[128,3072]{1,0:T(8,128)(2,1)S(1)} %convolution_convert_fusion, ...), kind=kLoop, calls=%fused_computation.22 | loop fusion | flops 2949120 | bytes 2367488 | tf_op jit(solution)/shard_map/convert_element_type | solution.py:435
  127.7 1.1 broadcast_multiply_fusion
  (118 shorter events, 10.6 us)
Async XLA Ops:
  0.6 40.6 %copy-start = (f32[2,225,12]{1,0,2:T(2,128)S(1)}, f32[2,225,12]{1,0,2:T(2,128)}, u32[]{:S(2)}) copy-start(f32[2,225,12]{1,0,2:T(2,128)} %param.16) | copy-start | bytes 64804
  2.0 8.8 %collective-permute-start.3 = (bf16[96,1536]{1,0:T(8,128)(2,1)S(1)}, bf16[96,1536]{1,0:T(8,128)(2,1)S(1)}, u32[]{:S(2)}, u32[]{:S(2)}) collective-permute-start(bf16[96,1536]{1,0:T(8,128)(2,1)S(1)} %broadcast_select_fusion), channel_id=1, source_target_pairs={{0,4},{4,0},{1,5},{5,1},{2,6},{6,2},{3,7},{7,3},{8,12},{12,8},{9,1... | collective-permute-start | bytes 884744 | tf_op jit(solution)/shard_map/ppermute | solution.py:27
  3.9 18.3 %copy-start.18 = (s32[2,2]{1,0:T(2,128)S(1)}, s32[2,2]{1,0:T(2,128)}, u32[]{:S(2)}) copy-start(s32[2,2]{1,0:T(2,128)} %param.14) | copy-start | bytes 52
  3.9 18.4 %copy-start.15 = (f32[1536]{0:T(1024)S(1)}, f32[1536]{0:T(1024)}, u32[]{:S(2)}) copy-start(f32[1536]{0:T(1024)} %param.12) | copy-start | bytes 18436
  4.1 10.2 %collective-permute-start = (bf16[128,1536]{1,0:T(8,128)(2,1)S(1)}, bf16[128,1536]{1,0:T(8,128)(2,1)S(1)}, u32[]{:S(2)}, u32[]{:S(2)}) collective-permute-start(bf16[128,1536]{1,0:T(8,128)(2,1)S(1)} %bitcast.48), channel_id=1, source_target_pairs={{0,15},{1,0},{2,1},{3,2},{4,3},{5,4},{6,5},{7,6},{8,7},{9,8},{10,9... | collective-permute-start | bytes 1179656 | tf_op jit(solution)/shard_map/ppermute | solution.py:18
  4.1 10.2 %collective-permute-start.1 = (bf16[128,1536]{1,0:T(8,128)(2,1)S(1)}, bf16[128,1536]{1,0:T(8,128)(2,1)S(1)}, u32[]{:S(2)}, u32[]{:S(2)}) collective-permute-start(bf16[128,1536]{1,0:T(8,128)(2,1)S(1)} %bitcast.50), channel_id=1, source_target_pairs={{0,15},{1,0},{2,1},{3,2},{4,3},{5,4},{6,5},{7,6},{8,7},{9,8},{10,9... | collective-permute-start | bytes 1179656 | tf_op jit(solution)/shard_map/ppermute | solution.py:18
  10.9 29.0 %copy-start.13 = (bf16[96,1536]{1,0:T(8,128)(2,1)}, bf16[96,1536]{1,0:T(8,128)(2,1)S(1)}, u32[]{:S(2)}) copy-start(bf16[96,1536]{1,0:T(8,128)(2,1)S(1)} %collective-permute-done.3.refs_5_) | copy-start | bytes 884740
  11.7 32.2 %copy-start.14 = (bf16[96,1536]{1,0:T(8,128)(2,1)}, bf16[96,1536]{1,0:T(8,128)(2,1)S(1)}, u32[]{:S(2)}) copy-start(bf16[96,1536]{1,0:T(8,128)(2,1)S(1)} %get-tuple-element.36.refs_4_) | copy-start | bytes 884740
  11.7 29.5 %copy-start.21 = (s32[64,64]{1,0:T(8,128)S(1)}, s32[64,64]{1,0:T(8,128)}, u32[]{:S(2)}) copy-start(s32[64,64]{1,0:T(8,128)} %param.15) | copy-start | bytes 49156
  11.7 15.5 %collective-permute-start.4 = (bf16[96,1536]{1,0:T(8,128)(2,1)}, bf16[96,1536]{1,0:T(8,128)(2,1)}, u32[]{:S(2)}, u32[]{:S(2)}) collective-permute-start(bf16[96,1536]{1,0:T(8,128)(2,1)} %get-tuple-element.69), channel_id=1, source_target_pairs={{0,8},{8,0},{1,9},{9,1},{2,10},{10,2},{3,11},{11,3},{4,12},{12,4},... | collective-permute-start | bytes 884744 | tf_op jit(solution)/shard_map/ppermute | solution.py:27
  14.3 15.6 %collective-permute-start.5 = (bf16[96,1536]{1,0:T(8,128)(2,1)S(1)}, bf16[96,1536]{1,0:T(8,128)(2,1)S(1)}, u32[]{:S(2)}, u32[]{:S(2)}) collective-permute-start(bf16[96,1536]{1,0:T(8,128)(2,1)S(1)} %get-tuple-element.36.refs_4_), channel_id=1, source_target_pairs={{0,2},{2,0},{1,3},{3,1},{4,6},{6,4},{5,7},{7,5},{8,10},{10,8},{9,1... | collective-permute-start | bytes 884744 | tf_op jit(solution)/shard_map/ppermute | solution.py:27
  24.7 20.0 %copy-start.4 = (bf16[2,768,128]{2,1,0:T(8,128)(2,1)}, bf16[2,768,128]{2,1,0:T(8,128)(2,1)S(1)}, u32[]{:S(2)}) copy-start(bf16[2,768,128]{2,1,0:T(8,128)(2,1)S(1)} %get-tuple-element.34.refs_0_) | copy-start | bytes 1179652
  24.8 11.7 %collective-permute-start.2 = (bf16[2,768,128]{2,1,0:T(8,128)(2,1)S(1)}, bf16[2,768,128]{2,1,0:T(8,128)(2,1)}, u32[]{:S(2)}, u32[]{:S(2)}) collective-permute-start(bf16[2,768,128]{2,1,0:T(8,128)(2,1)S(1)} %get-tuple-element.38), channel_id=1, source_target_pairs={{0,4},{4,0},{1,5},{5,1},{2,6},{6,2},{3,7},{7,3},{8,12},{12,8},{9,1... | collective-permute-start | bytes 1179656 | tf_op jit(solution)/shard_map/ppermute | solution.py:27
  29.9 9.4 %collective-permute-start.6 = (bf16[96,1536]{1,0:T(8,128)(2,1)}, bf16[96,1536]{1,0:T(8,128)(2,1)}, u32[]{:S(2)}, u32[]{:S(2)}) collective-permute-start(bf16[96,1536]{1,0:T(8,128)(2,1)} %collective-permute-done.4.refs_8_), channel_id=1, source_target_pairs={{0,16},{16,0},{1,17},{17,1},{2,18},{18,2},{3,19},{19,3},{4,20},{20... | collective-permute-start | bytes 884744 | tf_op jit(solution)/shard_map/ppermute | solution.py:27
  30.2 9.7 %collective-permute-start.11 = (bf16[96,1536]{1,0:T(8,128)(2,1)}, bf16[96,1536]{1,0:T(8,128)(2,1)}, u32[]{:S(2)}, u32[]{:S(2)}) collective-permute-start(bf16[96,1536]{1,0:T(8,128)(2,1)} %collective-permute-done.4.refs_8_), channel_id=1, source_target_pairs={{0,2},{2,0},{1,3},{3,1},{4,6},{6,4},{5,7},{7,5},{8,10},{10,8},{9,1... | collective-permute-start | bytes 884744 | tf_op jit(solution)/shard_map/ppermute | solution.py:27
  31.0 14.4 %collective-permute-start.8 = (bf16[2,768,128]{2,1,0:T(8,128)(2,1)S(1)}, bf16[2,768,128]{2,1,0:T(8,128)(2,1)S(1)}, u32[]{:S(2)}, u32[]{:S(2)}) collective-permute-start(bf16[2,768,128]{2,1,0:T(8,128)(2,1)S(1)} %get-tuple-element.34.refs_0_), channel_id=1, source_target_pairs={{0,4},{4,0},{1,5},{5,1},{2,6},{6,2},{3,7},{7,3},{8,12},{12,8},{9,1... | collective-permute-start | bytes 1179656 | tf_op jit(solution)/shard_map/ppermute | solution.py:27
  39.3 10.0 %collective-permute-start.9 = (bf16[2,768,128]{2,1,0:T(8,128)(2,1)}, bf16[2,768,128]{2,1,0:T(8,128)(2,1)S(1)}, u32[]{:S(2)}, u32[]{:S(2)}) collective-permute-start(bf16[2,768,128]{2,1,0:T(8,128)(2,1)} %collective-permute-done.2), channel_id=1, source_target_pairs={{0,1},{1,0},{2,3},{3,2},{4,5},{5,4},{6,7},{7,6},{8,9},{9,8},{10,11... | collective-permute-start | bytes 1179656 | tf_op jit(solution)/shard_map/ppermute | solution.py:27
  39.3 10.0 %collective-permute-start.7 = (bf16[2,768,128]{2,1,0:T(8,128)(2,1)S(1)}, bf16[2,768,128]{2,1,0:T(8,128)(2,1)S(1)}, u32[]{:S(2)}, u32[]{:S(2)}) collective-permute-start(bf16[2,768,128]{2,1,0:T(8,128)(2,1)S(1)} %get-tuple-element.38), channel_id=1, source_target_pairs={{0,1},{1,0},{2,3},{3,2},{4,5},{5,4},{6,7},{7,6},{8,9},{9,8},{10,11... | collective-permute-start | bytes 1179656 | tf_op jit(solution)/shard_map/ppermute | solution.py:27
  39.9 9.1 %collective-permute-start.10 = (bf16[96,1536]{1,0:T(8,128)(2,1)S(1)}, bf16[96,1536]{1,0:T(8,128)(2,1)}, u32[]{:S(2)}, u32[]{:S(2)}) collective-permute-start(bf16[96,1536]{1,0:T(8,128)(2,1)S(1)} %collective-permute-done.3.refs_5_), channel_id=1, source_target_pairs={{0,2},{2,0},{1,3},{3,1},{4,6},{6,4},{5,7},{7,5},{8,10},{10,8},{9,1... | collective-permute-start | bytes 884744 | tf_op jit(solution)/shard_map/ppermute | solution.py:27
  40.0 9.3 %collective-permute-start.12 = (bf16[96,1536]{1,0:T(8,128)(2,1)}, bf16[96,1536]{1,0:T(8,128)(2,1)}, u32[]{:S(2)}, u32[]{:S(2)}) collective-permute-start(bf16[96,1536]{1,0:T(8,128)(2,1)} %collective-permute-done.11.refs_10_), channel_id=1, source_target_pairs={{0,16},{16,0},{1,17},{17,1},{2,18},{18,2},{3,19},{19,3},{4,20},{20... | collective-permute-start | bytes 884744 | tf_op jit(solution)/shard_map/ppermute | solution.py:27
  56.6 2.6 %collective-permute-start.13 = (bf16[256,1536]{1,0:T(8,128)(2,1)}, bf16[256,1536]{1,0:T(8,128)(2,1)S(1)}, u32[]{:S(2)}, u32[]{:S(2)}) collective-permute-start(bf16[256,1536]{1,0:T(8,128)(2,1)} %get-tuple-element.42), channel_id=1, source_target_pairs={{0,1},{1,0},{2,3},{3,2},{4,5},{5,4},{6,7},{7,6},{8,9},{9,8},{10,11... | collective-permute-start | bytes 2359304 | tf_op jit(solution)/shard_map/ppermute | solution.py:27
  60.1 5.6 %collective-permute-start.14 = (bf16[768,1536]{1,0:T(8,128)(2,1)}, bf16[768,1536]{1,0:T(8,128)(2,1)S(1)}, u32[]{:S(2)}, u32[]{:S(2)}) collective-permute-start(bf16[768,1536]{1,0:T(8,128)(2,1)} %get-tuple-element.44.mine_ref), channel_id=1, source_target_pairs={{0,1},{1,0},{2,3},{3,2},{4,5},{5,4},{6,7},{7,6},{8,9},{9,8},{10,11... | collective-permute-start | bytes 7077896 | tf_op jit(solution)/shard_map/ppermute | solution.py:27
  64.4 9.1 %collective-permute-start.17 = (bf16[256,1536]{1,0:T(8,128)(2,1)}, bf16[256,1536]{1,0:T(8,128)(2,1)S(1)}, u32[]{:S(2)}, u32[]{:S(2)}) collective-permute-start(bf16[256,1536]{1,0:T(8,128)(2,1)} %attention.1.grad_ref.refs_4_), channel_id=1, source_target_pairs={{0,1},{1,0},{2,3},{3,2},{4,5},{5,4},{6,7},{7,6},{8,9},{9,8},{10,11... | collective-permute-start | bytes 2359304 | tf_op jit(solution)/shard_map/ppermute | solution.py:27
  70.7 26.3 %collective-permute-start.15 = (bf16[128,3072]{1,0:T(8,128)(2,1)S(1)}, bf16[128,3072]{1,0:T(8,128)(2,1)S(1)}, u32[]{:S(2)}, u32[]{:S(2)}) collective-permute-start(bf16[128,3072]{1,0:T(8,128)(2,1)S(1)} %get-tuple-element.46), channel_id=1, source_target_pairs={{0,4},{4,0},{1,5},{5,1},{2,6},{6,2},{3,7},{7,3},{8,12},{12,8},{9,1... | collective-permute-start | bytes 2359304 | tf_op jit(solution)/shard_map/ppermute | solution.py:27
  76.3 8.8 %collective-permute-start.18 = (bf16[96,1536]{1,0:T(8,128)(2,1)S(1)}, bf16[96,1536]{1,0:T(8,128)(2,1)S(1)}, u32[]{:S(2)}, u32[]{:S(2)}) collective-permute-start(bf16[96,1536]{1,0:T(8,128)(2,1)S(1)} %get-tuple-element.49), channel_id=1, source_target_pairs={{0,2},{2,0},{1,3},{3,1},{4,6},{6,4},{5,7},{7,5},{8,10},{10,8},{9,1... | collective-permute-start | bytes 884744 | tf_op jit(solution)/shard_map/ppermute | solution.py:27
  85.1 7.9 %collective-permute-start.20 = (bf16[96,1536]{1,0:T(8,128)(2,1)S(1)}, bf16[96,1536]{1,0:T(8,128)(2,1)S(1)}, u32[]{:S(2)}, u32[]{:S(2)}) collective-permute-start(bf16[96,1536]{1,0:T(8,128)(2,1)S(1)} %get-tuple-element.53), channel_id=1, source_target_pairs={{0,2},{2,0},{1,3},{3,1},{4,6},{6,4},{5,7},{7,5},{8,10},{10,8},{9,1... | collective-permute-start | bytes 884744 | tf_op jit(solution)/shard_map/ppermute | solution.py:27
  85.6 24.7 %collective-permute-start.19 = (bf16[96,1536]{1,0:T(8,128)(2,1)S(1)}, bf16[96,1536]{1,0:T(8,128)(2,1)S(1)}, u32[]{:S(2)}, u32[]{:S(2)}) collective-permute-start(bf16[96,1536]{1,0:T(8,128)(2,1)S(1)} %add_convert_fusion.4), channel_id=1, source_target_pairs={{0,8},{8,0},{1,9},{9,1},{2,10},{10,2},{3,11},{11,3},{4,12},{12,4},... | collective-permute-start | bytes 884744 | tf_op jit(solution)/shard_map/ppermute | solution.py:27
  93.0 17.2 %collective-permute-start.22 = (bf16[96,1536]{1,0:T(8,128)(2,1)S(1)}, bf16[96,1536]{1,0:T(8,128)(2,1)S(1)}, u32[]{:S(2)}, u32[]{:S(2)}) collective-permute-start(bf16[96,1536]{1,0:T(8,128)(2,1)S(1)} %get-tuple-element.59), channel_id=1, source_target_pairs={{0,2},{2,0},{1,3},{3,1},{4,6},{6,4},{5,7},{7,5},{8,10},{10,8},{9,1... | collective-permute-start | bytes 884744 | tf_op jit(solution)/shard_map/ppermute | solution.py:27
  97.1 24.3 %collective-permute-start.16 = (bf16[128,3072]{1,0:T(8,128)(2,1)S(1)}, bf16[128,3072]{1,0:T(8,128)(2,1)}, u32[]{:S(2)}, u32[]{:S(2)}) collective-permute-start(bf16[128,3072]{1,0:T(8,128)(2,1)S(1)} %add_convert_fusion), channel_id=1, source_target_pairs={{0,1},{1,2},{2,3},{3,4},{4,5},{5,6},{6,7},{7,8},{8,9},{9,10},{10,1... | collective-permute-start | bytes 2359304 | tf_op jit(solution)/shard_map/ppermute | solution.py:18
  110.4 11.0 %collective-permute-start.24 = (bf16[96,1536]{1,0:T(8,128)(2,1)S(1)}, bf16[96,1536]{1,0:T(8,128)(2,1)S(1)}, u32[]{:S(2)}, u32[]{:S(2)}) collective-permute-start(bf16[96,1536]{1,0:T(8,128)(2,1)S(1)} %add_convert_fusion.2), channel_id=1, source_target_pairs={{0,4},{4,0},{1,5},{5,1},{2,6},{6,2},{3,7},{7,3},{8,12},{12,8},{9,1... | collective-permute-start | bytes 884744 | tf_op jit(solution)/shard_map/ppermute | solution.py:27
  110.6 15.1 %collective-permute-start.21 = (bf16[96,1536]{1,0:T(8,128)(2,1)S(1)}, bf16[96,1536]{1,0:T(8,128)(2,1)S(1)}, u32[]{:S(2)}, u32[]{:S(2)}) collective-permute-start(bf16[96,1536]{1,0:T(8,128)(2,1)S(1)} %add_convert_fusion.3), channel_id=1, source_target_pairs={{0,8},{8,0},{1,9},{9,1},{2,10},{10,2},{3,11},{11,3},{4,12},{12,4},... | collective-permute-start | bytes 884744 | tf_op jit(solution)/shard_map/ppermute | solution.py:27
  110.8 16.6 %collective-permute-start.23 = (bf16[96,1536]{1,0:T(8,128)(2,1)S(1)}, bf16[96,1536]{1,0:T(8,128)(2,1)S(1)}, u32[]{:S(2)}, u32[]{:S(2)}) collective-permute-start(bf16[96,1536]{1,0:T(8,128)(2,1)S(1)} %get-tuple-element.60), channel_id=1, source_target_pairs={{0,2},{2,0},{1,3},{3,1},{4,6},{6,4},{5,7},{7,5},{8,10},{10,8},{9,1... | collective-permute-start | bytes 884744 | tf_op jit(solution)/shard_map/ppermute | solution.py:27
  (15 other events, 51.9 us)
